TPU v7x, 32 devices: a whole 2x2x4 slice. The times are simulated.
32 devices in a mesh: dp: 4 (over y, x), ctx: 8 (over z, core).
Axes of the slice: x: 2, y: 2, z: 4, core: 2. Of those that a mesh axis runs over, the one named last changes fastest.
Arguments:
- queries: bfloat16 [4, 1024, 4096], P('dp', 'ctx'), may hold values from -5 to 5
- query_tangent: bfloat16 [4, 1024, 4096], P('dp', 'ctx'), may hold values from -6 to 6
- keys: bfloat16 [4, 512, 4096], P('dp', 'ctx'), may hold values from -5 to 5
- key_tangent: bfloat16 [4, 512, 4096], P('dp', 'ctx'), may hold values from -6 to 6
- values: bfloat16 [4, 512, 4096], P('dp', 'ctx'), may hold values from -6 to 6
- value_tangent: bfloat16 [4, 512, 4096], P('dp', 'ctx'), may hold values from -6 to 6
- out_gain: bfloat16 [4096], replicated, may hold values from 0.5 to 2
- grad_y: bfloat16 [4, 1024, 4096], P('dp', 'ctx'), may hold values from -6 to 6
- grad_y_tan: bfloat16 [4, 1024, 4096], P('dp', 'ctx'), may hold values from -6 to 6
Outputs:
- query_gradient: bfloat16 [4, 1024, 4096], P('dp', 'ctx')
- query_tangent_gradient: bfloat16 [4, 1024, 4096], P('dp', 'ctx')
- key_gradient: bfloat16 [4, 512, 4096], P('dp', 'ctx')
- key_tangent_gradient: bfloat16 [4, 512, 4096], P('dp', 'ctx')
- value_gradient: bfloat16 [4, 512, 4096], P('dp', 'ctx')
- value_tangent_gradient: bfloat16 [4, 512, 4096], P('dp', 'ctx')
- gain_grad: float32 [4096], P('ctx')
All inputs are finite; a program needn't handle non-finite values.
Results may differ from a plain program's by a relative error of at most 0.0076.
Values may be sent and summed in bfloat16 or wider, within the bound.
No kernel may reach another device: no remote copies, remote signals or barrier semaphores. Data moves between devices by JAX's collectives and lax.ppermute only.
A program may use at most 128 MiB of HBM per device.

v0:
```python
import math

import jax
import jax.numpy as jnp
from jax import lax
from jax.sharding import PartitionSpec as P

HEAD_DIM = 128


def inner_product(pattern, left_op, right_op):
    return jnp.einsum(pattern, left_op, right_op, preferred_element_type=jnp.float32)


def block_terms(
    query_block,
    query_tangents,
    output_gradient,
    tangent_gradient,
    every_key,
    key_tangents,
    every_value,
    value_tangents,
    scale_factor,
):
    score_matrix = inner_product("zqc,pqc->qzp", query_block, every_key) * scale_factor
    score_tangent = (
        inner_product("zqc,pqc->qzp", query_tangents, every_key)
        + inner_product("zqc,pqc->qzp", query_block, key_tangents)
    ) * scale_factor
    row_max = jnp.max(score_matrix, axis=-1, keepdims=True)
    raised = jnp.exp(score_matrix - row_max)
    weights = raised / jnp.sum(raised, axis=-1, keepdims=True)
    offset = jnp.sum(weights * score_tangent, axis=-1, keepdims=True)
    weights_tan = weights * (score_tangent - offset)
    weight_reduced = weights.astype(jnp.bfloat16)
    tangent_reduced = weights_tan.astype(jnp.bfloat16)
    attention_output = inner_product("gsf,fgn->sgn", weight_reduced, every_value).astype(
        jnp.bfloat16
    )
    attention_tangent = (
        inner_product("gsf,fgn->sgn", tangent_reduced, every_value)
        + inner_product("gsf,fgn->sgn", weight_reduced, value_tangents)
    ).astype(jnp.bfloat16)
    weight_gradient = inner_product("zqc,pqc->qzp", output_gradient, every_value) + inner_product(
        "zqc,pqc->qzp", tangent_gradient, value_tangents
    )
    weight_tangent_gradient = inner_product("zqc,pqc->qzp", tangent_gradient, every_value)
    inner_sum = jnp.sum(weights * weight_tangent_gradient, axis=-1, keepdims=True)
    d_scores_tan = weights * (weight_tangent_gradient - inner_sum)
    totals = (
        weight_gradient
        + weight_tangent_gradient * (score_tangent - offset)
        - inner_sum * score_tangent
    )
    d_scores = weights * (totals - jnp.sum(weights * totals, axis=-1, keepdims=True))
    score_reduced = d_scores.astype(jnp.bfloat16)
    score_tangent_reduced = d_scores_tan.astype(jnp.bfloat16)
    query_gradient = (
        scale_factor
        * (
            inner_product("gsf,fgn->sgn", score_reduced, every_key)
            + inner_product("gsf,fgn->sgn", score_tangent_reduced, key_tangents)
        )
    ).astype(jnp.bfloat16)
    query_tangent_gradient = (
        scale_factor * inner_product("gsf,fgn->sgn", score_tangent_reduced, every_key)
    ).astype(jnp.bfloat16)
    key_gradient = scale_factor * (
        inner_product("cia,ick->ack", score_reduced, query_block)
        + inner_product("cia,ick->ack", score_tangent_reduced, query_tangents)
    )
    key_tangent_gradient = scale_factor * inner_product(
        "cia,ick->ack", score_tangent_reduced, query_block
    )
    value_gradient = inner_product("cia,ick->ack", weight_reduced, output_gradient) + inner_product(
        "cia,ick->ack", tangent_reduced, tangent_gradient
    )
    value_tangent_gradient = inner_product("cia,ick->ack", weight_reduced, tangent_gradient)
    return (
        (query_gradient, query_tangent_gradient, attention_output, attention_tangent),
        (key_gradient, key_tangent_gradient, value_gradient, value_tangent_gradient),
    )


def attention_grads(
    query_block,
    query_tangents,
    output_gradient,
    tangent_gradient,
    every_key,
    key_tangents,
    every_value,
    value_tangents,
):
    count = query_block.shape[0]
    block_rows = min(512, count)
    blocks = count // block_rows
    scale_factor = 1.0 / math.sqrt(query_block.shape[2])

    def advance(running, pieces):
        row_out, col_out = block_terms(
            pieces[0],
            pieces[1],
            pieces[2],
            pieces[3],
            every_key,
            key_tangents,
            every_value,
            value_tangents,
            scale_factor,
        )
        return (
            tuple((left_sum + right_sum for left_sum, right_sum in zip(running, col_out))),
            row_out,
        )

    zeros_init = jnp.zeros(every_key.shape, jnp.float32)
    split_rows = tuple(
        (
            array.reshape((blocks, block_rows) + array.shape[1:])
            for array in (query_block, query_tangents, output_gradient, tangent_gradient)
        )
    )
    running, row_out = lax.scan(
        advance, (zeros_init, zeros_init, zeros_init, zeros_init), split_rows
    )
    row_out = tuple((array.reshape((count,) + array.shape[2:]) for array in row_out))
    return (row_out, tuple((array.astype(jnp.bfloat16) for array in running)))


def per_device(
    queries, query_tangent, keys, key_tangent, values, value_tangent, out_gain, grad_y, grad_y_tan
):
    group_count = lax.axis_size("ctx")
    channels = queries.shape[2]
    local_heads = channels // (HEAD_DIM * group_count)

    def regroup(array):
        return array[0].reshape(array.shape[1], group_count, local_heads, HEAD_DIM)

    def tokens_back(array):
        return array.reshape(1, array.shape[0], channels)

    gain_rows = out_gain.reshape(1, group_count, local_heads, HEAD_DIM)
    pieces = (
        lax.all_to_all(regroup(queries), "ctx", split_axis=1, concat_axis=0, tiled=True),
        lax.all_to_all(regroup(query_tangent), "ctx", split_axis=1, concat_axis=0, tiled=True),
        lax.all_to_all(regroup(grad_y), "ctx", split_axis=1, concat_axis=0, tiled=True),
        lax.all_to_all(regroup(grad_y_tan), "ctx", split_axis=1, concat_axis=0, tiled=True),
        lax.all_to_all(regroup(keys), "ctx", split_axis=1, concat_axis=0, tiled=True),
        lax.all_to_all(regroup(key_tangent), "ctx", split_axis=1, concat_axis=0, tiled=True),
        lax.all_to_all(regroup(values), "ctx", split_axis=1, concat_axis=0, tiled=True),
        lax.all_to_all(regroup(value_tangent), "ctx", split_axis=1, concat_axis=0, tiled=True),
        lax.all_to_all(gain_rows, "ctx", split_axis=1, concat_axis=0, tiled=True),
    )
    unpack_pieces = pieces[:8]
    query_rows, query_tangents, cot_rows, cot_tan, key_rows, key_tan, value_rows, value_tan = tuple(
        (piece[:, 0] for piece in unpack_pieces)
    )
    gain_copy = pieces[8][0, 0].astype(jnp.float32)
    output_gradient = (cot_rows.astype(jnp.float32) * gain_copy).astype(jnp.bfloat16)
    tangent_gradient = (cot_tan.astype(jnp.float32) * gain_copy).astype(jnp.bfloat16)
    row_out, col_out = attention_grads(
        query_rows,
        query_tangents,
        output_gradient,
        tangent_gradient,
        key_rows,
        key_tan,
        value_rows,
        value_tan,
    )
    partial_value = jnp.sum(
        cot_rows.astype(jnp.float32) * row_out[2].astype(jnp.float32)
        + cot_tan.astype(jnp.float32) * row_out[3].astype(jnp.float32),
        axis=0,
    )
    returned = (
        lax.all_to_all(row_out[0][:, None], "ctx", split_axis=0, concat_axis=1, tiled=True),
        lax.all_to_all(row_out[1][:, None], "ctx", split_axis=0, concat_axis=1, tiled=True),
        lax.all_to_all(col_out[0][:, None], "ctx", split_axis=0, concat_axis=1, tiled=True),
        lax.all_to_all(col_out[1][:, None], "ctx", split_axis=0, concat_axis=1, tiled=True),
        lax.all_to_all(col_out[2][:, None], "ctx", split_axis=0, concat_axis=1, tiled=True),
        lax.all_to_all(col_out[3][:, None], "ctx", split_axis=0, concat_axis=1, tiled=True),
    )
    gathered = returned + (partial_value[None, None],)
    results = tuple((tokens_back(array) for array in gathered[:6]))
    gain_grad = lax.psum(gathered[6].reshape(local_heads * HEAD_DIM), "dp")
    return (results[0], results[1], results[2], results[3], results[4], results[5], gain_grad)


def solution(mesh):
    placed = (
        P("dp", "ctx", None),
        P("dp", "ctx", None),
        P("dp", "ctx", None),
        P("dp", "ctx", None),
        P("dp", "ctx", None),
        P("dp", "ctx", None),
        P(),
        P("dp", "ctx", None),
        P("dp", "ctx", None),
    )
    return jax.shard_map(
        per_device,
        mesh=mesh,
        in_specs=placed,
        out_specs=(
            P("dp", "ctx", None),
            P("dp", "ctx", None),
            P("dp", "ctx", None),
            P("dp", "ctx", None),
            P("dp", "ctx", None),
            P("dp", "ctx", None),
            P("ctx"),
        ),
        check_vma=False,
    )
```

profile of v0, /device:TPU:8, one launch (start us, length us, event | category | flops | bytes accessed | tf_op | source)
XLA Modules:
  0.0 456.3 jit_solution(2756029445916542119)
XLA Ops:
  16.5 10.8 %all-to-all-done.4 = bf16[64,8,4,128]{3,0,2,1:T(8,128)(2,1)S(1)} async-done(((bf16[64,8,4,128]{3,0,2,1:T(8,128)(2,1)}), bf16[64,8,4,128]{3,0,2,1:T(8,128)(2,1)S(1)}, u32[]{:S(2)}, u32[]{:S(2)}) %all-to-all-start.4) | async-done | bytes 524320 | tf_op jit(solution)/shard_map/all_to_all | solution.py:153
  35.3 10.8 %all-to-all-done.6 = bf16[64,8,4,128]{3,0,2,1:T(8,128)(2,1)S(1)} async-done(((bf16[64,8,4,128]{3,0,2,1:T(8,128)(2,1)}), bf16[64,8,4,128]{3,0,2,1:T(8,128)(2,1)S(1)}, u32[]{:S(2)}, u32[]{:S(2)}) %all-to-all-start.6) | async-done | bytes 524320 | tf_op jit(solution)/shard_map/all_to_all | solution.py:154
  54.1 10.8 %all-to-all-done.8 = bf16[64,8,4,128]{3,0,2,1:T(8,128)(2,1)S(1)} async-done(((bf16[64,8,4,128]{3,0,2,1:T(8,128)(2,1)}), bf16[64,8,4,128]{3,0,2,1:T(8,128)(2,1)S(1)}, u32[]{:S(2)}, u32[]{:S(2)}) %all-to-all-start.8) | async-done | bytes 524320 | tf_op jit(solution)/shard_map/all_to_all | solution.py:152
  64.8 6.6 %all-to-all-start.1 = ((bf16[64,8,4,128]{3,0,2,1:T(8,128)(2,1)}), bf16[64,8,4,128]{3,0,2,1:T(8,128)(2,1)S(1)}, u32[]{:S(2)}, u32[]{:S(2)}) async-start(bf16[64,8,4,128]{3,0,2,1:T(8,128)(2,1)} %copy.204), calls=%async_computation.1 | async-start | bytes 1048576 | tf_op jit(solution)/shard_map/all_to_all | solution.py:151
  72.8 10.8 %all-to-all-done.1 = bf16[64,8,4,128]{3,0,2,1:T(8,128)(2,1)S(1)} async-done(((bf16[64,8,4,128]{3,0,2,1:T(8,128)(2,1)}), bf16[64,8,4,128]{3,0,2,1:T(8,128)(2,1)S(1)}, u32[]{:S(2)}, u32[]{:S(2)}) %all-to-all-start.1) | async-done | bytes 524320 | tf_op jit(solution)/shard_map/all_to_all | solution.py:151
  83.6 6.7 %all-to-all-start.2 = ((bf16[128,8,4,128]{0,3,2,1:T(8,128)(2,1)}), bf16[128,8,4,128]{0,3,2,1:T(8,128)(2,1)S(1)}, u32[]{:S(2)}, u32[]{:S(2)}) async-start(bf16[128,8,4,128]{0,3,2,1:T(8,128)(2,1)} %bitcast.7), calls=%async_computation.2 | async-start | bytes 2097152 | tf_op jit(solution)/shard_map/all_to_all | solution.py:149
  91.6 21.8 %all-to-all-done.2 = bf16[128,8,4,128]{0,3,2,1:T(8,128)(2,1)S(1)} async-done(((bf16[128,8,4,128]{0,3,2,1:T(8,128)(2,1)}), bf16[128,8,4,128]{0,3,2,1:T(8,128)(2,1)S(1)}, u32[]{:S(2)}, u32[]{:S(2)}) %all-to-all-start.2) | async-done | bytes 1048608 | tf_op jit(solution)/shard_map/all_to_all | solution.py:149
  113.5 7.1 %all-to-all-start.5 = ((bf16[128,8,4,128]{0,3,2,1:T(8,128)(2,1)}), bf16[128,8,4,128]{0,3,2,1:T(8,128)(2,1)S(1)}, u32[]{:S(2)}, u32[]{:S(2)}) async-start(bf16[128,8,4,128]{0,3,2,1:T(8,128)(2,1)} %bitcast.17), calls=%async_computation.5 | async-start | bytes 2097152 | tf_op jit(solution)/shard_map/all_to_all | solution.py:150
  121.9 21.8 %all-to-all-done.5 = bf16[128,8,4,128]{0,3,2,1:T(8,128)(2,1)S(1)} async-done(((bf16[128,8,4,128]{0,3,2,1:T(8,128)(2,1)}), bf16[128,8,4,128]{0,3,2,1:T(8,128)(2,1)S(1)}, u32[]{:S(2)}, u32[]{:S(2)}) %all-to-all-start.5) | async-done | bytes 1048608 | tf_op jit(solution)/shard_map/all_to_all | solution.py:150
  143.7 7.0 %all-to-all-start.7 = ((bf16[128,8,4,128]{0,3,2,1:T(8,128)(2,1)}), bf16[128,8,4,128]{0,3,2,1:T(8,128)(2,1)S(1)}, u32[]{:S(2)}, u32[]{:S(2)}) async-start(bf16[128,8,4,128]{0,3,2,1:T(8,128)(2,1)} %bitcast.305), calls=%async_computation.7 | async-start | bytes 2097152 | tf_op jit(solution)/shard_map/all_to_all | solution.py:148
  152.9 20.8 %all-to-all-done.7 = bf16[128,8,4,128]{0,3,2,1:T(8,128)(2,1)S(1)} async-done(((bf16[128,8,4,128]{0,3,2,1:T(8,128)(2,1)}), bf16[128,8,4,128]{0,3,2,1:T(8,128)(2,1)S(1)}, u32[]{:S(2)}, u32[]{:S(2)}) %all-to-all-start.7) | async-done | bytes 1048608 | tf_op jit(solution)/shard_map/all_to_all | solution.py:148
  173.8 7.6 %all-to-all-start = ((bf16[128,8,4,128]{0,3,2,1:T(8,128)(2,1)}), bf16[128,8,4,128]{0,3,2,1:T(8,128)(2,1)}, u32[]{:S(2)}, u32[]{:S(2)}) async-start(bf16[128,8,4,128]{0,3,2,1:T(8,128)(2,1)} %bitcast.304), calls=%async_computation | async-start | bytes 2097152 | tf_op jit(solution)/shard_map/all_to_all | solution.py:147
  196.9 7.6 %all-to-all-done = bf16[128,8,4,128]{0,3,2,1:T(8,128)(2,1)} async-done(((bf16[128,8,4,128]{0,3,2,1:T(8,128)(2,1)}), bf16[128,8,4,128]{0,3,2,1:T(8,128)(2,1)}, u32[]{:S(2)}, u32[]{:S(2)}) %all-to-all-start) | async-done | bytes 1048608 | tf_op jit(solution)/shard_map/all_to_all | solution.py:147
  210.3 97.0 %while.25 = (s32[]{:T(128)}, f32[512,4,128]{0,2,1:T(8,128)}, f32[512,4,128]{0,2,1:T(8,128)}, f32[512,4,128]{0,2,1:T(8,128)}, f32[512,4,128]{0,2,1:T(8,128)}, /*i...) while((s32[]{:T(128)}, f32[512,4,128]{0,2,1:T(8,128)}, ...), condition=%wide.region_6.7_spmd.clone, body=%wide.region_0.6_spmd.clone.sunk | while | flops 4869583360 | bytes 230800624 | solution.py:125
  309.7 7.0 %all-to-all-start.11 = ((bf16[512,1,4,128]{3,2,1,0:T(4,128)(2,1)}), bf16[512,1,4,128]{3,2,1,0:T(4,128)(2,1)S(1)}, u32[]{:S(2)}, u32[]{:S(2)}) async-start(bf16[512,1,4,128]{3,2,1,0:T(4,128)(2,1)} %bitcast.39), calls=%async_computation.11 | async-start | bytes 1048576 | tf_op jit(solution)/shard_map/all_to_all | solution.py:182
  317.8 11.0 %all-to-all-done.11 = bf16[512,1,4,128]{3,2,1,0:T(4,128)(2,1)S(1)} async-done(((bf16[512,1,4,128]{3,2,1,0:T(4,128)(2,1)}), bf16[512,1,4,128]{3,2,1,0:T(4,128)(2,1)S(1)}, u32[]{:S(2)}, u32[]{:S(2)}) %all-to-all-start.11) | async-done | bytes 524320 | tf_op jit(solution)/shard_map/all_to_all | solution.py:182
  328.9 7.3 %all-to-all-start.12 = ((bf16[512,1,4,128]{3,2,1,0:T(4,128)(2,1)}), bf16[512,1,4,128]{3,2,1,0:T(4,128)(2,1)}, u32[]{:S(2)}, u32[]{:S(2)}) async-start(bf16[512,1,4,128]{3,2,1,0:T(4,128)(2,1)} %bitcast.42), calls=%async_computation.12 | async-start | bytes 1048576 | tf_op jit(solution)/shard_map/all_to_all | solution.py:183
  337.3 11.1 %all-to-all-done.12 = bf16[512,1,4,128]{3,2,1,0:T(4,128)(2,1)} async-done(((bf16[512,1,4,128]{3,2,1,0:T(4,128)(2,1)}), bf16[512,1,4,128]{3,2,1,0:T(4,128)(2,1)}, u32[]{:S(2)}, u32[]{:S(2)}) %all-to-all-start.12) | async-done | bytes 524320 | tf_op jit(solution)/shard_map/all_to_all | solution.py:183
  356.1 11.0 %all-to-all-done.13 = bf16[512,1,4,128]{3,2,1,0:T(4,128)(2,1)S(1)} async-done(((bf16[512,1,4,128]{3,2,1,0:T(4,128)(2,1)}), bf16[512,1,4,128]{3,2,1,0:T(4,128)(2,1)S(1)}, u32[]{:S(2)}, u32[]{:S(2)}) %all-to-all-start.13) | async-done | bytes 524320 | tf_op jit(solution)/shard_map/all_to_all | solution.py:184
  375.6 10.4 %all-to-all-done.14 = bf16[512,1,4,128]{3,2,1,0:T(4,128)(2,1)S(1)} async-done(((bf16[512,1,4,128]{3,2,1,0:T(4,128)(2,1)}), bf16[512,1,4,128]{3,2,1,0:T(4,128)(2,1)S(1)}, u32[]{:S(2)}, u32[]{:S(2)}) %all-to-all-start.14) | async-done | bytes 524320 | tf_op jit(solution)/shard_map/all_to_all | solution.py:185
  385.9 6.7 %all-to-all-start.9 = ((bf16[1024,1,4,128]{3,2,1,0:T(4,128)(2,1)}), bf16[1024,1,4,128]{3,2,1,0:T(4,128)(2,1)S(1)}, u32[]{:S(2)}, u32[]{:S(2)}) async-start(bf16[1024,1,4,128]{3,2,1,0:T(4,128)(2,1)} %copy.223), calls=%async_computation.9 | async-start | bytes 2097152 | tf_op jit(solution)/shard_map/all_to_all | solution.py:180
  394.5 21.3 %all-to-all-done.9 = bf16[1024,1,4,128]{3,2,1,0:T(4,128)(2,1)S(1)} async-done(((bf16[1024,1,4,128]{3,2,1,0:T(4,128)(2,1)}), bf16[1024,1,4,128]{3,2,1,0:T(4,128)(2,1)S(1)}, u32[]{:S(2)}, u32[]{:S(2)}) %all-to-all-start.9) | async-done | bytes 1048608 | tf_op jit(solution)/shard_map/all_to_all | solution.py:180
  415.8 7.7 %all-to-all-start.10 = ((bf16[1024,1,4,128]{3,2,1,0:T(4,128)(2,1)}), bf16[1024,1,4,128]{3,2,1,0:T(4,128)(2,1)}, u32[]{:S(2)}, u32[]{:S(2)}) async-start(bf16[1024,1,4,128]{3,2,1,0:T(4,128)(2,1)} %copy.227), calls=%async_computation.10 | async-start | bytes 2097152 | tf_op jit(solution)/shard_map/all_to_all | solution.py:181
  431.6 10.5 %psum.7 = f32[512]{0:T(512)} all-reduce(f32[512]{0:T(512)S(1)} %bitcast.318), channel_id=1, replica_groups=mesh['dp'=4,'ctx'=8] {'dp'}, use_global_device_ids=true, to_apply=%region_8.9 | all-reduce | flops 512 | bytes 4096 | tf_op jit(solution)/shard_map/psum | solution.py:189
  (241 shorter events, 200.6 us)
Async XLA Ops:
  0.6 9.6 %all-to-all-start.3 = ((bf16[1,8,4,128]{3,2,0,1:T(4,128)(2,1)}), bf16[1,8,4,128]{3,2,0,1:T(4,128)(2,1)S(1)}, u32[]{:S(2)}, u32[]{:S(2)}) async-start(bf16[1,8,4,128]{3,2,0,1:T(4,128)(2,1)} %bitcast.319), calls=%async_computation.3 | async-start | bytes 16384 | tf_op jit(solution)/shard_map/all_to_all | solution.py:155
  8.5 25.4 %copy-start.44 = (bf16[1,64,4096]{2,1,0:T(8,128)(2,1)S(1)}, bf16[1,64,4096]{2,1,0:T(8,128)(2,1)}, u32[]{:S(2)}) copy-start(bf16[1,64,4096]{2,1,0:T(8,128)(2,1)} %param.14) | copy-start | bytes 1572868
  10.3 17.0 %all-to-all-start.4 = ((bf16[64,8,4,128]{3,0,2,1:T(8,128)(2,1)}), bf16[64,8,4,128]{3,0,2,1:T(8,128)(2,1)S(1)}, u32[]{:S(2)}, u32[]{:S(2)}) async-start(bf16[64,8,4,128]{3,0,2,1:T(8,128)(2,1)} %copy.208), calls=%async_computation.4 | async-start | bytes 1048576 | tf_op jit(solution)/shard_map/all_to_all | solution.py:153
  16.5 36.2 %copy-start.45 = (bf16[1,64,4096]{2,1,0:T(8,128)(2,1)S(1)}, bf16[1,64,4096]{2,1,0:T(8,128)(2,1)}, u32[]{:S(2)}) copy-start(bf16[1,64,4096]{2,1,0:T(8,128)(2,1)} %param.13) | copy-start | bytes 1572868
  27.3 18.8 %all-to-all-start.6 = ((bf16[64,8,4,128]{3,0,2,1:T(8,128)(2,1)}), bf16[64,8,4,128]{3,0,2,1:T(8,128)(2,1)S(1)}, u32[]{:S(2)}, u32[]{:S(2)}) async-start(bf16[64,8,4,128]{3,0,2,1:T(8,128)(2,1)} %copy.212), calls=%async_computation.6 | async-start | bytes 1048576 | tf_op jit(solution)/shard_map/all_to_all | solution.py:154
  35.3 36.2 %copy-start.34 = (bf16[1,128,4096]{2,1,0:T(8,128)(2,1)S(1)}, bf16[1,128,4096]{2,1,0:T(8,128)(2,1)}, u32[]{:S(2)}) copy-start(bf16[1,128,4096]{2,1,0:T(8,128)(2,1)} %param.18) | copy-start | bytes 3145732
  46.1 18.8 %all-to-all-start.8 = ((bf16[64,8,4,128]{3,0,2,1:T(8,128)(2,1)}), bf16[64,8,4,128]{3,0,2,1:T(8,128)(2,1)S(1)}, u32[]{:S(2)}, u32[]{:S(2)}) async-start(bf16[64,8,4,128]{3,0,2,1:T(8,128)(2,1)} %copy.216), calls=%async_computation.8 | async-start | bytes 1048576 | tf_op jit(solution)/shard_map/all_to_all | solution.py:152
  64.8 18.8 %all-to-all-start.1 = ((bf16[64,8,4,128]{3,0,2,1:T(8,128)(2,1)}), bf16[64,8,4,128]{3,0,2,1:T(8,128)(2,1)S(1)}, u32[]{:S(2)}, u32[]{:S(2)}) async-start(bf16[64,8,4,128]{3,0,2,1:T(8,128)(2,1)} %copy.204), calls=%async_computation.1 | async-start | bytes 1048576 | tf_op jit(solution)/shard_map/all_to_all | solution.py:151
  83.6 29.8 %all-to-all-start.2 = ((bf16[128,8,4,128]{0,3,2,1:T(8,128)(2,1)}), bf16[128,8,4,128]{0,3,2,1:T(8,128)(2,1)S(1)}, u32[]{:S(2)}, u32[]{:S(2)}) async-start(bf16[128,8,4,128]{0,3,2,1:T(8,128)(2,1)} %bitcast.7), calls=%async_computation.2 | async-start | bytes 2097152 | tf_op jit(solution)/shard_map/all_to_all | solution.py:149
  113.5 71.9 %copy-start.15 = (bf16[128,8,4,128]{0,3,2,1:T(8,128)(2,1)}, bf16[128,8,4,128]{0,3,2,1:T(8,128)(2,1)S(1)}, u32[]{:S(2)}) copy-start(bf16[128,8,4,128]{0,3,2,1:T(8,128)(2,1)S(1)} %all-to-all-done.2) | copy-start | bytes 3145732
  113.5 30.2 %all-to-all-start.5 = ((bf16[128,8,4,128]{0,3,2,1:T(8,128)(2,1)}), bf16[128,8,4,128]{0,3,2,1:T(8,128)(2,1)S(1)}, u32[]{:S(2)}, u32[]{:S(2)}) async-start(bf16[128,8,4,128]{0,3,2,1:T(8,128)(2,1)} %bitcast.17), calls=%async_computation.5 | async-start | bytes 2097152 | tf_op jit(solution)/shard_map/all_to_all | solution.py:150
  143.7 46.3 %copy-start.17 = (bf16[128,8,4,128]{0,3,2,1:T(8,128)(2,1)}, bf16[128,8,4,128]{0,3,2,1:T(8,128)(2,1)S(1)}, u32[]{:S(2)}) copy-start(bf16[128,8,4,128]{0,3,2,1:T(8,128)(2,1)S(1)} %all-to-all-done.5) | copy-start | bytes 3145732
  143.7 30.1 %all-to-all-start.7 = ((bf16[128,8,4,128]{0,3,2,1:T(8,128)(2,1)}), bf16[128,8,4,128]{0,3,2,1:T(8,128)(2,1)S(1)}, u32[]{:S(2)}, u32[]{:S(2)}) async-start(bf16[128,8,4,128]{0,3,2,1:T(8,128)(2,1)} %bitcast.305), calls=%async_computation.7 | async-start | bytes 2097152 | tf_op jit(solution)/shard_map/all_to_all | solution.py:148
  173.8 30.7 %all-to-all-start = ((bf16[128,8,4,128]{0,3,2,1:T(8,128)(2,1)}), bf16[128,8,4,128]{0,3,2,1:T(8,128)(2,1)}, u32[]{:S(2)}, u32[]{:S(2)}) async-start(bf16[128,8,4,128]{0,3,2,1:T(8,128)(2,1)} %bitcast.304), calls=%async_computation | async-start | bytes 2097152 | tf_op jit(solution)/shard_map/all_to_all | solution.py:147
  309.7 19.1 %all-to-all-start.11 = ((bf16[512,1,4,128]{3,2,1,0:T(4,128)(2,1)}), bf16[512,1,4,128]{3,2,1,0:T(4,128)(2,1)S(1)}, u32[]{:S(2)}, u32[]{:S(2)}) async-start(bf16[512,1,4,128]{3,2,1,0:T(4,128)(2,1)} %bitcast.39), calls=%async_computation.11 | async-start | bytes 1048576 | tf_op jit(solution)/shard_map/all_to_all | solution.py:182
  316.7 19.4 %copy-start.14 = (f32[512,4,128]{0,2,1:T(8,128)S(1)}, f32[512,4,128]{0,2,1:T(8,128)}, u32[]{:S(2)}) copy-start(f32[512,4,128]{0,2,1:T(8,128)} %get-tuple-element.105) | copy-start | bytes 3145732
  328.9 19.5 %copy-start.23 = (bf16[512,1,4,128]{3,2,1,0:T(4,128)(2,1)}, bf16[512,1,4,128]{3,2,1,0:T(4,128)(2,1)S(1)}, u32[]{:S(2)}) copy-start(bf16[512,1,4,128]{3,2,1,0:T(4,128)(2,1)S(1)} %all-to-all-done.11) | copy-start | bytes 1572868
  328.9 19.5 %all-to-all-start.12 = ((bf16[512,1,4,128]{3,2,1,0:T(4,128)(2,1)}), bf16[512,1,4,128]{3,2,1,0:T(4,128)(2,1)}, u32[]{:S(2)}, u32[]{:S(2)}) async-start(bf16[512,1,4,128]{3,2,1,0:T(4,128)(2,1)} %bitcast.42), calls=%async_computation.12 | async-start | bytes 1048576 | tf_op jit(solution)/shard_map/all_to_all | solution.py:183
  336.1 18.9 %copy-start.11 = (f32[512,4,128]{0,2,1:T(8,128)S(1)}, f32[512,4,128]{0,2,1:T(8,128)}, u32[]{:S(2)}) copy-start(f32[512,4,128]{0,2,1:T(8,128)} %get-tuple-element.106) | copy-start | bytes 3145732
  348.4 18.8 %all-to-all-start.13 = ((bf16[512,1,4,128]{3,2,1,0:T(4,128)(2,1)}), bf16[512,1,4,128]{3,2,1,0:T(4,128)(2,1)S(1)}, u32[]{:S(2)}, u32[]{:S(2)}) async-start(bf16[512,1,4,128]{3,2,1,0:T(4,128)(2,1)} %bitcast.45), calls=%async_computation.13 | async-start | bytes 1048576 | tf_op jit(solution)/shard_map/all_to_all | solution.py:184
  367.2 18.8 %all-to-all-start.14 = ((bf16[512,1,4,128]{3,2,1,0:T(4,128)(2,1)}), bf16[512,1,4,128]{3,2,1,0:T(4,128)(2,1)S(1)}, u32[]{:S(2)}, u32[]{:S(2)}) async-start(bf16[512,1,4,128]{3,2,1,0:T(4,128)(2,1)} %bitcast.48), calls=%async_computation.14 | async-start | bytes 1048576 | tf_op jit(solution)/shard_map/all_to_all | solution.py:185
  373.8 18.9 %copy-start.42 = (bf16[2,512,4,128]{3,1,0,2:T(8,128)(2,1)S(1)}, bf16[2,512,4,128]{3,1,0,2:T(8,128)(2,1)}, u32[]{:S(2)}) copy-start(bf16[2,512,4,128]{3,1,0,2:T(8,128)(2,1)} %get-tuple-element.102) | copy-start | bytes 3145732
  385.9 29.8 %all-to-all-start.9 = ((bf16[1024,1,4,128]{3,2,1,0:T(4,128)(2,1)}), bf16[1024,1,4,128]{3,2,1,0:T(4,128)(2,1)S(1)}, u32[]{:S(2)}, u32[]{:S(2)}) async-start(bf16[1024,1,4,128]{3,2,1,0:T(4,128)(2,1)} %copy.223), calls=%async_computation.9 | async-start | bytes 2097152 | tf_op jit(solution)/shard_map/all_to_all | solution.py:180
  415.8 37.2 %all-to-all-start.10 = ((bf16[1024,1,4,128]{3,2,1,0:T(4,128)(2,1)}), bf16[1024,1,4,128]{3,2,1,0:T(4,128)(2,1)}, u32[]{:S(2)}, u32[]{:S(2)}) async-start(bf16[1024,1,4,128]{3,2,1,0:T(4,128)(2,1)} %copy.227), calls=%async_computation.10 | async-start | bytes 2097152 | tf_op jit(solution)/shard_map/all_to_all | solution.py:181
  (55 other events, 284.8 us)
where the time goes:
time: 460 us; the launch traced here: 456 us
  waiting for transfers between devices  182 us (40%)
  starting transfers between devices  100 us (22%)
  matrix products  78.3 us (17%)
  local copies, waits for them, and re-layouts  65 us (14%)
  other arithmetic  18.7 us (4%)
  blocking collectives  10.5 us (2%)
    dot_general x36, matrix products, inner_product(): jnp.einsum(pattern, left_op, right_op, preferred_element_type=jnp.float32)  78.3 us
    all_to_all x1, waiting for transfers between devices, per_device(): lax.all_to_all(regroup(grad_y_tan), 'ctx', split_axis=1, concat_axis=0, t...  21.8 us
    all_to_all x1, waiting for transfers between devices, per_device(): lax.all_to_all(regroup(grad_y), 'ctx', split_axis=1, concat_axis=0, tiled...  21.8 us
    all_to_all x1, waiting for transfers between devices, per_device(): lax.all_to_all(row_out[0][:, None], 'ctx', split_axis=0, concat_axis=1, t...  21.3 us
    all_to_all x1, waiting for transfers between devices, per_device(): lax.all_to_all(regroup(query_tangent), 'ctx', split_axis=1, concat_axis=0...  20.8 us
    unnamed x66, local copies, waits for them, and re-layouts  13.2 us
    all_to_all x1, waiting for transfers between devices, per_device(): lax.all_to_all(col_out[1][:, None], 'ctx', split_axis=0, concat_axis=1, t...  11.1 us
    all_to_all x1, waiting for transfers between devices, per_device(): lax.all_to_all(col_out[0][:, None], 'ctx', split_axis=0, concat_axis=1, t...  11 us
  transfers between devices with their start and end apart: 15, of which 14 were waited for; matrix products, arithmetic and copies ran while one was open for 12% of the time, Pallas kernels for 0%

commit v1 on v0

v1 whole, which is shorter than its diff:
```python
import functools
import math

import jax
import jax.numpy as jnp
from jax import lax
from jax.experimental import pallas as pl
from jax.experimental.pallas import tpu as pltpu
from jax.sharding import PartitionSpec as P

HEAD_DIM = 128
F32 = jnp.float32
BF16 = jnp.bfloat16


def chunk_sizes(heads):
    if heads < 8 or heads % 4:
        return (heads,)
    edge = heads // 8
    return (edge,) + (heads // 4,) * 3 + (edge,)


def dot(left, right, left_dim, right_dim):
    return lax.dot_general(
        left, right, (((left_dim,), (right_dim,)), ((), ())), preferred_element_type=F32
    )


def pack_kernel(where_ref, a_ref, b_ref, c_ref, d_ref, out_ref):
    heads = out_ref.shape[0]
    for h in range(heads):
        for i, ref in enumerate((a_ref, b_ref, c_ref, d_ref)):
            out_ref[h, :, i * HEAD_DIM : (i + 1) * HEAD_DIM] = ref[
                :, h * HEAD_DIM : (h + 1) * HEAD_DIM
            ]


def pack(where, arrays, halves, core_heads, first, count, block, partner_first):
    rows = arrays[0].shape[0]
    steps = count // block

    def column(i, where_ref):
        half = lax.rem(i // steps + where_ref[0] + (1 if partner_first else 0), 2)
        return (0, (half * core_heads + first) // block + lax.rem(i, steps))

    return pl.pallas_call(
        pack_kernel,
        grid_spec=pltpu.PrefetchScalarGridSpec(
            num_scalar_prefetch=1,
            grid=(halves * steps,),
            in_specs=[pl.BlockSpec((rows, block * HEAD_DIM), column)] * 4,
            out_specs=pl.BlockSpec(
                (block, rows, 4 * HEAD_DIM), lambda i, where_ref: (i, 0, 0)
            ),
        ),
        out_shape=jax.ShapeDtypeStruct((halves * count, rows, 4 * HEAD_DIM), BF16),
        cost_estimate=pl.CostEstimate(
            flops=0, bytes_accessed=halves * count * rows * 4 * HEAD_DIM * 4, transcendentals=0
        ),
    )(where, *arrays)


def attention_kernel(chips, scale, where_ref, *refs):
    q_ref, qt_ref, gy_ref, gyt_ref, gain_ref, qs_ref, own_ref = refs[:7]
    a_refs = refs[7 : 6 + chips]
    b_ref = refs[6 + chips]
    dq_ref, dqs_ref, da_ref, db_ref, d0_ref, gain_out, kbuf, dbuf = refs[7 + chips :]
    reach = where_ref[1]
    half_rows = own_ref.shape[3]
    rows_k = 2 * half_rows
    d = HEAD_DIM

    kbuf[0] = own_ref[...].reshape(rows_k, 4 * d)
    for j in range(1, chips):

        @pl.when(reach >= j)
        def _(j=j):
            kbuf[j] = a_refs[j - 1][...].reshape(rows_k, 4 * d)

        @pl.when(reach < j)
        def _(j=j):
            kbuf[j] = b_ref[jnp.clip(j - reach - 1, 0, chips - 2)].reshape(rows_k, 4 * d)

    every = kbuf[...].reshape(chips * rows_k, 4 * d)
    k, k_kt = every[:, :d], every[:, : 2 * d]
    v, v_vt = every[:, 2 * d : 3 * d], every[:, 2 * d :]
    swapped = qs_ref[0]
    q = jnp.concatenate([q_ref[...], swapped[:, :d]], axis=0)
    qt = jnp.concatenate([qt_ref[...], swapped[:, d : 2 * d]], axis=0)
    gy = jnp.concatenate([gy_ref[...], swapped[:, 2 * d : 3 * d]], axis=0).astype(F32)
    gyt = jnp.concatenate([gyt_ref[...], swapped[:, 3 * d :]], axis=0).astype(F32)
    gain = gain_ref[...].astype(F32)
    go = (gy * gain).astype(BF16)
    got = (gyt * gain).astype(BF16)

    scores = dot(q, k, 1, 1) * scale
    scores_tan = dot(jnp.concatenate([qt, q], axis=1), k_kt, 1, 1) * scale
    top = jnp.max(scores, axis=-1, keepdims=True)
    raised = jnp.exp(scores - top)
    probs = raised * (1.0 / jnp.sum(raised, axis=-1, keepdims=True))
    offset = jnp.sum(probs * scores_tan, axis=-1, keepdims=True)
    centred = scores_tan - offset
    probs_tan = probs * centred
    p_low = probs.astype(BF16)
    pt_low = probs_tan.astype(BF16)
    go_got = jnp.concatenate([go, got], axis=1)
    d_probs = dot(go_got, v_vt, 1, 1)
    d_probs_tan = dot(got, v, 1, 1)
    inner = jnp.sum(probs * d_probs_tan, axis=-1, keepdims=True)
    dst = probs * (d_probs_tan - inner)
    totals = d_probs + d_probs_tan * centred - inner * scores_tan
    ds = probs * (totals - jnp.sum(probs * totals, axis=-1, keepdims=True))
    ds_low = ds.astype(BF16)
    dst_low = dst.astype(BF16)

    out_pair = dot(p_low, v_vt, 1, 0)
    attn_out = out_pair[:, :d].astype(BF16).astype(F32)
    attn_tan = (dot(pt_low, v, 1, 0) + out_pair[:, d:]).astype(BF16).astype(F32)
    gain_out[0] = jnp.sum(gy * attn_out + gyt * attn_tan, axis=0, keepdims=True)

    q_pair = dot(dst_low, k_kt, 1, 0)
    dq = (scale * (dot(ds_low, k, 1, 0) + q_pair[:, d:])).astype(BF16)
    dqt = (scale * q_pair[:, :d]).astype(BF16)
    rows_q = q_ref.shape[0]
    dq_ref[0] = dq[:rows_q]
    dq_ref[1] = dqt[:rows_q]
    dqs_ref[0] = dq[rows_q:]
    dqs_ref[1] = dqt[rows_q:]

    k_pair = dot(dst_low, jnp.concatenate([q, qt], axis=1), 0, 0)
    dk = scale * (dot(ds_low, q, 0, 0) + k_pair[:, d:])
    dkt = scale * k_pair[:, :d]
    v_pair = dot(p_low, go_got, 0, 0)
    dv = v_pair[:, :d] + dot(pt_low, got, 0, 0)
    dvt = v_pair[:, d:]
    for i, part in enumerate((dk, dkt, dv, dvt)):
        columns = slice(i * d, (i + 1) * d)
        d0_ref[:, 0, :, columns] = part[:rows_k].reshape(2, half_rows, d)
        dbuf[:, :, columns] = part.astype(BF16).reshape(chips, rows_k, d)
    for j in range(1, chips):
        da_ref[j - 1] = dbuf[j].reshape(2, 1, half_rows, 4 * d)
        db_ref[j - 1] = dbuf[jnp.minimum(reach + j, chips - 1)].reshape(2, 1, half_rows, 4 * d)


def attention(where, rows_in, gain, swapped, own, along, other, core_heads, first):
    chips = len(along) + 1
    rows_q = rows_in[0].shape[0]
    heads, half_rows = own.shape[2], own.shape[3]
    rows_k = 2 * half_rows
    d = HEAD_DIM

    def column(h, where_ref):
        return (0, where_ref[0] * core_heads + first + h)

    payload = pl.BlockSpec((1, 2, 1, half_rows, 4 * d), lambda h, where_ref: (0, 0, h, 0, 0))
    slots = pl.BlockSpec(
        (chips - 1, 2, 1, half_rows, 4 * d), lambda h, where_ref: (0, 0, h, 0, 0)
    )
    queries_out = pl.BlockSpec((2, rows_q, d), lambda h, where_ref: (0, 0, h))
    pairs = heads * 2 * rows_q * chips * rows_k
    return pl.pallas_call(
        functools.partial(attention_kernel, chips, 1.0 / math.sqrt(d)),
        grid_spec=pltpu.PrefetchScalarGridSpec(
            num_scalar_prefetch=1,
            grid=(heads,),
            in_specs=[pl.BlockSpec((rows_q, d), column)] * 4
            + [
                pl.BlockSpec((1, d), column),
                pl.BlockSpec((1, rows_q, 4 * d), lambda h, where_ref: (first + h, 0, 0)),
            ]
            + [payload] * chips
            + [slots],
            out_specs=[
                queries_out,
                queries_out,
                slots,
                slots,
                pl.BlockSpec((2, 1, half_rows, 4 * d), lambda h, where_ref: (0, h, 0, 0)),
                pl.BlockSpec((1, 1, d), lambda h, where_ref: (h, 0, 0)),
            ],
            scratch_shapes=[
                pltpu.VMEM((chips, rows_k, 4 * d), BF16),
                pltpu.VMEM((chips, rows_k, 4 * d), BF16),
            ],
        ),
        out_shape=[
            jax.ShapeDtypeStruct((2, rows_q, heads * d), BF16),
            jax.ShapeDtypeStruct((2, rows_q, heads * d), BF16),
            jax.ShapeDtypeStruct((chips - 1, 2, heads, half_rows, 4 * d), BF16),
            jax.ShapeDtypeStruct((chips - 1, 2, heads, half_rows, 4 * d), BF16),
            jax.ShapeDtypeStruct((2, heads, half_rows, 4 * d), F32),
            jax.ShapeDtypeStruct((heads, 1, d), F32),
        ],
        compiler_params=pltpu.CompilerParams(vmem_limit_bytes=48 * 1024 * 1024),
        cost_estimate=pl.CostEstimate(
            flops=pairs * 36 * d, bytes_accessed=pairs * 16, transcendentals=pairs
        ),
    )(where, *rows_in, gain, swapped, own, *along, other)


def finish_kernel(where_ref, kept_ref, came_ref, *refs):
    total = kept_ref[...].astype(F32) + came_ref[...].astype(F32)
    heads = kept_ref.shape[1]
    for i, ref in enumerate(refs[-4:]):
        for h in range(heads):
            ref[:, h * HEAD_DIM : (h + 1) * HEAD_DIM] = total[
                0, h, :, i * HEAD_DIM : (i + 1) * HEAD_DIM
            ].astype(BF16)


def finish(where, kept, came, before, width, core_heads, first):
    heads, rows = kept.shape[1], kept.shape[2]
    block = math.gcd(heads, first) if first else heads
    steps = heads // block

    def column(i, where_ref):
        half = lax.rem(i // steps + where_ref[0], 2)
        return (0, (half * core_heads + first) // block + lax.rem(i, steps))

    old = list(before or ())
    return pl.pallas_call(
        finish_kernel,
        grid_spec=pltpu.PrefetchScalarGridSpec(
            num_scalar_prefetch=1,
            grid=(2 * steps,),
            in_specs=[
                pl.BlockSpec(
                    (1, block, rows, 4 * HEAD_DIM),
                    lambda i, where_ref: (i // steps, lax.rem(i, steps), 0, 0),
                ),
                pl.BlockSpec(
                    (1, block, rows, 4 * HEAD_DIM),
                    lambda i, where_ref: (1 - i // steps, lax.rem(i, steps), 0, 0),
                ),
            ]
            + [pl.BlockSpec(memory_space=pl.ANY)] * len(old),
            out_specs=[pl.BlockSpec((rows, block * HEAD_DIM), column)] * 4,
        ),
        out_shape=[jax.ShapeDtypeStruct((rows, width), BF16)] * 4,
        input_output_aliases={3 + i: i for i in range(len(old))},
        cost_estimate=pl.CostEstimate(
            flops=0, bytes_accessed=heads * rows * HEAD_DIM * 48, transcendentals=0
        ),
    )(where, kept, came, *old)


def per_device(
    queries, query_tangent, keys, key_tangent, values, value_tangent, out_gain, grad_y, grad_y_tan
):
    count = lax.axis_size("ctx")
    chips = count // 2
    width = queries.shape[2]
    core_heads = width // HEAD_DIM // 2
    place = lax.axis_index("ctx")
    core, chip = lax.rem(place, 2), place // 2
    where = jnp.stack([core, jnp.where(core == 0, chip, chips - 1 - chip)]).astype(jnp.int32)

    swap_pairs = [(i, i ^ 1) for i in range(count)]

    def swap(array):
        return lax.ppermute(array, "ctx", swap_pairs)

    def outward(array, step):
        pairs = [(2 * z, 2 * z + 2) for z in range(step - 1, chips - 1)]
        pairs += [(2 * z + 1, 2 * z - 1) for z in range(1, chips - step + 1)]
        return lax.ppermute(array, "ctx", pairs)

    def homeward(array, far):
        pairs = [(2 * z, 2 * z - 2) for z in range(far, chips)]
        pairs += [(2 * z + 1, 2 * z + 3) for z in range(0, chips - far)]
        return lax.ppermute(array, "ctx", pairs)

    rows_in = (queries[0], query_tangent[0], grad_y[0], grad_y_tan[0])
    key_in = (keys[0], key_tangent[0], values[0], value_tangent[0])
    rows_k = key_in[0].shape[0]
    gain = out_gain.reshape(1, width)
    sizes = chunk_sizes(core_heads)
    starts = [sum(sizes[:i]) for i in range(len(sizes))]

    owns = []
    for first, heads in zip(starts, sizes):
        block = math.gcd(heads, first) if first else heads
        mine = pack(where, key_in, 2, core_heads, first, heads, block, False)
        mine = mine.reshape(2, heads, rows_k, 4 * HEAD_DIM)
        theirs = swap(mine)
        owns.append(jnp.stack([mine, theirs[::-1]], axis=1))

    packed_rows = pack(
        where, rows_in, 1, core_heads, 0, core_heads, math.gcd(core_heads, 4), True
    )
    swapped = swap(packed_rows)

    gradients = None
    parts, sent, gains = [], [], []
    for index, (first, heads) in enumerate(zip(starts, sizes)):
        along = []
        moving = owns[index]
        for step in range(1, chips):
            moving = outward(moving, step)
            along.append(moving)
        other = swap(jnp.stack([a[1] for a in along]))
        dq, dq_other, d_along, d_other, d_own, gain_part = attention(
            where, rows_in, gain, swapped, owns[index], along, other, core_heads, first
        )
        gains.append(gain_part.reshape(heads * HEAD_DIM))
        parts.append(dq)
        sent.append(dq_other)
        d_theirs = swap(d_other)
        arrived = None
        for far in range(chips - 1, 0, -1):
            payload = jnp.stack([d_along[far - 1], d_theirs[far - 1]])
            if arrived is not None:
                payload = (payload.astype(F32) + arrived.astype(F32)).astype(BF16)
            arrived = homeward(payload, far)
        total = arrived.astype(F32)
        total = jnp.stack([total[0] + d_own, total[1]]).astype(BF16)
        came = swap(total[:, 1])
        gradients = finish(
            where, total[:, 0], came, gradients, width, core_heads, first
        )

    dq_mine = jnp.concatenate(parts, axis=2)
    dq_theirs = swap(jnp.concatenate(sent, axis=2))
    halves = jnp.where(
        core == 0,
        jnp.concatenate([dq_mine, dq_theirs], axis=2),
        jnp.concatenate([dq_theirs, dq_mine], axis=2),
    )
    gain_mine = jnp.concatenate(gains)
    gain_zero = jnp.zeros_like(gain_mine)
    gain_all = jnp.where(
        core == 0,
        jnp.concatenate([gain_mine, gain_zero]),
        jnp.concatenate([gain_zero, gain_mine]),
    )
    gain_all = lax.psum(gain_all, ("dp", "ctx"))
    gain_grad = lax.dynamic_slice_in_dim(gain_all, place * (width // count), width // count)
    return (halves[0][None], halves[1][None]) + tuple(g[None] for g in gradients) + (gain_grad,)


def solution(mesh):
    tokens = P("dp", "ctx", None)
    return jax.shard_map(
        per_device,
        mesh=mesh,
        in_specs=(tokens,) * 6 + (P(),) + (tokens,) * 2,
        out_specs=(tokens,) * 6 + (P("ctx"),),
        check_vma=False,
    )
```

time: 460 us -> 394 us (0.86)
  waiting for transfers between devices: 182 us -> 60.6 us
  matrix products: 78.3 us -> 0 us
  Pallas kernels: 0 us -> 76.9 us
  starting transfers between devices: 100 us -> 144 us
  blocking collectives: 10.5 us -> 39.8 us
  local copies, waits for them, and re-layouts: 65 us -> 44.7 us
    all_to_all x15 -> x0, waiting for transfers between devices: 182 us -> none  [the longest x1 21.8 us: per_device(): lax.all_to_all(regroup(grad_y_tan), 'ctx', split_axis=1, concat_axis=0, t...]
    ppermute x0 -> x52, starting transfers between devices: none -> 144 us  [the longest x22 73.3 us: swap(): return lax.ppermute(array, 'ctx', swap_pairs)]
    all_to_all x15 -> x0, starting transfers between devices: 100 us -> none  [the longest x1 7.65 us: per_device(): lax.all_to_all(row_out[1][:, None], 'ctx', split_axis=0, concat_axis=1, t...]
    dot_general x36 -> x0, matrix products: 78.3 us -> none  [inner_product(): jnp.einsum(pattern, left_op, right_op, preferred_element_type=jnp.float32)]
    pallas_call x0 -> x16, Pallas kernels: none -> 76.9 us  [the longest x5 39.5 us: attention(): pl.pallas_call(functools.partial(attention_kernel, chips, 1.0 / math.sqrt...]
    ppermute x0 -> x52, waiting for transfers between devices: none -> 60.6 us  [the longest x15 50.5 us: homeward(): return lax.ppermute(array, 'ctx', pairs)]
    psum x1, blocking collectives: 10.5 us -> 39.8 us  [per_device(): gain_all = lax.psum(gain_all, ('dp', 'ctx'))]
    slice x0 -> x31, local copies, waits for them, and re-layouts: none -> 21 us  [the longest x10 10.7 us: per_device(): payload = jnp.stack([d_along[far - 1], d_theirs[far - 1]])]
  transfers between devices with their start and end apart: 15 -> 52, of which waited for: 14 -> 8; matrix products, arithmetic and copies ran while one was open for 12% -> 15% of each run, Pallas kernels for 0% -> 19%
where the time goes in v1:
time: 394 us; the launch traced here: 388 us
  starting transfers between devices  144 us (37%)
  Pallas kernels  76.9 us (20%)
  waiting for transfers between devices  60.6 us (15%)
  local copies, waits for them, and re-layouts  44.7 us (11%)
  blocking collectives  39.8 us (10%)
  other arithmetic  20.4 us (5%)
    ppermute x22, starting transfers between devices, swap(): return lax.ppermute(array, 'ctx', swap_pairs)  73.3 us
    ppermute x15, waiting for transfers between devices, homeward(): return lax.ppermute(array, 'ctx', pairs)  50.5 us
    ppermute x15, starting transfers between devices, outward(): return lax.ppermute(array, 'ctx', pairs)  44.4 us
    psum x1, blocking collectives, per_device(): gain_all = lax.psum(gain_all, ('dp', 'ctx'))  39.8 us
    pallas_call x5, Pallas kernels, attention(): pl.pallas_call(functools.partial(attention_kernel, chips, 1.0 / math.sqrt...  39.5 us
    ppermute x15, starting transfers between devices, homeward(): return lax.ppermute(array, 'ctx', pairs)  26 us
    pallas_call x6, Pallas kernels, pack(): pl.pallas_call(pack_kernel, grid_spec=pltpu.PrefetchScalarGridSpec(num_sc...  20.4 us
    pallas_call x5, Pallas kernels, finish(): pl.pallas_call(finish_kernel, grid_spec=pltpu.PrefetchScalarGridSpec(num_...  17 us
  transfers between devices with their start and end apart: 52, of which 8 were waited for; matrix products, arithmetic and copies ran while one was open for 15% of the time, Pallas kernels for 19%

profile of v1, /device:TPU:8, one launch (start us, length us, event | category | flops | bytes accessed | tf_op | source)
XLA Modules:
  0.0 388.3 jit_solution(11734947017573774681)
XLA Ops:
  17.4 4.7 %shard_map.144 = bf16[16,128,512]{2,1,0:T(8,128)(2,1)} custom-call(s32[2]{0:T(128)} %pad_add_fusion.where_ref, bf16[128,4096]{1,0:T(8,128)(2,1)} %bitcast.104, bf16[128,4096]{1,0:T(8,128)(2,1)} %bitcast.110, bf16[128,4096]{1,0:T(8,128)(2,1)} %bitcast.116, bf16[128,4096]{1,0:T(8,128)(2,1)} %bitcast.122), custom_call_target="tpu_custom_call" | custom-call | bytes 4194304 | tf_op jit(solution)/shard_map/pallas_call | solution.py:46
  49.5 13.0 %collective-permute-start.5 = (bf16[3,2,2,64,512]{4,3,2,1,0:T(8,128)(2,1)S(1)}, bf16[3,2,2,64,512]{4,3,2,1,0:T(8,128)(2,1)S(1)}, u32[]{:S(2)}, u32[]{:S(2)}) collective-permute-start(bf16[3,2,2,64,512]{4,3,2,1,0:T(8,128)(2,1)S(1)} %pad_maximum_fusion.9), channel_id=1, source_target_pairs={{0,1},{1,0},{2,3},{3,2},{4,5},{5,4},{6,7},{7,6},{8,9},{9,8},{10,11... | collective-permute-start | bytes 2359304 | tf_op jit(solution)/shard_map/ppermute | solution.py:261
  65.8 6.3 %collective-permute-start.8 = (bf16[2,2,4,64,512]{4,3,2,1,0:T(8,128)(2,1)}, bf16[2,2,4,64,512]{4,3,2,1,0:T(8,128)(2,1)}, u32[]{:S(2)}, u32[]{:S(2)}) collective-permute-start(bf16[2,2,4,64,512]{4,3,2,1,0:T(8,128)(2,1)} %collective-permute-done.7.refs_7_), channel_id=1, source_target_pairs={{2,4},{4,6},{3,1},{5,3},{10,12},{12,14},{11,9},{13,11},{18,20},{20... | collective-permute-start | bytes 3145736 | tf_op jit(solution)/shard_map/ppermute | solution.py:266
  72.0 5.5 %collective-permute-start.13 = (bf16[2,2,4,64,512]{4,3,2,1,0:T(8,128)(2,1)}, bf16[2,2,4,64,512]{4,3,2,1,0:T(8,128)(2,1)}, u32[]{:S(2)}, u32[]{:S(2)}) collective-permute-start(bf16[2,2,4,64,512]{4,3,2,1,0:T(8,128)(2,1)} %collective-permute-done.12.refs_7_), channel_id=1, source_target_pairs={{2,4},{4,6},{3,1},{5,3},{10,12},{12,14},{11,9},{13,11},{18,20},{20... | collective-permute-start | bytes 3145736 | tf_op jit(solution)/shard_map/ppermute | solution.py:266
  78.4 5.1 %shard_map.146 = (bf16[2,128,256]{2,1,0:T(8,128)(2,1)S(1)}, bf16[2,128,256]{2,1,0:T(8,128)(2,1)S(1)}, bf16[3,2,2,64,512]{4,3,2,1,0:T(8,128)(2,1)S(1)}, bf16[3,2,...) custom-call(s32[2]{0:T(128)S(1)} %copy-done.24, ...), custom_call_target="tpu_custom_call" | custom-call | flops 1207959552 | bytes 4194304 | tf_op jit(solution)/shard_map/pallas_call | solution.py:161
  83.7 5.1 %collective-permute-start.18 = (bf16[2,2,4,64,512]{4,3,2,1,0:T(8,128)(2,1)S(1)}, bf16[2,2,4,64,512]{4,3,2,1,0:T(8,128)(2,1)}, u32[]{:S(2)}, u32[]{:S(2)}) collective-permute-start(bf16[2,2,4,64,512]{4,3,2,1,0:T(8,128)(2,1)S(1)} %collective-permute-done.17.refs_7_), channel_id=1, source_target_pairs={{2,4},{4,6},{3,1},{5,3},{10,12},{12,14},{11,9},{13,11},{18,20},{20... | collective-permute-start | bytes 3145736 | tf_op jit(solution)/shard_map/ppermute | solution.py:266
  88.8 5.1 %shard_map.154 = (bf16[2,128,256]{2,1,0:T(8,128)(2,1)S(1)}, bf16[2,128,256]{2,1,0:T(8,128)(2,1)S(1)}, bf16[3,2,2,64,512]{4,3,2,1,0:T(8,128)(2,1)S(1)}, bf16[3,2,...) custom-call(s32[2]{0:T(128)S(1)} %copy-done.24, ...), custom_call_target="tpu_custom_call" | custom-call | flops 1207959552 | bytes 4194304 | tf_op jit(solution)/shard_map/pallas_call | solution.py:161
  96.3 4.3 %collective-permute-done.13.refs_8_ = bf16[2,2,4,64,512]{4,3,2,1,0:T(8,128)(2,1)} collective-permute-done((bf16[2,2,4,64,512]{4,3,2,1,0:T(8,128)(2,1)}, bf16[2,2,4,64,512]{4,3,2,1,0:T(8,128)(2,1)}, u32[]{:S(2)}, u32[]{:S(2)}) %collective-permute-start.13) | collective-permute-done | bytes 1048608 | tf_op jit(solution)/shard_map/ppermute | solution.py:266
  106.3 5.4 %collective-permute-done.18.refs_8_ = bf16[2,2,4,64,512]{4,3,2,1,0:T(8,128)(2,1)} collective-permute-done((bf16[2,2,4,64,512]{4,3,2,1,0:T(8,128)(2,1)S(1)}, bf16[2,2,4,64,512]{4,3,2,1,0:T(8,128)(2,1)}, u32[]{:S(2)}, u32[]{:S(2)}) %collective-permute-start.18) | collective-permute-done | bytes 1048608 | tf_op jit(solution)/shard_map/ppermute | solution.py:266
  127.2 11.2 %collective-permute-start.10 = (bf16[3,2,4,64,512]{4,3,2,1,0:T(8,128)(2,1)}, bf16[3,2,4,64,512]{4,3,2,1,0:T(8,128)(2,1)}, u32[]{:S(2)}, u32[]{:S(2)}) collective-permute-start(bf16[3,2,4,64,512]{4,3,2,1,0:T(8,128)(2,1)} %pad_maximum_fusion), channel_id=1, source_target_pairs={{0,1},{1,0},{2,3},{3,2},{4,5},{5,4},{6,7},{7,6},{8,9},{9,8},{10,11... | collective-permute-start | bytes 4718600 | tf_op jit(solution)/shard_map/ppermute | solution.py:261
  142.7 4.0 %collective-permute-start.15 = (bf16[3,2,4,64,512]{4,3,2,1,0:T(8,128)(2,1)}, bf16[3,2,4,64,512]{4,3,2,1,0:T(8,128)(2,1)}, u32[]{:S(2)}, u32[]{:S(2)}) collective-permute-start(bf16[3,2,4,64,512]{4,3,2,1,0:T(8,128)(2,1)} %pad_maximum_fusion.1), channel_id=1, source_target_pairs={{0,1},{1,0},{2,3},{3,2},{4,5},{5,4},{6,7},{7,6},{8,9},{9,8},{10,11... | collective-permute-start | bytes 4718600 | tf_op jit(solution)/shard_map/ppermute | solution.py:261
  153.3 4.5 %collective-permute-start.20 = (bf16[3,2,4,64,512]{4,3,2,1,0:T(8,128)(2,1)}, bf16[3,2,4,64,512]{4,3,2,1,0:T(8,128)(2,1)}, u32[]{:S(2)}, u32[]{:S(2)}) collective-permute-start(bf16[3,2,4,64,512]{4,3,2,1,0:T(8,128)(2,1)} %pad_maximum_fusion.2), channel_id=1, source_target_pairs={{0,1},{1,0},{2,3},{3,2},{4,5},{5,4},{6,7},{7,6},{8,9},{9,8},{10,11... | collective-permute-start | bytes 4718600 | tf_op jit(solution)/shard_map/ppermute | solution.py:261
  165.6 4.0 %collective-permute-done.30 = bf16[2,2,2,64,512]{4,3,2,0,1:T(8,128)(2,1)S(1)} collective-permute-done((bf16[2,2,2,64,512]{4,3,2,0,1:T(8,128)(2,1)S(1)}, bf16[2,2,2,64,512]{4,3,2,0,1:T(8,128)(2,1)S(1)}, u32[]{:S(2)}, u32[]{:S(2)}) %collective-permute-start.30) | collective-permute-done | bytes 524320 | tf_op jit(solution)/shard_map/ppermute | solution.py:271
  175.3 9.8 %shard_map.148 = (bf16[2,128,512]{2,1,0:T(8,128)(2,1)S(1)}, bf16[2,128,512]{2,1,0:T(8,128)(2,1)S(1)}, bf16[3,2,4,64,512]{4,3,2,1,0:T(8,128)(2,1)}, bf16[3,2,4,64...) custom-call(s32[2]{0:T(128)S(1)} %copy-done.25, bf16[128,4096]{1,0:T(8,128)(2,1)S(1)} %bitcast.107, ...), custom_call_target="tpu_custom_call" | custom-call | flops 2415919104 | bytes 8388608 | tf_op jit(solution)/shard_map/pallas_call | solution.py:161
  188.9 9.8 %shard_map.150 = (bf16[2,128,512]{2,1,0:T(8,128)(2,1)S(1)}, bf16[2,128,512]{2,1,0:T(8,128)(2,1)S(1)}, bf16[3,2,4,64,512]{4,3,2,1,0:T(8,128)(2,1)}, bf16[3,2,4,64...) custom-call(s32[2]{0:T(128)S(1)} %copy-done.25, bf16[128,4096]{1,0:T(8,128)(2,1)S(1)} %bitcast.108, ...), custom_call_target="tpu_custom_call" | custom-call | flops 2415919104 | bytes 8388608 | tf_op jit(solution)/shard_map/pallas_call | solution.py:161
  202.9 9.7 %shard_map.152 = (bf16[2,128,512]{2,1,0:T(8,128)(2,1)S(1)}, bf16[2,128,512]{2,1,0:T(8,128)(2,1)S(1)}, bf16[3,2,4,64,512]{4,3,2,1,0:T(8,128)(2,1)}, bf16[3,2,4,64...) custom-call(s32[2]{0:T(128)S(1)} %copy-done.25, bf16[128,4096]{1,0:T(8,128)(2,1)S(1)} %bitcast.109, ...), custom_call_target="tpu_custom_call" | custom-call | flops 2415919104 | bytes 8388608 | tf_op jit(solution)/shard_map/pallas_call | solution.py:161
  220.5 39.8 %psum.7 = f32[4096]{0:T(1024)S(1)} all-reduce(f32[4096]{0:T(1024)S(1)} %broadcast_select_fusion.1), channel_id=1, replica_groups=mesh['dp'=4,'ctx'=8] {'dp','ctx'}, use_global_device_ids=true, to_apply=%region_0.1 | all-reduce | flops 4096 | bytes 32768 | tf_op jit(solution)/shard_map/psum | solution.py:336
  276.7 19.9 %collective-permute-done.44 = bf16[2,2,4,64,512]{4,3,2,0,1:T(8,128)(2,1)S(1)} collective-permute-done((bf16[2,2,4,64,512]{4,3,2,0,1:T(8,128)(2,1)S(1)}, bf16[2,2,4,64,512]{4,3,2,0,1:T(8,128)(2,1)S(1)}, u32[]{:S(2)}, u32[]{:S(2)}) %collective-permute-start.44) | collective-permute-done | bytes 1048608 | tf_op jit(solution)/shard_map/ppermute | solution.py:271
  299.1 8.9 %collective-permute-done.39 = bf16[2,2,4,64,512]{4,3,2,0,1:T(8,128)(2,1)S(1)} collective-permute-done((bf16[2,2,4,64,512]{4,3,2,0,1:T(8,128)(2,1)S(1)}, bf16[2,2,4,64,512]{4,3,2,0,1:T(8,128)(2,1)S(1)}, u32[]{:S(2)}, u32[]{:S(2)}) %collective-permute-start.39) | collective-permute-done | bytes 1048608 | tf_op jit(solution)/shard_map/ppermute | solution.py:271
  310.3 9.0 %collective-permute-done.34 = bf16[2,2,4,64,512]{4,3,2,0,1:T(8,128)(2,1)S(1)} collective-permute-done((bf16[2,2,4,64,512]{4,3,2,0,1:T(8,128)(2,1)S(1)}, bf16[2,2,4,64,512]{4,3,2,0,1:T(8,128)(2,1)S(1)}, u32[]{:S(2)}, u32[]{:S(2)}) %collective-permute-start.34) | collective-permute-done | bytes 1048608 | tf_op jit(solution)/shard_map/ppermute | solution.py:271
  321.7 8.7 %collective-permute-done.45 = bf16[2,2,4,64,512]{4,3,2,0,1:T(8,128)(2,1)S(1)} collective-permute-done((bf16[2,2,4,64,512]{4,3,2,0,1:T(8,128)(2,1)S(1)}, bf16[2,2,4,64,512]{4,3,2,0,1:T(8,128)(2,1)S(1)}, u32[]{:S(2)}, u32[]{:S(2)}) %collective-permute-start.45) | collective-permute-done | bytes 1048608 | tf_op jit(solution)/shard_map/ppermute | solution.py:271
  331.6 16.1 %collective-permute-start.46 = (bf16[2,4,64,512]{3,2,1,0:T(8,128)(2,1)S(1)}, bf16[2,4,64,512]{3,2,1,0:T(8,128)(2,1)S(1)}, u32[]{:S(2)}, u32[]{:S(2)}) collective-permute-start(bf16[2,4,64,512]{3,2,1,0:T(8,128)(2,1)S(1)} %get-tuple-element.127), channel_id=1, source_target_pairs={{0,1},{1,0},{2,3},{3,2},{4,5},{5,4},{6,7},{7,6},{8,9},{9,8},{10,11... | collective-permute-start | bytes 1572872 | tf_op jit(solution)/shard_map/ppermute | solution.py:261
  348.8 9.8 %collective-permute-start.41 = (bf16[2,4,64,512]{3,2,1,0:T(8,128)(2,1)S(1)}, bf16[2,4,64,512]{3,2,1,0:T(8,128)(2,1)S(1)}, u32[]{:S(2)}, u32[]{:S(2)}) collective-permute-start(bf16[2,4,64,512]{3,2,1,0:T(8,128)(2,1)S(1)} %get-tuple-element.129), channel_id=1, source_target_pairs={{0,1},{1,0},{2,3},{3,2},{4,5},{5,4},{6,7},{7,6},{8,9},{9,8},{10,11... | collective-permute-start | bytes 1572872 | tf_op jit(solution)/shard_map/ppermute | solution.py:261
  359.7 10.1 %collective-permute-start.36 = (bf16[2,4,64,512]{3,2,1,0:T(8,128)(2,1)S(1)}, bf16[2,4,64,512]{3,2,1,0:T(8,128)(2,1)S(1)}, u32[]{:S(2)}, u32[]{:S(2)}) collective-permute-start(bf16[2,4,64,512]{3,2,1,0:T(8,128)(2,1)S(1)} %get-tuple-element.131), channel_id=1, source_target_pairs={{0,1},{1,0},{2,3},{3,2},{4,5},{5,4},{6,7},{7,6},{8,9},{9,8},{10,11... | collective-permute-start | bytes 1572872 | tf_op jit(solution)/shard_map/ppermute | solution.py:261
  (317 shorter events, 156.3 us)
Async XLA Ops:
  22.0 55.7 %collective-permute-start = (bf16[16,128,512]{2,1,0:T(8,128)(2,1)}, bf16[16,128,512]{2,1,0:T(8,128)(2,1)}, u32[]{:S(2)}, u32[]{:S(2)}) collective-permute-start(bf16[16,128,512]{2,1,0:T(8,128)(2,1)} %shard_map.144), channel_id=1, source_target_pairs={{0,1},{1,0},{2,3},{3,2},{4,5},{5,4},{6,7},{7,6},{8,9},{9,8},{10,11... | collective-permute-start | bytes 6291464 | tf_op jit(solution)/shard_map/ppermute | solution.py:261
  33.8 28.9 %collective-permute-start.7 = (bf16[2,2,4,64,512]{4,3,2,1,0:T(8,128)(2,1)}, bf16[2,2,4,64,512]{4,3,2,1,0:T(8,128)(2,1)}, u32[]{:S(2)}, u32[]{:S(2)}) collective-permute-start(bf16[2,2,4,64,512]{4,3,2,1,0:T(8,128)(2,1)} %pad_maximum_fusion.3.refs_6_), channel_id=1, source_target_pairs={{0,2},{2,4},{4,6},{3,1},{5,3},{7,5},{8,10},{10,12},{12,14},{11,9},... | collective-permute-start | bytes 3145736 | tf_op jit(solution)/shard_map/ppermute | solution.py:266
  49.5 28.9 %collective-permute-start.5 = (bf16[3,2,2,64,512]{4,3,2,1,0:T(8,128)(2,1)S(1)}, bf16[3,2,2,64,512]{4,3,2,1,0:T(8,128)(2,1)S(1)}, u32[]{:S(2)}, u32[]{:S(2)}) collective-permute-start(bf16[3,2,2,64,512]{4,3,2,1,0:T(8,128)(2,1)S(1)} %pad_maximum_fusion.9), channel_id=1, source_target_pairs={{0,1},{1,0},{2,3},{3,2},{4,5},{5,4},{6,7},{7,6},{8,9},{9,8},{10,11... | collective-permute-start | bytes 2359304 | tf_op jit(solution)/shard_map/ppermute | solution.py:261
  65.8 28.9 %collective-permute-start.8 = (bf16[2,2,4,64,512]{4,3,2,1,0:T(8,128)(2,1)}, bf16[2,2,4,64,512]{4,3,2,1,0:T(8,128)(2,1)}, u32[]{:S(2)}, u32[]{:S(2)}) collective-permute-start(bf16[2,2,4,64,512]{4,3,2,1,0:T(8,128)(2,1)} %collective-permute-done.7.refs_7_), channel_id=1, source_target_pairs={{2,4},{4,6},{3,1},{5,3},{10,12},{12,14},{11,9},{13,11},{18,20},{20... | collective-permute-start | bytes 3145736 | tf_op jit(solution)/shard_map/ppermute | solution.py:266
  72.0 28.6 %collective-permute-start.13 = (bf16[2,2,4,64,512]{4,3,2,1,0:T(8,128)(2,1)}, bf16[2,2,4,64,512]{4,3,2,1,0:T(8,128)(2,1)}, u32[]{:S(2)}, u32[]{:S(2)}) collective-permute-start(bf16[2,2,4,64,512]{4,3,2,1,0:T(8,128)(2,1)} %collective-permute-done.12.refs_7_), channel_id=1, source_target_pairs={{2,4},{4,6},{3,1},{5,3},{10,12},{12,14},{11,9},{13,11},{18,20},{20... | collective-permute-start | bytes 3145736 | tf_op jit(solution)/shard_map/ppermute | solution.py:266
  83.7 28.0 %collective-permute-start.18 = (bf16[2,2,4,64,512]{4,3,2,1,0:T(8,128)(2,1)S(1)}, bf16[2,2,4,64,512]{4,3,2,1,0:T(8,128)(2,1)}, u32[]{:S(2)}, u32[]{:S(2)}) collective-permute-start(bf16[2,2,4,64,512]{4,3,2,1,0:T(8,128)(2,1)S(1)} %collective-permute-done.17.refs_7_), channel_id=1, source_target_pairs={{2,4},{4,6},{3,1},{5,3},{10,12},{12,14},{11,9},{13,11},{18,20},{20... | collective-permute-start | bytes 3145736 | tf_op jit(solution)/shard_map/ppermute | solution.py:266
  94.6 27.5 %collective-permute-start.9 = (bf16[2,2,4,64,512]{4,3,2,1,0:T(8,128)(2,1)}, bf16[2,2,4,64,512]{4,3,2,1,0:T(8,128)(2,1)}, u32[]{:S(2)}, u32[]{:S(2)}) collective-permute-start(bf16[2,2,4,64,512]{4,3,2,1,0:T(8,128)(2,1)} %collective-permute-done.8.refs_8_), channel_id=1, source_target_pairs={{4,6},{3,1},{12,14},{11,9},{20,22},{19,17},{28,30},{27,25}} | collective-permute-start | bytes 3145736 | tf_op jit(solution)/shard_map/ppermute | solution.py:266
  100.6 37.8 %collective-permute-start.14 = (bf16[2,2,4,64,512]{4,3,2,1,0:T(8,128)(2,1)}, bf16[2,2,4,64,512]{4,3,2,1,0:T(8,128)(2,1)S(1)}, u32[]{:S(2)}, u32[]{:S(2)}) collective-permute-start(bf16[2,2,4,64,512]{4,3,2,1,0:T(8,128)(2,1)} %collective-permute-done.13.refs_8_), channel_id=1, source_target_pairs={{4,6},{3,1},{12,14},{11,9},{20,22},{19,17},{28,30},{27,25}} | collective-permute-start | bytes 3145736 | tf_op jit(solution)/shard_map/ppermute | solution.py:266
  111.7 35.0 %collective-permute-start.19 = (bf16[2,2,4,64,512]{4,3,2,1,0:T(8,128)(2,1)}, bf16[2,2,4,64,512]{4,3,2,1,0:T(8,128)(2,1)}, u32[]{:S(2)}, u32[]{:S(2)}) collective-permute-start(bf16[2,2,4,64,512]{4,3,2,1,0:T(8,128)(2,1)} %collective-permute-done.18.refs_8_), channel_id=1, source_target_pairs={{4,6},{3,1},{12,14},{11,9},{20,22},{19,17},{28,30},{27,25}} | collective-permute-start | bytes 3145736 | tf_op jit(solution)/shard_map/ppermute | solution.py:266
  127.2 46.3 %collective-permute-start.10 = (bf16[3,2,4,64,512]{4,3,2,1,0:T(8,128)(2,1)}, bf16[3,2,4,64,512]{4,3,2,1,0:T(8,128)(2,1)}, u32[]{:S(2)}, u32[]{:S(2)}) collective-permute-start(bf16[3,2,4,64,512]{4,3,2,1,0:T(8,128)(2,1)} %pad_maximum_fusion), channel_id=1, source_target_pairs={{0,1},{1,0},{2,3},{3,2},{4,5},{5,4},{6,7},{7,6},{8,9},{9,8},{10,11... | collective-permute-start | bytes 4718600 | tf_op jit(solution)/shard_map/ppermute | solution.py:261
  142.7 46.2 %collective-permute-start.15 = (bf16[3,2,4,64,512]{4,3,2,1,0:T(8,128)(2,1)}, bf16[3,2,4,64,512]{4,3,2,1,0:T(8,128)(2,1)}, u32[]{:S(2)}, u32[]{:S(2)}) collective-permute-start(bf16[3,2,4,64,512]{4,3,2,1,0:T(8,128)(2,1)} %pad_maximum_fusion.1), channel_id=1, source_target_pairs={{0,1},{1,0},{2,3},{3,2},{4,5},{5,4},{6,7},{7,6},{8,9},{9,8},{10,11... | collective-permute-start | bytes 4718600 | tf_op jit(solution)/shard_map/ppermute | solution.py:261
  153.3 49.6 %collective-permute-start.20 = (bf16[3,2,4,64,512]{4,3,2,1,0:T(8,128)(2,1)}, bf16[3,2,4,64,512]{4,3,2,1,0:T(8,128)(2,1)}, u32[]{:S(2)}, u32[]{:S(2)}) collective-permute-start(bf16[3,2,4,64,512]{4,3,2,1,0:T(8,128)(2,1)} %pad_maximum_fusion.2), channel_id=1, source_target_pairs={{0,1},{1,0},{2,3},{3,2},{4,5},{5,4},{6,7},{7,6},{8,9},{9,8},{10,11... | collective-permute-start | bytes 4718600 | tf_op jit(solution)/shard_map/ppermute | solution.py:261
  170.6 215.1 %collective-permute-start.31 = (bf16[2,2,64,512]{3,2,1,0:T(8,128)(2,1)}, bf16[2,2,64,512]{3,2,1,0:T(8,128)(2,1)}, u32[]{:S(2)}, u32[]{:S(2)}) collective-permute-start(bf16[2,2,64,512]{3,2,1,0:T(8,128)(2,1)} %get-tuple-element.149), channel_id=1, source_target_pairs={{0,1},{1,0},{2,3},{3,2},{4,5},{5,4},{6,7},{7,6},{8,9},{9,8},{10,11... | collective-permute-start | bytes 786440 | tf_op jit(solution)/shard_map/ppermute | solution.py:261
  188.8 73.8 %collective-permute-start.42 = (bf16[3,2,4,64,512]{4,3,2,0,1:T(8,128)(2,1)}, bf16[3,2,4,64,512]{4,3,2,0,1:T(8,128)(2,1)}, u32[]{:S(2)}, u32[]{:S(2)}) collective-permute-start(bf16[3,2,4,64,512]{4,3,2,0,1:T(8,128)(2,1)} %copy.48), channel_id=1, source_target_pairs={{0,1},{1,0},{2,3},{3,2},{4,5},{5,4},{6,7},{7,6},{8,9},{9,8},{10,11... | collective-permute-start | bytes 4718600 | tf_op jit(solution)/shard_map/ppermute | solution.py:261
  202.5 62.5 %collective-permute-start.37 = (bf16[3,2,4,64,512]{4,3,2,0,1:T(8,128)(2,1)}, bf16[3,2,4,64,512]{4,3,2,0,1:T(8,128)(2,1)}, u32[]{:S(2)}, u32[]{:S(2)}) collective-permute-start(bf16[3,2,4,64,512]{4,3,2,0,1:T(8,128)(2,1)} %copy.43), channel_id=1, source_target_pairs={{0,1},{1,0},{2,3},{3,2},{4,5},{5,4},{6,7},{7,6},{8,9},{9,8},{10,11... | collective-permute-start | bytes 4718600 | tf_op jit(solution)/shard_map/ppermute | solution.py:261
  215.9 51.5 %collective-permute-start.32 = (bf16[3,2,4,64,512]{4,3,2,0,1:T(8,128)(2,1)}, bf16[3,2,4,64,512]{4,3,2,0,1:T(8,128)(2,1)}, u32[]{:S(2)}, u32[]{:S(2)}) collective-permute-start(bf16[3,2,4,64,512]{4,3,2,0,1:T(8,128)(2,1)} %copy.38), channel_id=1, source_target_pairs={{0,1},{1,0},{2,3},{3,2},{4,5},{5,4},{6,7},{7,6},{8,9},{9,8},{10,11... | collective-permute-start | bytes 4718600 | tf_op jit(solution)/shard_map/ppermute | solution.py:261
  218.9 51.1 %collective-permute-start.26 = (bf16[2,128,2048]{2,1,0:T(8,128)(2,1)}, bf16[2,128,2048]{2,1,0:T(8,128)(2,1)}, u32[]{:S(2)}, u32[]{:S(2)}) collective-permute-start(bf16[2,128,2048]{2,1,0:T(8,128)(2,1)} %constant_dynamic-update-slice_fusion), channel_id=1, source_target_pairs={{0,1},{1,0},{2,3},{3,2},{4,5},{5,4},{6,7},{7,6},{8,9},{9,8},{10,11... | collective-permute-start | bytes 3145736 | tf_op jit(solution)/shard_map/ppermute | solution.py:261
  273.5 34.5 %collective-permute-start.39 = (bf16[2,2,4,64,512]{4,3,2,0,1:T(8,128)(2,1)S(1)}, bf16[2,2,4,64,512]{4,3,2,0,1:T(8,128)(2,1)S(1)}, u32[]{:S(2)}, u32[]{:S(2)}) collective-permute-start(bf16[2,2,4,64,512]{4,3,2,0,1:T(8,128)(2,1)S(1)} %add_convert_fusion.3), channel_id=1, source_target_pairs={{4,2},{6,4},{1,3},{3,5},{12,10},{14,12},{9,11},{11,13},{20,18},{22... | collective-permute-start | bytes 3145736 | tf_op jit(solution)/shard_map/ppermute | solution.py:271
  275.3 44.0 %collective-permute-start.34 = (bf16[2,2,4,64,512]{4,3,2,0,1:T(8,128)(2,1)S(1)}, bf16[2,2,4,64,512]{4,3,2,0,1:T(8,128)(2,1)S(1)}, u32[]{:S(2)}, u32[]{:S(2)}) collective-permute-start(bf16[2,2,4,64,512]{4,3,2,0,1:T(8,128)(2,1)S(1)} %add_convert_fusion.5), channel_id=1, source_target_pairs={{4,2},{6,4},{1,3},{3,5},{12,10},{14,12},{9,11},{11,13},{20,18},{22... | collective-permute-start | bytes 3145736 | tf_op jit(solution)/shard_map/ppermute | solution.py:271
  297.0 33.5 %collective-permute-start.45 = (bf16[2,2,4,64,512]{4,3,2,0,1:T(8,128)(2,1)S(1)}, bf16[2,2,4,64,512]{4,3,2,0,1:T(8,128)(2,1)S(1)}, u32[]{:S(2)}, u32[]{:S(2)}) collective-permute-start(bf16[2,2,4,64,512]{4,3,2,0,1:T(8,128)(2,1)S(1)} %add_convert_fusion), channel_id=1, source_target_pairs={{2,0},{4,2},{6,4},{1,3},{3,5},{5,7},{10,8},{12,10},{14,12},{9,11},... | collective-permute-start | bytes 3145736 | tf_op jit(solution)/shard_map/ppermute | solution.py:271
  308.3 39.3 %collective-permute-start.40 = (bf16[2,2,4,64,512]{4,3,2,0,1:T(8,128)(2,1)S(1)}, bf16[2,2,4,64,512]{4,3,2,0,1:T(8,128)(2,1)S(1)}, u32[]{:S(2)}, u32[]{:S(2)}) collective-permute-start(bf16[2,2,4,64,512]{4,3,2,0,1:T(8,128)(2,1)S(1)} %add_convert_fusion.2), channel_id=1, source_target_pairs={{2,0},{4,2},{6,4},{1,3},{3,5},{5,7},{10,8},{12,10},{14,12},{9,11},... | collective-permute-start | bytes 3145736 | tf_op jit(solution)/shard_map/ppermute | solution.py:271
  319.6 39.1 %collective-permute-start.35 = (bf16[2,2,4,64,512]{4,3,2,0,1:T(8,128)(2,1)S(1)}, bf16[2,2,4,64,512]{4,3,2,0,1:T(8,128)(2,1)S(1)}, u32[]{:S(2)}, u32[]{:S(2)}) collective-permute-start(bf16[2,2,4,64,512]{4,3,2,0,1:T(8,128)(2,1)S(1)} %add_convert_fusion.4), channel_id=1, source_target_pairs={{2,0},{4,2},{6,4},{1,3},{3,5},{5,7},{10,8},{12,10},{14,12},{9,11},... | collective-permute-start | bytes 3145736 | tf_op jit(solution)/shard_map/ppermute | solution.py:271
  331.6 39.7 %collective-permute-start.46 = (bf16[2,4,64,512]{3,2,1,0:T(8,128)(2,1)S(1)}, bf16[2,4,64,512]{3,2,1,0:T(8,128)(2,1)S(1)}, u32[]{:S(2)}, u32[]{:S(2)}) collective-permute-start(bf16[2,4,64,512]{3,2,1,0:T(8,128)(2,1)S(1)} %get-tuple-element.127), channel_id=1, source_target_pairs={{0,1},{1,0},{2,3},{3,2},{4,5},{5,4},{6,7},{7,6},{8,9},{9,8},{10,11... | collective-permute-start | bytes 1572872 | tf_op jit(solution)/shard_map/ppermute | solution.py:261
  348.8 27.3 %collective-permute-start.41 = (bf16[2,4,64,512]{3,2,1,0:T(8,128)(2,1)S(1)}, bf16[2,4,64,512]{3,2,1,0:T(8,128)(2,1)S(1)}, u32[]{:S(2)}, u32[]{:S(2)}) collective-permute-start(bf16[2,4,64,512]{3,2,1,0:T(8,128)(2,1)S(1)} %get-tuple-element.129), channel_id=1, source_target_pairs={{0,1},{1,0},{2,3},{3,2},{4,5},{5,4},{6,7},{7,6},{8,9},{9,8},{10,11... | collective-permute-start | bytes 1572872 | tf_op jit(solution)/shard_map/ppermute | solution.py:261
  (86 other events, 957.1 us)

commit v2 on v1

--- a/solution.py
+++ b/solution.py
@@ -60,11 +60,14 @@
     )(where, *arrays)
 
 
-def attention_kernel(chips, scale, where_ref, *refs):
+def attention_kernel(chips, extra, scale, where_ref, *refs):
     q_ref, qt_ref, gy_ref, gyt_ref, gain_ref, qs_ref, own_ref = refs[:7]
     a_refs = refs[7 : 6 + chips]
     b_ref = refs[6 + chips]
-    dq_ref, dqs_ref, da_ref, db_ref, d0_ref, gain_out, kbuf, dbuf = refs[7 + chips :]
+    outs = refs[7 + chips + extra :]
+    dq_ref, dqs_ref, db_ref, d0_ref, gain_out = outs[:5]
+    da_refs = outs[5 : 4 + chips]
+    kbuf, dbuf = outs[4 + chips :]
     reach = where_ref[1]
     half_rows = own_ref.shape[3]
     rows_k = 2 * half_rows
@@ -138,11 +141,11 @@
         d0_ref[:, 0, :, columns] = part[:rows_k].reshape(2, half_rows, d)
         dbuf[:, :, columns] = part.astype(BF16).reshape(chips, rows_k, d)
     for j in range(1, chips):
-        da_ref[j - 1] = dbuf[j].reshape(2, 1, half_rows, 4 * d)
+        da_refs[j - 1][...] = dbuf[j].reshape(2, 1, half_rows, 4 * d)
         db_ref[j - 1] = dbuf[jnp.minimum(reach + j, chips - 1)].reshape(2, 1, half_rows, 4 * d)
 
 
-def attention(where, rows_in, gain, swapped, own, along, other, core_heads, first):
+def attention(where, rows_in, gain, swapped, own, along, other, core_heads, first, before):
     chips = len(along) + 1
     rows_q = rows_in[0].shape[0]
     heads, half_rows = own.shape[2], own.shape[3]
@@ -159,7 +162,7 @@
     queries_out = pl.BlockSpec((2, rows_q, d), lambda h, where_ref: (0, 0, h))
     pairs = heads * 2 * rows_q * chips * rows_k
     return pl.pallas_call(
-        functools.partial(attention_kernel, chips, 1.0 / math.sqrt(d)),
+        functools.partial(attention_kernel, chips, len(before), 1.0 / math.sqrt(d)),
         grid_spec=pltpu.PrefetchScalarGridSpec(
             num_scalar_prefetch=1,
             grid=(heads,),
@@ -169,15 +172,17 @@
                 pl.BlockSpec((1, rows_q, 4 * d), lambda h, where_ref: (first + h, 0, 0)),
             ]
             + [payload] * chips
-            + [slots],
+            + [slots]
+            + [pl.BlockSpec(memory_space=pl.ANY)] * len(before),
             out_specs=[
                 queries_out,
                 queries_out,
                 slots,
-                slots,
                 pl.BlockSpec((2, 1, half_rows, 4 * d), lambda h, where_ref: (0, h, 0, 0)),
                 pl.BlockSpec((1, 1, d), lambda h, where_ref: (h, 0, 0)),
-            ],
+            ]
+            + [pl.BlockSpec((2, 1, half_rows, 4 * d), lambda h, where_ref: (0, h, 0, 0))]
+            * (chips - 1),
             scratch_shapes=[
                 pltpu.VMEM((chips, rows_k, 4 * d), BF16),
                 pltpu.VMEM((chips, rows_k, 4 * d), BF16),
@@ -187,29 +192,31 @@
             jax.ShapeDtypeStruct((2, rows_q, heads * d), BF16),
             jax.ShapeDtypeStruct((2, rows_q, heads * d), BF16),
             jax.ShapeDtypeStruct((chips - 1, 2, heads, half_rows, 4 * d), BF16),
-            jax.ShapeDtypeStruct((chips - 1, 2, heads, half_rows, 4 * d), BF16),
             jax.ShapeDtypeStruct((2, heads, half_rows, 4 * d), F32),
             jax.ShapeDtypeStruct((heads, 1, d), F32),
-        ],
+        ]
+        + [jax.ShapeDtypeStruct((2, heads, half_rows, 4 * d), BF16)] * (chips - 1),
         compiler_params=pltpu.CompilerParams(vmem_limit_bytes=48 * 1024 * 1024),
         cost_estimate=pl.CostEstimate(
             flops=pairs * 36 * d, bytes_accessed=pairs * 16, transcendentals=pairs
         ),
-    )(where, *rows_in, gain, swapped, own, *along, other)
-
-
-def finish_kernel(where_ref, kept_ref, came_ref, *refs):
-    total = kept_ref[...].astype(F32) + came_ref[...].astype(F32)
-    heads = kept_ref.shape[1]
+    )(where, *rows_in, gain, swapped, own, *along, other, *before)
+
+
+def finish_kernel(where_ref, arrived_ref, own_ref, came_ref, *refs):
+    half = pl.program_id(0) // (pl.num_programs(0) // 2)
+    heads = came_ref.shape[1]
+    mine = jnp.where(half == 0, own_ref[0], jnp.zeros_like(own_ref[0]))
+    total = arrived_ref[0, 0].astype(F32) + came_ref[0].astype(F32) + mine
     for i, ref in enumerate(refs[-4:]):
         for h in range(heads):
             ref[:, h * HEAD_DIM : (h + 1) * HEAD_DIM] = total[
-                0, h, :, i * HEAD_DIM : (i + 1) * HEAD_DIM
+                h, :, i * HEAD_DIM : (i + 1) * HEAD_DIM
             ].astype(BF16)
 
 
-def finish(where, kept, came, before, width, core_heads, first):
-    heads, rows = kept.shape[1], kept.shape[2]
+def finish(where, arrived, own, came, before, width, core_heads, first):
+    heads, rows = came.shape[1], came.shape[2]
     block = math.gcd(heads, first) if first else heads
     steps = heads // block
 
@@ -218,6 +225,7 @@
         return (0, (half * core_heads + first) // block + lax.rem(i, steps))
 
     old = list(before or ())
+    size = (block, rows, 4 * HEAD_DIM)
     return pl.pallas_call(
         finish_kernel,
         grid_spec=pltpu.PrefetchScalarGridSpec(
@@ -225,23 +233,37 @@
             grid=(2 * steps,),
             in_specs=[
                 pl.BlockSpec(
-                    (1, block, rows, 4 * HEAD_DIM),
-                    lambda i, where_ref: (i // steps, lax.rem(i, steps), 0, 0),
+                    (1, 1) + size, lambda i, where_ref: (i // steps, 0, lax.rem(i, steps), 0, 0)
                 ),
+                pl.BlockSpec((1,) + size, lambda i, where_ref: (0, lax.rem(i, steps), 0, 0)),
                 pl.BlockSpec(
-                    (1, block, rows, 4 * HEAD_DIM),
-                    lambda i, where_ref: (1 - i // steps, lax.rem(i, steps), 0, 0),
+                    (1,) + size, lambda i, where_ref: (1 - i // steps, lax.rem(i, steps), 0, 0)
                 ),
             ]
             + [pl.BlockSpec(memory_space=pl.ANY)] * len(old),
             out_specs=[pl.BlockSpec((rows, block * HEAD_DIM), column)] * 4,
         ),
         out_shape=[jax.ShapeDtypeStruct((rows, width), BF16)] * 4,
-        input_output_aliases={3 + i: i for i in range(len(old))},
+        input_output_aliases={4 + i: i for i in range(len(old))},
         cost_estimate=pl.CostEstimate(
             flops=0, bytes_accessed=heads * rows * HEAD_DIM * 48, transcendentals=0
         ),
-    )(where, kept, came, *old)
+    )(where, arrived, own, came, *old)
+
+
+def after(array, *before):
+    return lax.optimization_barrier((array,) + before)[0] if before else array
+
+
+def sum_over(array, axis):
+    size = lax.axis_size(axis)
+    if size & (size - 1):
+        return lax.psum(array, axis)
+    far = 1
+    while far < size:
+        array = array + lax.ppermute(array, axis, [(i, i ^ far) for i in range(size)])
+        far *= 2
+    return array
 
 
 def per_device(
@@ -290,51 +312,104 @@
     )
     swapped = swap(packed_rows)
 
+    parts = len(sizes)
+    along = [[] for _ in sizes]
+    results = [None] * parts
+    arrived = [None] * parts
     gradients = None
-    parts, sent, gains = [], [], []
-    for index, (first, heads) in enumerate(zip(starts, sizes)):
-        along = []
-        moving = owns[index]
-        for step in range(1, chips):
-            moving = outward(moving, step)
-            along.append(moving)
-        other = swap(jnp.stack([a[1] for a in along]))
-        dq, dq_other, d_along, d_other, d_own, gain_part = attention(
-            where, rows_in, gain, swapped, owns[index], along, other, core_heads, first
+
+    def gather(index, *before):
+        step = len(along[index]) + 1
+        moving = along[index][-1] if along[index] else owns[index]
+        along[index].append(outward(after(moving, *before), step))
+
+    def attend(index, *before):
+        first = starts[index]
+        other = swap(jnp.stack([a[1] for a in along[index]]))
+        out = attention(
+            where,
+            rows_in,
+            gain,
+            swapped,
+            owns[index],
+            along[index],
+            other,
+            core_heads,
+            first,
+            before,
         )
-        gains.append(gain_part.reshape(heads * HEAD_DIM))
-        parts.append(dq)
-        sent.append(dq_other)
-        d_theirs = swap(d_other)
-        arrived = None
-        for far in range(chips - 1, 0, -1):
-            payload = jnp.stack([d_along[far - 1], d_theirs[far - 1]])
-            if arrived is not None:
-                payload = (payload.astype(F32) + arrived.astype(F32)).astype(BF16)
-            arrived = homeward(payload, far)
-        total = arrived.astype(F32)
-        total = jnp.stack([total[0] + d_own, total[1]]).astype(BF16)
-        came = swap(total[:, 1])
-        gradients = finish(
-            where, total[:, 0], came, gradients, width, core_heads, first
+        results[index] = (out[0], out[1], out[3], out[4], out[5:], swap(out[2]))
+        return out[3]
+
+    def homewards(index, far, *before):
+        d_along, d_theirs = results[index][4:]
+        payload = jnp.stack([d_along[far - 1], d_theirs[far - 1]])
+        if arrived[index] is not None:
+            payload = (payload.astype(F32) + arrived[index].astype(F32)).astype(BF16)
+        arrived[index] = homeward(after(payload, *before), far)
+
+    def conclude(index, gradients):
+        own = results[index][2]
+        leaving = jnp.stack(
+            [arrived[index][0, 1].astype(F32) + own[1], arrived[index][1, 1].astype(F32)]
+        ).astype(BF16)
+        return finish(
+            where,
+            arrived[index],
+            own,
+            swap(leaving),
+            gradients,
+            width,
+            core_heads,
+            starts[index],
         )
 
-    dq_mine = jnp.concatenate(parts, axis=2)
-    dq_theirs = swap(jnp.concatenate(sent, axis=2))
+    for step in range(1, chips):
+        gather(0)
+    gather(1, along[0][0])
+    if parts > 2:
+        gather(2, along[0][1])
+    ready = along[0][-1]
+    for index in range(parts):
+        if index + 1 < parts:
+            while len(along[index + 1]) < chips - 2:
+                gather(index + 1, ready)
+        if index:
+            homewards(index - 1, chips - 2, ready)
+        done = attend(index)
+        if index + 1 < parts:
+            gather(index + 1, done)
+        if index + 3 < parts:
+            gather(index + 3, done)
+        if index:
+            for far in range(chips - 3, 0, -1):
+                homewards(index - 1, far, done)
+        homewards(index, chips - 1)
+        if index + 1 < parts:
+            ready = along[index + 1][-1]
+        if index > 1:
+            gradients = conclude(index - 2, gradients)
+    gain_mine = jnp.concatenate([r[3].reshape(-1) for r in results])
+    gain_zero = jnp.zeros_like(gain_mine)
+    gain_all = jnp.where(
+        core == 0,
+        jnp.concatenate([gain_mine, gain_zero]),
+        jnp.concatenate([gain_zero, gain_mine]),
+    ).reshape(count, width // count)
+    gain_all = lax.all_to_all(gain_all, "ctx", split_axis=0, concat_axis=0, tiled=True)
+    gain_grad = sum_over(jnp.sum(gain_all, axis=0), "dp")
+    for far in range(chips - 2, 0, -1):
+        homewards(parts - 1, far)
+    gradients = conclude(parts - 2, gradients)
+    gradients = conclude(parts - 1, gradients)
+
+    dq_mine = jnp.concatenate([r[0] for r in results], axis=2)
+    dq_theirs = swap(jnp.concatenate([r[1] for r in results], axis=2))
     halves = jnp.where(
         core == 0,
         jnp.concatenate([dq_mine, dq_theirs], axis=2),
         jnp.concatenate([dq_theirs, dq_mine], axis=2),
     )
-    gain_mine = jnp.concatenate(gains)
-    gain_zero = jnp.zeros_like(gain_mine)
-    gain_all = jnp.where(
-        core == 0,
-        jnp.concatenate([gain_mine, gain_zero]),
-        jnp.concatenate([gain_zero, gain_mine]),
-    )
-    gain_all = lax.psum(gain_all, ("dp", "ctx"))
-    gain_grad = lax.dynamic_slice_in_dim(gain_all, place * (width // count), width // count)
     return (halves[0][None], halves[1][None]) + tuple(g[None] for g in gradients) + (gain_grad,)
 
 

time: 394 us -> 364 us (0.924)
  waiting for transfers between devices: 60.6 us -> 105 us
  starting transfers between devices: 144 us -> 104 us
  blocking collectives: 39.8 us -> 0 us
    ppermute x22, starting transfers between devices: 73.3 us -> 12.7 us  [swap(): return lax.ppermute(array, 'ctx', swap_pairs)]
    psum x1 -> x0, blocking collectives: 39.8 us -> none  [per_device(): gain_all = lax.psum(gain_all, ('dp', 'ctx'))]
    ppermute x15, waiting for transfers between devices: 9.77 us -> 31.6 us  [outward(): return lax.ppermute(array, 'ctx', pairs)]
    unnamed x134 -> x186, local copies, waits for them, and re-layouts: 12.3 us -> 26.5 us
    ppermute x15, waiting for transfers between devices: 50.5 us -> 64.6 us  [homeward(): return lax.ppermute(array, 'ctx', pairs)]
    ppermute x15, starting transfers between devices: 44.4 us -> 57.9 us  [outward(): return lax.ppermute(array, 'ctx', pairs)]
    pallas_call x5 -> x0, local copies, waits for them, and re-layouts: 8.9 us -> none  [attention(): pl.pallas_call(functools.partial(attention_kernel, chips, 1.0 / math.sqrt...]
    all_to_all x0 -> x1, starting transfers between devices: none -> 7.13 us  [per_device(): lax.all_to_all(gain_all, 'ctx', split_axis=0, concat_axis=0, tiled=True)]
  transfers between devices with their start and end apart: 52 -> 55, of which waited for: 8 -> 16; matrix products, arithmetic and copies ran while one was open for 15% -> 15% of each run, Pallas kernels for 19% -> 20%
where the time goes in v2:
time: 364 us; the launch traced here: 359 us
  waiting for transfers between devices  105 us (29%)
  starting transfers between devices  104 us (29%)
  Pallas kernels  77.9 us (21%)
  local copies, waits for them, and re-layouts  47.5 us (13%)
  other arithmetic  22.9 us (6%)
    ppermute x15, waiting for transfers between devices, homeward(): return lax.ppermute(array, 'ctx', pairs)  64.6 us
    ppermute x15, starting transfers between devices, outward(): return lax.ppermute(array, 'ctx', pairs)  57.9 us
    pallas_call x5, Pallas kernels, attention(): pl.pallas_call(functools.partial(attention_kernel, chips, len(before), 1....  39.3 us
    ppermute x15, waiting for transfers between devices, outward(): return lax.ppermute(array, 'ctx', pairs)  31.6 us
    unnamed x186, local copies, waits for them, and re-layouts  26.5 us
    ppermute x15, starting transfers between devices, homeward(): return lax.ppermute(array, 'ctx', pairs)  23.2 us
    pallas_call x6, Pallas kernels, pack(): pl.pallas_call(pack_kernel, grid_spec=pltpu.PrefetchScalarGridSpec(num_sc...  20.7 us
    pallas_call x5, Pallas kernels, finish(): pl.pallas_call(finish_kernel, grid_spec=pltpu.PrefetchScalarGridSpec(num_...  17.9 us
  transfers between devices with their start and end apart: 55, of which 16 were waited for; matrix products, arithmetic and copies ran while one was open for 15% of the time, Pallas kernels for 20%

profile of v2, /device:TPU:8, one launch (start us, length us, event | category | flops | bytes accessed | tf_op | source)
XLA Modules:
  0.0 359.3 jit_solution(17272746500585638391)
XLA Ops:
  11.4 4.8 %shard_map.144 = bf16[16,128,512]{2,1,0:T(8,128)(2,1)} custom-call(s32[2]{0:T(128)} %pad_add_fusion.where_ref, bf16[128,4096]{1,0:T(8,128)(2,1)} %bitcast.90, bf16[128,4096]{1,0:T(8,128)(2,1)} %bitcast.96, bf16[128,4096]{1,0:T(8,128)(2,1)} %bitcast.122, bf16[128,4096]{1,0:T(8,128)(2,1)} %bitcast.128), custom_call_target="tpu_custom_call" | custom-call | bytes 4194304 | tf_op jit(solution)/shard_map/pallas_call | solution.py:46
  29.9 10.5 %collective-permute-done.7.refs_7_ = bf16[2,2,4,64,512]{4,3,2,1,0:T(8,128)(2,1)S(1)} collective-permute-done((bf16[2,2,4,64,512]{4,3,2,1,0:T(8,128)(2,1)S(1)}, bf16[2,2,4,64,512]{4,3,2,1,0:T(8,128)(2,1)S(1)}, u32[]{:S(2)}, u32[]{:S(2)}) %collective-permute-start.7) | collective-permute-done | bytes 1048608 | tf_op jit(solution)/shard_map/ppermute | solution.py:288
  40.4 10.1 %collective-permute-start.8 = (bf16[2,2,4,64,512]{4,3,2,1,0:T(8,128)(2,1)S(1)}, bf16[2,2,4,64,512]{4,3,2,1,0:T(8,128)(2,1)}, u32[]{:S(2)}, u32[]{:S(2)}) collective-permute-start(bf16[2,2,4,64,512]{4,3,2,1,0:T(8,128)(2,1)S(1)} %collective-permute-done.7.refs_7_), channel_id=1, source_target_pairs={{2,4},{4,6},{3,1},{5,3},{10,12},{12,14},{11,9},{13,11},{18,20},{20... | collective-permute-start | bytes 3145736 | tf_op jit(solution)/shard_map/ppermute | solution.py:288
  53.1 5.1 %shard_map.146 = (bf16[2,128,256]{2,1,0:T(8,128)(2,1)S(1)}, bf16[2,128,256]{2,1,0:T(8,128)(2,1)S(1)}, bf16[3,2,2,64,512]{4,3,2,1,0:T(8,128)(2,1)S(1)}, f32[2,2,6...) custom-call(s32[2]{0:T(128)S(1)} %copy-done.43, ...), custom_call_target="tpu_custom_call" | custom-call | flops 1207959552 | bytes 4194304 | tf_op jit(solution)/shard_map/pallas_call | solution.py:164
  71.5 7.2 %collective-permute-start.12 = (bf16[2,2,4,64,512]{4,3,2,1,0:T(8,128)(2,1)S(1)}, bf16[2,2,4,64,512]{4,3,2,1,0:T(8,128)(2,1)S(1)}, u32[]{:S(2)}, u32[]{:S(2)}) collective-permute-start(bf16[2,2,4,64,512]{4,3,2,1,0:T(8,128)(2,1)S(1)} %pad_maximum_fusion.4.refs_6_), channel_id=1, source_target_pairs={{0,2},{2,4},{4,6},{3,1},{5,3},{7,5},{8,10},{10,12},{12,14},{11,9},... | collective-permute-start | bytes 3145736 | tf_op jit(solution)/shard_map/ppermute | solution.py:288
  81.4 9.6 %collective-permute-done.12.refs_7_ = bf16[2,2,4,64,512]{4,3,2,1,0:T(8,128)(2,1)S(1)} collective-permute-done((bf16[2,2,4,64,512]{4,3,2,1,0:T(8,128)(2,1)S(1)}, bf16[2,2,4,64,512]{4,3,2,1,0:T(8,128)(2,1)S(1)}, u32[]{:S(2)}, u32[]{:S(2)}) %collective-permute-start.12) | collective-permute-done | bytes 1048608 | tf_op jit(solution)/shard_map/ppermute | solution.py:288
  91.0 5.3 %collective-permute-start.13 = (bf16[2,2,4,64,512]{4,3,2,1,0:T(8,128)(2,1)S(1)}, bf16[2,2,4,64,512]{4,3,2,1,0:T(8,128)(2,1)}, u32[]{:S(2)}, u32[]{:S(2)}) collective-permute-start(bf16[2,2,4,64,512]{4,3,2,1,0:T(8,128)(2,1)S(1)} %collective-permute-done.12.refs_7_), channel_id=1, source_target_pairs={{2,4},{4,6},{3,1},{5,3},{10,12},{12,14},{11,9},{13,11},{18,20},{20... | collective-permute-start | bytes 3145736 | tf_op jit(solution)/shard_map/ppermute | solution.py:288
  97.5 9.7 %shard_map.148 = (bf16[2,128,512]{2,1,0:T(8,128)(2,1)S(1)}, bf16[2,128,512]{2,1,0:T(8,128)(2,1)S(1)}, bf16[3,2,4,64,512]{4,3,2,1,0:T(8,128)(2,1)}, f32[2,4,64,51...) custom-call(s32[2]{0:T(128)S(1)} %copy-done.44, ...), custom_call_target="tpu_custom_call" | custom-call | flops 2415919104 | bytes 8388608 | tf_op jit(solution)/shard_map/pallas_call | solution.py:164
  118.7 5.1 %collective-permute-start.17 = (bf16[2,2,4,64,512]{4,3,2,1,0:T(8,128)(2,1)S(1)}, bf16[2,2,4,64,512]{4,3,2,1,0:T(8,128)(2,1)}, u32[]{:S(2)}, u32[]{:S(2)}) collective-permute-start(bf16[2,2,4,64,512]{4,3,2,1,0:T(8,128)(2,1)S(1)} %pad_maximum_fusion.5.refs_6_), channel_id=1, source_target_pairs={{0,2},{2,4},{4,6},{3,1},{5,3},{7,5},{8,10},{10,12},{12,14},{11,9},... | collective-permute-start | bytes 3145736 | tf_op jit(solution)/shard_map/ppermute | solution.py:288
  130.7 5.7 %collective-permute-done.17.refs_7_ = bf16[2,2,4,64,512]{4,3,2,1,0:T(8,128)(2,1)} collective-permute-done((bf16[2,2,4,64,512]{4,3,2,1,0:T(8,128)(2,1)S(1)}, bf16[2,2,4,64,512]{4,3,2,1,0:T(8,128)(2,1)}, u32[]{:S(2)}, u32[]{:S(2)}) %collective-permute-start.17) | collective-permute-done | bytes 1048608 | tf_op jit(solution)/shard_map/ppermute | solution.py:288
  136.5 5.2 %collective-permute-start.18 = (bf16[2,2,4,64,512]{4,3,2,1,0:T(8,128)(2,1)}, bf16[2,2,4,64,512]{4,3,2,1,0:T(8,128)(2,1)}, u32[]{:S(2)}, u32[]{:S(2)}) collective-permute-start(bf16[2,2,4,64,512]{4,3,2,1,0:T(8,128)(2,1)} %collective-permute-done.17.refs_7_), channel_id=1, source_target_pairs={{2,4},{4,6},{3,1},{5,3},{10,12},{12,14},{11,9},{13,11},{18,20},{20... | collective-permute-start | bytes 3145736 | tf_op jit(solution)/shard_map/ppermute | solution.py:288
  149.0 9.7 %shard_map.150 = (bf16[2,128,512]{2,1,0:T(8,128)(2,1)S(1)}, bf16[2,128,512]{2,1,0:T(8,128)(2,1)S(1)}, bf16[3,2,4,64,512]{4,3,2,1,0:T(8,128)(2,1)}, f32[2,4,64,51...) custom-call(s32[2]{0:T(128)S(1)} %copy-done.45, ...), custom_call_target="tpu_custom_call" | custom-call | flops 2415919104 | bytes 8388608 | tf_op jit(solution)/shard_map/pallas_call | solution.py:164
  162.0 5.0 %collective-permute-start.37 = (bf16[3,2,4,64,512]{4,3,2,1,0:T(8,128)(2,1)}, bf16[3,2,4,64,512]{4,3,2,1,0:T(8,128)(2,1)S(1)}, u32[]{:S(2)}, u32[]{:S(2)}) collective-permute-start(bf16[3,2,4,64,512]{4,3,2,1,0:T(8,128)(2,1)} %get-tuple-element.125), channel_id=1, source_target_pairs={{0,1},{1,0},{2,3},{3,2},{4,5},{5,4},{6,7},{7,6},{8,9},{9,8},{10,11... | collective-permute-start | bytes 4718600 | tf_op jit(solution)/shard_map/ppermute | solution.py:283
  193.1 5.2 %collective-permute-done.44 = bf16[2,2,4,64,512]{4,3,2,1,0:T(8,128)(2,1)S(1)} collective-permute-done((bf16[2,2,4,64,512]{4,3,2,1,0:T(8,128)(2,1)S(1)}, bf16[2,2,4,64,512]{4,3,2,1,0:T(8,128)(2,1)S(1)}, u32[]{:S(2)}, u32[]{:S(2)}) %collective-permute-start.44) | collective-permute-done | bytes 1048608 | tf_op jit(solution)/shard_map/ppermute | solution.py:293
  201.6 4.7 %collective-permute-start.23 = (bf16[2,2,2,64,512]{4,3,2,1,0:T(8,128)(2,1)}, bf16[2,2,2,64,512]{4,3,2,1,0:T(8,128)(2,1)}, u32[]{:S(2)}, u32[]{:S(2)}) collective-permute-start(bf16[2,2,2,64,512]{4,3,2,1,0:T(8,128)(2,1)} %collective-permute-done.22.refs_7_), channel_id=1, source_target_pairs={{2,4},{4,6},{3,1},{5,3},{10,12},{12,14},{11,9},{13,11},{18,20},{20... | collective-permute-start | bytes 1572872 | tf_op jit(solution)/shard_map/ppermute | solution.py:288
  216.6 9.7 %shard_map.152 = (bf16[2,128,512]{2,1,0:T(8,128)(2,1)S(1)}, bf16[2,128,512]{2,1,0:T(8,128)(2,1)S(1)}, bf16[3,2,4,64,512]{4,3,2,1,0:T(8,128)(2,1)}, f32[2,4,64,51...) custom-call(s32[2]{0:T(128)S(1)} %copy-done.46, ...), custom_call_target="tpu_custom_call" | custom-call | flops 2415919104 | bytes 8388608 | tf_op jit(solution)/shard_map/pallas_call | solution.py:164
  240.2 8.3 %collective-permute-done.39 = bf16[2,2,4,64,512]{4,3,2,1,0:T(8,128)(2,1)S(1)} collective-permute-done((bf16[2,2,4,64,512]{4,3,2,1,0:T(8,128)(2,1)S(1)}, bf16[2,2,4,64,512]{4,3,2,1,0:T(8,128)(2,1)S(1)}, u32[]{:S(2)}, u32[]{:S(2)}) %collective-permute-start.39) | collective-permute-done | bytes 1048608 | tf_op jit(solution)/shard_map/ppermute | solution.py:293
  251.9 5.2 %shard_map.154 = (bf16[2,128,256]{2,1,0:T(8,128)(2,1)S(1)}, bf16[2,128,256]{2,1,0:T(8,128)(2,1)S(1)}, bf16[3,2,2,64,512]{4,3,2,1,0:T(8,128)(2,1)S(1)}, f32[2,2,6...) custom-call(s32[2]{0:T(128)S(1)} %copy-done.46, ...), custom_call_target="tpu_custom_call" | custom-call | flops 1207959552 | bytes 4194304 | tf_op jit(solution)/shard_map/pallas_call | solution.py:164
  258.7 7.1 %all-to-all-start = ((f32[8,1,512]{2,1,0:T(1,128)}), f32[8,1,512]{2,1,0:T(1,128)S(1)}, u32[]{:S(2)}, u32[]{:S(2)}) async-start(f32[8,1,512]{2,1,0:T(1,128)} %bitcast.59), calls=%async_computation | async-start | bytes 32768 | tf_op jit(solution)/shard_map/all_to_all | solution.py:399
  266.5 4.2 %shard_map.156 = (bf16[64,4096]{1,0:T(8,128)(2,1)}, bf16[64,4096]{1,0:T(8,128)(2,1)}, bf16[64,4096]{1,0:T(8,128)(2,1)}, bf16[64,4096]{1,0:T(8,128)(2,1)}) custom-call(s32[2]{0:T(128)} %pad_add_fusion.where_ref, ...), custom_call_target="tpu_custom_call", output_to_operand_aliasing={{0}: (4, {}), {1}: (5, {}), {2}: (6, {}), {3}: (7, {})} | custom-call | bytes 1572864 | tf_op jit(solution)/shard_map/pallas_call | solution.py:229
  290.8 30.0 %collective-permute-done.29 = bf16[2,2,2,64,512]{4,3,2,1,0:T(8,128)(2,1)S(1)} collective-permute-done((bf16[2,2,2,64,512]{4,3,2,1,0:T(8,128)(2,1)S(1)}, bf16[2,2,2,64,512]{4,3,2,1,0:T(8,128)(2,1)S(1)}, u32[]{:S(2)}, u32[]{:S(2)}) %collective-permute-start.29) | collective-permute-done | bytes 524320 | tf_op jit(solution)/shard_map/ppermute | solution.py:293
  325.4 6.6 %collective-permute-done.30.arrived_ref = bf16[2,2,2,64,512]{4,3,2,1,0:T(8,128)(2,1)S(1)} collective-permute-done((bf16[2,2,2,64,512]{4,3,2,1,0:T(8,128)(2,1)S(1)}, bf16[2,2,2,64,512]{4,3,2,1,0:T(8,128)(2,1)S(1)}, u32[]{:S(2)}, u32[]{:S(2)}) %collective-permute-start.30) | collective-permute-done | bytes 524320 | tf_op jit(solution)/shard_map/ppermute | solution.py:293
  332.9 10.3 %collective-permute-done.35.arrived_ref = bf16[2,2,4,64,512]{4,3,2,1,0:T(8,128)(2,1)S(1)} collective-permute-done((bf16[2,2,4,64,512]{4,3,2,1,0:T(8,128)(2,1)S(1)}, bf16[2,2,4,64,512]{4,3,2,1,0:T(8,128)(2,1)S(1)}, u32[]{:S(2)}, u32[]{:S(2)}) %collective-permute-start.35) | collective-permute-done | bytes 1048608 | tf_op jit(solution)/shard_map/ppermute | solution.py:293
  346.6 4.2 %shard_map.157 = (bf16[64,4096]{1,0:T(8,128)(2,1)}, bf16[64,4096]{1,0:T(8,128)(2,1)}, bf16[64,4096]{1,0:T(8,128)(2,1)}, bf16[64,4096]{1,0:T(8,128)(2,1)}) custom-call(s32[2]{0:T(128)} %pad_add_fusion.where_ref, ...), custom_call_target="tpu_custom_call", output_to_operand_aliasing={{0}: (4, {}), {1}: (5, {}), {2}: (6, {}), {3}: (7, {})} | custom-call | bytes 1572864 | tf_op jit(solution)/shard_map/pallas_call | solution.py:229
  (366 shorter events, 168.2 us)
Async XLA Ops:
  16.2 34.6 %collective-permute-start = (bf16[16,128,512]{2,1,0:T(8,128)(2,1)}, bf16[16,128,512]{2,1,0:T(8,128)(2,1)S(1)}, u32[]{:S(2)}, u32[]{:S(2)}) collective-permute-start(bf16[16,128,512]{2,1,0:T(8,128)(2,1)} %shard_map.144), channel_id=1, source_target_pairs={{0,1},{1,0},{2,3},{3,2},{4,5},{5,4},{6,7},{7,6},{8,9},{9,8},{10,11... | collective-permute-start | bytes 6291464 | tf_op jit(solution)/shard_map/ppermute | solution.py:283
  40.4 22.0 %collective-permute-start.8 = (bf16[2,2,4,64,512]{4,3,2,1,0:T(8,128)(2,1)S(1)}, bf16[2,2,4,64,512]{4,3,2,1,0:T(8,128)(2,1)}, u32[]{:S(2)}, u32[]{:S(2)}) collective-permute-start(bf16[2,2,4,64,512]{4,3,2,1,0:T(8,128)(2,1)S(1)} %collective-permute-done.7.refs_7_), channel_id=1, source_target_pairs={{2,4},{4,6},{3,1},{5,3},{10,12},{12,14},{11,9},{13,11},{18,20},{20... | collective-permute-start | bytes 3145736 | tf_op jit(solution)/shard_map/ppermute | solution.py:288
  71.5 19.5 %collective-permute-start.12 = (bf16[2,2,4,64,512]{4,3,2,1,0:T(8,128)(2,1)S(1)}, bf16[2,2,4,64,512]{4,3,2,1,0:T(8,128)(2,1)S(1)}, u32[]{:S(2)}, u32[]{:S(2)}) collective-permute-start(bf16[2,2,4,64,512]{4,3,2,1,0:T(8,128)(2,1)S(1)} %pad_maximum_fusion.4.refs_6_), channel_id=1, source_target_pairs={{0,2},{2,4},{4,6},{3,1},{5,3},{7,5},{8,10},{10,12},{12,14},{11,9},... | collective-permute-start | bytes 3145736 | tf_op jit(solution)/shard_map/ppermute | solution.py:288
  91.0 18.8 %collective-permute-start.13 = (bf16[2,2,4,64,512]{4,3,2,1,0:T(8,128)(2,1)S(1)}, bf16[2,2,4,64,512]{4,3,2,1,0:T(8,128)(2,1)}, u32[]{:S(2)}, u32[]{:S(2)}) collective-permute-start(bf16[2,2,4,64,512]{4,3,2,1,0:T(8,128)(2,1)S(1)} %collective-permute-done.12.refs_7_), channel_id=1, source_target_pairs={{2,4},{4,6},{3,1},{5,3},{10,12},{12,14},{11,9},{13,11},{18,20},{20... | collective-permute-start | bytes 3145736 | tf_op jit(solution)/shard_map/ppermute | solution.py:288
  117.4 29.1 %collective-permute-start.42 = (bf16[3,2,4,64,512]{4,3,2,1,0:T(8,128)(2,1)}, bf16[3,2,4,64,512]{4,3,2,1,0:T(8,128)(2,1)}, u32[]{:S(2)}, u32[]{:S(2)}) collective-permute-start(bf16[3,2,4,64,512]{4,3,2,1,0:T(8,128)(2,1)} %get-tuple-element.131), channel_id=1, source_target_pairs={{0,1},{1,0},{2,3},{3,2},{4,5},{5,4},{6,7},{7,6},{8,9},{9,8},{10,11... | collective-permute-start | bytes 4718600 | tf_op jit(solution)/shard_map/ppermute | solution.py:283
  127.4 21.6 %collective-permute-start.15 = (bf16[3,2,4,64,512]{4,3,2,1,0:T(8,128)(2,1)}, bf16[3,2,4,64,512]{4,3,2,1,0:T(8,128)(2,1)}, u32[]{:S(2)}, u32[]{:S(2)}) collective-permute-start(bf16[3,2,4,64,512]{4,3,2,1,0:T(8,128)(2,1)} %pad_maximum_fusion.1), channel_id=1, source_target_pairs={{0,1},{1,0},{2,3},{3,2},{4,5},{5,4},{6,7},{7,6},{8,9},{9,8},{10,11... | collective-permute-start | bytes 4718600 | tf_op jit(solution)/shard_map/ppermute | solution.py:283
  136.5 23.6 %collective-permute-start.18 = (bf16[2,2,4,64,512]{4,3,2,1,0:T(8,128)(2,1)}, bf16[2,2,4,64,512]{4,3,2,1,0:T(8,128)(2,1)}, u32[]{:S(2)}, u32[]{:S(2)}) collective-permute-start(bf16[2,2,4,64,512]{4,3,2,1,0:T(8,128)(2,1)} %collective-permute-done.17.refs_7_), channel_id=1, source_target_pairs={{2,4},{4,6},{3,1},{5,3},{10,12},{12,14},{11,9},{13,11},{18,20},{20... | collective-permute-start | bytes 3145736 | tf_op jit(solution)/shard_map/ppermute | solution.py:288
  145.2 25.1 %collective-permute-start.49 = (bf16[2,2,2,64,512]{4,3,2,1,0:T(8,128)(2,1)S(1)}, bf16[2,2,2,64,512]{4,3,2,1,0:T(8,128)(2,1)S(1)}, u32[]{:S(2)}, u32[]{:S(2)}) collective-permute-start(bf16[2,2,2,64,512]{4,3,2,1,0:T(8,128)(2,1)S(1)} %add_convert_fusion.7), channel_id=1, source_target_pairs={{4,2},{6,4},{1,3},{3,5},{12,10},{14,12},{9,11},{11,13},{20,18},{22... | collective-permute-start | bytes 1572872 | tf_op jit(solution)/shard_map/ppermute | solution.py:293
  148.1 31.0 %collective-permute-start.43 = (bf16[2,2,4,64,512]{4,3,2,1,0:T(8,128)(2,1)S(1)}, bf16[2,2,4,64,512]{4,3,2,1,0:T(8,128)(2,1)S(1)}, u32[]{:S(2)}, u32[]{:S(2)}) collective-permute-start(bf16[2,2,4,64,512]{4,3,2,1,0:T(8,128)(2,1)S(1)} %pad_maximum_fusion.8), channel_id=1, source_target_pairs={{6,4},{1,3},{14,12},{9,11},{22,20},{17,19},{30,28},{25,27}} | collective-permute-start | bytes 3145736 | tf_op jit(solution)/shard_map/ppermute | solution.py:293
  160.0 20.9 %collective-permute-start.19 = (bf16[2,2,4,64,512]{4,3,2,1,0:T(8,128)(2,1)}, bf16[2,2,4,64,512]{4,3,2,1,0:T(8,128)(2,1)S(1)}, u32[]{:S(2)}, u32[]{:S(2)}) collective-permute-start(bf16[2,2,4,64,512]{4,3,2,1,0:T(8,128)(2,1)} %collective-permute-done.18.refs_8_), channel_id=1, source_target_pairs={{4,6},{3,1},{12,14},{11,9},{20,22},{19,17},{28,30},{27,25}} | collective-permute-start | bytes 3145736 | tf_op jit(solution)/shard_map/ppermute | solution.py:288
  162.0 27.1 %collective-permute-start.37 = (bf16[3,2,4,64,512]{4,3,2,1,0:T(8,128)(2,1)}, bf16[3,2,4,64,512]{4,3,2,1,0:T(8,128)(2,1)S(1)}, u32[]{:S(2)}, u32[]{:S(2)}) collective-permute-start(bf16[3,2,4,64,512]{4,3,2,1,0:T(8,128)(2,1)} %get-tuple-element.125), channel_id=1, source_target_pairs={{0,1},{1,0},{2,3},{3,2},{4,5},{5,4},{6,7},{7,6},{8,9},{9,8},{10,11... | collective-permute-start | bytes 4718600 | tf_op jit(solution)/shard_map/ppermute | solution.py:283
  170.5 31.1 %collective-permute-start.22 = (bf16[2,2,2,64,512]{4,3,2,1,0:T(8,128)(2,1)S(1)}, bf16[2,2,2,64,512]{4,3,2,1,0:T(8,128)(2,1)}, u32[]{:S(2)}, u32[]{:S(2)}) collective-permute-start(bf16[2,2,2,64,512]{4,3,2,1,0:T(8,128)(2,1)S(1)} %pad_maximum_fusion.12.refs_6_), channel_id=1, source_target_pairs={{0,2},{2,4},{4,6},{3,1},{5,3},{7,5},{8,10},{10,12},{12,14},{11,9},... | collective-permute-start | bytes 1572872 | tf_op jit(solution)/shard_map/ppermute | solution.py:288
  182.5 33.4 %collective-permute-start.20 = (bf16[3,2,4,64,512]{4,3,2,1,0:T(8,128)(2,1)}, bf16[3,2,4,64,512]{4,3,2,1,0:T(8,128)(2,1)}, u32[]{:S(2)}, u32[]{:S(2)}) collective-permute-start(bf16[3,2,4,64,512]{4,3,2,1,0:T(8,128)(2,1)} %pad_maximum_fusion.2), channel_id=1, source_target_pairs={{0,1},{1,0},{2,3},{3,2},{4,5},{5,4},{6,7},{7,6},{8,9},{9,8},{10,11... | collective-permute-start | bytes 4718600 | tf_op jit(solution)/shard_map/ppermute | solution.py:283
  191.2 38.4 %collective-permute-start.38 = (bf16[2,2,4,64,512]{4,3,2,1,0:T(8,128)(2,1)}, bf16[2,2,4,64,512]{4,3,2,1,0:T(8,128)(2,1)}, u32[]{:S(2)}, u32[]{:S(2)}) collective-permute-start(bf16[2,2,4,64,512]{4,3,2,1,0:T(8,128)(2,1)} %pad_maximum_fusion.7), channel_id=1, source_target_pairs={{6,4},{1,3},{14,12},{9,11},{22,20},{17,19},{30,28},{25,27}} | collective-permute-start | bytes 3145736 | tf_op jit(solution)/shard_map/ppermute | solution.py:293
  199.6 33.9 %collective-permute-start.45 = (bf16[2,2,4,64,512]{4,3,2,1,0:T(8,128)(2,1)}, bf16[2,2,4,64,512]{4,3,2,1,0:T(8,128)(2,1)}, u32[]{:S(2)}, u32[]{:S(2)}) collective-permute-start(bf16[2,2,4,64,512]{4,3,2,1,0:T(8,128)(2,1)} %add_convert_fusion), channel_id=1, source_target_pairs={{2,0},{4,2},{6,4},{1,3},{3,5},{5,7},{10,8},{12,10},{14,12},{9,11},... | collective-permute-start | bytes 3145736 | tf_op jit(solution)/shard_map/ppermute | solution.py:293
  201.6 27.2 %collective-permute-start.23 = (bf16[2,2,2,64,512]{4,3,2,1,0:T(8,128)(2,1)}, bf16[2,2,2,64,512]{4,3,2,1,0:T(8,128)(2,1)}, u32[]{:S(2)}, u32[]{:S(2)}) collective-permute-start(bf16[2,2,2,64,512]{4,3,2,1,0:T(8,128)(2,1)} %collective-permute-done.22.refs_7_), channel_id=1, source_target_pairs={{2,4},{4,6},{3,1},{5,3},{10,12},{12,14},{11,9},{13,11},{18,20},{20... | collective-permute-start | bytes 1572872 | tf_op jit(solution)/shard_map/ppermute | solution.py:288
  234.6 45.6 %collective-permute-start.32 = (bf16[3,2,4,64,512]{4,3,2,1,0:T(8,128)(2,1)}, bf16[3,2,4,64,512]{4,3,2,1,0:T(8,128)(2,1)}, u32[]{:S(2)}, u32[]{:S(2)}) collective-permute-start(bf16[3,2,4,64,512]{4,3,2,1,0:T(8,128)(2,1)} %get-tuple-element.119), channel_id=1, source_target_pairs={{0,1},{1,0},{2,3},{3,2},{4,5},{5,4},{6,7},{7,6},{8,9},{9,8},{10,11... | collective-permute-start | bytes 4718600 | tf_op jit(solution)/shard_map/ppermute | solution.py:283
  238.9 27.6 %collective-permute-start.46 = (bf16[2,4,64,512]{3,2,1,0:T(8,128)(2,1)}, bf16[2,4,64,512]{3,2,1,0:T(8,128)(2,1)}, u32[]{:S(2)}, u32[]{:S(2)}) collective-permute-start(bf16[2,4,64,512]{3,2,1,0:T(8,128)(2,1)} %pad_maximum_fusion.16), channel_id=1, source_target_pairs={{0,1},{1,0},{2,3},{3,2},{4,5},{5,4},{6,7},{7,6},{8,9},{9,8},{10,11... | collective-permute-start | bytes 1572872 | tf_op jit(solution)/shard_map/ppermute | solution.py:283
  249.8 32.7 %collective-permute-start.40 = (bf16[2,2,4,64,512]{4,3,2,1,0:T(8,128)(2,1)}, bf16[2,2,4,64,512]{4,3,2,1,0:T(8,128)(2,1)}, u32[]{:S(2)}, u32[]{:S(2)}) collective-permute-start(bf16[2,2,4,64,512]{4,3,2,1,0:T(8,128)(2,1)} %add_convert_fusion.2), channel_id=1, source_target_pairs={{2,0},{4,2},{6,4},{1,3},{3,5},{5,7},{10,8},{12,10},{14,12},{9,11},... | collective-permute-start | bytes 3145736 | tf_op jit(solution)/shard_map/ppermute | solution.py:293
  284.6 61.2 %collective-permute-start.41 = (bf16[2,4,64,512]{3,2,1,0:T(8,128)(2,1)S(1)}, bf16[2,4,64,512]{3,2,1,0:T(8,128)(2,1)S(1)}, u32[]{:S(2)}, u32[]{:S(2)}) collective-permute-start(bf16[2,4,64,512]{3,2,1,0:T(8,128)(2,1)S(1)} %pad_maximum_fusion.15), channel_id=1, source_target_pairs={{0,1},{1,0},{2,3},{3,2},{4,5},{5,4},{6,7},{7,6},{8,9},{9,8},{10,11... | collective-permute-start | bytes 1572872 | tf_op jit(solution)/shard_map/ppermute | solution.py:283
  287.6 35.2 %collective-permute-start.34 = (bf16[2,2,4,64,512]{4,3,2,1,0:T(8,128)(2,1)S(1)}, bf16[2,2,4,64,512]{4,3,2,1,0:T(8,128)(2,1)S(1)}, u32[]{:S(2)}, u32[]{:S(2)}) collective-permute-start(bf16[2,2,4,64,512]{4,3,2,1,0:T(8,128)(2,1)S(1)} %add_convert_fusion.5), channel_id=1, source_target_pairs={{4,2},{6,4},{1,3},{3,5},{12,10},{14,12},{9,11},{11,13},{20,18},{22... | collective-permute-start | bytes 3145736 | tf_op jit(solution)/shard_map/ppermute | solution.py:293
  289.2 31.6 %collective-permute-start.29 = (bf16[2,2,2,64,512]{4,3,2,1,0:T(8,128)(2,1)S(1)}, bf16[2,2,2,64,512]{4,3,2,1,0:T(8,128)(2,1)S(1)}, u32[]{:S(2)}, u32[]{:S(2)}) collective-permute-start(bf16[2,2,2,64,512]{4,3,2,1,0:T(8,128)(2,1)S(1)} %add_convert_fusion.9), channel_id=1, source_target_pairs={{4,2},{6,4},{1,3},{3,5},{12,10},{14,12},{9,11},{11,13},{20,18},{22... | collective-permute-start | bytes 1572872 | tf_op jit(solution)/shard_map/ppermute | solution.py:293
  323.2 20.0 %collective-permute-start.35 = (bf16[2,2,4,64,512]{4,3,2,1,0:T(8,128)(2,1)S(1)}, bf16[2,2,4,64,512]{4,3,2,1,0:T(8,128)(2,1)S(1)}, u32[]{:S(2)}, u32[]{:S(2)}) collective-permute-start(bf16[2,2,4,64,512]{4,3,2,1,0:T(8,128)(2,1)S(1)} %add_convert_fusion.4), channel_id=1, source_target_pairs={{2,0},{4,2},{6,4},{1,3},{3,5},{5,7},{10,8},{12,10},{14,12},{9,11},... | collective-permute-start | bytes 3145736 | tf_op jit(solution)/shard_map/ppermute | solution.py:293
  332.9 23.0 %collective-permute-start.31 = (bf16[2,2,64,512]{3,2,1,0:T(8,128)(2,1)}, bf16[2,2,64,512]{3,2,1,0:T(8,128)(2,1)S(1)}, u32[]{:S(2)}, u32[]{:S(2)}) collective-permute-start(bf16[2,2,64,512]{3,2,1,0:T(8,128)(2,1)} %pad_maximum_fusion.18), channel_id=1, source_target_pairs={{0,1},{1,0},{2,3},{3,2},{4,5},{5,4},{6,7},{7,6},{8,9},{9,8},{10,11... | collective-permute-start | bytes 786440 | tf_op jit(solution)/shard_map/ppermute | solution.py:283
  (115 other events, 1266.8 us)

commit v3 on v0

v3 whole, which is shorter than its diff:
```python
import functools
import math

import jax
import jax.numpy as jnp
from jax import lax
from jax.experimental import pallas as pl
from jax.experimental.pallas import tpu as pltpu
from jax.sharding import PartitionSpec as P

HEAD_DIM = 128
MEMBERS = 4
F32 = jnp.float32
BF16 = jnp.bfloat16


def dot(left, right, left_dim, right_dim):
    return lax.dot_general(
        left, right, (((left_dim,), (right_dim,)), ((), ())), preferred_element_type=F32
    )


def pack_kernel(a_ref, b_ref, c_ref, d_ref, out_ref):
    for h in range(out_ref.shape[1]):
        for i, ref in enumerate((a_ref, b_ref, c_ref, d_ref)):
            out_ref[0, h, :, i * HEAD_DIM : (i + 1) * HEAD_DIM] = ref[
                :, h * HEAD_DIM : (h + 1) * HEAD_DIM
            ]


def pack(arrays, local_heads, first, count, block):
    rows = arrays[0].shape[0]
    steps = count // block

    def column(member, i):
        return (0, (member * local_heads + first) // block + i)

    return pl.pallas_call(
        pack_kernel,
        grid=(MEMBERS, steps),
        in_specs=[pl.BlockSpec((rows, block * HEAD_DIM), column)] * 4,
        out_specs=pl.BlockSpec(
            (1, block, rows, 4 * HEAD_DIM), lambda member, i: (member, i, 0, 0)
        ),
        out_shape=jax.ShapeDtypeStruct((MEMBERS, count, rows, 4 * HEAD_DIM), BF16),
        cost_estimate=pl.CostEstimate(
            flops=0, bytes_accessed=MEMBERS * count * rows * HEAD_DIM * 16, transcendentals=0
        ),
    )(*arrays)


def unpack_kernel(in_ref, *refs):
    outs = refs[-(in_ref.shape[3] // HEAD_DIM) :]
    for h in range(in_ref.shape[1]):
        for i, ref in enumerate(outs):
            ref[:, h * HEAD_DIM : (h + 1) * HEAD_DIM] = in_ref[
                0, h, :, i * HEAD_DIM : (i + 1) * HEAD_DIM
            ]


def unpack(packed, before, width, local_heads, first):
    count, rows = packed.shape[1], packed.shape[2]
    results = packed.shape[3] // HEAD_DIM
    old = list(before or ())
    return pl.pallas_call(
        unpack_kernel,
        grid=(MEMBERS,),
        in_specs=[
            pl.BlockSpec(
                (1, count, rows, results * HEAD_DIM), lambda member: (member, 0, 0, 0)
            )
        ]
        + [pl.BlockSpec(memory_space=pl.ANY)] * len(old),
        out_specs=[
            pl.BlockSpec(
                (rows, count * HEAD_DIM),
                lambda member: (0, (member * local_heads + first) // count),
            )
        ]
        * results,
        out_shape=[jax.ShapeDtypeStruct((rows, width), BF16)] * results,
        input_output_aliases={1 + i: i for i in range(len(old))},
        cost_estimate=pl.CostEstimate(
            flops=0, bytes_accessed=packed.size * 4, transcendentals=0
        ),
    )(packed, *old)


def attention_kernel(groups, block, scale, rows_ref, gain_ref, *refs):
    key_refs, outs = refs[:groups], refs[groups:]
    dq_ref, gain_out, own_out = outs[:3]
    other_outs = outs[3:]
    d = HEAD_DIM
    members, _, part_rows, _ = rows_ref.shape
    key_rows = key_refs[0].shape[2]
    rows_k = members * key_rows
    every = jnp.concatenate([ref[...].reshape(rows_k, 4 * d) for ref in key_refs], axis=0)
    k, k_kt = every[:, :d], every[:, : 2 * d]
    v, v_vt = every[:, 2 * d : 3 * d], every[:, 2 * d :]
    gain = gain_ref[...].astype(F32)
    sums = None
    step = block // part_rows
    for start in range(0, members, step):
        rows = rows_ref[start : start + step].reshape(block, 4 * d)
        q, qt = rows[:, :d], rows[:, d : 2 * d]
        gy = rows[:, 2 * d : 3 * d].astype(F32)
        gyt = rows[:, 3 * d :].astype(F32)
        go = (gy * gain).astype(BF16)
        got = (gyt * gain).astype(BF16)
        go_got = jnp.concatenate([go, got], axis=1)

        scores = dot(q, k, 1, 1) * scale
        scores_tan = dot(jnp.concatenate([qt, q], axis=1), k_kt, 1, 1) * scale
        d_probs = dot(go_got, v_vt, 1, 1)
        d_probs_tan = dot(got, v, 1, 1)
        top = jnp.max(scores, axis=-1, keepdims=True)
        raised = jnp.exp(scores - top)
        probs = raised * (1.0 / jnp.sum(raised, axis=-1, keepdims=True))
        offset = jnp.sum(probs * scores_tan, axis=-1, keepdims=True)
        centred = scores_tan - offset
        p_low = probs.astype(BF16)
        pt_low = (probs * centred).astype(BF16)
        inner = jnp.sum(probs * d_probs_tan, axis=-1, keepdims=True)
        dst_low = (probs * (d_probs_tan - inner)).astype(BF16)
        totals = d_probs + d_probs_tan * centred - inner * scores_tan
        ds = probs * (totals - jnp.sum(probs * totals, axis=-1, keepdims=True))
        ds_low = ds.astype(BF16)

        out_pair = dot(p_low, v_vt, 1, 0)
        attn_out = out_pair[:, :d].astype(BF16).astype(F32)
        attn_tan = (dot(pt_low, v, 1, 0) + out_pair[:, d:]).astype(BF16).astype(F32)
        gain_sum = jnp.sum(gy * attn_out + gyt * attn_tan, axis=0, keepdims=True)
        q_pair = dot(dst_low, k_kt, 1, 0)
        dq = scale * (dot(ds_low, k, 1, 0) + q_pair[:, d:])
        dqt = scale * q_pair[:, :d]
        both = jnp.concatenate([dq, dqt], axis=1).astype(BF16)
        dq_ref[start : start + step] = both.reshape(step, 1, part_rows, 2 * d)

        k_pair = dot(dst_low, rows[:, : 2 * d], 0, 0)
        v_pair = dot(p_low, go_got, 0, 0)
        terms = (
            dot(ds_low, q, 0, 0) + k_pair[:, d:],
            k_pair[:, :d],
            v_pair[:, :d] + dot(pt_low, got, 0, 0),
            v_pair[:, d:],
            gain_sum,
        )
        sums = terms if sums is None else tuple(a + b for a, b in zip(sums, terms))
    dk, dkt, dv, dvt, gain_sum = sums
    gain_out[0] = gain_sum
    for i, part in enumerate((scale * dk, scale * dkt, dv, dvt)):
        columns = slice(i * d, (i + 1) * d)
        for g, ref in enumerate((own_out,) + other_outs):
            ref[:, 0, :, columns] = (
                part[g * rows_k : (g + 1) * rows_k]
                .reshape(members, key_rows, d)
                .astype(ref.dtype)
            )


def attention(rows, gain, key_parts, gain_column, row_first, heads):
    groups = len(key_parts)
    members, _, part_rows, _ = rows.shape
    key_rows = key_parts[0].shape[2]
    d = HEAD_DIM
    block = 2 * part_rows
    keys_spec = pl.BlockSpec((members, 1, key_rows, 4 * d), lambda h, at: (0, h, 0, 0))
    keys_shape = (members, heads, key_rows, 4 * d)
    pairs = heads * members * part_rows * groups * members * key_rows
    return pl.pallas_call(
        lambda at, *refs: attention_kernel(groups, block, 1.0 / math.sqrt(d), *refs),
        grid_spec=pltpu.PrefetchScalarGridSpec(
            num_scalar_prefetch=1,
            grid=(heads,),
            in_specs=[
                pl.BlockSpec(
                    (members, 1, part_rows, 4 * d), lambda h, at: (0, row_first + h, 0, 0)
                ),
                pl.BlockSpec((1, d), lambda h, at: (0, at[0] + h)),
            ]
            + [keys_spec] * groups,
            out_specs=[
                pl.BlockSpec((members, 1, part_rows, 2 * d), lambda h, at: (0, h, 0, 0)),
                pl.BlockSpec((1, 1, d), lambda h, at: (h, 0, 0)),
            ]
            + [keys_spec] * groups,
        ),
        out_shape=[
            jax.ShapeDtypeStruct((members, heads, part_rows, 2 * d), BF16),
            jax.ShapeDtypeStruct((heads, 1, d), F32),
            jax.ShapeDtypeStruct(keys_shape, F32),
        ]
        + [jax.ShapeDtypeStruct(keys_shape, BF16)] * (groups - 1),
        compiler_params=pltpu.CompilerParams(vmem_limit_bytes=48 * 1024 * 1024),
        cost_estimate=pl.CostEstimate(
            flops=pairs * 36 * d, bytes_accessed=pairs * 8, transcendentals=pairs
        ),
    )(gain_column, rows, gain, *key_parts)


def after(array, *before):
    return lax.optimization_barrier((array,) + before)[0] if before else array


def sum_over(array, axis):
    size = lax.axis_size(axis)
    if size & (size - 1):
        return lax.psum(array, axis)
    far = 1
    while far < size:
        array = array + lax.ppermute(array, axis, [(i, i ^ far) for i in range(size)])
        far *= 2
    return array


def per_device(
    queries, query_tangent, keys, key_tangent, values, value_tangent, out_gain, grad_y, grad_y_tan
):
    count = lax.axis_size("ctx")
    groups = count // MEMBERS
    width = queries.shape[2]
    local_heads = width // HEAD_DIM // MEMBERS
    place = lax.axis_index("ctx")
    member = lax.rem(place, MEMBERS)
    teams = [[g * MEMBERS + i for i in range(MEMBERS)] for g in range(groups)]

    def exchange(array):
        return lax.all_to_all(
            array, "ctx", split_axis=0, concat_axis=0, tiled=True, axis_index_groups=teams
        )

    def shift(array, far):
        pairs = [(i, (i + far * MEMBERS) % count) for i in range(count)]
        return lax.ppermute(array, "ctx", pairs)

    rows_in = (queries[0], query_tangent[0], grad_y[0], grad_y_tan[0])
    key_in = (keys[0], key_tangent[0], values[0], value_tangent[0])
    gain = out_gain.reshape(1, width)
    size = max(1, local_heads // 4)
    parts = local_heads // size

    key_first = exchange(pack(key_in, local_heads, 0, size, size))
    key_rest = exchange(
        after(pack(key_in, local_heads, size, local_heads - size, size), key_first)
    )
    rows_first = exchange(after(pack(rows_in, local_heads, 0, size, size), key_rest))
    rows_rest = exchange(
        after(pack(rows_in, local_heads, size, local_heads - size, size), rows_first)
    )

    owns, others = [], []
    for index in range(parts):
        own = key_first if index == 0 else key_rest[:, (index - 1) * size : index * size]
        owns.append(own)
        others.append([shift(own, far) for far in range(1, groups)])

    results = []
    for index in range(parts):
        column = (member * local_heads + index * size).astype(jnp.int32).reshape(1)
        out = attention(
            rows_first if index == 0 else rows_rest,
            gain,
            [owns[index]] + others[index],
            column,
            0 if index == 0 else (index - 1) * size,
            size,
        )
        total = out[2]
        for far in range(1, groups):
            total = total + shift(out[2 + far], -far).astype(F32)
        results.append((out[0], out[1], total.astype(BF16)))

    def back(which, indices):
        return exchange(jnp.concatenate([results[i][which] for i in indices], axis=1))

    query_grads = key_grads = None
    half = parts // 2
    for indices in (range(half), range(half, parts)):
        query_grads = unpack(
            back(0, indices), query_grads, width, local_heads, indices[0] * size
        )
    gain_mine = jnp.concatenate([r[1] for r in results]).reshape(-1)
    gain_all = lax.dynamic_update_slice_in_dim(
        jnp.zeros((width,), F32), gain_mine, member * (width // MEMBERS), 0
    ).reshape(count, width // count)
    gain_all = lax.all_to_all(gain_all, "ctx", split_axis=0, concat_axis=0, tiled=True)
    gain_grad = sum_over(jnp.sum(gain_all, axis=0), "dp")
    for indices in (range(half),) + tuple(range(i, i + 1) for i in range(half, parts)):
        key_grads = unpack(back(2, indices), key_grads, width, local_heads, indices[0] * size)
    return tuple(g[None] for g in tuple(query_grads) + tuple(key_grads)) + (gain_grad,)


def solution(mesh):
    tokens = P("dp", "ctx", None)
    return jax.shard_map(
        per_device,
        mesh=mesh,
        in_specs=(tokens,) * 6 + (P(),) + (tokens,) * 2,
        out_specs=(tokens,) * 6 + (P("ctx"),),
        check_vma=False,
    )
```

time: 460 us -> 340 us (0.74)
  matrix products: 78.3 us -> 0 us
  Pallas kernels: 0 us -> 64.3 us
  local copies, waits for them, and re-layouts: 65 us -> 11.1 us
  starting transfers between devices: 100 us -> 68.9 us
  blocking collectives: 10.5 us -> 0 us
  other arithmetic: 18.7 us -> 9.81 us
    all_to_all x15 -> x10, waiting for transfers between devices: 182 us -> 45.8 us  [the longest x9 43.9 us: exchange(): lax.all_to_all(array, 'ctx', split_axis=0, concat_axis=0, tiled=True, axi...]
    ppermute x0 -> x10, waiting for transfers between devices: none -> 135 us  [the longest x8 131 us: shift(): return lax.ppermute(array, 'ctx', pairs)]
    dot_general x36 -> x0, matrix products: 78.3 us -> none  [inner_product(): jnp.einsum(pattern, left_op, right_op, preferred_element_type=jnp.float32)]
    pallas_call x0 -> x13, Pallas kernels: none -> 64.3 us  [the longest x4 26.3 us: attention(): pl.pallas_call(lambda at, *refs: attention_kernel(groups, block, 1.0 / ma...]
    all_to_all x15 -> x10, starting transfers between devices: 100 us -> 56.4 us  [the longest x9 50.3 us: exchange(): lax.all_to_all(array, 'ctx', split_axis=0, concat_axis=0, tiled=True, axi...]
    all_to_all x18 -> x0, local copies, waits for them, and re-layouts: 15.4 us -> none  [the longest x1 2.42 us: per_device(): lax.all_to_all(regroup(query_tangent), 'ctx', split_axis=1, concat_axis=0...]
    ppermute x0 -> x10, starting transfers between devices: none -> 12.5 us  [the longest x8 9.42 us: shift(): return lax.ppermute(array, 'ctx', pairs)]
    convert_element_type x4 -> x0, local copies, waits for them, and re-layouts: 11.2 us -> none  [the longest x1 2.94 us: per_device(): cot_rows.astype(jnp.float32) * gain_copy]
  transfers between devices with their start and end apart: 15 -> 20, of which waited for: 14 -> 16; matrix products, arithmetic and copies ran while one was open for 12% -> 4% of each run, Pallas kernels for 0% -> 17%
where the time goes in v3:
time: 340 us; the launch traced here: 336 us
  waiting for transfers between devices  181 us (53%)
  starting transfers between devices  68.9 us (20%)
  Pallas kernels  64.3 us (19%)
  local copies, waits for them, and re-layouts  11.1 us (3%)
  other arithmetic  9.81 us (3%)
    ppermute x8, waiting for transfers between devices, shift(): return lax.ppermute(array, 'ctx', pairs)  131 us
    all_to_all x9, starting transfers between devices, exchange(): lax.all_to_all(array, 'ctx', split_axis=0, concat_axis=0, tiled=True, axi...  50.3 us
    all_to_all x9, waiting for transfers between devices, exchange(): lax.all_to_all(array, 'ctx', split_axis=0, concat_axis=0, tiled=True, axi...  43.9 us
    pallas_call x4, Pallas kernels, attention(): pl.pallas_call(lambda at, *refs: attention_kernel(groups, block, 1.0 / ma...  26.3 us
    pallas_call x4, Pallas kernels, pack(): pl.pallas_call(pack_kernel, grid=(MEMBERS, steps), in_specs=[pl.BlockSpec...  21.4 us
    pallas_call x5, Pallas kernels, unpack(): pl.pallas_call(unpack_kernel, grid=(MEMBERS,), in_specs=[pl.BlockSpec((1,...  16.6 us
    ppermute x8, starting transfers between devices, shift(): return lax.ppermute(array, 'ctx', pairs)  9.42 us
  transfers between devices with their start and end apart: 20, of which 16 were waited for; matrix products, arithmetic and copies ran while one was open for 4% of the time, Pallas kernels for 17%

profile of v3, /device:TPU:8, one launch (start us, length us, event | category | flops | bytes accessed | tf_op | source)
XLA Modules:
  0.0 335.9 jit_solution(16246518444709118959)
XLA Ops:
  7.1 6.9 %shard_map.146 = bf16[4,6,64,512]{3,2,1,0:T(8,128)(2,1)} custom-call(bf16[64,4096]{1,0:T(8,128)(2,1)} %bitcast.29, bf16[64,4096]{1,0:T(8,128)(2,1)} %bitcast.31, bf16[64,4096]{1,0:T(8,128)(2,1)} %bitcast.33, bf16[64,4096]{1,0:T(8,128)(2,1)} %bitcast.35), custom_call_target="tpu_custom_call" | custom-call | bytes 3145728 | tf_op jit(solution)/shard_map/pallas_call | solution.py:38
  14.1 5.2 %all-to-all-start.1 = ((bf16[4,6,64,512]{3,2,1,0:T(8,128)(2,1)}), bf16[4,6,64,512]{3,2,1,0:T(8,128)(2,1)S(1)}, u32[]{:S(2)}, u32[]{:S(2)}) async-start(bf16[4,6,64,512]{3,2,1,0:T(8,128)(2,1)} %shard_map.146), calls=%async_computation.1 | async-start | bytes 3145728 | tf_op jit(solution)/shard_map/all_to_all | solution.py:228
  22.7 15.0 %all-to-all-done.1 = bf16[4,6,64,512]{3,2,1,0:T(8,128)(2,1)S(1)} async-done(((bf16[4,6,64,512]{3,2,1,0:T(8,128)(2,1)}), bf16[4,6,64,512]{3,2,1,0:T(8,128)(2,1)S(1)}, u32[]{:S(2)}, u32[]{:S(2)}) %all-to-all-start.1) | async-done | bytes 1572896 | tf_op jit(solution)/shard_map/all_to_all | solution.py:228
  37.7 5.2 %all-to-all-start.2 = ((bf16[4,2,128,512]{3,2,1,0:T(8,128)(2,1)}), bf16[4,2,128,512]{3,2,1,0:T(8,128)(2,1)S(1)}, u32[]{:S(2)}, u32[]{:S(2)}) async-start(bf16[4,2,128,512]{3,2,1,0:T(8,128)(2,1)} %shard_map.145), calls=%async_computation.2 | async-start | bytes 2097152 | tf_op jit(solution)/shard_map/all_to_all | solution.py:228
  42.9 8.1 %shard_map.144 = bf16[4,6,128,512]{3,2,1,0:T(8,128)(2,1)} custom-call(bf16[128,4096]{1,0:T(8,128)(2,1)} %bitcast.21, bf16[128,4096]{1,0:T(8,128)(2,1)} %bitcast.23, bf16[128,4096]{1,0:T(8,128)(2,1)} %bitcast.25, bf16[128,4096]{1,0:T(8,128)(2,1)} %bitcast.27), custom_call_target="tpu_custom_call" | custom-call | bytes 6291456 | tf_op jit(solution)/shard_map/pallas_call | solution.py:38
  55.7 6.3 %all-to-all-start.3 = ((bf16[4,6,128,512]{3,2,1,0:T(8,128)(2,1)}), bf16[4,6,128,512]{3,2,1,0:T(8,128)(2,1)}, u32[]{:S(2)}, u32[]{:S(2)}) async-start(bf16[4,6,128,512]{3,2,1,0:T(8,128)(2,1)} %shard_map.144), calls=%async_computation.3 | async-start | bytes 6291456 | tf_op jit(solution)/shard_map/all_to_all | solution.py:228
  70.8 41.1 %collective-permute-done.2.refs_3_ = bf16[4,2,64,512]{3,2,1,0:T(8,128)(2,1)S(1)} collective-permute-done((bf16[4,2,64,512]{3,2,1,0:T(8,128)(2,1)S(1)}, bf16[4,2,64,512]{3,2,1,0:T(8,128)(2,1)S(1)}, u32[]{:S(2)}, u32[]{:S(2)}) %collective-permute-start.2) | collective-permute-done | bytes 524320 | tf_op jit(solution)/shard_map/ppermute | solution.py:234
  111.9 5.6 %shard_map.150 = (bf16[4,2,128,256]{3,2,1,0:T(8,128)(2,1)S(1)}, f32[2,1,128]{2,1,0:T(1,128)S(1)}, f32[4,2,64,512]{3,2,1,0:T(8,128)S(1)}, bf16[4,2,64,512]{3,2,1,0:T(8,128)(2,1)S(1)}) custom-call(s32[1]{0:T(128)} %bitcast.10.at, bf16[4,2,128,512]{3,2,1,0:T(8,128)(2,1)S(1)} %all-to-all-done.2.refs_0_, bf16[1,4096]{1,0:T(2,128)(2,1)S(1)} %reshape.37.refs_1_, ...), custom_call_target="tpu_custom_call" | custom-call | flops 2415919104 | bytes 4194304 | tf_op jit(solution)/shard_map/pallas_call | solution.py:170
  123.2 8.4 %all-to-all-done.3.refs_0_ = bf16[4,6,128,512]{3,2,1,0:T(8,128)(2,1)} async-done(((bf16[4,6,128,512]{3,2,1,0:T(8,128)(2,1)}), bf16[4,6,128,512]{3,2,1,0:T(8,128)(2,1)}, u32[]{:S(2)}, u32[]{:S(2)}) %all-to-all-start.3) | async-done | bytes 3145760 | tf_op jit(solution)/shard_map/all_to_all | solution.py:228
  131.6 7.3 %shard_map.148 = (bf16[4,2,128,256]{3,2,1,0:T(8,128)(2,1)S(1)}, f32[2,1,128]{2,1,0:T(1,128)S(1)}, f32[4,2,64,512]{3,2,1,0:T(8,128)S(1)}, bf16[4,2,64,512]{3,2,1,0:T(8,128)(2,1)}) custom-call(s32[1]{0:T(128)} %bitcast.at, bf16[4,6,128,512]{3,2,1,0:T(8,128)(2,1)} %all-to-all-done.3.refs_0_, bf16[1,4096]{1,0:T(2,128)(2,1)S(1)} %reshape.37.refs_1_, ...), custom_call_target="tpu_custom_call" | custom-call | flops 2415919104 | bytes 4194304 | tf_op jit(solution)/shard_map/pallas_call | solution.py:170
  139.9 16.3 %collective-permute-done.3.refs_3_ = bf16[4,2,64,512]{3,2,1,0:T(8,128)(2,1)} collective-permute-done((bf16[4,2,64,512]{3,2,1,0:T(8,128)(2,1)}, bf16[4,2,64,512]{3,2,1,0:T(8,128)(2,1)}, u32[]{:S(2)}, u32[]{:S(2)}) %collective-permute-start.3) | collective-permute-done | bytes 524320 | tf_op jit(solution)/shard_map/ppermute | solution.py:234
  156.3 6.7 %shard_map.151 = (bf16[4,2,128,256]{3,2,1,0:T(8,128)(2,1)S(1)}, f32[2,1,128]{2,1,0:T(1,128)S(1)}, f32[4,2,64,512]{3,2,1,0:T(8,128)S(1)}, bf16[4,2,64,512]{3,2,1,0:T(8,128)(2,1)S(1)}) custom-call(s32[1]{0:T(128)} %bitcast.11.at, bf16[4,6,128,512]{3,2,1,0:T(8,128)(2,1)} %all-to-all-done.3.refs_0_, bf16[1,4096]{1,0:T(2,128)(2,1)S(1)} %reshape.37.refs_1_, ...), custom_call_target="tpu_custom_call" | custom-call | flops 2415919104 | bytes 4194304 | tf_op jit(solution)/shard_map/pallas_call | solution.py:170
  167.5 6.7 %shard_map.149 = (bf16[4,2,128,256]{3,2,1,0:T(8,128)(2,1)S(1)}, f32[2,1,128]{2,1,0:T(1,128)S(1)}, f32[4,2,64,512]{3,2,1,0:T(8,128)S(1)}, bf16[4,2,64,512]{3,2,1,0:T(8,128)(2,1)S(1)}) custom-call(s32[1]{0:T(128)} %bitcast.9.at, bf16[4,6,128,512]{3,2,1,0:T(8,128)(2,1)} %all-to-all-done.3.refs_0_, bf16[1,4096]{1,0:T(2,128)(2,1)S(1)} %reshape.37.refs_1_, ...), custom_call_target="tpu_custom_call" | custom-call | flops 2415919104 | bytes 4194304 | tf_op jit(solution)/shard_map/pallas_call | solution.py:170
  177.8 6.1 %all-to-all-start.9 = ((f32[8,1,512]{2,1,0:T(1,128)}), f32[8,1,512]{2,1,0:T(1,128)S(1)}, u32[]{:S(2)}, u32[]{:S(2)}) async-start(f32[8,1,512]{2,1,0:T(1,128)} %bitcast.19), calls=%async_computation.9 | async-start | bytes 32768 | tf_op jit(solution)/shard_map/all_to_all | solution.py:286
  188.2 5.5 %all-to-all-start.7 = ((bf16[4,2,64,512]{3,2,1,0:T(8,128)(2,1)}), bf16[4,2,64,512]{3,2,1,0:T(8,128)(2,1)}, u32[]{:S(2)}, u32[]{:S(2)}) async-start(bf16[4,2,64,512]{3,2,1,0:T(8,128)(2,1)} %add_convert_fusion.2), calls=%async_computation.7 | async-start | bytes 1048576 | tf_op jit(solution)/shard_map/all_to_all | solution.py:228
  196.0 5.0 %all-to-all-done.7.in_ref = bf16[4,2,64,512]{3,2,1,0:T(8,128)(2,1)} async-done(((bf16[4,2,64,512]{3,2,1,0:T(8,128)(2,1)}), bf16[4,2,64,512]{3,2,1,0:T(8,128)(2,1)}, u32[]{:S(2)}, u32[]{:S(2)}) %all-to-all-start.7) | async-done | bytes 524320 | tf_op jit(solution)/shard_map/all_to_all | solution.py:228
  201.0 5.9 %all-to-all-start.4 = ((bf16[4,4,128,256]{3,2,1,0:T(8,128)(2,1)}), bf16[4,4,128,256]{3,2,1,0:T(8,128)(2,1)}, u32[]{:S(2)}, u32[]{:S(2)}) async-start(bf16[4,4,128,256]{3,2,1,0:T(8,128)(2,1)} %pad_maximum_fusion), calls=%async_computation.4 | async-start | bytes 2097152 | tf_op jit(solution)/shard_map/all_to_all | solution.py:228
  209.1 10.6 %all-to-all-done.4.in_ref = bf16[4,4,128,256]{3,2,1,0:T(8,128)(2,1)} async-done(((bf16[4,4,128,256]{3,2,1,0:T(8,128)(2,1)}), bf16[4,4,128,256]{3,2,1,0:T(8,128)(2,1)}, u32[]{:S(2)}, u32[]{:S(2)}) %all-to-all-start.4) | async-done | bytes 1048608 | tf_op jit(solution)/shard_map/all_to_all | solution.py:228
  219.8 5.9 %all-to-all-start.5 = ((bf16[4,4,128,256]{3,2,1,0:T(8,128)(2,1)}), bf16[4,4,128,256]{3,2,1,0:T(8,128)(2,1)}, u32[]{:S(2)}, u32[]{:S(2)}) async-start(bf16[4,4,128,256]{3,2,1,0:T(8,128)(2,1)} %pad_maximum_fusion.1), calls=%async_computation.5 | async-start | bytes 2097152 | tf_op jit(solution)/shard_map/all_to_all | solution.py:228
  228.6 32.7 %collective-permute-done.6 = bf16[4,2,64,512]{3,2,1,0:T(8,128)(2,1)S(1)} collective-permute-done((bf16[4,2,64,512]{3,2,1,0:T(8,128)(2,1)}, bf16[4,2,64,512]{3,2,1,0:T(8,128)(2,1)S(1)}, u32[]{:S(2)}, u32[]{:S(2)}) %collective-permute-start.6) | collective-permute-done | bytes 524320 | tf_op jit(solution)/shard_map/ppermute | solution.py:234
  261.5 10.3 %collective-permute-done.7 = bf16[4,2,64,512]{3,2,1,0:T(8,128)(2,1)S(1)} collective-permute-done((bf16[4,2,64,512]{3,2,1,0:T(8,128)(2,1)}, bf16[4,2,64,512]{3,2,1,0:T(8,128)(2,1)S(1)}, u32[]{:S(2)}, u32[]{:S(2)}) %collective-permute-start.7) | collective-permute-done | bytes 524320 | tf_op jit(solution)/shard_map/ppermute | solution.py:234
  273.0 6.7 %all-to-all-start.8 = ((bf16[4,4,64,512]{3,2,1,0:T(8,128)(2,1)}), bf16[4,4,64,512]{3,2,1,0:T(8,128)(2,1)S(1)}, u32[]{:S(2)}, u32[]{:S(2)}) async-start(bf16[4,4,64,512]{3,2,1,0:T(8,128)(2,1)} %pad_maximum_fusion.2), calls=%async_computation.8 | async-start | bytes 2097152 | tf_op jit(solution)/shard_map/all_to_all | solution.py:228
  280.0 23.5 %collective-permute-done.4 = bf16[4,2,64,512]{3,2,1,0:T(8,128)(2,1)S(1)} collective-permute-done((bf16[4,2,64,512]{3,2,1,0:T(8,128)(2,1)S(1)}, bf16[4,2,64,512]{3,2,1,0:T(8,128)(2,1)S(1)}, u32[]{:S(2)}, u32[]{:S(2)}) %collective-permute-start.4) | collective-permute-done | bytes 524320 | tf_op jit(solution)/shard_map/ppermute | solution.py:234
  304.4 6.2 %all-to-all-start.6 = ((bf16[4,2,64,512]{3,2,1,0:T(8,128)(2,1)}), bf16[4,2,64,512]{3,2,1,0:T(8,128)(2,1)S(1)}, u32[]{:S(2)}, u32[]{:S(2)}) async-start(bf16[4,2,64,512]{3,2,1,0:T(8,128)(2,1)} %add_convert_fusion.3), calls=%async_computation.6 | async-start | bytes 1048576 | tf_op jit(solution)/shard_map/all_to_all | solution.py:228
  (70 shorter events, 77.9 us)
Async XLA Ops:
  3.6 10.5 %all-to-all-start = ((bf16[4,2,64,512]{3,2,1,0:T(8,128)(2,1)}), bf16[4,2,64,512]{3,2,1,0:T(8,128)(2,1)S(1)}, u32[]{:S(2)}, u32[]{:S(2)}) async-start(bf16[4,2,64,512]{3,2,1,0:T(8,128)(2,1)} %shard_map.147), calls=%async_computation | async-start | bytes 1048576 | tf_op jit(solution)/shard_map/all_to_all | solution.py:228
  14.1 23.6 %all-to-all-start.1 = ((bf16[4,6,64,512]{3,2,1,0:T(8,128)(2,1)}), bf16[4,6,64,512]{3,2,1,0:T(8,128)(2,1)S(1)}, u32[]{:S(2)}, u32[]{:S(2)}) async-start(bf16[4,6,64,512]{3,2,1,0:T(8,128)(2,1)} %shard_map.146), calls=%async_computation.1 | async-start | bytes 3145728 | tf_op jit(solution)/shard_map/all_to_all | solution.py:228
  37.7 13.2 %copy-start.9 = (bf16[4,6,64,512]{3,2,1,0:T(8,128)(2,1)}, bf16[4,6,64,512]{3,2,1,0:T(8,128)(2,1)S(1)}, u32[]{:S(2)}) copy-start(bf16[4,6,64,512]{3,2,1,0:T(8,128)(2,1)S(1)} %all-to-all-done.1) | copy-start | bytes 4718596
  37.7 18.0 %all-to-all-start.2 = ((bf16[4,2,128,512]{3,2,1,0:T(8,128)(2,1)}), bf16[4,2,128,512]{3,2,1,0:T(8,128)(2,1)S(1)}, u32[]{:S(2)}, u32[]{:S(2)}) async-start(bf16[4,2,128,512]{3,2,1,0:T(8,128)(2,1)} %shard_map.145), calls=%async_computation.2 | async-start | bytes 2097152 | tf_op jit(solution)/shard_map/all_to_all | solution.py:228
  55.7 75.9 %all-to-all-start.3 = ((bf16[4,6,128,512]{3,2,1,0:T(8,128)(2,1)}), bf16[4,6,128,512]{3,2,1,0:T(8,128)(2,1)}, u32[]{:S(2)}, u32[]{:S(2)}) async-start(bf16[4,6,128,512]{3,2,1,0:T(8,128)(2,1)} %shard_map.144), calls=%async_computation.3 | async-start | bytes 6291456 | tf_op jit(solution)/shard_map/all_to_all | solution.py:228
  62.0 8.6 %copy-start.12 = (bf16[4096]{0:T(1024)(128)(2,1)S(1)}, bf16[4096]{0:T(1024)(128)(2,1)}, u32[]{:S(2)}) copy-start(bf16[4096]{0:T(1024)(128)(2,1)} %param.15) | copy-start | bytes 24580
  62.0 49.9 %collective-permute-start.2 = (bf16[4,2,64,512]{3,2,1,0:T(8,128)(2,1)S(1)}, bf16[4,2,64,512]{3,2,1,0:T(8,128)(2,1)S(1)}, u32[]{:S(2)}, u32[]{:S(2)}) collective-permute-start(bf16[4,2,64,512]{3,2,1,0:T(8,128)(2,1)S(1)} %all-to-all-done.refs_2_), channel_id=1, source_target_pairs={{0,4},{1,5},{2,6},{3,7},{4,0},{5,1},{6,2},{7,3},{8,12},{9,13},{10,... | collective-permute-start | bytes 1572872 | tf_op jit(solution)/shard_map/ppermute | solution.py:234
  67.7 55.5 %collective-permute-start = (bf16[4,2,64,512]{3,2,1,0:T(8,128)(2,1)}, bf16[4,2,64,512]{3,2,1,0:T(8,128)(2,1)}, u32[]{:S(2)}, u32[]{:S(2)}) collective-permute-start(bf16[4,2,64,512]{3,2,1,0:T(8,128)(2,1)} %get-tuple-element.79.refs_2_), channel_id=1, source_target_pairs={{0,4},{1,5},{2,6},{3,7},{4,0},{5,1},{6,2},{7,3},{8,12},{9,13},{10,... | collective-permute-start | bytes 1572872 | tf_op jit(solution)/shard_map/ppermute | solution.py:234
  67.7 88.5 %collective-permute-start.3 = (bf16[4,2,64,512]{3,2,1,0:T(8,128)(2,1)}, bf16[4,2,64,512]{3,2,1,0:T(8,128)(2,1)}, u32[]{:S(2)}, u32[]{:S(2)}) collective-permute-start(bf16[4,2,64,512]{3,2,1,0:T(8,128)(2,1)} %get-tuple-element.77.refs_2_), channel_id=1, source_target_pairs={{0,4},{1,5},{2,6},{3,7},{4,0},{5,1},{6,2},{7,3},{8,12},{9,13},{10,... | collective-permute-start | bytes 1572872 | tf_op jit(solution)/shard_map/ppermute | solution.py:234
  70.7 96.8 %collective-permute-start.1 = (bf16[4,2,64,512]{3,2,1,0:T(8,128)(2,1)}, bf16[4,2,64,512]{3,2,1,0:T(8,128)(2,1)}, u32[]{:S(2)}, u32[]{:S(2)}) collective-permute-start(bf16[4,2,64,512]{3,2,1,0:T(8,128)(2,1)} %get-tuple-element.78.refs_2_), channel_id=1, source_target_pairs={{0,4},{1,5},{2,6},{3,7},{4,0},{5,1},{6,2},{7,3},{8,12},{9,13},{10,... | collective-permute-start | bytes 1572872 | tf_op jit(solution)/shard_map/ppermute | solution.py:234
  139.9 23.0 %copy-start.3 = (bf16[4,2,128,256]{3,2,1,0:T(8,128)(2,1)}, bf16[4,2,128,256]{3,2,1,0:T(8,128)(2,1)S(1)}, u32[]{:S(2)}) copy-start(bf16[4,2,128,256]{3,2,1,0:T(8,128)(2,1)S(1)} %get-tuple-element.45) | copy-start | bytes 1572868
  139.9 44.0 %collective-permute-start.5 = (bf16[4,2,64,512]{3,2,1,0:T(8,128)(2,1)}, bf16[4,2,64,512]{3,2,1,0:T(8,128)(2,1)}, u32[]{:S(2)}, u32[]{:S(2)}) collective-permute-start(bf16[4,2,64,512]{3,2,1,0:T(8,128)(2,1)} %get-tuple-element.56), channel_id=1, source_target_pairs={{0,4},{1,5},{2,6},{3,7},{4,0},{5,1},{6,2},{7,3},{8,12},{9,13},{10,... | collective-permute-start | bytes 1572872 | tf_op jit(solution)/shard_map/ppermute | solution.py:234
  177.8 10.3 %all-to-all-start.9 = ((f32[8,1,512]{2,1,0:T(1,128)}), f32[8,1,512]{2,1,0:T(1,128)S(1)}, u32[]{:S(2)}, u32[]{:S(2)}) async-start(f32[8,1,512]{2,1,0:T(1,128)} %bitcast.19), calls=%async_computation.9 | async-start | bytes 32768 | tf_op jit(solution)/shard_map/all_to_all | solution.py:286
  188.2 12.8 %all-to-all-start.7 = ((bf16[4,2,64,512]{3,2,1,0:T(8,128)(2,1)}), bf16[4,2,64,512]{3,2,1,0:T(8,128)(2,1)}, u32[]{:S(2)}, u32[]{:S(2)}) async-start(bf16[4,2,64,512]{3,2,1,0:T(8,128)(2,1)} %add_convert_fusion.2), calls=%async_computation.7 | async-start | bytes 1048576 | tf_op jit(solution)/shard_map/all_to_all | solution.py:228
  201.0 18.8 %all-to-all-start.4 = ((bf16[4,4,128,256]{3,2,1,0:T(8,128)(2,1)}), bf16[4,4,128,256]{3,2,1,0:T(8,128)(2,1)}, u32[]{:S(2)}, u32[]{:S(2)}) async-start(bf16[4,4,128,256]{3,2,1,0:T(8,128)(2,1)} %pad_maximum_fusion), calls=%async_computation.4 | async-start | bytes 2097152 | tf_op jit(solution)/shard_map/all_to_all | solution.py:228
  219.8 53.2 %all-to-all-start.5 = ((bf16[4,4,128,256]{3,2,1,0:T(8,128)(2,1)}), bf16[4,4,128,256]{3,2,1,0:T(8,128)(2,1)}, u32[]{:S(2)}, u32[]{:S(2)}) async-start(bf16[4,4,128,256]{3,2,1,0:T(8,128)(2,1)} %pad_maximum_fusion.1), calls=%async_computation.5 | async-start | bytes 2097152 | tf_op jit(solution)/shard_map/all_to_all | solution.py:228
  225.7 35.7 %collective-permute-start.6 = (bf16[4,2,64,512]{3,2,1,0:T(8,128)(2,1)}, bf16[4,2,64,512]{3,2,1,0:T(8,128)(2,1)S(1)}, u32[]{:S(2)}, u32[]{:S(2)}) collective-permute-start(bf16[4,2,64,512]{3,2,1,0:T(8,128)(2,1)} %copy-done.5), channel_id=1, source_target_pairs={{0,4},{1,5},{2,6},{3,7},{4,0},{5,1},{6,2},{7,3},{8,12},{9,13},{10,... | collective-permute-start | bytes 1572872 | tf_op jit(solution)/shard_map/ppermute | solution.py:234
  226.2 45.6 %collective-permute-start.7 = (bf16[4,2,64,512]{3,2,1,0:T(8,128)(2,1)}, bf16[4,2,64,512]{3,2,1,0:T(8,128)(2,1)S(1)}, u32[]{:S(2)}, u32[]{:S(2)}) collective-permute-start(bf16[4,2,64,512]{3,2,1,0:T(8,128)(2,1)} %copy-done.8), channel_id=1, source_target_pairs={{0,4},{1,5},{2,6},{3,7},{4,0},{5,1},{6,2},{7,3},{8,12},{9,13},{10,... | collective-permute-start | bytes 1572872 | tf_op jit(solution)/shard_map/ppermute | solution.py:234
  273.0 31.4 %all-to-all-start.8 = ((bf16[4,4,64,512]{3,2,1,0:T(8,128)(2,1)}), bf16[4,4,64,512]{3,2,1,0:T(8,128)(2,1)S(1)}, u32[]{:S(2)}, u32[]{:S(2)}) async-start(bf16[4,4,64,512]{3,2,1,0:T(8,128)(2,1)} %pad_maximum_fusion.2), calls=%async_computation.8 | async-start | bytes 2097152 | tf_op jit(solution)/shard_map/all_to_all | solution.py:228
  279.7 23.8 %collective-permute-start.4 = (bf16[4,2,64,512]{3,2,1,0:T(8,128)(2,1)S(1)}, bf16[4,2,64,512]{3,2,1,0:T(8,128)(2,1)S(1)}, u32[]{:S(2)}, u32[]{:S(2)}) collective-permute-start(bf16[4,2,64,512]{3,2,1,0:T(8,128)(2,1)S(1)} %copy-done.7), channel_id=1, source_target_pairs={{0,4},{1,5},{2,6},{3,7},{4,0},{5,1},{6,2},{7,3},{8,12},{9,13},{10,... | collective-permute-start | bytes 1572872 | tf_op jit(solution)/shard_map/ppermute | solution.py:234
  304.4 20.9 %copy-start.10 = (bf16[4,4,64,512]{3,2,1,0:T(8,128)(2,1)}, bf16[4,4,64,512]{3,2,1,0:T(8,128)(2,1)S(1)}, u32[]{:S(2)}) copy-start(bf16[4,4,64,512]{3,2,1,0:T(8,128)(2,1)S(1)} %all-to-all-done.8.in_ref) | copy-start | bytes 3145732
  304.4 27.5 %all-to-all-start.6 = ((bf16[4,2,64,512]{3,2,1,0:T(8,128)(2,1)}), bf16[4,2,64,512]{3,2,1,0:T(8,128)(2,1)S(1)}, u32[]{:S(2)}, u32[]{:S(2)}) async-start(bf16[4,2,64,512]{3,2,1,0:T(8,128)(2,1)} %add_convert_fusion.3), calls=%async_computation.6 | async-start | bytes 1048576 | tf_op jit(solution)/shard_map/all_to_all | solution.py:228
  310.7 3.6 %collective-permute-start.8 = (f32[512]{0:T(512)S(1)}, f32[512]{0:T(512)S(1)}, u32[]{:S(2)}, u32[]{:S(2)}) collective-permute-start(f32[512]{0:T(512)S(1)} %reduce_sum.9), channel_id=1, source_target_pairs={{0,8},{8,0},{16,24},{24,16},{1,9},{9,1},{17,25},{25,17},{2,10},{10... | collective-permute-start | bytes 6152 | tf_op jit(solution)/shard_map/ppermute | solution.py:211
  314.4 3.6 %collective-permute-start.9 = (f32[512]{0:T(512)S(1)}, f32[512]{0:T(512)S(1)}, u32[]{:S(2)}, u32[]{:S(2)}) collective-permute-start(f32[512]{0:T(512)S(1)} %add.38), channel_id=1, source_target_pairs={{0,16},{8,24},{16,0},{24,8},{1,17},{9,25},{17,1},{25,9},{2,18},{10... | collective-permute-start | bytes 6152 | tf_op jit(solution)/shard_map/ppermute | solution.py:211
  (9 other events, 13.3 us)

commit v4 on v3

v4 whole, which is shorter than its diff:
```python
import functools
import math

import jax
import jax.numpy as jnp
from jax import lax
from jax.experimental import pallas as pl
from jax.experimental.pallas import tpu as pltpu
from jax.sharding import PartitionSpec as P

HEAD_DIM = 128
MEMBERS = 4
F32 = jnp.float32
BF16 = jnp.bfloat16


def dot(left, right, left_dim, right_dim):
    return lax.dot_general(
        left, right, (((left_dim,), (right_dim,)), ((), ())), preferred_element_type=F32
    )


def pack_kernel(table_ref, *refs):
    ins, outs = refs[: 4 * MEMBERS], refs[4 * MEMBERS :]
    for j, out_ref in enumerate(outs):
        for h in range(out_ref.shape[0]):
            for i, ref in enumerate(ins[4 * j : 4 * j + 4]):
                out_ref[h, :, i * HEAD_DIM : (i + 1) * HEAD_DIM] = ref[
                    :, h * HEAD_DIM : (h + 1) * HEAD_DIM
                ]


def pack(table, arrays, local_heads, first, count):
    rows = arrays[0].shape[0]
    block = math.gcd(count, first, 2)
    steps = count // block

    def columns(j):
        return pl.BlockSpec(
            (rows, block * HEAD_DIM),
            lambda i, table_ref: (0, (table_ref[j] * local_heads + first) // block + i),
        )

    return pl.pallas_call(
        pack_kernel,
        grid_spec=pltpu.PrefetchScalarGridSpec(
            num_scalar_prefetch=1,
            grid=(steps,),
            in_specs=[columns(j) for j in range(MEMBERS) for _ in range(4)],
            out_specs=[
                pl.BlockSpec((block, rows, 4 * HEAD_DIM), lambda i, table_ref: (i, 0, 0))
            ]
            * MEMBERS,
        ),
        out_shape=[jax.ShapeDtypeStruct((count, rows, 4 * HEAD_DIM), BF16)] * MEMBERS,
        cost_estimate=pl.CostEstimate(
            flops=0, bytes_accessed=MEMBERS * count * rows * HEAD_DIM * 16, transcendentals=0
        ),
    )(table, *(list(arrays) * MEMBERS))


def unpack_kernel(terms, results, table_ref, *refs):
    outs = refs[-results:]
    for j in range(MEMBERS):

        @pl.when(pl.program_id(0) == j)
        def _(j=j):
            total = refs[j][...].astype(F32)
            for t in range(1, terms):
                total = total + refs[t * MEMBERS + j][...].astype(F32)
            for h in range(total.shape[0]):
                for i, ref in enumerate(outs):
                    ref[:, h * HEAD_DIM : (h + 1) * HEAD_DIM] = total[
                        h, :, i * HEAD_DIM : (i + 1) * HEAD_DIM
                    ].astype(BF16)


def unpack(table, pieces, before, width, local_heads, first):
    terms = len(pieces) // MEMBERS
    count, rows, lanes = pieces[0].shape
    results = lanes // HEAD_DIM
    old = list(before or ())
    return pl.pallas_call(
        functools.partial(unpack_kernel, terms, results),
        grid_spec=pltpu.PrefetchScalarGridSpec(
            num_scalar_prefetch=1,
            grid=(MEMBERS,),
            in_specs=[pl.BlockSpec((count, rows, lanes), lambda j, table_ref: (0, 0, 0))]
            * len(pieces)
            + [pl.BlockSpec(memory_space=pl.ANY)] * len(old),
            out_specs=[
                pl.BlockSpec(
                    (rows, count * HEAD_DIM),
                    lambda j, table_ref: (0, (table_ref[j] * local_heads + first) // count),
                )
            ]
            * results,
        ),
        out_shape=[jax.ShapeDtypeStruct((rows, width), BF16)] * results,
        input_output_aliases={1 + len(pieces) + i: i for i in range(len(old))},
        compiler_params=pltpu.CompilerParams(vmem_limit_bytes=32 * 1024 * 1024),
        cost_estimate=pl.CostEstimate(
            flops=0, bytes_accessed=count * rows * lanes * MEMBERS * 8, transcendentals=0
        ),
    )(table, *pieces, *old)


def attention_kernel(pieces, scale, table_ref, gain_ref, *refs):
    row_refs, key_refs = refs[:MEMBERS], refs[MEMBERS : MEMBERS + pieces]
    outs = refs[MEMBERS + pieces :]
    gain_out, dq_refs, key_outs = outs[0], outs[1 : 1 + MEMBERS], outs[1 + MEMBERS :]
    d = HEAD_DIM
    part_rows, key_rows = row_refs[0].shape[1], key_refs[0].shape[1]
    every = jnp.concatenate([ref[0] for ref in key_refs], axis=0)
    k, k_kt = every[:, :d], every[:, : 2 * d]
    v, v_vt = every[:, 2 * d : 3 * d], every[:, 2 * d :]
    gain = gain_ref[...].astype(F32)
    sums = None
    for start in range(0, MEMBERS, 2):
        rows = jnp.concatenate([row_refs[start][0], row_refs[start + 1][0]], axis=0)
        q, qt = rows[:, :d], rows[:, d : 2 * d]
        gy = rows[:, 2 * d : 3 * d].astype(F32)
        gyt = rows[:, 3 * d :].astype(F32)
        go = (gy * gain).astype(BF16)
        got = (gyt * gain).astype(BF16)
        go_got = jnp.concatenate([go, got], axis=1)

        scores = dot(q, k, 1, 1) * scale
        scores_tan = dot(jnp.concatenate([qt, q], axis=1), k_kt, 1, 1) * scale
        d_probs = dot(go_got, v_vt, 1, 1)
        d_probs_tan = dot(got, v, 1, 1)
        top = jnp.max(scores, axis=-1, keepdims=True)
        raised = jnp.exp(scores - top)
        probs = raised * (1.0 / jnp.sum(raised, axis=-1, keepdims=True))
        offset = jnp.sum(probs * scores_tan, axis=-1, keepdims=True)
        centred = scores_tan - offset
        p_low = probs.astype(BF16)
        pt_low = (probs * centred).astype(BF16)
        inner = jnp.sum(probs * d_probs_tan, axis=-1, keepdims=True)
        dst_low = (probs * (d_probs_tan - inner)).astype(BF16)
        totals = d_probs + d_probs_tan * centred - inner * scores_tan
        ds = probs * (totals - jnp.sum(probs * totals, axis=-1, keepdims=True))
        ds_low = ds.astype(BF16)

        out_pair = dot(p_low, v_vt, 1, 0)
        attn_out = out_pair[:, :d].astype(BF16).astype(F32)
        attn_tan = (dot(pt_low, v, 1, 0) + out_pair[:, d:]).astype(BF16).astype(F32)
        gain_sum = jnp.sum(gy * attn_out + gyt * attn_tan, axis=0, keepdims=True)
        q_pair = dot(dst_low, k_kt, 1, 0)
        dq = scale * (dot(ds_low, k, 1, 0) + q_pair[:, d:])
        dqt = scale * q_pair[:, :d]
        both = jnp.concatenate([dq, dqt], axis=1).astype(BF16)
        dq_refs[start][0] = both[:part_rows]
        dq_refs[start + 1][0] = both[part_rows:]

        k_pair = dot(dst_low, rows[:, : 2 * d], 0, 0)
        v_pair = dot(p_low, go_got, 0, 0)
        terms = (
            dot(ds_low, q, 0, 0) + k_pair[:, d:],
            k_pair[:, :d],
            v_pair[:, :d] + dot(pt_low, got, 0, 0),
            v_pair[:, d:],
            gain_sum,
        )
        sums = terms if sums is None else tuple(a + b for a, b in zip(sums, terms))
    dk, dkt, dv, dvt, gain_sum = sums
    gain_out[0] = gain_sum
    for i, part in enumerate((scale * dk, scale * dkt, dv, dvt)):
        columns = slice(i * d, (i + 1) * d)
        for p, ref in enumerate(key_outs):
            ref[0, :, columns] = part[p * key_rows : (p + 1) * key_rows].astype(ref.dtype)


def attention(table, gain, rows, keys, local_heads, first, count):
    part_rows, key_rows = rows[0].shape[1], keys[0].shape[1]
    d = HEAD_DIM

    def spec(rows_of, lanes):
        return pl.BlockSpec((1, rows_of, lanes), lambda h, table_ref: (h, 0, 0))

    pairs = count * MEMBERS * part_rows * len(keys) * key_rows
    return pl.pallas_call(
        functools.partial(attention_kernel, len(keys), 1.0 / math.sqrt(d)),
        grid_spec=pltpu.PrefetchScalarGridSpec(
            num_scalar_prefetch=1,
            grid=(count,),
            in_specs=[
                pl.BlockSpec(
                    (1, d), lambda h, table_ref: (0, table_ref[0] * local_heads + first + h)
                )
            ]
            + [spec(part_rows, 4 * d)] * MEMBERS
            + [spec(key_rows, 4 * d)] * len(keys),
            out_specs=[spec(1, d)]
            + [spec(part_rows, 2 * d)] * MEMBERS
            + [spec(key_rows, 4 * d)] * len(keys),
        ),
        out_shape=[jax.ShapeDtypeStruct((count, 1, d), F32)]
        + [jax.ShapeDtypeStruct((count, part_rows, 2 * d), BF16)] * MEMBERS
        + [jax.ShapeDtypeStruct((count, key_rows, 4 * d), F32)]
        + [jax.ShapeDtypeStruct((count, key_rows, 4 * d), BF16)] * (len(keys) - 1),
        compiler_params=pltpu.CompilerParams(vmem_limit_bytes=48 * 1024 * 1024),
        cost_estimate=pl.CostEstimate(
            flops=pairs * 36 * d, bytes_accessed=pairs * 8, transcendentals=pairs
        ),
    )(table, gain, *rows, *keys)


def sum_over(array, axis):
    size = lax.axis_size(axis)
    if size & (size - 1):
        return lax.psum(array, axis)
    far = 1
    while far < size:
        array = array + lax.ppermute(array, axis, [(i, i ^ far) for i in range(size)])
        far *= 2
    return array


def per_device(
    queries, query_tangent, keys, key_tangent, values, value_tangent, out_gain, grad_y, grad_y_tan
):
    count = lax.axis_size("ctx")
    groups = count // MEMBERS
    width = queries.shape[2]
    local_heads = width // HEAD_DIM // MEMBERS
    place = lax.axis_index("ctx")
    member, group = lax.rem(place, MEMBERS), place // MEMBERS
    table = jnp.stack([member ^ j for j in range(MEMBERS)]).astype(jnp.int32)

    def send(array, far, j):
        pairs = [(i, (i + far * MEMBERS) % count ^ j) for i in range(count)]
        return array if far == 0 and j == 0 else lax.ppermute(array, "ctx", pairs)

    rows_in = (queries[0], query_tangent[0], grad_y[0], grad_y_tan[0])
    key_in = (keys[0], key_tangent[0], values[0], value_tangent[0])
    gain = out_gain.reshape(1, width)
    half = max(1, local_heads // 2)
    firsts = tuple(range(0, local_heads, half))

    keys_of, rows_of = [], []
    for first in firsts:
        packed = pack(table, key_in, local_heads, first, half)
        far_keys = [
            send(packed[j], far, j) for far in range(1, groups) for j in range(MEMBERS)
        ]
        keys_of.append([send(packed[j], 0, j) for j in range(MEMBERS)] + far_keys)
        packed = pack(table, rows_in, local_heads, first, half)
        rows_of.append([send(packed[j], 0, j) for j in range(MEMBERS)])

    outs = []
    query_grads = key_grads = None
    for first, rows, keys_here in zip(firsts, rows_of, keys_of):
        out = attention(table, gain, rows, keys_here, local_heads, first, half)
        outs.append(out)
        grads = out[1 + MEMBERS :]
        far_back = [
            send(grads[far * MEMBERS + j], -far, j)
            for far in range(1, groups)
            for j in range(MEMBERS)
        ]
        back = [send(grads[j], 0, j) for j in range(MEMBERS)] + far_back
        key_grads = unpack(table, back, key_grads, width, local_heads, first)
        back = [send(out[1 + j], 0, j) for j in range(MEMBERS)]
        query_grads = unpack(table, back, query_grads, width, local_heads, first)

    gain_mine = jnp.concatenate([out[0] for out in outs]).reshape(-1)
    gain_mine = sum_over(gain_mine, "dp")
    gain_all = gain_mine
    for far in range(1, groups):
        gain_all = gain_all + send(gain_mine, far, 0)
    gain_part = lax.dynamic_slice_in_dim(gain_all, group * (width // count), width // count)
    gain_grad = lax.ppermute(
        gain_part,
        "ctx",
        [(g * MEMBERS + r, r * groups + g) for g in range(groups) for r in range(MEMBERS)],
    )
    return tuple(g[None] for g in tuple(query_grads) + tuple(key_grads)) + (gain_grad,)


def solution(mesh):
    tokens = P("dp", "ctx", None)
    return jax.shard_map(
        per_device,
        mesh=mesh,
        in_specs=(tokens,) * 6 + (P(),) + (tokens,) * 2,
        out_specs=(tokens,) * 6 + (P("ctx"),),
        check_vma=False,
    )
```

time: 340 us -> 276 us (0.81)
  waiting for transfers between devices: 181 us -> 146 us
  Pallas kernels: 64.3 us -> 48.6 us
  starting transfers between devices: 68.9 us -> 58.2 us
  local copies, waits for them, and re-layouts: 11.1 us -> 20.3 us
  other arithmetic: 9.81 us -> 0.63 us
    all_to_all x10 -> x0, starting transfers between devices: 56.4 us -> none  [the longest x9 50.3 us: exchange(): lax.all_to_all(array, 'ctx', split_axis=0, concat_axis=0, tiled=True, axi...]
    all_to_all x10 -> x0, waiting for transfers between devices: 45.8 us -> none  [the longest x9 43.9 us: exchange(): lax.all_to_all(array, 'ctx', split_axis=0, concat_axis=0, tiled=True, axi...]
    ppermute x8 -> x42, starting transfers between devices: 9.42 us -> 55.2 us  [the longest x41 53.1 us: send(): return array if far == 0 and j == 0 else lax.ppermute(array, 'ctx', pairs)]
    pallas_call x13 -> x10, Pallas kernels: 64.3 us -> 48.6 us  [the longest x2 25.5 us: attention(): pl.pallas_call(functools.partial(attention_kernel, len(keys), 1.0 / math....]
    unnamed x26 -> x99, local copies, waits for them, and re-layouts: 6.56 us -> 20.3 us
    ppermute x8 -> x42, waiting for transfers between devices: 131 us -> 142 us  [the longest x41 142 us: send(): return array if far == 0 and j == 0 else lax.ppermute(array, 'ctx', pairs)]
    concatenate x4 -> x1, other arithmetic: 5.59 us -> 0.01 us  [per_device(): gain_mine = jnp.concatenate([out[0] for out in outs]).reshape(-1)]
    convert_element_type x4 -> x0, other arithmetic: 3.6 us -> none  [per_device(): results.append((out[0], out[1], total.astype(BF16)))]
  transfers between devices with their start and end apart: 20 -> 44, of which waited for: 16 -> 22; matrix products, arithmetic and copies ran while one was open for 4% -> 0% of each run, Pallas kernels for 17% -> 11%
where the time goes in v4:
time: 276 us; the launch traced here: 275 us
  waiting for transfers between devices  146 us (53%)
  starting transfers between devices  58.2 us (21%)
  Pallas kernels  48.6 us (18%)
  local copies, waits for them, and re-layouts  20.3 us (7%)
    ppermute x41, waiting for transfers between devices, send(): return array if far == 0 and j == 0 else lax.ppermute(array, 'ctx', pairs)  142 us
    ppermute x41, starting transfers between devices, send(): return array if far == 0 and j == 0 else lax.ppermute(array, 'ctx', pairs)  53.1 us
    pallas_call x2, Pallas kernels, attention(): pl.pallas_call(functools.partial(attention_kernel, len(keys), 1.0 / math....  25.5 us
    unnamed x99, local copies, waits for them, and re-layouts  20.3 us
    pallas_call x4, Pallas kernels, pack(): pl.pallas_call(pack_kernel, grid_spec=pltpu.PrefetchScalarGridSpec(num_sc...  13.7 us
    pallas_call x4, Pallas kernels, unpack(): pl.pallas_call(functools.partial(unpack_kernel, terms, results), grid_spe...  9.46 us
  transfers between devices with their start and end apart: 44, of which 22 were waited for; matrix products, arithmetic and copies ran while one was open for 0% of the time, Pallas kernels for 11%

profile of v4, /device:TPU:8, one launch (start us, length us, event | category | flops | bytes accessed | tf_op | source)
XLA Modules:
  0.0 275.2 jit_solution(152328632574092239)
XLA Ops:
  1.2 3.1 %shard_map.148 = (bf16[4,64,512]{2,1,0:T(8,128)(2,1)}, bf16[4,64,512]{2,1,0:T(8,128)(2,1)}, bf16[4,64,512]{2,1,0:T(8,128)(2,1)}, bf16[4,64,512]{2,1,0:T(8,128)(2,1)}) custom-call(s32[4]{0:T(128)} %pad_add_fusion.table_ref, bf16[64,4096]{1,0:T(8,128)(2,1)} %bitcast.51, bf16[64,4096]{1,0:T(8,128)(2,1)} %bitcast.59, bf16[64,4096]{1,0:T(8,128)(2,1)} %bitcast.67, ...), custom_call_target="tpu_custom_call" | custom-call | bytes 2097152 | tf_op jit(solution)/shard_map/pallas_call | solution.py:44
  11.1 3.1 %shard_map.145 = (bf16[4,64,512]{2,1,0:T(8,128)(2,1)}, bf16[4,64,512]{2,1,0:T(8,128)(2,1)}, bf16[4,64,512]{2,1,0:T(8,128)(2,1)}, bf16[4,64,512]{2,1,0:T(8,128)(2,1)}) custom-call(s32[4]{0:T(128)} %pad_add_fusion.table_ref, bf16[64,4096]{1,0:T(8,128)(2,1)} %bitcast.55, bf16[64,4096]{1,0:T(8,128)(2,1)} %bitcast.63, bf16[64,4096]{1,0:T(8,128)(2,1)} %bitcast.71, ...), custom_call_target="tpu_custom_call" | custom-call | bytes 2097152 | tf_op jit(solution)/shard_map/pallas_call | solution.py:44
  14.2 8.0 %collective-permute-done.17.refs_6_ = bf16[4,64,512]{2,1,0:T(8,128)(2,1)S(1)} collective-permute-done((bf16[4,64,512]{2,1,0:T(8,128)(2,1)}, bf16[4,64,512]{2,1,0:T(8,128)(2,1)S(1)}, u32[]{:S(2)}, u32[]{:S(2)}) %collective-permute-start.17) | collective-permute-done | bytes 262176 | tf_op jit(solution)/shard_map/ppermute | solution.py:233
  22.9 4.7 %collective-permute-done.18.refs_7_ = bf16[4,64,512]{2,1,0:T(8,128)(2,1)S(1)} collective-permute-done((bf16[4,64,512]{2,1,0:T(8,128)(2,1)}, bf16[4,64,512]{2,1,0:T(8,128)(2,1)S(1)}, u32[]{:S(2)}, u32[]{:S(2)}) %collective-permute-start.18) | collective-permute-done | bytes 262176 | tf_op jit(solution)/shard_map/ppermute | solution.py:233
  31.3 12.7 %collective-permute-done.20.refs_9_ = bf16[4,64,512]{2,1,0:T(8,128)(2,1)S(1)} collective-permute-done((bf16[4,64,512]{2,1,0:T(8,128)(2,1)}, bf16[4,64,512]{2,1,0:T(8,128)(2,1)S(1)}, u32[]{:S(2)}, u32[]{:S(2)}) %collective-permute-start.20) | collective-permute-done | bytes 262176 | tf_op jit(solution)/shard_map/ppermute | solution.py:233
  45.1 3.8 %shard_map.147 = (bf16[4,128,512]{2,1,0:T(8,128)(2,1)}, bf16[4,128,512]{2,1,0:T(8,128)(2,1)}, bf16[4,128,512]{2,1,0:T(8,128)(2,1)}, bf16[4,128,512]{2,1,0:T(8,128)(2,1)}) custom-call(s32[4]{0:T(128)} %pad_add_fusion.table_ref, bf16[128,4096]{1,0:T(8,128)(2,1)} %bitcast.19, bf16[128,4096]{1,0:T(8,128)(2,1)} %bitcast.27, bf16[128,4096]{1,0:T(8,128)(2,1)} %bitcast.35, ...), custom_call_target="tpu_custom_call" | custom-call | bytes 4194304 | tf_op jit(solution)/shard_map/pallas_call | solution.py:44
  50.3 4.2 %collective-permute-done.22.refs_11_ = bf16[4,64,512]{2,1,0:T(8,128)(2,1)S(1)} collective-permute-done((bf16[4,64,512]{2,1,0:T(8,128)(2,1)S(1)}, bf16[4,64,512]{2,1,0:T(8,128)(2,1)S(1)}, u32[]{:S(2)}, u32[]{:S(2)}) %collective-permute-start.22) | collective-permute-done | bytes 262176 | tf_op jit(solution)/shard_map/ppermute | solution.py:233
  61.3 3.8 %shard_map.144 = (bf16[4,128,512]{2,1,0:T(8,128)(2,1)}, bf16[4,128,512]{2,1,0:T(8,128)(2,1)}, bf16[4,128,512]{2,1,0:T(8,128)(2,1)}, bf16[4,128,512]{2,1,0:T(8,128)(2,1)}) custom-call(s32[4]{0:T(128)} %pad_add_fusion.table_ref, bf16[128,4096]{1,0:T(8,128)(2,1)} %bitcast.23, bf16[128,4096]{1,0:T(8,128)(2,1)} %bitcast.31, bf16[128,4096]{1,0:T(8,128)(2,1)} %bitcast.39, ...), custom_call_target="tpu_custom_call" | custom-call | bytes 4194304 | tf_op jit(solution)/shard_map/pallas_call | solution.py:44
  65.1 23.3 %collective-permute-done.6.refs_8_ = bf16[4,64,512]{2,1,0:T(8,128)(2,1)S(1)} collective-permute-done((bf16[4,64,512]{2,1,0:T(8,128)(2,1)S(1)}, bf16[4,64,512]{2,1,0:T(8,128)(2,1)S(1)}, u32[]{:S(2)}, u32[]{:S(2)}) %collective-permute-start.6) | collective-permute-done | bytes 262176 | tf_op jit(solution)/shard_map/ppermute | solution.py:233
  89.1 4.0 %collective-permute-done.7.refs_9_ = bf16[4,64,512]{2,1,0:T(8,128)(2,1)S(1)} collective-permute-done((bf16[4,64,512]{2,1,0:T(8,128)(2,1)S(1)}, bf16[4,64,512]{2,1,0:T(8,128)(2,1)S(1)}, u32[]{:S(2)}, u32[]{:S(2)}) %collective-permute-start.7) | collective-permute-done | bytes 262176 | tf_op jit(solution)/shard_map/ppermute | solution.py:233
  99.4 12.7 %shard_map.149 = (f32[4,1,128]{2,1,0:T(1,128)S(1)}, bf16[4,128,256]{2,1,0:T(8,128)(2,1)S(1)}, bf16[4,128,256]{2,1,0:T(8,128)(2,1)S(1)}, bf16[4,128,256]{2,1,0:T(...) custom-call(s32[4]{0:T(128)S(1)} %copy-done, ...), custom_call_target="tpu_custom_call" | custom-call | flops 4831838208 | bytes 8388608 | tf_op jit(solution)/shard_map/pallas_call | solution.py:182
  119.6 12.8 %shard_map.146 = (f32[4,1,128]{2,1,0:T(1,128)S(1)}, bf16[4,128,256]{2,1,0:T(8,128)(2,1)S(1)}, bf16[4,128,256]{2,1,0:T(8,128)(2,1)S(1)}, bf16[4,128,256]{2,1,0:T(...) custom-call(s32[4]{0:T(128)S(1)} %copy-done, ...), custom_call_target="tpu_custom_call" | custom-call | flops 4831838208 | bytes 8388608 | tf_op jit(solution)/shard_map/pallas_call | solution.py:182
  143.1 13.9 %collective-permute-start.42 = (f32[1024]{0:T(1024)S(1)}, f32[1024]{0:T(1024)S(1)}, u32[]{:S(2)}, u32[]{:S(2)}) collective-permute-start(f32[1024]{0:T(1024)S(1)} %add.14), channel_id=1, source_target_pairs={{0,4},{1,5},{2,6},{3,7},{4,0},{5,1},{6,2},{7,3},{8,12},{9,13},{10,... | collective-permute-start | bytes 12296 | tf_op jit(solution)/shard_map/ppermute | solution.py:233
  160.8 3.1 %collective-permute-start.33 = (bf16[4,64,512]{2,1,0:T(8,128)(2,1)}, bf16[4,64,512]{2,1,0:T(8,128)(2,1)S(1)}, u32[]{:S(2)}, u32[]{:S(2)}) collective-permute-start(bf16[4,64,512]{2,1,0:T(8,128)(2,1)} %copy-done.17), channel_id=1, source_target_pairs={{0,1},{1,0},{2,3},{3,2},{4,5},{5,4},{6,7},{7,6},{8,9},{9,8},{10,11... | collective-permute-start | bytes 786440 | tf_op jit(solution)/shard_map/ppermute | solution.py:233
  168.3 10.9 %collective-permute-done.34.refs_2_ = bf16[4,64,512]{2,1,0:T(8,128)(2,1)S(1)} collective-permute-done((bf16[4,64,512]{2,1,0:T(8,128)(2,1)}, bf16[4,64,512]{2,1,0:T(8,128)(2,1)S(1)}, u32[]{:S(2)}, u32[]{:S(2)}) %collective-permute-start.34) | collective-permute-done | bytes 262176 | tf_op jit(solution)/shard_map/ppermute | solution.py:233
  180.6 3.6 %collective-permute-done.35.refs_3_ = bf16[4,64,512]{2,1,0:T(8,128)(2,1)S(1)} collective-permute-done((bf16[4,64,512]{2,1,0:T(8,128)(2,1)}, bf16[4,64,512]{2,1,0:T(8,128)(2,1)S(1)}, u32[]{:S(2)}, u32[]{:S(2)}) %collective-permute-start.35) | collective-permute-done | bytes 262176 | tf_op jit(solution)/shard_map/ppermute | solution.py:233
  186.8 13.9 %collective-permute-done.37.refs_5_ = bf16[4,64,512]{2,1,0:T(8,128)(2,1)S(1)} collective-permute-done((bf16[4,64,512]{2,1,0:T(8,128)(2,1)}, bf16[4,64,512]{2,1,0:T(8,128)(2,1)S(1)}, u32[]{:S(2)}, u32[]{:S(2)}) %collective-permute-start.37) | collective-permute-done | bytes 262176 | tf_op jit(solution)/shard_map/ppermute | solution.py:233
  200.7 7.8 %collective-permute-done.38.refs_6_ = bf16[4,64,512]{2,1,0:T(8,128)(2,1)S(1)} collective-permute-done((bf16[4,64,512]{2,1,0:T(8,128)(2,1)}, bf16[4,64,512]{2,1,0:T(8,128)(2,1)S(1)}, u32[]{:S(2)}, u32[]{:S(2)}) %collective-permute-start.38) | collective-permute-done | bytes 262176 | tf_op jit(solution)/shard_map/ppermute | solution.py:233
  208.5 4.0 %collective-permute-done.39.refs_7_ = bf16[4,64,512]{2,1,0:T(8,128)(2,1)S(1)} collective-permute-done((bf16[4,64,512]{2,1,0:T(8,128)(2,1)}, bf16[4,64,512]{2,1,0:T(8,128)(2,1)S(1)}, u32[]{:S(2)}, u32[]{:S(2)}) %collective-permute-start.39) | collective-permute-done | bytes 262176 | tf_op jit(solution)/shard_map/ppermute | solution.py:233
  216.9 3.1 %collective-permute-done.25.refs_3_ = bf16[4,128,256]{2,1,0:T(8,128)(2,1)S(1)} collective-permute-done((bf16[4,128,256]{2,1,0:T(8,128)(2,1)S(1)}, bf16[4,128,256]{2,1,0:T(8,128)(2,1)S(1)}, u32[]{:S(2)}, u32[]{:S(2)}) %collective-permute-start.25) | collective-permute-done | bytes 262176 | tf_op jit(solution)/shard_map/ppermute | solution.py:233
  224.3 11.6 %collective-permute-done.11.refs_2_ = bf16[4,128,256]{2,1,0:T(8,128)(2,1)S(1)} collective-permute-done((bf16[4,128,256]{2,1,0:T(8,128)(2,1)}, bf16[4,128,256]{2,1,0:T(8,128)(2,1)S(1)}, u32[]{:S(2)}, u32[]{:S(2)}) %collective-permute-start.11) | collective-permute-done | bytes 262176 | tf_op jit(solution)/shard_map/ppermute | solution.py:233
  237.5 4.1 %collective-permute-done.12.refs_3_ = bf16[4,128,256]{2,1,0:T(8,128)(2,1)S(1)} collective-permute-done((bf16[4,128,256]{2,1,0:T(8,128)(2,1)}, bf16[4,128,256]{2,1,0:T(8,128)(2,1)S(1)}, u32[]{:S(2)}, u32[]{:S(2)}) %collective-permute-start.12) | collective-permute-done | bytes 262176 | tf_op jit(solution)/shard_map/ppermute | solution.py:233
  249.5 17.4 %collective-permute-done.31.refs_6_ = bf16[4,64,512]{2,1,0:T(8,128)(2,1)S(1)} collective-permute-done((bf16[4,64,512]{2,1,0:T(8,128)(2,1)S(1)}, bf16[4,64,512]{2,1,0:T(8,128)(2,1)S(1)}, u32[]{:S(2)}, u32[]{:S(2)}) %collective-permute-start.31) | collective-permute-done | bytes 262176 | tf_op jit(solution)/shard_map/ppermute | solution.py:233
  266.9 5.3 %collective-permute-done.32.refs_7_ = bf16[4,64,512]{2,1,0:T(8,128)(2,1)S(1)} collective-permute-done((bf16[4,64,512]{2,1,0:T(8,128)(2,1)S(1)}, bf16[4,64,512]{2,1,0:T(8,128)(2,1)S(1)}, u32[]{:S(2)}, u32[]{:S(2)}) %collective-permute-start.32) | collective-permute-done | bytes 262176 | tf_op jit(solution)/shard_map/ppermute | solution.py:233
  (180 shorter events, 79.3 us)
Async XLA Ops:
  8.8 35.1 %collective-permute-start.20 = (bf16[4,64,512]{2,1,0:T(8,128)(2,1)}, bf16[4,64,512]{2,1,0:T(8,128)(2,1)S(1)}, u32[]{:S(2)}, u32[]{:S(2)}) collective-permute-start(bf16[4,64,512]{2,1,0:T(8,128)(2,1)} %get-tuple-element.78), channel_id=1, source_target_pairs={{0,5},{1,4},{2,7},{3,6},{4,1},{5,0},{6,3},{7,2},{8,13},{9,12},{10,... | collective-permute-start | bytes 786440 | tf_op jit(solution)/shard_map/ppermute | solution.py:233
  9.6 40.0 %collective-permute-start.21 = (bf16[4,64,512]{2,1,0:T(8,128)(2,1)}, bf16[4,64,512]{2,1,0:T(8,128)(2,1)S(1)}, u32[]{:S(2)}, u32[]{:S(2)}) collective-permute-start(bf16[4,64,512]{2,1,0:T(8,128)(2,1)} %get-tuple-element.79), channel_id=1, source_target_pairs={{0,6},{1,7},{2,4},{3,5},{4,2},{5,3},{6,0},{7,1},{8,14},{9,15},{10,... | collective-permute-start | bytes 786440 | tf_op jit(solution)/shard_map/ppermute | solution.py:233
  22.9 31.6 %collective-permute-start.22 = (bf16[4,64,512]{2,1,0:T(8,128)(2,1)S(1)}, bf16[4,64,512]{2,1,0:T(8,128)(2,1)S(1)}, u32[]{:S(2)}, u32[]{:S(2)}) collective-permute-start(bf16[4,64,512]{2,1,0:T(8,128)(2,1)S(1)} %copy-done.48), channel_id=1, source_target_pairs={{0,7},{1,6},{2,5},{3,4},{4,3},{5,2},{6,1},{7,0},{8,15},{9,14},{10,... | collective-permute-start | bytes 786440 | tf_op jit(solution)/shard_map/ppermute | solution.py:233
  28.3 27.0 %collective-permute-start.3 = (bf16[4,64,512]{2,1,0:T(8,128)(2,1)}, bf16[4,64,512]{2,1,0:T(8,128)(2,1)S(1)}, u32[]{:S(2)}, u32[]{:S(2)}) collective-permute-start(bf16[4,64,512]{2,1,0:T(8,128)(2,1)} %get-tuple-element.66), channel_id=1, source_target_pairs={{0,1},{1,0},{2,3},{3,2},{4,5},{5,4},{6,7},{7,6},{8,9},{9,8},{10,11... | collective-permute-start | bytes 786440 | tf_op jit(solution)/shard_map/ppermute | solution.py:233
  29.0 27.9 %collective-permute-start.4 = (bf16[4,64,512]{2,1,0:T(8,128)(2,1)}, bf16[4,64,512]{2,1,0:T(8,128)(2,1)S(1)}, u32[]{:S(2)}, u32[]{:S(2)}) collective-permute-start(bf16[4,64,512]{2,1,0:T(8,128)(2,1)} %get-tuple-element.67), channel_id=1, source_target_pairs={{0,2},{1,3},{2,0},{3,1},{4,6},{5,7},{6,4},{7,5},{8,10},{9,11},{10,... | collective-permute-start | bytes 786440 | tf_op jit(solution)/shard_map/ppermute | solution.py:233
  50.3 43.5 %collective-permute-start.13 = (bf16[4,128,512]{2,1,0:T(8,128)(2,1)}, bf16[4,128,512]{2,1,0:T(8,128)(2,1)}, u32[]{:S(2)}, u32[]{:S(2)}) collective-permute-start(bf16[4,128,512]{2,1,0:T(8,128)(2,1)} %get-tuple-element.74), channel_id=1, source_target_pairs={{0,1},{1,0},{2,3},{3,2},{4,5},{5,4},{6,7},{7,6},{8,9},{9,8},{10,11... | collective-permute-start | bytes 1572872 | tf_op jit(solution)/shard_map/ppermute | solution.py:233
  55.3 40.2 %collective-permute-start.14 = (bf16[4,128,512]{2,1,0:T(8,128)(2,1)}, bf16[4,128,512]{2,1,0:T(8,128)(2,1)}, u32[]{:S(2)}, u32[]{:S(2)}) collective-permute-start(bf16[4,128,512]{2,1,0:T(8,128)(2,1)} %get-tuple-element.75), channel_id=1, source_target_pairs={{0,2},{1,3},{2,0},{3,1},{4,6},{5,7},{6,4},{7,5},{8,10},{9,11},{10,... | collective-permute-start | bytes 1572872 | tf_op jit(solution)/shard_map/ppermute | solution.py:233
  56.0 39.5 %collective-permute-start.15 = (bf16[4,128,512]{2,1,0:T(8,128)(2,1)}, bf16[4,128,512]{2,1,0:T(8,128)(2,1)}, u32[]{:S(2)}, u32[]{:S(2)}) collective-permute-start(bf16[4,128,512]{2,1,0:T(8,128)(2,1)} %get-tuple-element.76), channel_id=1, source_target_pairs={{0,3},{1,2},{2,1},{3,0},{4,7},{5,6},{6,5},{7,4},{8,11},{9,10},{10,... | collective-permute-start | bytes 1572872 | tf_op jit(solution)/shard_map/ppermute | solution.py:233
  57.7 30.8 %collective-permute-start.6 = (bf16[4,64,512]{2,1,0:T(8,128)(2,1)S(1)}, bf16[4,64,512]{2,1,0:T(8,128)(2,1)S(1)}, u32[]{:S(2)}, u32[]{:S(2)}) collective-permute-start(bf16[4,64,512]{2,1,0:T(8,128)(2,1)S(1)} %copy-done.14), channel_id=1, source_target_pairs={{0,4},{1,5},{2,6},{3,7},{4,0},{5,1},{6,2},{7,3},{8,12},{9,13},{10,... | collective-permute-start | bytes 786440 | tf_op jit(solution)/shard_map/ppermute | solution.py:233
  60.3 32.8 %collective-permute-start.7 = (bf16[4,64,512]{2,1,0:T(8,128)(2,1)S(1)}, bf16[4,64,512]{2,1,0:T(8,128)(2,1)S(1)}, u32[]{:S(2)}, u32[]{:S(2)}) collective-permute-start(bf16[4,64,512]{2,1,0:T(8,128)(2,1)S(1)} %copy-done.47), channel_id=1, source_target_pairs={{0,5},{1,4},{2,7},{3,6},{4,1},{5,0},{6,3},{7,2},{8,13},{9,12},{10,... | collective-permute-start | bytes 786440 | tf_op jit(solution)/shard_map/ppermute | solution.py:233
  89.1 28.6 %collective-permute-start = (bf16[4,128,512]{2,1,0:T(8,128)(2,1)}, bf16[4,128,512]{2,1,0:T(8,128)(2,1)S(1)}, u32[]{:S(2)}, u32[]{:S(2)}) collective-permute-start(bf16[4,128,512]{2,1,0:T(8,128)(2,1)} %get-tuple-element.62), channel_id=1, source_target_pairs={{0,1},{1,0},{2,3},{3,2},{4,5},{5,4},{6,7},{7,6},{8,9},{9,8},{10,11... | collective-permute-start | bytes 1572872 | tf_op jit(solution)/shard_map/ppermute | solution.py:233
  93.8 24.0 %collective-permute-start.1 = (bf16[4,128,512]{2,1,0:T(8,128)(2,1)}, bf16[4,128,512]{2,1,0:T(8,128)(2,1)S(1)}, u32[]{:S(2)}, u32[]{:S(2)}) collective-permute-start(bf16[4,128,512]{2,1,0:T(8,128)(2,1)} %get-tuple-element.63), channel_id=1, source_target_pairs={{0,2},{1,3},{2,0},{3,1},{4,6},{5,7},{6,4},{7,5},{8,10},{9,11},{10,... | collective-permute-start | bytes 1572872 | tf_op jit(solution)/shard_map/ppermute | solution.py:233
  93.8 24.9 %collective-permute-start.2 = (bf16[4,128,512]{2,1,0:T(8,128)(2,1)}, bf16[4,128,512]{2,1,0:T(8,128)(2,1)S(1)}, u32[]{:S(2)}, u32[]{:S(2)}) collective-permute-start(bf16[4,128,512]{2,1,0:T(8,128)(2,1)} %get-tuple-element.64), channel_id=1, source_target_pairs={{0,3},{1,2},{2,1},{3,0},{4,7},{5,6},{6,5},{7,4},{8,11},{9,10},{10,... | collective-permute-start | bytes 1572872 | tf_op jit(solution)/shard_map/ppermute | solution.py:233
  165.7 35.0 %collective-permute-start.37 = (bf16[4,64,512]{2,1,0:T(8,128)(2,1)}, bf16[4,64,512]{2,1,0:T(8,128)(2,1)S(1)}, u32[]{:S(2)}, u32[]{:S(2)}) collective-permute-start(bf16[4,64,512]{2,1,0:T(8,128)(2,1)} %copy-done.9), channel_id=1, source_target_pairs={{0,5},{1,4},{2,7},{3,6},{4,1},{5,0},{6,3},{7,2},{8,13},{9,12},{10,... | collective-permute-start | bytes 786440 | tf_op jit(solution)/shard_map/ppermute | solution.py:233
  168.3 40.2 %collective-permute-start.38 = (bf16[4,64,512]{2,1,0:T(8,128)(2,1)}, bf16[4,64,512]{2,1,0:T(8,128)(2,1)S(1)}, u32[]{:S(2)}, u32[]{:S(2)}) collective-permute-start(bf16[4,64,512]{2,1,0:T(8,128)(2,1)} %copy-done.8), channel_id=1, source_target_pairs={{0,6},{1,7},{2,4},{3,5},{4,2},{5,3},{6,0},{7,1},{8,14},{9,15},{10,... | collective-permute-start | bytes 786440 | tf_op jit(solution)/shard_map/ppermute | solution.py:233
  179.2 33.3 %collective-permute-start.39 = (bf16[4,64,512]{2,1,0:T(8,128)(2,1)}, bf16[4,64,512]{2,1,0:T(8,128)(2,1)S(1)}, u32[]{:S(2)}, u32[]{:S(2)}) collective-permute-start(bf16[4,64,512]{2,1,0:T(8,128)(2,1)} %copy-done.7), channel_id=1, source_target_pairs={{0,7},{1,6},{2,5},{3,4},{4,3},{5,2},{6,1},{7,0},{8,15},{9,14},{10,... | collective-permute-start | bytes 786440 | tf_op jit(solution)/shard_map/ppermute | solution.py:233
  184.3 28.3 %collective-permute-start.26 = (bf16[4,64,512]{2,1,0:T(8,128)(2,1)}, bf16[4,64,512]{2,1,0:T(8,128)(2,1)S(1)}, u32[]{:S(2)}, u32[]{:S(2)}) collective-permute-start(bf16[4,64,512]{2,1,0:T(8,128)(2,1)} %copy-done.13), channel_id=1, source_target_pairs={{0,1},{1,0},{2,3},{3,2},{4,5},{5,4},{6,7},{7,6},{8,9},{9,8},{10,11... | collective-permute-start | bytes 786440 | tf_op jit(solution)/shard_map/ppermute | solution.py:233
  184.3 29.2 %collective-permute-start.27 = (bf16[4,64,512]{2,1,0:T(8,128)(2,1)}, bf16[4,64,512]{2,1,0:T(8,128)(2,1)S(1)}, u32[]{:S(2)}, u32[]{:S(2)}) collective-permute-start(bf16[4,64,512]{2,1,0:T(8,128)(2,1)} %copy-done.11), channel_id=1, source_target_pairs={{0,2},{1,3},{2,0},{3,1},{4,6},{5,7},{6,4},{7,5},{8,10},{9,11},{10,... | collective-permute-start | bytes 786440 | tf_op jit(solution)/shard_map/ppermute | solution.py:233
  215.2 26.4 %collective-permute-start.12 = (bf16[4,128,256]{2,1,0:T(8,128)(2,1)}, bf16[4,128,256]{2,1,0:T(8,128)(2,1)S(1)}, u32[]{:S(2)}, u32[]{:S(2)}) collective-permute-start(bf16[4,128,256]{2,1,0:T(8,128)(2,1)} %copy-done.4), channel_id=1, source_target_pairs={{0,3},{1,2},{2,1},{3,0},{4,7},{5,6},{6,5},{7,4},{8,11},{9,10},{10,... | collective-permute-start | bytes 786440 | tf_op jit(solution)/shard_map/ppermute | solution.py:233
  215.3 34.0 %collective-permute-start.28 = (bf16[4,64,512]{2,1,0:T(8,128)(2,1)S(1)}, bf16[4,64,512]{2,1,0:T(8,128)(2,1)S(1)}, u32[]{:S(2)}, u32[]{:S(2)}) collective-permute-start(bf16[4,64,512]{2,1,0:T(8,128)(2,1)S(1)} %get-tuple-element.92), channel_id=1, source_target_pairs={{0,3},{1,2},{2,1},{3,0},{4,7},{5,6},{6,5},{7,4},{8,11},{9,10},{10,... | collective-permute-start | bytes 786440 | tf_op jit(solution)/shard_map/ppermute | solution.py:233
  220.0 29.3 %collective-permute-start.29 = (bf16[4,64,512]{2,1,0:T(8,128)(2,1)S(1)}, bf16[4,64,512]{2,1,0:T(8,128)(2,1)S(1)}, u32[]{:S(2)}, u32[]{:S(2)}) collective-permute-start(bf16[4,64,512]{2,1,0:T(8,128)(2,1)S(1)} %get-tuple-element.93), channel_id=1, source_target_pairs={{0,4},{1,5},{2,6},{3,7},{4,0},{5,1},{6,2},{7,3},{8,12},{9,13},{10,... | collective-permute-start | bytes 786440 | tf_op jit(solution)/shard_map/ppermute | solution.py:233
  222.0 27.5 %collective-permute-start.30 = (bf16[4,64,512]{2,1,0:T(8,128)(2,1)S(1)}, bf16[4,64,512]{2,1,0:T(8,128)(2,1)S(1)}, u32[]{:S(2)}, u32[]{:S(2)}) collective-permute-start(bf16[4,64,512]{2,1,0:T(8,128)(2,1)S(1)} %get-tuple-element.94), channel_id=1, source_target_pairs={{0,5},{1,4},{2,7},{3,6},{4,1},{5,0},{6,3},{7,2},{8,13},{9,12},{10,... | collective-permute-start | bytes 786440 | tf_op jit(solution)/shard_map/ppermute | solution.py:233
  236.0 30.9 %collective-permute-start.31 = (bf16[4,64,512]{2,1,0:T(8,128)(2,1)S(1)}, bf16[4,64,512]{2,1,0:T(8,128)(2,1)S(1)}, u32[]{:S(2)}, u32[]{:S(2)}) collective-permute-start(bf16[4,64,512]{2,1,0:T(8,128)(2,1)S(1)} %get-tuple-element.95), channel_id=1, source_target_pairs={{0,6},{1,7},{2,4},{3,5},{4,2},{5,3},{6,0},{7,1},{8,14},{9,15},{10,... | collective-permute-start | bytes 786440 | tf_op jit(solution)/shard_map/ppermute | solution.py:233
  241.6 30.6 %collective-permute-start.32 = (bf16[4,64,512]{2,1,0:T(8,128)(2,1)S(1)}, bf16[4,64,512]{2,1,0:T(8,128)(2,1)S(1)}, u32[]{:S(2)}, u32[]{:S(2)}) collective-permute-start(bf16[4,64,512]{2,1,0:T(8,128)(2,1)S(1)} %get-tuple-element.96), channel_id=1, source_target_pairs={{0,7},{1,6},{2,5},{3,4},{4,3},{5,2},{6,1},{7,0},{8,15},{9,14},{10,... | collective-permute-start | bytes 786440 | tf_op jit(solution)/shard_map/ppermute | solution.py:233
  (69 other events, 806.9 us)

commit v5 on v4

v5 whole, which is shorter than its diff:
```python
import functools
import math

import jax
import jax.numpy as jnp
from jax import lax
from jax.experimental import pallas as pl
from jax.experimental.pallas import tpu as pltpu
from jax.sharding import PartitionSpec as P

HEAD_DIM = 128
MEMBERS = 4
DEPTH = 5
F32 = jnp.float32
BF16 = jnp.bfloat16


def dot(left, right, left_dim, right_dim):
    return lax.dot_general(
        left, right, (((left_dim,), (right_dim,)), ((), ())), preferred_element_type=F32
    )


def pack_kernel(groups_of_refs, table_ref, *refs):
    ins, outs = refs[: -MEMBERS], refs[-MEMBERS:]
    each = 4 * groups_of_refs
    for j, out_ref in enumerate(outs):
        for h in range(out_ref.shape[0]):
            row = 0
            for n, ref in enumerate(ins[each * j : each * (j + 1)]):
                i = n % 4
                out_ref[h, row : row + ref.shape[0], i * HEAD_DIM : (i + 1) * HEAD_DIM] = ref[
                    :, h * HEAD_DIM : (h + 1) * HEAD_DIM
                ]
                if i == 3:
                    row += ref.shape[0]


def pack(table, arrays, local_heads, first, count):
    rows = sum(a.shape[0] for a in arrays) // 4
    block = math.gcd(count, first, 2)
    steps = count // block

    def columns(array, j):
        return pl.BlockSpec(
            (array.shape[0], block * HEAD_DIM),
            lambda i, table_ref: (0, (table_ref[j] * local_heads + first) // block + i),
        )

    return pl.pallas_call(
        functools.partial(pack_kernel, len(arrays) // 4),
        grid_spec=pltpu.PrefetchScalarGridSpec(
            num_scalar_prefetch=1,
            grid=(steps,),
            in_specs=[columns(a, j) for j in range(MEMBERS) for a in arrays],
            out_specs=[
                pl.BlockSpec((block, rows, 4 * HEAD_DIM), lambda i, table_ref: (i, 0, 0))
            ]
            * MEMBERS,
        ),
        out_shape=[jax.ShapeDtypeStruct((count, rows, 4 * HEAD_DIM), BF16)] * MEMBERS,
        compiler_params=pltpu.CompilerParams(vmem_limit_bytes=32 * 1024 * 1024),
        cost_estimate=pl.CostEstimate(
            flops=0, bytes_accessed=MEMBERS * count * rows * HEAD_DIM * 16, transcendentals=0
        ),
    )(table, *(list(arrays) * MEMBERS))


def unpack_kernel(pieces, table_ref, *refs):
    outs = refs[-6:]
    key_rows, half_rows = outs[0].shape[0], outs[4].shape[0] // 2
    d = HEAD_DIM
    for j in range(MEMBERS):

        @pl.when(pl.program_id(0) == j)
        def _(j=j):
            near = refs[j]
            total = near[:, :key_rows].astype(F32)
            for p in range(MEMBERS + j, pieces, MEMBERS):
                total = total + refs[p][...].astype(F32)
            for h in range(total.shape[0]):
                columns = slice(h * d, (h + 1) * d)
                for i, ref in enumerate(outs[:4]):
                    ref[:, columns] = total[h, :, i * d : (i + 1) * d].astype(BF16)
                for i, ref in enumerate(outs[4:]):
                    ref[:half_rows, columns] = near[h, key_rows:, i * d : (i + 1) * d]
                    ref[half_rows:, columns] = near[h, key_rows:, (i + 2) * d : (i + 3) * d]


def unpack(table, pieces, before, rows_q, rows_k, width, local_heads, first):
    count, lanes = pieces[0].shape[0], 4 * HEAD_DIM
    old = list(before or ())
    rows_of = [rows_k] * 4 + [rows_q] * 2
    return pl.pallas_call(
        functools.partial(unpack_kernel, len(pieces)),
        grid_spec=pltpu.PrefetchScalarGridSpec(
            num_scalar_prefetch=1,
            grid=(MEMBERS,),
            in_specs=[
                pl.BlockSpec((count, p.shape[1], lanes), lambda j, table_ref: (0, 0, 0))
                for p in pieces
            ]
            + [pl.BlockSpec(memory_space=pl.ANY)] * len(old),
            out_specs=[
                pl.BlockSpec(
                    (rows, count * HEAD_DIM),
                    lambda j, table_ref: (0, (table_ref[j] * local_heads + first) // count),
                )
                for rows in rows_of
            ],
        ),
        out_shape=[jax.ShapeDtypeStruct((rows, width), BF16) for rows in rows_of],
        input_output_aliases={1 + len(pieces) + i: i for i in range(len(old))},
        compiler_params=pltpu.CompilerParams(vmem_limit_bytes=32 * 1024 * 1024),
        cost_estimate=pl.CostEstimate(
            flops=0, bytes_accessed=count * rows_k * lanes * MEMBERS * 16, transcendentals=0
        ),
    )(table, *pieces, *old)


def attention_kernel(pieces, key_rows, scale, table_ref, gain_ref, *refs):
    near_refs, far_refs = refs[:MEMBERS], refs[MEMBERS:pieces]
    gain_out, key_outs = refs[pieces], refs[pieces + 1 :]
    d = HEAD_DIM
    part_rows = near_refs[0].shape[1] - key_rows
    every = jnp.concatenate(
        [ref[0, :key_rows] for ref in near_refs] + [ref[0] for ref in far_refs], axis=0
    )
    k, k_kt = every[:, :d], every[:, : 2 * d]
    v, v_vt = every[:, 2 * d : 3 * d], every[:, 2 * d :]
    gain = gain_ref[...].astype(F32)
    sums = None
    for start in range(0, MEMBERS, 2):
        rows = jnp.concatenate(
            [near_refs[start][0, key_rows:], near_refs[start + 1][0, key_rows:]], axis=0
        )
        q, qt = rows[:, :d], rows[:, d : 2 * d]
        gy = rows[:, 2 * d : 3 * d].astype(F32)
        gyt = rows[:, 3 * d :].astype(F32)
        go = (gy * gain).astype(BF16)
        got = (gyt * gain).astype(BF16)
        go_got = jnp.concatenate([go, got], axis=1)

        scores = dot(q, k, 1, 1) * scale
        scores_tan = dot(jnp.concatenate([qt, q], axis=1), k_kt, 1, 1) * scale
        d_probs = dot(go_got, v_vt, 1, 1)
        d_probs_tan = dot(got, v, 1, 1)
        top = jnp.max(scores, axis=-1, keepdims=True)
        raised = jnp.exp(scores - top)
        probs = raised * (1.0 / jnp.sum(raised, axis=-1, keepdims=True))
        offset = jnp.sum(probs * scores_tan, axis=-1, keepdims=True)
        centred = scores_tan - offset
        p_low = probs.astype(BF16)
        pt_low = (probs * centred).astype(BF16)
        inner = jnp.sum(probs * d_probs_tan, axis=-1, keepdims=True)
        dst_low = (probs * (d_probs_tan - inner)).astype(BF16)
        totals = d_probs + d_probs_tan * centred - inner * scores_tan
        ds = probs * (totals - jnp.sum(probs * totals, axis=-1, keepdims=True))
        ds_low = ds.astype(BF16)

        out_pair = dot(p_low, v_vt, 1, 0)
        attn_out = out_pair[:, :d].astype(BF16).astype(F32)
        attn_tan = (dot(pt_low, v, 1, 0) + out_pair[:, d:]).astype(BF16).astype(F32)
        gain_sum = jnp.sum(gy * attn_out + gyt * attn_tan, axis=0, keepdims=True)
        q_pair = dot(dst_low, k_kt, 1, 0)
        dq = scale * (dot(ds_low, k, 1, 0) + q_pair[:, d:])
        dqt = scale * q_pair[:, :d]
        both = jnp.concatenate([dq, dqt], axis=1).astype(BF16)
        for n in range(4):
            key_outs[start + n // 2][0, key_rows:, (n % 2) * 2 * d : (n % 2 + 1) * 2 * d] = both[
                n * part_rows // 2 : (n + 1) * part_rows // 2
            ]

        k_pair = dot(dst_low, rows[:, : 2 * d], 0, 0)
        v_pair = dot(p_low, go_got, 0, 0)
        terms = (
            dot(ds_low, q, 0, 0) + k_pair[:, d:],
            k_pair[:, :d],
            v_pair[:, :d] + dot(pt_low, got, 0, 0),
            v_pair[:, d:],
            gain_sum,
        )
        sums = terms if sums is None else tuple(a + b for a, b in zip(sums, terms))
    dk, dkt, dv, dvt, gain_sum = sums
    gain_out[0] = gain_sum
    for i, part in enumerate((scale * dk, scale * dkt, dv, dvt)):
        columns = slice(i * d, (i + 1) * d)
        for p, ref in enumerate(key_outs):
            ref[0, :key_rows, columns] = part[p * key_rows : (p + 1) * key_rows].astype(ref.dtype)


def attention(table, gain, pieces, key_rows, local_heads, first, count):
    d = HEAD_DIM
    part_rows = pieces[0].shape[1] - key_rows
    home_rows = [key_rows + part_rows // 2] * MEMBERS
    home_rows += [key_rows] * (len(pieces) - MEMBERS)

    def spec(rows_of, lanes):
        return pl.BlockSpec((1, rows_of, lanes), lambda h, table_ref: (h, 0, 0))

    pairs = count * MEMBERS * part_rows * len(pieces) * key_rows
    return pl.pallas_call(
        functools.partial(attention_kernel, len(pieces), key_rows, 1.0 / math.sqrt(d)),
        grid_spec=pltpu.PrefetchScalarGridSpec(
            num_scalar_prefetch=1,
            grid=(count,),
            in_specs=[
                pl.BlockSpec(
                    (1, d), lambda h, table_ref: (0, table_ref[0] * local_heads + first + h)
                )
            ]
            + [spec(p.shape[1], 4 * d) for p in pieces],
            out_specs=[spec(1, d)] + [spec(rows, 4 * d) for rows in home_rows],
        ),
        out_shape=[jax.ShapeDtypeStruct((count, 1, d), F32)]
        + [jax.ShapeDtypeStruct((count, rows, 4 * d), BF16) for rows in home_rows],
        compiler_params=pltpu.CompilerParams(vmem_limit_bytes=48 * 1024 * 1024),
        cost_estimate=pl.CostEstimate(
            flops=pairs * 36 * d, bytes_accessed=pairs * 8, transcendentals=pairs
        ),
    )(table, gain, *pieces)


def after(array, *before):
    return lax.optimization_barrier((array,) + before)[0] if before else array


def sum_over(array, axis):
    size = lax.axis_size(axis)
    if size & (size - 1):
        return lax.psum(array, axis)
    far = 1
    while far < size:
        array = array + lax.ppermute(array, axis, [(i, i ^ far) for i in range(size)])
        far *= 2
    return array


def per_device(
    queries, query_tangent, keys, key_tangent, values, value_tangent, out_gain, grad_y, grad_y_tan
):
    count = lax.axis_size("ctx")
    groups = count // MEMBERS
    width = queries.shape[2]
    local_heads = width // HEAD_DIM // MEMBERS
    place = lax.axis_index("ctx")
    member, group = lax.rem(place, MEMBERS), place // MEMBERS
    table = jnp.stack([member ^ j for j in range(MEMBERS)]).astype(jnp.int32)

    rows_in = (queries[0], query_tangent[0], grad_y[0], grad_y_tan[0])
    key_in = (keys[0], key_tangent[0], values[0], value_tangent[0])
    rows_q, rows_k = rows_in[0].shape[0], key_in[0].shape[0]
    gain = out_gain.reshape(1, width)
    half = max(1, local_heads // 2)
    firsts = (0, half)
    flow = []

    def send(array, far, j):
        if far == 0 and j == 0:
            return array
        pairs = [(i, (i + far * MEMBERS) % count ^ j) for i in range(count)]
        if len(flow) >= DEPTH:
            array = after(array, flow[-DEPTH])
        flow.append(lax.ppermute(array, "ctx", pairs))
        return flow[-1]

    def spread(near, far_pieces, sign):
        near, far_pieces = list(near), list(far_pieces)
        order = (2, 3, 1, 0)
        for n, j in enumerate(order):
            for far in range(1, groups):
                p = (far - 1) * MEMBERS + n
                far_pieces[p] = send(far_pieces[p], sign * far, n)
            near[j] = send(near[j], 0, j)
        return near + far_pieces

    def outward(first, *before):
        arrays = (after(key_in[0], *before),) + key_in[1:]
        far_pieces = pack(table, arrays, local_heads, first, half)
        near = pack(table, arrays + rows_in, local_heads, first, half)
        return spread(near, list(far_pieces) * (groups - 1), 1)

    def attend(first, pieces, *before):
        pieces = [after(pieces[0], *before)] + pieces[1:]
        out = attention(table, gain, pieces, rows_k, local_heads, first, half)
        return out[0], out[1 : 1 + MEMBERS], out[1 + MEMBERS :]

    pieces0 = outward(firsts[0])
    pieces1 = outward(firsts[1])
    out0 = attend(firsts[0], pieces0)
    back0 = spread(out0[1], out0[2], -1)
    out1 = attend(firsts[1], pieces1, back0[MEMBERS])
    back1 = spread(out1[1], out1[2], -1)
    gain_mine = jnp.concatenate([out0[0], out1[0]]).reshape(groups, width // count)
    gain_part = 0.0
    for far in range(groups):
        whose = lax.rem(group + far, groups)
        piece = lax.dynamic_slice_in_dim(gain_mine, whose, 1)[0]
        pairs = [
            (g * MEMBERS + r, r * groups + (g + far) % groups)
            for g in range(groups)
            for r in range(MEMBERS)
        ]
        gain_part = gain_part + lax.ppermute(piece, "ctx", pairs)
    gain_grad = sum_over(after(gain_part, back1[MEMBERS]), "dp")
    grads = unpack(table, back0, None, rows_q, rows_k, width, local_heads, firsts[0])
    grads = unpack(table, back1, grads, rows_q, rows_k, width, local_heads, firsts[1])
    return tuple(g[None] for g in tuple(grads[4:]) + tuple(grads[:4])) + (gain_grad,)


def solution(mesh):
    tokens = P("dp", "ctx", None)
    return jax.shard_map(
        per_device,
        mesh=mesh,
        in_specs=(tokens,) * 6 + (P(),) + (tokens,) * 2,
        out_specs=(tokens,) * 6 + (P("ctx"),),
        check_vma=False,
    )
```

time: 276 us -> 248 us (0.90)
  local copies, waits for them, and re-layouts: 20.3 us -> 9.64 us
  starting transfers between devices: 58.2 us -> 50.9 us
  Pallas kernels: 48.6 us -> 43.3 us
  waiting for transfers between devices: 146 us -> 142 us
    unnamed x99 -> x44, local copies, waits for them, and re-layouts: 20.3 us -> 9.61 us
    ppermute x42 -> x30, starting transfers between devices: 55.2 us -> 47.9 us  [the longest x28 46 us: send(): flow.append(lax.ppermute(array, 'ctx', pairs))]
    pallas_call x10 -> x8, Pallas kernels: 48.6 us -> 43.3 us  [the longest x2 26.8 us: attention(): pl.pallas_call(functools.partial(attention_kernel, len(pieces), key_rows,...]
    ppermute x42 -> x30, waiting for transfers between devices: 142 us -> 140 us  [the longest x28 121 us: send(): flow.append(lax.ppermute(array, 'ctx', pairs))]
  transfers between devices with their start and end apart: 44 -> 32, of which waited for: 22 -> 15; matrix products, arithmetic and copies ran while one was open for 0% -> 0% of each run, Pallas kernels for 11% -> 15%
where the time goes in v5:
time: 248 us; the launch traced here: 247 us
  waiting for transfers between devices  142 us (57%)
  starting transfers between devices  50.9 us (21%)
  Pallas kernels  43.3 us (17%)
  local copies, waits for them, and re-layouts  9.64 us (4%)
    ppermute x28, waiting for transfers between devices, send(): flow.append(lax.ppermute(array, 'ctx', pairs))  121 us
    ppermute x28, starting transfers between devices, send(): flow.append(lax.ppermute(array, 'ctx', pairs))  46 us
    pallas_call x2, Pallas kernels, attention(): pl.pallas_call(functools.partial(attention_kernel, len(pieces), key_rows,...  26.8 us
    ppermute x2, waiting for transfers between devices, per_device(): gain_part = gain_part + lax.ppermute(piece, 'ctx', pairs)  18.5 us
    pallas_call x4, Pallas kernels, pack(): pl.pallas_call(functools.partial(pack_kernel, len(arrays) // 4), grid_spe...  9.8 us
    unnamed x44, local copies, waits for them, and re-layouts  9.61 us
    pallas_call x2, Pallas kernels, unpack(): pl.pallas_call(functools.partial(unpack_kernel, len(pieces)), grid_spec=p...  6.72 us
  transfers between devices with their start and end apart: 32, of which 15 were waited for; matrix products, arithmetic and copies ran while one was open for 0% of the time, Pallas kernels for 15%

profile of v5, /device:TPU:8, one launch (start us, length us, event | category | flops | bytes accessed | tf_op | source)
XLA Modules:
  0.0 247.1 jit_solution(9272039636083698125)
XLA Ops:
  9.3 3.2 %shard_map.145 = (bf16[4,192,512]{2,1,0:T(8,128)(2,1)S(1)}, bf16[4,192,512]{2,1,0:T(8,128)(2,1)S(1)}, bf16[4,192,512]{2,1,0:T(8,128)(2,1)S(1)}, bf16[4,192,512]{2,1,0:T(8,128)(2,1)S(1)}) custom-call(s32[4]{0:T(128)S(1)} %pad_add_fusion.table_ref, bf16[64,4096]{1,0:T(8,128)(2,1)S(1)} %bitcast.24, bf16[64,4096]{1,0:T(8,128)(2,1)S(1)} %bitcast.40, ...), custom_call_target="tpu_custom_call" | custom-call | bytes 6291456 | tf_op jit(solution)/shard_map/pallas_call | solution.py:50
  13.7 6.6 %collective-permute-done.refs_4_ = bf16[4,64,512]{2,1,0:T(8,128)(2,1)S(1)} collective-permute-done((bf16[4,64,512]{2,1,0:T(8,128)(2,1)S(1)}, bf16[4,64,512]{2,1,0:T(8,128)(2,1)S(1)}, u32[]{:S(2)}, u32[]{:S(2)}) %collective-permute-start) | collective-permute-done | bytes 262176 | tf_op jit(solution)/shard_map/ppermute | solution.py:264
  20.4 3.5 %collective-permute-start.4 = (bf16[4,64,512]{2,1,0:T(8,128)(2,1)S(1)}, bf16[4,64,512]{2,1,0:T(8,128)(2,1)S(1)}, u32[]{:S(2)}, u32[]{:S(2)}) collective-permute-start(bf16[4,64,512]{2,1,0:T(8,128)(2,1)S(1)} %get-tuple-element.85), channel_id=1, source_target_pairs={{0,5},{1,4},{2,7},{3,6},{4,1},{5,0},{6,3},{7,2},{8,13},{9,12},{10,... | collective-permute-start | bytes 786440 | tf_op jit(solution)/shard_map/ppermute | solution.py:264
  25.6 28.2 %collective-permute-done.4.refs_5_ = bf16[4,64,512]{2,1,0:T(8,128)(2,1)S(1)} collective-permute-done((bf16[4,64,512]{2,1,0:T(8,128)(2,1)S(1)}, bf16[4,64,512]{2,1,0:T(8,128)(2,1)S(1)}, u32[]{:S(2)}, u32[]{:S(2)}) %collective-permute-start.4) | collective-permute-done | bytes 262176 | tf_op jit(solution)/shard_map/ppermute | solution.py:264
  54.5 3.2 %shard_map.144 = (bf16[4,192,512]{2,1,0:T(8,128)(2,1)S(1)}, bf16[4,192,512]{2,1,0:T(8,128)(2,1)S(1)}, bf16[4,192,512]{2,1,0:T(8,128)(2,1)S(1)}, bf16[4,192,512]{2,1,0:T(8,128)(2,1)S(1)}) custom-call(s32[4]{0:T(128)S(1)} %pad_add_fusion.table_ref, bf16[64,4096]{1,0:T(8,128)(2,1)S(1)} %bitcast.32, bf16[64,4096]{1,0:T(8,128)(2,1)S(1)} %bitcast.48, ...), custom_call_target="tpu_custom_call" | custom-call | bytes 6291456 | tf_op jit(solution)/shard_map/pallas_call | solution.py:50
  57.7 3.4 %collective-permute-start.11 = (bf16[4,192,512]{2,1,0:T(8,128)(2,1)S(1)}, bf16[4,192,512]{2,1,0:T(8,128)(2,1)S(1)}, u32[]{:S(2)}, u32[]{:S(2)}) collective-permute-start(bf16[4,192,512]{2,1,0:T(8,128)(2,1)S(1)} %get-tuple-element.99), channel_id=1, source_target_pairs={{0,2},{1,3},{2,0},{3,1},{4,6},{5,7},{6,4},{7,5},{8,10},{9,11},{10,... | collective-permute-start | bytes 2359304 | tf_op jit(solution)/shard_map/ppermute | solution.py:264
  62.1 4.8 %collective-permute-done.9.refs_4_ = bf16[4,64,512]{2,1,0:T(8,128)(2,1)S(1)} collective-permute-done((bf16[4,64,512]{2,1,0:T(8,128)(2,1)S(1)}, bf16[4,64,512]{2,1,0:T(8,128)(2,1)S(1)}, u32[]{:S(2)}, u32[]{:S(2)}) %collective-permute-start.9) | collective-permute-done | bytes 262176 | tf_op jit(solution)/shard_map/ppermute | solution.py:264
  66.8 3.9 %collective-permute-start.12 = (bf16[4,192,512]{2,1,0:T(8,128)(2,1)S(1)}, bf16[4,192,512]{2,1,0:T(8,128)(2,1)S(1)}, u32[]{:S(2)}, u32[]{:S(2)}) collective-permute-start(bf16[4,192,512]{2,1,0:T(8,128)(2,1)S(1)} %get-tuple-element.101), channel_id=1, source_target_pairs={{0,3},{1,2},{2,1},{3,0},{4,7},{5,6},{6,5},{7,4},{8,11},{9,10},{10,... | collective-permute-start | bytes 2359304 | tf_op jit(solution)/shard_map/ppermute | solution.py:264
  70.7 4.0 %collective-permute-done.5.refs_6_ = bf16[4,64,512]{2,1,0:T(8,128)(2,1)S(1)} collective-permute-done((bf16[4,64,512]{2,1,0:T(8,128)(2,1)S(1)}, bf16[4,64,512]{2,1,0:T(8,128)(2,1)S(1)}, u32[]{:S(2)}, u32[]{:S(2)}) %collective-permute-start.5) | collective-permute-done | bytes 262176 | tf_op jit(solution)/shard_map/ppermute | solution.py:264
  74.8 13.2 %collective-permute-start.7 = (bf16[4,64,512]{2,1,0:T(8,128)(2,1)S(1)}, bf16[4,64,512]{2,1,0:T(8,128)(2,1)S(1)}, u32[]{:S(2)}, u32[]{:S(2)}) collective-permute-start(bf16[4,64,512]{2,1,0:T(8,128)(2,1)S(1)} %get-tuple-element.91), channel_id=1, source_target_pairs={{0,5},{1,4},{2,7},{3,6},{4,1},{5,0},{6,3},{7,2},{8,13},{9,12},{10,... | collective-permute-start | bytes 786440 | tf_op jit(solution)/shard_map/ppermute | solution.py:264
  89.0 13.4 %shard_map.147 = (f32[4,1,128]{2,1,0:T(1,128)S(1)}, bf16[4,128,512]{2,1,0:T(8,128)(2,1)S(1)}, bf16[4,128,512]{2,1,0:T(8,128)(2,1)}, bf16[4,128,512]{2,1,0:T(8,12...) custom-call(s32[4]{0:T(128)S(1)} %pad_add_fusion.table_ref, ...), custom_call_target="tpu_custom_call" | custom-call | flops 4831838208 | bytes 8388608 | tf_op jit(solution)/shard_map/pallas_call | solution.py:202
  102.4 12.1 %collective-permute-done.7.refs_5_ = bf16[4,64,512]{2,1,0:T(8,128)(2,1)S(1)} collective-permute-done((bf16[4,64,512]{2,1,0:T(8,128)(2,1)S(1)}, bf16[4,64,512]{2,1,0:T(8,128)(2,1)S(1)}, u32[]{:S(2)}, u32[]{:S(2)}) %collective-permute-start.7) | collective-permute-done | bytes 262176 | tf_op jit(solution)/shard_map/ppermute | solution.py:264
  118.6 3.1 %collective-permute-start.15 = (bf16[4,64,512]{2,1,0:T(8,128)(2,1)S(1)}, bf16[4,64,512]{2,1,0:T(8,128)(2,1)S(1)}, u32[]{:S(2)}, u32[]{:S(2)}) collective-permute-start(bf16[4,64,512]{2,1,0:T(8,128)(2,1)S(1)} %get-tuple-element.110), channel_id=1, source_target_pairs={{0,5},{1,4},{2,7},{3,6},{4,1},{5,0},{6,3},{7,2},{8,13},{9,12},{10,... | collective-permute-start | bytes 786440 | tf_op jit(solution)/shard_map/ppermute | solution.py:264
  121.7 14.6 %collective-permute-done.8.refs_4_ = bf16[4,64,512]{2,1,0:T(8,128)(2,1)S(1)} collective-permute-done((bf16[4,64,512]{2,1,0:T(8,128)(2,1)S(1)}, bf16[4,64,512]{2,1,0:T(8,128)(2,1)S(1)}, u32[]{:S(2)}, u32[]{:S(2)}) %collective-permute-start.8) | collective-permute-done | bytes 262176 | tf_op jit(solution)/shard_map/ppermute | solution.py:264
  138.7 4.0 %collective-permute-done.14.refs_7_ = bf16[4,64,512]{2,1,0:T(8,128)(2,1)S(1)} collective-permute-done((bf16[4,64,512]{2,1,0:T(8,128)(2,1)S(1)}, bf16[4,64,512]{2,1,0:T(8,128)(2,1)S(1)}, u32[]{:S(2)}, u32[]{:S(2)}) %collective-permute-start.14) | collective-permute-done | bytes 262176 | tf_op jit(solution)/shard_map/ppermute | solution.py:264
  142.7 13.4 %shard_map.149 = (f32[4,1,128]{2,1,0:T(1,128)S(1)}, bf16[4,128,512]{2,1,0:T(8,128)(2,1)S(1)}, bf16[4,128,512]{2,1,0:T(8,128)(2,1)S(1)}, bf16[4,128,512]{2,1,0:T(...) custom-call(s32[4]{0:T(128)S(1)} %pad_add_fusion.table_ref, ...), custom_call_target="tpu_custom_call" | custom-call | flops 4831838208 | bytes 8388608 | tf_op jit(solution)/shard_map/pallas_call | solution.py:202
  160.5 3.8 %collective-permute-start.19 = (bf16[4,128,512]{2,1,0:T(8,128)(2,1)}, bf16[4,128,512]{2,1,0:T(8,128)(2,1)S(1)}, u32[]{:S(2)}, u32[]{:S(2)}) collective-permute-start(bf16[4,128,512]{2,1,0:T(8,128)(2,1)} %get-tuple-element.116), channel_id=1, source_target_pairs={{0,2},{1,3},{2,0},{3,1},{4,6},{5,7},{6,4},{7,5},{8,10},{9,11},{10,... | collective-permute-start | bytes 1572872 | tf_op jit(solution)/shard_map/ppermute | solution.py:264
  166.4 15.5 %collective-permute-done.28 = f32[512]{0:T(512)S(1)} collective-permute-done((f32[512]{0:T(512)S(1)}, f32[512]{0:T(512)S(1)}, u32[]{:S(2)}, u32[]{:S(2)}) %collective-permute-start.28) | collective-permute-done | bytes 2080 | tf_op jit(solution)/shard_map/ppermute | solution.py:304
  188.6 9.8 %collective-permute-done.22.refs_6_ = bf16[4,64,512]{2,1,0:T(8,128)(2,1)S(1)} collective-permute-done((bf16[4,64,512]{2,1,0:T(8,128)(2,1)}, bf16[4,64,512]{2,1,0:T(8,128)(2,1)S(1)}, u32[]{:S(2)}, u32[]{:S(2)}) %collective-permute-start.22) | collective-permute-done | bytes 262176 | tf_op jit(solution)/shard_map/ppermute | solution.py:264
  199.9 4.7 %collective-permute-done.25.refs_7_ = bf16[4,64,512]{2,1,0:T(8,128)(2,1)S(1)} collective-permute-done((bf16[4,64,512]{2,1,0:T(8,128)(2,1)}, bf16[4,64,512]{2,1,0:T(8,128)(2,1)S(1)}, u32[]{:S(2)}, u32[]{:S(2)}) %collective-permute-start.25) | collective-permute-done | bytes 262176 | tf_op jit(solution)/shard_map/ppermute | solution.py:264
  210.8 19.1 %collective-permute-done.23.refs_5_ = bf16[4,64,512]{2,1,0:T(8,128)(2,1)S(1)} collective-permute-done((bf16[4,64,512]{2,1,0:T(8,128)(2,1)}, bf16[4,64,512]{2,1,0:T(8,128)(2,1)S(1)}, u32[]{:S(2)}, u32[]{:S(2)}) %collective-permute-start.23) | collective-permute-done | bytes 262176 | tf_op jit(solution)/shard_map/ppermute | solution.py:264
  229.9 7.6 %collective-permute-done.27.refs_7_ = bf16[4,64,512]{2,1,0:T(8,128)(2,1)S(1)} collective-permute-done((bf16[4,64,512]{2,1,0:T(8,128)(2,1)}, bf16[4,64,512]{2,1,0:T(8,128)(2,1)S(1)}, u32[]{:S(2)}, u32[]{:S(2)}) %collective-permute-start.27) | collective-permute-done | bytes 262176 | tf_op jit(solution)/shard_map/ppermute | solution.py:264
  237.5 5.7 %collective-permute-done.26.refs_6_ = bf16[4,64,512]{2,1,0:T(8,128)(2,1)S(1)} collective-permute-done((bf16[4,64,512]{2,1,0:T(8,128)(2,1)}, bf16[4,64,512]{2,1,0:T(8,128)(2,1)S(1)}, u32[]{:S(2)}, u32[]{:S(2)}) %collective-permute-start.26) | collective-permute-done | bytes 262176 | tf_op jit(solution)/shard_map/ppermute | solution.py:264
  243.3 3.8 %shard_map.151 = (bf16[64,4096]{1,0:T(8,128)(2,1)}, bf16[64,4096]{1,0:T(8,128)(2,1)}, bf16[64,4096]{1,0:T(8,128)(2,1)}, bf16[64,4096]{1,0:T(8,128)(2,1)}, bf16[1...) custom-call(s32[4]{0:T(128)S(1)} %pad_add_fusion.table_ref, ...), custom_call_target="tpu_custom_call", output_to_operand_aliasing={{0}: (9, {}), {1}: (10, {}), {2}: (11, {}), {3}: (12, {}), ... | custom-call | bytes 8388608 | tf_op jit(solution)/shard_map/pallas_call | solution.py:94
  (100 shorter events, 41.6 us)
Async XLA Ops:
  12.5 45.2 %collective-permute-start.3 = (bf16[4,192,512]{2,1,0:T(8,128)(2,1)S(1)}, bf16[4,192,512]{2,1,0:T(8,128)(2,1)S(1)}, u32[]{:S(2)}, u32[]{:S(2)}) collective-permute-start(bf16[4,192,512]{2,1,0:T(8,128)(2,1)S(1)} %get-tuple-element.84), channel_id=1, source_target_pairs={{0,3},{1,2},{2,1},{3,0},{4,7},{5,6},{6,5},{7,4},{8,11},{9,10},{10,... | collective-permute-start | bytes 2359304 | tf_op jit(solution)/shard_map/ppermute | solution.py:264
  12.6 48.6 %collective-permute-start.2 = (bf16[4,192,512]{2,1,0:T(8,128)(2,1)S(1)}, bf16[4,192,512]{2,1,0:T(8,128)(2,1)S(1)}, u32[]{:S(2)}, u32[]{:S(2)}) collective-permute-start(bf16[4,192,512]{2,1,0:T(8,128)(2,1)S(1)} %get-tuple-element.83), channel_id=1, source_target_pairs={{0,2},{1,3},{2,0},{3,1},{4,6},{5,7},{6,4},{7,5},{8,10},{9,11},{10,... | collective-permute-start | bytes 2359304 | tf_op jit(solution)/shard_map/ppermute | solution.py:264
  20.4 46.5 %collective-permute-start.1 = (bf16[4,192,512]{2,1,0:T(8,128)(2,1)S(1)}, bf16[4,192,512]{2,1,0:T(8,128)(2,1)S(1)}, u32[]{:S(2)}, u32[]{:S(2)}) collective-permute-start(bf16[4,192,512]{2,1,0:T(8,128)(2,1)S(1)} %get-tuple-element.82), channel_id=1, source_target_pairs={{0,1},{1,0},{2,3},{3,2},{4,5},{5,4},{6,7},{7,6},{8,9},{9,8},{10,11... | collective-permute-start | bytes 2359304 | tf_op jit(solution)/shard_map/ppermute | solution.py:264
  20.4 33.5 %collective-permute-start.4 = (bf16[4,64,512]{2,1,0:T(8,128)(2,1)S(1)}, bf16[4,64,512]{2,1,0:T(8,128)(2,1)S(1)}, u32[]{:S(2)}, u32[]{:S(2)}) collective-permute-start(bf16[4,64,512]{2,1,0:T(8,128)(2,1)S(1)} %get-tuple-element.85), channel_id=1, source_target_pairs={{0,5},{1,4},{2,7},{3,6},{4,1},{5,0},{6,3},{7,2},{8,13},{9,12},{10,... | collective-permute-start | bytes 786440 | tf_op jit(solution)/shard_map/ppermute | solution.py:264
  57.7 56.8 %collective-permute-start.11 = (bf16[4,192,512]{2,1,0:T(8,128)(2,1)S(1)}, bf16[4,192,512]{2,1,0:T(8,128)(2,1)S(1)}, u32[]{:S(2)}, u32[]{:S(2)}) collective-permute-start(bf16[4,192,512]{2,1,0:T(8,128)(2,1)S(1)} %get-tuple-element.99), channel_id=1, source_target_pairs={{0,2},{1,3},{2,0},{3,1},{4,6},{5,7},{6,4},{7,5},{8,10},{9,11},{10,... | collective-permute-start | bytes 2359304 | tf_op jit(solution)/shard_map/ppermute | solution.py:264
  61.2 26.8 %collective-permute-start.6 = (bf16[4,64,512]{2,1,0:T(8,128)(2,1)S(1)}, bf16[4,64,512]{2,1,0:T(8,128)(2,1)S(1)}, u32[]{:S(2)}, u32[]{:S(2)}) collective-permute-start(bf16[4,64,512]{2,1,0:T(8,128)(2,1)S(1)} %get-tuple-element.88), channel_id=1, source_target_pairs={{0,7},{1,6},{2,5},{3,4},{4,3},{5,2},{6,1},{7,0},{8,15},{9,14},{10,... | collective-permute-start | bytes 786440 | tf_op jit(solution)/shard_map/ppermute | solution.py:264
  66.8 49.8 %collective-permute-start.10 = (bf16[4,192,512]{2,1,0:T(8,128)(2,1)S(1)}, bf16[4,192,512]{2,1,0:T(8,128)(2,1)S(1)}, u32[]{:S(2)}, u32[]{:S(2)}) collective-permute-start(bf16[4,192,512]{2,1,0:T(8,128)(2,1)S(1)} %get-tuple-element.97), channel_id=1, source_target_pairs={{0,1},{1,0},{2,3},{3,2},{4,5},{5,4},{6,7},{7,6},{8,9},{9,8},{10,11... | collective-permute-start | bytes 2359304 | tf_op jit(solution)/shard_map/ppermute | solution.py:264
  66.8 69.5 %collective-permute-start.12 = (bf16[4,192,512]{2,1,0:T(8,128)(2,1)S(1)}, bf16[4,192,512]{2,1,0:T(8,128)(2,1)S(1)}, u32[]{:S(2)}, u32[]{:S(2)}) collective-permute-start(bf16[4,192,512]{2,1,0:T(8,128)(2,1)S(1)} %get-tuple-element.101), channel_id=1, source_target_pairs={{0,3},{1,2},{2,1},{3,0},{4,7},{5,6},{6,5},{7,4},{8,11},{9,10},{10,... | collective-permute-start | bytes 2359304 | tf_op jit(solution)/shard_map/ppermute | solution.py:264
  74.8 39.8 %collective-permute-start.7 = (bf16[4,64,512]{2,1,0:T(8,128)(2,1)S(1)}, bf16[4,64,512]{2,1,0:T(8,128)(2,1)S(1)}, u32[]{:S(2)}, u32[]{:S(2)}) collective-permute-start(bf16[4,64,512]{2,1,0:T(8,128)(2,1)S(1)} %get-tuple-element.91), channel_id=1, source_target_pairs={{0,5},{1,4},{2,7},{3,6},{4,1},{5,0},{6,3},{7,2},{8,13},{9,12},{10,... | collective-permute-start | bytes 786440 | tf_op jit(solution)/shard_map/ppermute | solution.py:264
  87.9 30.7 %collective-permute-start.13 = (bf16[4,64,512]{2,1,0:T(8,128)(2,1)S(1)}, bf16[4,64,512]{2,1,0:T(8,128)(2,1)S(1)}, u32[]{:S(2)}, u32[]{:S(2)}) collective-permute-start(bf16[4,64,512]{2,1,0:T(8,128)(2,1)S(1)} %get-tuple-element.103), channel_id=1, source_target_pairs={{0,6},{1,7},{2,4},{3,5},{4,2},{5,3},{6,0},{7,1},{8,14},{9,15},{10,... | collective-permute-start | bytes 786440 | tf_op jit(solution)/shard_map/ppermute | solution.py:264
  114.5 21.8 %collective-permute-start.8 = (bf16[4,64,512]{2,1,0:T(8,128)(2,1)S(1)}, bf16[4,64,512]{2,1,0:T(8,128)(2,1)S(1)}, u32[]{:S(2)}, u32[]{:S(2)}) collective-permute-start(bf16[4,64,512]{2,1,0:T(8,128)(2,1)S(1)} %get-tuple-element.92), channel_id=1, source_target_pairs={{0,4},{1,5},{2,6},{3,7},{4,0},{5,1},{6,2},{7,3},{8,12},{9,13},{10,... | collective-permute-start | bytes 786440 | tf_op jit(solution)/shard_map/ppermute | solution.py:264
  114.5 28.2 %collective-permute-start.14 = (bf16[4,64,512]{2,1,0:T(8,128)(2,1)S(1)}, bf16[4,64,512]{2,1,0:T(8,128)(2,1)S(1)}, u32[]{:S(2)}, u32[]{:S(2)}) collective-permute-start(bf16[4,64,512]{2,1,0:T(8,128)(2,1)S(1)} %get-tuple-element.105), channel_id=1, source_target_pairs={{0,7},{1,6},{2,5},{3,4},{4,3},{5,2},{6,1},{7,0},{8,15},{9,14},{10,... | collective-permute-start | bytes 786440 | tf_op jit(solution)/shard_map/ppermute | solution.py:264
  116.6 44.0 %collective-permute-start.18 = (bf16[4,128,512]{2,1,0:T(8,128)(2,1)S(1)}, bf16[4,128,512]{2,1,0:T(8,128)(2,1)S(1)}, u32[]{:S(2)}, u32[]{:S(2)}) collective-permute-start(bf16[4,128,512]{2,1,0:T(8,128)(2,1)S(1)} %get-tuple-element.115), channel_id=1, source_target_pairs={{0,3},{1,2},{2,1},{3,0},{4,7},{5,6},{6,5},{7,4},{8,11},{9,10},{10,... | collective-permute-start | bytes 1572872 | tf_op jit(solution)/shard_map/ppermute | solution.py:264
  118.6 41.2 %collective-permute-start.15 = (bf16[4,64,512]{2,1,0:T(8,128)(2,1)S(1)}, bf16[4,64,512]{2,1,0:T(8,128)(2,1)S(1)}, u32[]{:S(2)}, u32[]{:S(2)}) collective-permute-start(bf16[4,64,512]{2,1,0:T(8,128)(2,1)S(1)} %get-tuple-element.110), channel_id=1, source_target_pairs={{0,5},{1,4},{2,7},{3,6},{4,1},{5,0},{6,3},{7,2},{8,13},{9,12},{10,... | collective-permute-start | bytes 786440 | tf_op jit(solution)/shard_map/ppermute | solution.py:264
  136.3 50.0 %collective-permute-start.20 = (bf16[4,128,512]{2,1,0:T(8,128)(2,1)}, bf16[4,128,512]{2,1,0:T(8,128)(2,1)S(1)}, u32[]{:S(2)}, u32[]{:S(2)}) collective-permute-start(bf16[4,128,512]{2,1,0:T(8,128)(2,1)} %get-tuple-element.119), channel_id=1, source_target_pairs={{0,1},{1,0},{2,3},{3,2},{4,5},{5,4},{6,7},{7,6},{8,9},{9,8},{10,11... | collective-permute-start | bytes 1572872 | tf_op jit(solution)/shard_map/ppermute | solution.py:264
  136.4 50.0 %collective-permute-start.24 = (bf16[4,128,512]{2,1,0:T(8,128)(2,1)}, bf16[4,128,512]{2,1,0:T(8,128)(2,1)S(1)}, u32[]{:S(2)}, u32[]{:S(2)}) collective-permute-start(bf16[4,128,512]{2,1,0:T(8,128)(2,1)} %get-tuple-element.128), channel_id=1, source_target_pairs={{0,2},{1,3},{2,0},{3,1},{4,6},{5,7},{6,4},{7,5},{8,10},{9,11},{10,... | collective-permute-start | bytes 1572872 | tf_op jit(solution)/shard_map/ppermute | solution.py:264
  160.5 24.3 %collective-permute-start.16 = (bf16[4,64,512]{2,1,0:T(8,128)(2,1)}, bf16[4,64,512]{2,1,0:T(8,128)(2,1)}, u32[]{:S(2)}, u32[]{:S(2)}) collective-permute-start(bf16[4,64,512]{2,1,0:T(8,128)(2,1)} %get-tuple-element.111), channel_id=1, source_target_pairs={{0,4},{1,5},{2,6},{3,7},{4,0},{5,1},{6,2},{7,3},{8,12},{9,13},{10,... | collective-permute-start | bytes 786440 | tf_op jit(solution)/shard_map/ppermute | solution.py:264
  160.5 39.4 %collective-permute-start.19 = (bf16[4,128,512]{2,1,0:T(8,128)(2,1)}, bf16[4,128,512]{2,1,0:T(8,128)(2,1)S(1)}, u32[]{:S(2)}, u32[]{:S(2)}) collective-permute-start(bf16[4,128,512]{2,1,0:T(8,128)(2,1)} %get-tuple-element.116), channel_id=1, source_target_pairs={{0,2},{1,3},{2,0},{3,1},{4,6},{5,7},{6,4},{7,5},{8,10},{9,11},{10,... | collective-permute-start | bytes 1572872 | tf_op jit(solution)/shard_map/ppermute | solution.py:264
  186.4 43.6 %collective-permute-start.21 = (bf16[4,128,512]{2,1,0:T(8,128)(2,1)}, bf16[4,128,512]{2,1,0:T(8,128)(2,1)S(1)}, u32[]{:S(2)}, u32[]{:S(2)}) collective-permute-start(bf16[4,128,512]{2,1,0:T(8,128)(2,1)} %copy-done.11), channel_id=1, source_target_pairs={{0,3},{1,2},{2,1},{3,0},{4,7},{5,6},{6,5},{7,4},{8,11},{9,10},{10,... | collective-permute-start | bytes 1572872 | tf_op jit(solution)/shard_map/ppermute | solution.py:264
  186.4 18.2 %collective-permute-start.25 = (bf16[4,64,512]{2,1,0:T(8,128)(2,1)}, bf16[4,64,512]{2,1,0:T(8,128)(2,1)S(1)}, u32[]{:S(2)}, u32[]{:S(2)}) collective-permute-start(bf16[4,64,512]{2,1,0:T(8,128)(2,1)} %copy-done.12), channel_id=1, source_target_pairs={{0,7},{1,6},{2,5},{3,4},{4,3},{5,2},{6,1},{7,0},{8,15},{9,14},{10,... | collective-permute-start | bytes 786440 | tf_op jit(solution)/shard_map/ppermute | solution.py:264
  188.4 41.5 %collective-permute-start.17 = (bf16[4,128,512]{2,1,0:T(8,128)(2,1)}, bf16[4,128,512]{2,1,0:T(8,128)(2,1)S(1)}, u32[]{:S(2)}, u32[]{:S(2)}) collective-permute-start(bf16[4,128,512]{2,1,0:T(8,128)(2,1)} %copy-done.10), channel_id=1, source_target_pairs={{0,1},{1,0},{2,3},{3,2},{4,5},{5,4},{6,7},{7,6},{8,9},{9,8},{10,11... | collective-permute-start | bytes 1572872 | tf_op jit(solution)/shard_map/ppermute | solution.py:264
  199.9 30.0 %collective-permute-start.23 = (bf16[4,64,512]{2,1,0:T(8,128)(2,1)}, bf16[4,64,512]{2,1,0:T(8,128)(2,1)S(1)}, u32[]{:S(2)}, u32[]{:S(2)}) collective-permute-start(bf16[4,64,512]{2,1,0:T(8,128)(2,1)} %copy-done.16), channel_id=1, source_target_pairs={{0,5},{1,4},{2,7},{3,6},{4,1},{5,0},{6,3},{7,2},{8,13},{9,12},{10,... | collective-permute-start | bytes 786440 | tf_op jit(solution)/shard_map/ppermute | solution.py:264
  204.6 33.0 %collective-permute-start.27 = (bf16[4,64,512]{2,1,0:T(8,128)(2,1)}, bf16[4,64,512]{2,1,0:T(8,128)(2,1)S(1)}, u32[]{:S(2)}, u32[]{:S(2)}) collective-permute-start(bf16[4,64,512]{2,1,0:T(8,128)(2,1)} %copy-done.15), channel_id=1, source_target_pairs={{0,7},{1,6},{2,5},{3,4},{4,3},{5,2},{6,1},{7,0},{8,15},{9,14},{10,... | collective-permute-start | bytes 786440 | tf_op jit(solution)/shard_map/ppermute | solution.py:264
  204.9 38.4 %collective-permute-start.26 = (bf16[4,64,512]{2,1,0:T(8,128)(2,1)}, bf16[4,64,512]{2,1,0:T(8,128)(2,1)S(1)}, u32[]{:S(2)}, u32[]{:S(2)}) collective-permute-start(bf16[4,64,512]{2,1,0:T(8,128)(2,1)} %copy-done.14), channel_id=1, source_target_pairs={{0,6},{1,7},{2,4},{3,5},{4,2},{5,3},{6,0},{7,1},{8,14},{9,15},{10,... | collective-permute-start | bytes 786440 | tf_op jit(solution)/shard_map/ppermute | solution.py:264
  (30 other events, 323.9 us)

commit v6 on v5

--- a/solution.py
+++ b/solution.py
@@ -11,6 +11,8 @@
 HEAD_DIM = 128
 MEMBERS = 4
 DEPTH = 5
+ORDER = ((True, 0), (False, 2), (True, 1), (False, 3), (True, 2), (False, 1), (True, 3))
+VMEM = 60 * 1024 * 1024
 F32 = jnp.float32
 BF16 = jnp.bfloat16
 
@@ -36,7 +38,7 @@
                     row += ref.shape[0]
 
 
-def pack(table, arrays, local_heads, first, count):
+def pack(table, arrays, local_heads, first, count, vmem):
     rows = sum(a.shape[0] for a in arrays) // 4
     block = math.gcd(count, first, 2)
     steps = count // block
@@ -59,7 +61,7 @@
             * MEMBERS,
         ),
         out_shape=[jax.ShapeDtypeStruct((count, rows, 4 * HEAD_DIM), BF16)] * MEMBERS,
-        compiler_params=pltpu.CompilerParams(vmem_limit_bytes=32 * 1024 * 1024),
+        compiler_params=pltpu.CompilerParams(vmem_limit_bytes=vmem),
         cost_estimate=pl.CostEstimate(
             flops=0, bytes_accessed=MEMBERS * count * rows * HEAD_DIM * 16, transcendentals=0
         ),
@@ -111,7 +113,7 @@
         ),
         out_shape=[jax.ShapeDtypeStruct((rows, width), BF16) for rows in rows_of],
         input_output_aliases={1 + len(pieces) + i: i for i in range(len(old))},
-        compiler_params=pltpu.CompilerParams(vmem_limit_bytes=32 * 1024 * 1024),
+        compiler_params=pltpu.CompilerParams(vmem_limit_bytes=VMEM // 2),
         cost_estimate=pl.CostEstimate(
             flops=0, bytes_accessed=count * rows_k * lanes * MEMBERS * 16, transcendentals=0
         ),
@@ -214,7 +216,7 @@
         ),
         out_shape=[jax.ShapeDtypeStruct((count, 1, d), F32)]
         + [jax.ShapeDtypeStruct((count, rows, 4 * d), BF16) for rows in home_rows],
-        compiler_params=pltpu.CompilerParams(vmem_limit_bytes=48 * 1024 * 1024),
+        compiler_params=pltpu.CompilerParams(vmem_limit_bytes=VMEM),
         cost_estimate=pl.CostEstimate(
             flops=pairs * 36 * d, bytes_accessed=pairs * 8, transcendentals=pairs
         ),
@@ -223,17 +225,6 @@
 
 def after(array, *before):
     return lax.optimization_barrier((array,) + before)[0] if before else array
-
-
-def sum_over(array, axis):
-    size = lax.axis_size(axis)
-    if size & (size - 1):
-        return lax.psum(array, axis)
-    far = 1
-    while far < size:
-        array = array + lax.ppermute(array, axis, [(i, i ^ far) for i in range(size)])
-        far *= 2
-    return array
 
 
 def per_device(
@@ -264,20 +255,24 @@
         flow.append(lax.ppermute(array, "ctx", pairs))
         return flow[-1]
 
-    def spread(near, far_pieces, sign):
+    def spread(near, far_pieces, sign, *before):
         near, far_pieces = list(near), list(far_pieces)
-        order = (2, 3, 1, 0)
-        for n, j in enumerate(order):
+        for n, (is_far, j) in enumerate(ORDER):
+            ready = before if n == 6 else ()
+            if not is_far:
+                near[j] = send(after(near[j], *ready), 0, j)
+                continue
             for far in range(1, groups):
-                p = (far - 1) * MEMBERS + n
-                far_pieces[p] = send(far_pieces[p], sign * far, n)
-            near[j] = send(near[j], 0, j)
+                p = (far - 1) * MEMBERS + j
+                far_pieces[p] = send(after(far_pieces[p], *ready), sign * far, j)
         return near + far_pieces
 
     def outward(first, *before):
         arrays = (after(key_in[0], *before),) + key_in[1:]
-        far_pieces = pack(table, arrays, local_heads, first, half)
-        near = pack(table, arrays + rows_in, local_heads, first, half)
+        far_pieces = pack(
+            table, arrays, local_heads, first, half, VMEM if first == 0 else VMEM // 2
+        )
+        near = pack(table, arrays + rows_in, local_heads, first, half, VMEM // 2)
         return spread(near, list(far_pieces) * (groups - 1), 1)
 
     def attend(first, pieces, *before):
@@ -290,9 +285,11 @@
     out0 = attend(firsts[0], pieces0)
     back0 = spread(out0[1], out0[2], -1)
     out1 = attend(firsts[1], pieces1, back0[MEMBERS])
-    back1 = spread(out1[1], out1[2], -1)
+    grads = unpack(table, back0, None, rows_q, rows_k, width, local_heads, firsts[0])
+    back1 = spread(out1[1], out1[2], -1, grads[0])
     gain_mine = jnp.concatenate([out0[0], out1[0]]).reshape(groups, width // count)
-    gain_part = 0.0
+    gain_mine = lax.psum(gain_mine, "dp")
+    gain_grad = 0.0
     for far in range(groups):
         whose = lax.rem(group + far, groups)
         piece = lax.dynamic_slice_in_dim(gain_mine, whose, 1)[0]
@@ -301,9 +298,7 @@
             for g in range(groups)
             for r in range(MEMBERS)
         ]
-        gain_part = gain_part + lax.ppermute(piece, "ctx", pairs)
-    gain_grad = sum_over(after(gain_part, back1[MEMBERS]), "dp")
-    grads = unpack(table, back0, None, rows_q, rows_k, width, local_heads, firsts[0])
+        gain_grad = gain_grad + lax.ppermute(after(piece, flow[-6]), "ctx", pairs)
     grads = unpack(table, back1, grads, rows_q, rows_k, width, local_heads, firsts[1])
     return tuple(g[None] for g in tuple(grads[4:]) + tuple(grads[:4])) + (gain_grad,)
 

time: 248 us -> 240 us (0.968)
  waiting for transfers between devices: 142 us -> 115 us
  blocking collectives: 0 us -> 9.93 us
  Pallas kernels: 43.3 us -> 47.9 us
  local copies, waits for them, and re-layouts: 9.64 us -> 12.4 us
    ppermute x4 -> x2, waiting for transfers between devices: 20.4 us -> 0.01 us  [per_device(): gain_grad = gain_grad + lax.ppermute(after(piece, flow[-6]), 'ctx', pairs)]
    psum x0 -> x1, blocking collectives: none -> 9.93 us  [per_device(): gain_mine = lax.psum(gain_mine, 'dp')]
    ppermute x28, waiting for transfers between devices: 121 us -> 115 us  [send(): flow.append(lax.ppermute(array, 'ctx', pairs))]
    pallas_call x4, Pallas kernels: 9.8 us -> 12.8 us  [pack(): pl.pallas_call(functools.partial(pack_kernel, len(arrays) // 4), grid_spe...]
    ppermute x28, starting transfers between devices: 46 us -> 48.8 us  [send(): flow.append(lax.ppermute(array, 'ctx', pairs))]
    unnamed x44 -> x84, local copies, waits for them, and re-layouts: 9.61 us -> 11.8 us
  transfers between devices with their start and end apart: 32 -> 30, of which waited for: 15 -> 14; matrix products, arithmetic and copies ran while one was open for 0% -> 1% of each run, Pallas kernels for 15% -> 17%
where the time goes in v6:
time: 240 us; the launch traced here: 239 us
  waiting for transfers between devices  115 us (48%)
  starting transfers between devices  52.1 us (22%)
  Pallas kernels  47.9 us (20%)
  local copies, waits for them, and re-layouts  12.4 us (5%)
  blocking collectives  9.93 us (4%)
    ppermute x28, waiting for transfers between devices, send(): flow.append(lax.ppermute(array, 'ctx', pairs))  115 us
    ppermute x28, starting transfers between devices, send(): flow.append(lax.ppermute(array, 'ctx', pairs))  48.8 us
    pallas_call x2, Pallas kernels, attention(): pl.pallas_call(functools.partial(attention_kernel, len(pieces), key_rows,...  27.3 us
    pallas_call x4, Pallas kernels, pack(): pl.pallas_call(functools.partial(pack_kernel, len(arrays) // 4), grid_spe...  12.8 us
    unnamed x84, local copies, waits for them, and re-layouts  11.8 us
    psum x1, blocking collectives, per_device(): gain_mine = lax.psum(gain_mine, 'dp')  9.93 us
    pallas_call x2, Pallas kernels, unpack(): pl.pallas_call(functools.partial(unpack_kernel, len(pieces)), grid_spec=p...  7.85 us
  transfers between devices with their start and end apart: 30, of which 14 were waited for; matrix products, arithmetic and copies ran while one was open for 1% of the time, Pallas kernels for 17%

profile of v6, /device:TPU:8, one launch (start us, length us, event | category | flops | bytes accessed | tf_op | source)
XLA Modules:
  0.0 239.3 jit_solution(7373146423517753419)
XLA Ops:
  1.3 3.2 %shard_map.146 = (bf16[4,64,512]{2,1,0:T(8,128)(2,1)}, bf16[4,64,512]{2,1,0:T(8,128)(2,1)}, bf16[4,64,512]{2,1,0:T(8,128)(2,1)}, bf16[4,64,512]{2,1,0:T(8,128)(2,1)}) custom-call(s32[4]{0:T(128)} %pad_add_fusion.table_ref, bf16[64,4096]{1,0:T(8,128)(2,1)} %bitcast.20, bf16[64,4096]{1,0:T(8,128)(2,1)} %bitcast.36, bf16[64,4096]{1,0:T(8,128)(2,1)} %bitcast.52, ...), custom_call_target="tpu_custom_call" | custom-call | bytes 2097152 | tf_op jit(solution)/shard_map/pallas_call | solution.py:52
  11.5 3.2 %shard_map.145 = (bf16[4,192,512]{2,1,0:T(8,128)(2,1)S(1)}, bf16[4,192,512]{2,1,0:T(8,128)(2,1)S(1)}, bf16[4,192,512]{2,1,0:T(8,128)(2,1)S(1)}, bf16[4,192,512]{2,1,0:T(8,128)(2,1)S(1)}) custom-call(s32[4]{0:T(128)S(1)} %copy-done.15, bf16[64,4096]{1,0:T(8,128)(2,1)S(1)} %bitcast.24, bf16[64,4096]{1,0:T(8,128)(2,1)S(1)} %bitcast.40, ...), custom_call_target="tpu_custom_call" | custom-call | bytes 6291456 | tf_op jit(solution)/shard_map/pallas_call | solution.py:52
  19.3 2.9 %collective-permute-start.4 = (bf16[4,64,512]{2,1,0:T(8,128)(2,1)S(1)}, bf16[4,64,512]{2,1,0:T(8,128)(2,1)S(1)}, u32[]{:S(2)}, u32[]{:S(2)}) collective-permute-start(bf16[4,64,512]{2,1,0:T(8,128)(2,1)S(1)} %copy-done.41), channel_id=1, source_target_pairs={{0,5},{1,4},{2,7},{3,6},{4,1},{5,0},{6,3},{7,2},{8,13},{9,12},{10,... | collective-permute-start | bytes 786440 | tf_op jit(solution)/shard_map/ppermute | solution.py:255
  24.6 30.5 %collective-permute-done.4.refs_5_ = bf16[4,64,512]{2,1,0:T(8,128)(2,1)S(1)} collective-permute-done((bf16[4,64,512]{2,1,0:T(8,128)(2,1)S(1)}, bf16[4,64,512]{2,1,0:T(8,128)(2,1)S(1)}, u32[]{:S(2)}, u32[]{:S(2)}) %collective-permute-start.4) | collective-permute-done | bytes 262176 | tf_op jit(solution)/shard_map/ppermute | solution.py:255
  55.9 4.1 %shard_map.144 = (bf16[4,192,512]{2,1,0:T(8,128)(2,1)S(1)}, bf16[4,192,512]{2,1,0:T(8,128)(2,1)}, bf16[4,192,512]{2,1,0:T(8,128)(2,1)}, bf16[4,192,512]{2,1,0:T(8,128)(2,1)}) custom-call(s32[4]{0:T(128)S(1)} %copy-done.15, bf16[64,4096]{1,0:T(8,128)(2,1)S(1)} %bitcast.32, bf16[64,4096]{1,0:T(8,128)(2,1)S(1)} %bitcast.48, bf16[64,4096]{1,0:T(8,128)(2,1)S(1)} %bitcast.64, ...), custom_call_target="tpu_custom_call" | custom-call | bytes 6291456 | tf_op jit(solution)/shard_map/pallas_call | solution.py:52
  60.0 4.6 %collective-permute-start.11 = (bf16[4,192,512]{2,1,0:T(8,128)(2,1)}, bf16[4,192,512]{2,1,0:T(8,128)(2,1)S(1)}, u32[]{:S(2)}, u32[]{:S(2)}) collective-permute-start(bf16[4,192,512]{2,1,0:T(8,128)(2,1)} %get-tuple-element.101), channel_id=1, source_target_pairs={{0,2},{1,3},{2,0},{3,1},{4,6},{5,7},{6,4},{7,5},{8,10},{9,11},{10,... | collective-permute-start | bytes 2359304 | tf_op jit(solution)/shard_map/ppermute | solution.py:255
  65.3 2.9 %collective-permute-done.9.refs_4_ = bf16[4,64,512]{2,1,0:T(8,128)(2,1)S(1)} collective-permute-done((bf16[4,64,512]{2,1,0:T(8,128)(2,1)S(1)}, bf16[4,64,512]{2,1,0:T(8,128)(2,1)S(1)}, u32[]{:S(2)}, u32[]{:S(2)}) %collective-permute-start.9) | collective-permute-done | bytes 262176 | tf_op jit(solution)/shard_map/ppermute | solution.py:255
  68.2 4.3 %collective-permute-start.12 = (bf16[4,192,512]{2,1,0:T(8,128)(2,1)}, bf16[4,192,512]{2,1,0:T(8,128)(2,1)}, u32[]{:S(2)}, u32[]{:S(2)}) collective-permute-start(bf16[4,192,512]{2,1,0:T(8,128)(2,1)} %get-tuple-element.103), channel_id=1, source_target_pairs={{0,3},{1,2},{2,1},{3,0},{4,7},{5,6},{6,5},{7,4},{8,11},{9,10},{10,... | collective-permute-start | bytes 2359304 | tf_op jit(solution)/shard_map/ppermute | solution.py:255
  73.1 3.4 %collective-permute-done.5.refs_6_ = bf16[4,64,512]{2,1,0:T(8,128)(2,1)S(1)} collective-permute-done((bf16[4,64,512]{2,1,0:T(8,128)(2,1)S(1)}, bf16[4,64,512]{2,1,0:T(8,128)(2,1)S(1)}, u32[]{:S(2)}, u32[]{:S(2)}) %collective-permute-start.5) | collective-permute-done | bytes 262176 | tf_op jit(solution)/shard_map/ppermute | solution.py:255
  76.5 13.5 %collective-permute-start.7 = (bf16[4,64,512]{2,1,0:T(8,128)(2,1)}, bf16[4,64,512]{2,1,0:T(8,128)(2,1)S(1)}, u32[]{:S(2)}, u32[]{:S(2)}) collective-permute-start(bf16[4,64,512]{2,1,0:T(8,128)(2,1)} %get-tuple-element.93), channel_id=1, source_target_pairs={{0,5},{1,4},{2,7},{3,6},{4,1},{5,0},{6,3},{7,2},{8,13},{9,12},{10,... | collective-permute-start | bytes 786440 | tf_op jit(solution)/shard_map/ppermute | solution.py:255
  90.7 13.7 %shard_map.147 = (f32[4,1,128]{2,1,0:T(1,128)}, bf16[4,128,512]{2,1,0:T(8,128)(2,1)}, bf16[4,128,512]{2,1,0:T(8,128)(2,1)}, bf16[4,128,512]{2,1,0:T(8,128)(2,1)}...) custom-call(s32[4]{0:T(128)} %pad_add_fusion.table_ref, ...), custom_call_target="tpu_custom_call" | custom-call | flops 4831838208 | bytes 8388608 | tf_op jit(solution)/shard_map/pallas_call | solution.py:204
  104.4 10.3 %collective-permute-done.7.refs_5_ = bf16[4,64,512]{2,1,0:T(8,128)(2,1)S(1)} collective-permute-done((bf16[4,64,512]{2,1,0:T(8,128)(2,1)}, bf16[4,64,512]{2,1,0:T(8,128)(2,1)S(1)}, u32[]{:S(2)}, u32[]{:S(2)}) %collective-permute-start.7) | collective-permute-done | bytes 262176 | tf_op jit(solution)/shard_map/ppermute | solution.py:255
  123.8 15.0 %collective-permute-done.8.refs_4_ = bf16[4,64,512]{2,1,0:T(8,128)(2,1)S(1)} collective-permute-done((bf16[4,64,512]{2,1,0:T(8,128)(2,1)}, bf16[4,64,512]{2,1,0:T(8,128)(2,1)S(1)}, u32[]{:S(2)}, u32[]{:S(2)}) %collective-permute-start.8) | collective-permute-done | bytes 262176 | tf_op jit(solution)/shard_map/ppermute | solution.py:255
  140.0 5.0 %collective-permute-done.14.refs_7_ = bf16[4,64,512]{2,1,0:T(8,128)(2,1)S(1)} collective-permute-done((bf16[4,64,512]{2,1,0:T(8,128)(2,1)S(1)}, bf16[4,64,512]{2,1,0:T(8,128)(2,1)S(1)}, u32[]{:S(2)}, u32[]{:S(2)}) %collective-permute-start.14) | collective-permute-done | bytes 262176 | tf_op jit(solution)/shard_map/ppermute | solution.py:255
  145.7 13.6 %shard_map.149 = (f32[4,1,128]{2,1,0:T(1,128)}, bf16[4,128,512]{2,1,0:T(8,128)(2,1)}, bf16[4,128,512]{2,1,0:T(8,128)(2,1)}, bf16[4,128,512]{2,1,0:T(8,128)(2,1)}...) custom-call(s32[4]{0:T(128)} %pad_add_fusion.table_ref, ...), custom_call_target="tpu_custom_call" | custom-call | flops 4831838208 | bytes 8388608 | tf_op jit(solution)/shard_map/pallas_call | solution.py:204
  160.1 4.0 %collective-permute-start.16 = (bf16[4,64,512]{2,1,0:T(8,128)(2,1)}, bf16[4,64,512]{2,1,0:T(8,128)(2,1)S(1)}, u32[]{:S(2)}, u32[]{:S(2)}) collective-permute-start(bf16[4,64,512]{2,1,0:T(8,128)(2,1)} %get-tuple-element.113), channel_id=1, source_target_pairs={{0,4},{1,5},{2,6},{3,7},{4,0},{5,1},{6,2},{7,3},{8,12},{9,13},{10,... | collective-permute-start | bytes 786440 | tf_op jit(solution)/shard_map/ppermute | solution.py:255
  164.1 7.0 %collective-permute-done.24.refs_2_ = bf16[4,128,512]{2,1,0:T(8,128)(2,1)S(1)} collective-permute-done((bf16[4,128,512]{2,1,0:T(8,128)(2,1)}, bf16[4,128,512]{2,1,0:T(8,128)(2,1)S(1)}, u32[]{:S(2)}, u32[]{:S(2)}) %collective-permute-start.24) | collective-permute-done | bytes 524320 | tf_op jit(solution)/shard_map/ppermute | solution.py:255
  173.0 9.0 %collective-permute-done.16.refs_4_ = bf16[4,64,512]{2,1,0:T(8,128)(2,1)S(1)} collective-permute-done((bf16[4,64,512]{2,1,0:T(8,128)(2,1)}, bf16[4,64,512]{2,1,0:T(8,128)(2,1)S(1)}, u32[]{:S(2)}, u32[]{:S(2)}) %collective-permute-start.16) | collective-permute-done | bytes 262176 | tf_op jit(solution)/shard_map/ppermute | solution.py:255
  183.4 9.9 %psum.7 = f32[2,512]{1,0:T(2,128)S(1)} all-reduce(f32[2,512]{1,0:T(2,128)S(1)} %reshape.21), channel_id=1, replica_groups=mesh['dp'=4,'ctx'=8] {'dp'}, use_global_device_ids=true, to_apply=%region_0.1 | all-reduce | flops 1024 | bytes 8192 | tf_op jit(solution)/shard_map/psum | solution.py:291
  200.0 3.9 %shard_map.150 = (bf16[64,4096]{1,0:T(8,128)(2,1)}, bf16[64,4096]{1,0:T(8,128)(2,1)}, bf16[64,4096]{1,0:T(8,128)(2,1)}, bf16[64,4096]{1,0:T(8,128)(2,1)}, bf16[1...) custom-call(s32[4]{0:T(128)S(1)} %copy-done.16, bf16[4,128,512]{2,1,0:T(8,128)(2,1)S(1)} %copy-done.9, ...), custom_call_target="tpu_custom_call" | custom-call | bytes 8388608 | tf_op jit(solution)/shard_map/pallas_call | solution.py:96
  208.0 12.7 %collective-permute-done.23.refs_5_ = bf16[4,64,512]{2,1,0:T(8,128)(2,1)S(1)} collective-permute-done((bf16[4,64,512]{2,1,0:T(8,128)(2,1)}, bf16[4,64,512]{2,1,0:T(8,128)(2,1)S(1)}, u32[]{:S(2)}, u32[]{:S(2)}) %collective-permute-start.23) | collective-permute-done | bytes 262176 | tf_op jit(solution)/shard_map/ppermute | solution.py:255
  220.8 8.6 %collective-permute-done.26.refs_6_ = bf16[4,64,512]{2,1,0:T(8,128)(2,1)S(1)} collective-permute-done((bf16[4,64,512]{2,1,0:T(8,128)(2,1)S(1)}, bf16[4,64,512]{2,1,0:T(8,128)(2,1)S(1)}, u32[]{:S(2)}, u32[]{:S(2)}) %collective-permute-start.26) | collective-permute-done | bytes 262176 | tf_op jit(solution)/shard_map/ppermute | solution.py:255
  229.4 5.9 %collective-permute-done.27.refs_7_ = bf16[4,64,512]{2,1,0:T(8,128)(2,1)S(1)} collective-permute-done((bf16[4,64,512]{2,1,0:T(8,128)(2,1)S(1)}, bf16[4,64,512]{2,1,0:T(8,128)(2,1)S(1)}, u32[]{:S(2)}, u32[]{:S(2)}) %collective-permute-start.27) | collective-permute-done | bytes 262176 | tf_op jit(solution)/shard_map/ppermute | solution.py:255
  235.3 3.9 %shard_map.151 = (bf16[64,4096]{1,0:T(8,128)(2,1)}, bf16[64,4096]{1,0:T(8,128)(2,1)}, bf16[64,4096]{1,0:T(8,128)(2,1)}, bf16[64,4096]{1,0:T(8,128)(2,1)}, bf16[1...) custom-call(s32[4]{0:T(128)S(1)} %copy-done.16, ...), custom_call_target="tpu_custom_call", output_to_operand_aliasing={{0}: (9, {}), {1}: (10, {}), {2}: (11, {}), {3}: (12, {}), ... | custom-call | bytes 8388608 | tf_op jit(solution)/shard_map/pallas_call | solution.py:96
  (135 shorter events, 43.2 us)
Async XLA Ops:
  14.7 45.2 %collective-permute-start.3 = (bf16[4,192,512]{2,1,0:T(8,128)(2,1)S(1)}, bf16[4,192,512]{2,1,0:T(8,128)(2,1)S(1)}, u32[]{:S(2)}, u32[]{:S(2)}) collective-permute-start(bf16[4,192,512]{2,1,0:T(8,128)(2,1)S(1)} %get-tuple-element.86), channel_id=1, source_target_pairs={{0,3},{1,2},{2,1},{3,0},{4,7},{5,6},{6,5},{7,4},{8,11},{9,10},{10,... | collective-permute-start | bytes 2359304 | tf_op jit(solution)/shard_map/ppermute | solution.py:255
  14.8 49.8 %collective-permute-start.2 = (bf16[4,192,512]{2,1,0:T(8,128)(2,1)S(1)}, bf16[4,192,512]{2,1,0:T(8,128)(2,1)S(1)}, u32[]{:S(2)}, u32[]{:S(2)}) collective-permute-start(bf16[4,192,512]{2,1,0:T(8,128)(2,1)S(1)} %get-tuple-element.85), channel_id=1, source_target_pairs={{0,2},{1,3},{2,0},{3,1},{4,6},{5,7},{6,4},{7,5},{8,10},{9,11},{10,... | collective-permute-start | bytes 2359304 | tf_op jit(solution)/shard_map/ppermute | solution.py:255
  18.6 49.6 %collective-permute-start.1 = (bf16[4,192,512]{2,1,0:T(8,128)(2,1)S(1)}, bf16[4,192,512]{2,1,0:T(8,128)(2,1)S(1)}, u32[]{:S(2)}, u32[]{:S(2)}) collective-permute-start(bf16[4,192,512]{2,1,0:T(8,128)(2,1)S(1)} %get-tuple-element.84), channel_id=1, source_target_pairs={{0,1},{1,0},{2,3},{3,2},{4,5},{5,4},{6,7},{7,6},{8,9},{9,8},{10,11... | collective-permute-start | bytes 2359304 | tf_op jit(solution)/shard_map/ppermute | solution.py:255
  19.3 35.8 %collective-permute-start.4 = (bf16[4,64,512]{2,1,0:T(8,128)(2,1)S(1)}, bf16[4,64,512]{2,1,0:T(8,128)(2,1)S(1)}, u32[]{:S(2)}, u32[]{:S(2)}) collective-permute-start(bf16[4,64,512]{2,1,0:T(8,128)(2,1)S(1)} %copy-done.41), channel_id=1, source_target_pairs={{0,5},{1,4},{2,7},{3,6},{4,1},{5,0},{6,3},{7,2},{8,13},{9,12},{10,... | collective-permute-start | bytes 786440 | tf_op jit(solution)/shard_map/ppermute | solution.py:255
  60.0 56.7 %collective-permute-start.11 = (bf16[4,192,512]{2,1,0:T(8,128)(2,1)}, bf16[4,192,512]{2,1,0:T(8,128)(2,1)S(1)}, u32[]{:S(2)}, u32[]{:S(2)}) collective-permute-start(bf16[4,192,512]{2,1,0:T(8,128)(2,1)} %get-tuple-element.101), channel_id=1, source_target_pairs={{0,2},{1,3},{2,0},{3,1},{4,6},{5,7},{6,4},{7,5},{8,10},{9,11},{10,... | collective-permute-start | bytes 2359304 | tf_op jit(solution)/shard_map/ppermute | solution.py:255
  64.6 25.4 %collective-permute-start.6 = (bf16[4,64,512]{2,1,0:T(8,128)(2,1)S(1)}, bf16[4,64,512]{2,1,0:T(8,128)(2,1)S(1)}, u32[]{:S(2)}, u32[]{:S(2)}) collective-permute-start(bf16[4,64,512]{2,1,0:T(8,128)(2,1)S(1)} %copy-done.34), channel_id=1, source_target_pairs={{0,7},{1,6},{2,5},{3,4},{4,3},{5,2},{6,1},{7,0},{8,15},{9,14},{10,... | collective-permute-start | bytes 786440 | tf_op jit(solution)/shard_map/ppermute | solution.py:255
  68.2 51.0 %collective-permute-start.10 = (bf16[4,192,512]{2,1,0:T(8,128)(2,1)}, bf16[4,192,512]{2,1,0:T(8,128)(2,1)S(1)}, u32[]{:S(2)}, u32[]{:S(2)}) collective-permute-start(bf16[4,192,512]{2,1,0:T(8,128)(2,1)} %get-tuple-element.99), channel_id=1, source_target_pairs={{0,1},{1,0},{2,3},{3,2},{4,5},{5,4},{6,7},{7,6},{8,9},{9,8},{10,11... | collective-permute-start | bytes 2359304 | tf_op jit(solution)/shard_map/ppermute | solution.py:255
  68.2 70.6 %collective-permute-start.12 = (bf16[4,192,512]{2,1,0:T(8,128)(2,1)}, bf16[4,192,512]{2,1,0:T(8,128)(2,1)}, u32[]{:S(2)}, u32[]{:S(2)}) collective-permute-start(bf16[4,192,512]{2,1,0:T(8,128)(2,1)} %get-tuple-element.103), channel_id=1, source_target_pairs={{0,3},{1,2},{2,1},{3,0},{4,7},{5,6},{6,5},{7,4},{8,11},{9,10},{10,... | collective-permute-start | bytes 2359304 | tf_op jit(solution)/shard_map/ppermute | solution.py:255
  76.5 38.2 %collective-permute-start.7 = (bf16[4,64,512]{2,1,0:T(8,128)(2,1)}, bf16[4,64,512]{2,1,0:T(8,128)(2,1)S(1)}, u32[]{:S(2)}, u32[]{:S(2)}) collective-permute-start(bf16[4,64,512]{2,1,0:T(8,128)(2,1)} %get-tuple-element.93), channel_id=1, source_target_pairs={{0,5},{1,4},{2,7},{3,6},{4,1},{5,0},{6,3},{7,2},{8,13},{9,12},{10,... | collective-permute-start | bytes 786440 | tf_op jit(solution)/shard_map/ppermute | solution.py:255
  90.0 31.4 %collective-permute-start.13 = (bf16[4,64,512]{2,1,0:T(8,128)(2,1)}, bf16[4,64,512]{2,1,0:T(8,128)(2,1)S(1)}, u32[]{:S(2)}, u32[]{:S(2)}) collective-permute-start(bf16[4,64,512]{2,1,0:T(8,128)(2,1)} %get-tuple-element.105), channel_id=1, source_target_pairs={{0,6},{1,7},{2,4},{3,5},{4,2},{5,3},{6,0},{7,1},{8,14},{9,15},{10,... | collective-permute-start | bytes 786440 | tf_op jit(solution)/shard_map/ppermute | solution.py:255
  114.7 24.1 %collective-permute-start.8 = (bf16[4,64,512]{2,1,0:T(8,128)(2,1)}, bf16[4,64,512]{2,1,0:T(8,128)(2,1)S(1)}, u32[]{:S(2)}, u32[]{:S(2)}) collective-permute-start(bf16[4,64,512]{2,1,0:T(8,128)(2,1)} %get-tuple-element.94), channel_id=1, source_target_pairs={{0,4},{1,5},{2,6},{3,7},{4,0},{5,1},{6,2},{7,3},{8,12},{9,13},{10,... | collective-permute-start | bytes 786440 | tf_op jit(solution)/shard_map/ppermute | solution.py:255
  116.6 28.4 %collective-permute-start.14 = (bf16[4,64,512]{2,1,0:T(8,128)(2,1)S(1)}, bf16[4,64,512]{2,1,0:T(8,128)(2,1)S(1)}, u32[]{:S(2)}, u32[]{:S(2)}) collective-permute-start(bf16[4,64,512]{2,1,0:T(8,128)(2,1)S(1)} %copy-done.20), channel_id=1, source_target_pairs={{0,7},{1,6},{2,5},{3,4},{4,3},{5,2},{6,1},{7,0},{8,15},{9,14},{10,... | collective-permute-start | bytes 786440 | tf_op jit(solution)/shard_map/ppermute | solution.py:255
  120.1 39.2 %collective-permute-start.18 = (bf16[4,128,512]{2,1,0:T(8,128)(2,1)}, bf16[4,128,512]{2,1,0:T(8,128)(2,1)S(1)}, u32[]{:S(2)}, u32[]{:S(2)}) collective-permute-start(bf16[4,128,512]{2,1,0:T(8,128)(2,1)} %get-tuple-element.117), channel_id=1, source_target_pairs={{0,3},{1,2},{2,1},{3,0},{4,7},{5,6},{6,5},{7,4},{8,11},{9,10},{10,... | collective-permute-start | bytes 1572872 | tf_op jit(solution)/shard_map/ppermute | solution.py:255
  121.4 38.0 %collective-permute-start.15 = (bf16[4,64,512]{2,1,0:T(8,128)(2,1)}, bf16[4,64,512]{2,1,0:T(8,128)(2,1)S(1)}, u32[]{:S(2)}, u32[]{:S(2)}) collective-permute-start(bf16[4,64,512]{2,1,0:T(8,128)(2,1)} %get-tuple-element.112), channel_id=1, source_target_pairs={{0,5},{1,4},{2,7},{3,6},{4,1},{5,0},{6,3},{7,2},{8,13},{9,12},{10,... | collective-permute-start | bytes 786440 | tf_op jit(solution)/shard_map/ppermute | solution.py:255
  138.8 32.3 %collective-permute-start.20 = (bf16[4,128,512]{2,1,0:T(8,128)(2,1)}, bf16[4,128,512]{2,1,0:T(8,128)(2,1)S(1)}, u32[]{:S(2)}, u32[]{:S(2)}) collective-permute-start(bf16[4,128,512]{2,1,0:T(8,128)(2,1)} %get-tuple-element.121), channel_id=1, source_target_pairs={{0,1},{1,0},{2,3},{3,2},{4,5},{5,4},{6,7},{7,6},{8,9},{9,8},{10,11... | collective-permute-start | bytes 1572872 | tf_op jit(solution)/shard_map/ppermute | solution.py:255
  138.8 32.3 %collective-permute-start.24 = (bf16[4,128,512]{2,1,0:T(8,128)(2,1)}, bf16[4,128,512]{2,1,0:T(8,128)(2,1)S(1)}, u32[]{:S(2)}, u32[]{:S(2)}) collective-permute-start(bf16[4,128,512]{2,1,0:T(8,128)(2,1)} %get-tuple-element.130), channel_id=1, source_target_pairs={{0,2},{1,3},{2,0},{3,1},{4,6},{5,7},{6,4},{7,5},{8,10},{9,11},{10,... | collective-permute-start | bytes 1572872 | tf_op jit(solution)/shard_map/ppermute | solution.py:255
  159.3 34.2 %collective-permute-start.19 = (bf16[4,128,512]{2,1,0:T(8,128)(2,1)}, bf16[4,128,512]{2,1,0:T(8,128)(2,1)S(1)}, u32[]{:S(2)}, u32[]{:S(2)}) collective-permute-start(bf16[4,128,512]{2,1,0:T(8,128)(2,1)} %get-tuple-element.118), channel_id=1, source_target_pairs={{0,2},{1,3},{2,0},{3,1},{4,6},{5,7},{6,4},{7,5},{8,10},{9,11},{10,... | collective-permute-start | bytes 1572872 | tf_op jit(solution)/shard_map/ppermute | solution.py:255
  164.1 31.4 %collective-permute-start.22 = (bf16[4,64,512]{2,1,0:T(8,128)(2,1)}, bf16[4,64,512]{2,1,0:T(8,128)(2,1)}, u32[]{:S(2)}, u32[]{:S(2)}) collective-permute-start(bf16[4,64,512]{2,1,0:T(8,128)(2,1)} %get-tuple-element.125), channel_id=1, source_target_pairs={{0,6},{1,7},{2,4},{3,5},{4,2},{5,3},{6,0},{7,1},{8,14},{9,15},{10,... | collective-permute-start | bytes 786440 | tf_op jit(solution)/shard_map/ppermute | solution.py:255
  171.1 27.2 %collective-permute-start.25 = (bf16[4,64,512]{2,1,0:T(8,128)(2,1)}, bf16[4,64,512]{2,1,0:T(8,128)(2,1)}, u32[]{:S(2)}, u32[]{:S(2)}) collective-permute-start(bf16[4,64,512]{2,1,0:T(8,128)(2,1)} %get-tuple-element.131), channel_id=1, source_target_pairs={{0,7},{1,6},{2,5},{3,4},{4,3},{5,2},{6,1},{7,0},{8,15},{9,14},{10,... | collective-permute-start | bytes 786440 | tf_op jit(solution)/shard_map/ppermute | solution.py:255
  171.1 49.7 %collective-permute-start.21 = (bf16[4,128,512]{2,1,0:T(8,128)(2,1)}, bf16[4,128,512]{2,1,0:T(8,128)(2,1)S(1)}, u32[]{:S(2)}, u32[]{:S(2)}) collective-permute-start(bf16[4,128,512]{2,1,0:T(8,128)(2,1)} %get-tuple-element.122), channel_id=1, source_target_pairs={{0,3},{1,2},{2,1},{3,0},{4,7},{5,6},{6,5},{7,4},{8,11},{9,10},{10,... | collective-permute-start | bytes 1572872 | tf_op jit(solution)/shard_map/ppermute | solution.py:255
  182.7 38.1 %collective-permute-start.17 = (bf16[4,128,512]{2,1,0:T(8,128)(2,1)}, bf16[4,128,512]{2,1,0:T(8,128)(2,1)}, u32[]{:S(2)}, u32[]{:S(2)}) collective-permute-start(bf16[4,128,512]{2,1,0:T(8,128)(2,1)} %get-tuple-element.114), channel_id=1, source_target_pairs={{0,1},{1,0},{2,3},{3,2},{4,5},{5,4},{6,7},{7,6},{8,9},{9,8},{10,11... | collective-permute-start | bytes 1572872 | tf_op jit(solution)/shard_map/ppermute | solution.py:255
  198.3 22.4 %collective-permute-start.23 = (bf16[4,64,512]{2,1,0:T(8,128)(2,1)}, bf16[4,64,512]{2,1,0:T(8,128)(2,1)S(1)}, u32[]{:S(2)}, u32[]{:S(2)}) collective-permute-start(bf16[4,64,512]{2,1,0:T(8,128)(2,1)} %get-tuple-element.126), channel_id=1, source_target_pairs={{0,5},{1,4},{2,7},{3,6},{4,1},{5,0},{6,3},{7,2},{8,13},{9,12},{10,... | collective-permute-start | bytes 786440 | tf_op jit(solution)/shard_map/ppermute | solution.py:255
  203.9 25.5 %collective-permute-start.26 = (bf16[4,64,512]{2,1,0:T(8,128)(2,1)S(1)}, bf16[4,64,512]{2,1,0:T(8,128)(2,1)S(1)}, u32[]{:S(2)}, u32[]{:S(2)}) collective-permute-start(bf16[4,64,512]{2,1,0:T(8,128)(2,1)S(1)} %copy-done.30), channel_id=1, source_target_pairs={{0,6},{1,7},{2,4},{3,5},{4,2},{5,3},{6,0},{7,1},{8,14},{9,15},{10,... | collective-permute-start | bytes 786440 | tf_op jit(solution)/shard_map/ppermute | solution.py:255
  205.5 29.9 %collective-permute-start.27 = (bf16[4,64,512]{2,1,0:T(8,128)(2,1)S(1)}, bf16[4,64,512]{2,1,0:T(8,128)(2,1)S(1)}, u32[]{:S(2)}, u32[]{:S(2)}) collective-permute-start(bf16[4,64,512]{2,1,0:T(8,128)(2,1)S(1)} %copy-done.29), channel_id=1, source_target_pairs={{0,7},{1,6},{2,5},{3,4},{4,3},{5,2},{6,1},{7,0},{8,15},{9,14},{10,... | collective-permute-start | bytes 786440 | tf_op jit(solution)/shard_map/ppermute | solution.py:255
  (48 other events, 609.0 us)

commit v7 on v6

--- a/solution.py
+++ b/solution.py
@@ -11,7 +11,7 @@
 HEAD_DIM = 128
 MEMBERS = 4
 DEPTH = 5
-ORDER = ((True, 0), (False, 2), (True, 1), (False, 3), (True, 2), (False, 1), (True, 3))
+ORDER = ((True, 0), (False, 3), (True, 1), (False, 2), (True, 3), (False, 1), (True, 2))
 VMEM = 60 * 1024 * 1024
 F32 = jnp.float32
 BF16 = jnp.bfloat16
@@ -68,17 +68,17 @@
     )(table, *(list(arrays) * MEMBERS))
 
 
-def unpack_kernel(pieces, table_ref, *refs):
+def unpack_kernel(members, pieces, table_ref, *refs):
     outs = refs[-6:]
     key_rows, half_rows = outs[0].shape[0], outs[4].shape[0] // 2
     d = HEAD_DIM
-    for j in range(MEMBERS):
+    for j in range(members):
 
         @pl.when(pl.program_id(0) == j)
         def _(j=j):
             near = refs[j]
             total = near[:, :key_rows].astype(F32)
-            for p in range(MEMBERS + j, pieces, MEMBERS):
+            for p in range(members + j, pieces, members):
                 total = total + refs[p][...].astype(F32)
             for h in range(total.shape[0]):
                 columns = slice(h * d, (h + 1) * d)
@@ -89,15 +89,17 @@
                     ref[half_rows:, columns] = near[h, key_rows:, (i + 2) * d : (i + 3) * d]
 
 
-def unpack(table, pieces, before, rows_q, rows_k, width, local_heads, first):
+def unpack(table, chosen, pieces, before, rows_q, rows_k, width, local_heads, first):
     count, lanes = pieces[0].shape[0], 4 * HEAD_DIM
     old = list(before or ())
+    pieces = [p for n, p in enumerate(pieces) if n % MEMBERS in chosen]
+    table = jnp.stack([table[j] for j in chosen])
     rows_of = [rows_k] * 4 + [rows_q] * 2
     return pl.pallas_call(
-        functools.partial(unpack_kernel, len(pieces)),
+        functools.partial(unpack_kernel, len(chosen), len(pieces)),
         grid_spec=pltpu.PrefetchScalarGridSpec(
             num_scalar_prefetch=1,
-            grid=(MEMBERS,),
+            grid=(len(chosen),),
             in_specs=[
                 pl.BlockSpec((count, p.shape[1], lanes), lambda j, table_ref: (0, 0, 0))
                 for p in pieces
@@ -285,7 +287,9 @@
     out0 = attend(firsts[0], pieces0)
     back0 = spread(out0[1], out0[2], -1)
     out1 = attend(firsts[1], pieces1, back0[MEMBERS])
-    grads = unpack(table, back0, None, rows_q, rows_k, width, local_heads, firsts[0])
+    grads = unpack(
+        table, (0, 1, 2, 3), back0, None, rows_q, rows_k, width, local_heads, firsts[0]
+    )
     back1 = spread(out1[1], out1[2], -1, grads[0])
     gain_mine = jnp.concatenate([out0[0], out1[0]]).reshape(groups, width // count)
     gain_mine = lax.psum(gain_mine, "dp")
@@ -299,7 +303,10 @@
             for r in range(MEMBERS)
         ]
         gain_grad = gain_grad + lax.ppermute(after(piece, flow[-6]), "ctx", pairs)
-    grads = unpack(table, back1, grads, rows_q, rows_k, width, local_heads, firsts[1])
+    for chosen in ((0, 1, 3), (2,)):
+        grads = unpack(
+            table, chosen, back1, grads, rows_q, rows_k, width, local_heads, firsts[1]
+        )
     return tuple(g[None] for g in tuple(grads[4:]) + tuple(grads[:4])) + (gain_grad,)
 
 

time: 240 us -> 235 us (0.979)
  waiting for transfers between devices: 115 us -> 111 us
    ppermute x28, waiting for transfers between devices: 115 us -> 111 us  [send(): flow.append(lax.ppermute(array, 'ctx', pairs))]
    pallas_call x2 -> x3, Pallas kernels: 7.85 us -> 8.39 us  [unpack(): pl.pallas_call(functools.partial(unpack_kernel, len(chosen), len(pieces))...]
  transfers between devices with their start and end apart: 30 -> 30, of which waited for: 14 -> 14; matrix products, arithmetic and copies ran while one was open for 1% -> 1% of each run, Pallas kernels for 17% -> 19%
where the time goes in v7:
time: 235 us
  waiting for transfers between devices  111 us (47%)
  starting transfers between devices  49.8 us (21%)
  Pallas kernels  48.4 us (21%)
  local copies, waits for them, and re-layouts  13.2 us (6%)
  blocking collectives  9.91 us (4%)
    ppermute x28, waiting for transfers between devices, send(): flow.append(lax.ppermute(array, 'ctx', pairs))  111 us
    ppermute x28, starting transfers between devices, send(): flow.append(lax.ppermute(array, 'ctx', pairs))  47.6 us
    pallas_call x2, Pallas kernels, attention(): pl.pallas_call(functools.partial(attention_kernel, len(pieces), key_rows,...  27.3 us
    pallas_call x4, Pallas kernels, pack(): pl.pallas_call(functools.partial(pack_kernel, len(arrays) // 4), grid_spe...  12.7 us
    unnamed x84, local copies, waits for them, and re-layouts  12.5 us
    psum x1, blocking collectives, per_device(): gain_mine = lax.psum(gain_mine, 'dp')  9.91 us
    pallas_call x3, Pallas kernels, unpack(): pl.pallas_call(functools.partial(unpack_kernel, len(chosen), len(pieces))...  8.39 us
  transfers between devices with their start and end apart: 30, of which 14 were waited for; matrix products, arithmetic and copies ran while one was open for 1% of the time, Pallas kernels for 19%

profile of v7, /device:TPU:8, one launch (start us, length us, event | category | flops | bytes accessed | tf_op | source)
XLA Modules:
  0.0 235.0 jit_solution(13149912306786974232)
XLA Ops:
  1.3 3.2 %shard_map.146 = (bf16[4,64,512]{2,1,0:T(8,128)(2,1)}, bf16[4,64,512]{2,1,0:T(8,128)(2,1)}, bf16[4,64,512]{2,1,0:T(8,128)(2,1)}, bf16[4,64,512]{2,1,0:T(8,128)(2,1)}) custom-call(s32[4]{0:T(128)} %pad_add_fusion.table_ref, bf16[64,4096]{1,0:T(8,128)(2,1)} %bitcast.20, bf16[64,4096]{1,0:T(8,128)(2,1)} %bitcast.36, bf16[64,4096]{1,0:T(8,128)(2,1)} %bitcast.52, ...), custom_call_target="tpu_custom_call" | custom-call | bytes 2097152 | tf_op jit(solution)/shard_map/pallas_call | solution.py:52
  11.5 3.2 %shard_map.145 = (bf16[4,192,512]{2,1,0:T(8,128)(2,1)S(1)}, bf16[4,192,512]{2,1,0:T(8,128)(2,1)S(1)}, bf16[4,192,512]{2,1,0:T(8,128)(2,1)S(1)}, bf16[4,192,512]{2,1,0:T(8,128)(2,1)S(1)}) custom-call(s32[4]{0:T(128)S(1)} %copy-done.15, bf16[64,4096]{1,0:T(8,128)(2,1)S(1)} %bitcast.24, bf16[64,4096]{1,0:T(8,128)(2,1)S(1)} %bitcast.40, ...), custom_call_target="tpu_custom_call" | custom-call | bytes 6291456 | tf_op jit(solution)/shard_map/pallas_call | solution.py:52
  15.7 2.9 %collective-permute-done.refs_4_ = bf16[4,64,512]{2,1,0:T(8,128)(2,1)S(1)} collective-permute-done((bf16[4,64,512]{2,1,0:T(8,128)(2,1)}, bf16[4,64,512]{2,1,0:T(8,128)(2,1)S(1)}, u32[]{:S(2)}, u32[]{:S(2)}) %collective-permute-start) | collective-permute-done | bytes 262176 | tf_op jit(solution)/shard_map/ppermute | solution.py:257
  24.6 29.2 %collective-permute-done.4.refs_5_ = bf16[4,64,512]{2,1,0:T(8,128)(2,1)S(1)} collective-permute-done((bf16[4,64,512]{2,1,0:T(8,128)(2,1)S(1)}, bf16[4,64,512]{2,1,0:T(8,128)(2,1)S(1)}, u32[]{:S(2)}, u32[]{:S(2)}) %collective-permute-start.4) | collective-permute-done | bytes 262176 | tf_op jit(solution)/shard_map/ppermute | solution.py:257
  55.2 4.0 %shard_map.144 = (bf16[4,192,512]{2,1,0:T(8,128)(2,1)S(1)}, bf16[4,192,512]{2,1,0:T(8,128)(2,1)}, bf16[4,192,512]{2,1,0:T(8,128)(2,1)}, bf16[4,192,512]{2,1,0:T(8,128)(2,1)}) custom-call(s32[4]{0:T(128)S(1)} %copy-done.15, bf16[64,4096]{1,0:T(8,128)(2,1)S(1)} %bitcast.32, bf16[64,4096]{1,0:T(8,128)(2,1)S(1)} %bitcast.48, bf16[64,4096]{1,0:T(8,128)(2,1)S(1)} %bitcast.64, ...), custom_call_target="tpu_custom_call" | custom-call | bytes 6291456 | tf_op jit(solution)/shard_map/pallas_call | solution.py:52
  59.3 3.9 %collective-permute-start.12 = (bf16[4,192,512]{2,1,0:T(8,128)(2,1)}, bf16[4,192,512]{2,1,0:T(8,128)(2,1)S(1)}, u32[]{:S(2)}, u32[]{:S(2)}) collective-permute-start(bf16[4,192,512]{2,1,0:T(8,128)(2,1)} %get-tuple-element.109), channel_id=1, source_target_pairs={{0,3},{1,2},{2,1},{3,0},{4,7},{5,6},{6,5},{7,4},{8,11},{9,10},{10,... | collective-permute-start | bytes 2359304 | tf_op jit(solution)/shard_map/ppermute | solution.py:257
  64.3 3.2 %collective-permute-done.9.refs_4_ = bf16[4,64,512]{2,1,0:T(8,128)(2,1)S(1)} collective-permute-done((bf16[4,64,512]{2,1,0:T(8,128)(2,1)S(1)}, bf16[4,64,512]{2,1,0:T(8,128)(2,1)S(1)}, u32[]{:S(2)}, u32[]{:S(2)}) %collective-permute-start.9) | collective-permute-done | bytes 262176 | tf_op jit(solution)/shard_map/ppermute | solution.py:257
  67.6 4.3 %collective-permute-start.11 = (bf16[4,192,512]{2,1,0:T(8,128)(2,1)}, bf16[4,192,512]{2,1,0:T(8,128)(2,1)}, u32[]{:S(2)}, u32[]{:S(2)}) collective-permute-start(bf16[4,192,512]{2,1,0:T(8,128)(2,1)} %get-tuple-element.107), channel_id=1, source_target_pairs={{0,2},{1,3},{2,0},{3,1},{4,6},{5,7},{6,4},{7,5},{8,10},{9,11},{10,... | collective-permute-start | bytes 2359304 | tf_op jit(solution)/shard_map/ppermute | solution.py:257
  72.5 3.4 %collective-permute-done.6.refs_7_ = bf16[4,64,512]{2,1,0:T(8,128)(2,1)S(1)} collective-permute-done((bf16[4,64,512]{2,1,0:T(8,128)(2,1)S(1)}, bf16[4,64,512]{2,1,0:T(8,128)(2,1)S(1)}, u32[]{:S(2)}, u32[]{:S(2)}) %collective-permute-start.6) | collective-permute-done | bytes 262176 | tf_op jit(solution)/shard_map/ppermute | solution.py:257
  75.9 14.0 %collective-permute-start.7 = (bf16[4,64,512]{2,1,0:T(8,128)(2,1)}, bf16[4,64,512]{2,1,0:T(8,128)(2,1)S(1)}, u32[]{:S(2)}, u32[]{:S(2)}) collective-permute-start(bf16[4,64,512]{2,1,0:T(8,128)(2,1)} %get-tuple-element.99), channel_id=1, source_target_pairs={{0,5},{1,4},{2,7},{3,6},{4,1},{5,0},{6,3},{7,2},{8,13},{9,12},{10,... | collective-permute-start | bytes 786440 | tf_op jit(solution)/shard_map/ppermute | solution.py:257
  90.6 13.7 %shard_map.147 = (f32[4,1,128]{2,1,0:T(1,128)}, bf16[4,128,512]{2,1,0:T(8,128)(2,1)}, bf16[4,128,512]{2,1,0:T(8,128)(2,1)}, bf16[4,128,512]{2,1,0:T(8,128)(2,1)}...) custom-call(s32[4]{0:T(128)} %pad_add_fusion.table_ref, ...), custom_call_target="tpu_custom_call" | custom-call | flops 4831838208 | bytes 8388608 | tf_op jit(solution)/shard_map/pallas_call | solution.py:206
  104.3 10.6 %collective-permute-done.7.refs_5_ = bf16[4,64,512]{2,1,0:T(8,128)(2,1)S(1)} collective-permute-done((bf16[4,64,512]{2,1,0:T(8,128)(2,1)}, bf16[4,64,512]{2,1,0:T(8,128)(2,1)S(1)}, u32[]{:S(2)}, u32[]{:S(2)}) %collective-permute-start.7) | collective-permute-done | bytes 262176 | tf_op jit(solution)/shard_map/ppermute | solution.py:257
  121.3 3.1 %collective-permute-start.19 = (bf16[4,64,512]{2,1,0:T(8,128)(2,1)}, bf16[4,64,512]{2,1,0:T(8,128)(2,1)S(1)}, u32[]{:S(2)}, u32[]{:S(2)}) collective-permute-start(bf16[4,64,512]{2,1,0:T(8,128)(2,1)} %get-tuple-element.125), channel_id=1, source_target_pairs={{0,5},{1,4},{2,7},{3,6},{4,1},{5,0},{6,3},{7,2},{8,13},{9,12},{10,... | collective-permute-start | bytes 786440 | tf_op jit(solution)/shard_map/ppermute | solution.py:257
  124.4 13.5 %collective-permute-done.8.refs_4_ = bf16[4,64,512]{2,1,0:T(8,128)(2,1)S(1)} collective-permute-done((bf16[4,64,512]{2,1,0:T(8,128)(2,1)}, bf16[4,64,512]{2,1,0:T(8,128)(2,1)S(1)}, u32[]{:S(2)}, u32[]{:S(2)}) %collective-permute-start.8) | collective-permute-done | bytes 262176 | tf_op jit(solution)/shard_map/ppermute | solution.py:257
  139.6 4.4 %collective-permute-done.13.refs_6_ = bf16[4,64,512]{2,1,0:T(8,128)(2,1)S(1)} collective-permute-done((bf16[4,64,512]{2,1,0:T(8,128)(2,1)S(1)}, bf16[4,64,512]{2,1,0:T(8,128)(2,1)S(1)}, u32[]{:S(2)}, u32[]{:S(2)}) %collective-permute-start.13) | collective-permute-done | bytes 262176 | tf_op jit(solution)/shard_map/ppermute | solution.py:257
  144.7 13.6 %shard_map.149 = (f32[4,1,128]{2,1,0:T(1,128)}, bf16[4,128,512]{2,1,0:T(8,128)(2,1)}, bf16[4,128,512]{2,1,0:T(8,128)(2,1)}, bf16[4,128,512]{2,1,0:T(8,128)(2,1)}...) custom-call(s32[4]{0:T(128)} %pad_add_fusion.table_ref, ...), custom_call_target="tpu_custom_call" | custom-call | flops 4831838208 | bytes 8388608 | tf_op jit(solution)/shard_map/pallas_call | solution.py:206
  159.1 3.1 %collective-permute-start.24 = (bf16[4,64,512]{2,1,0:T(8,128)(2,1)}, bf16[4,64,512]{2,1,0:T(8,128)(2,1)S(1)}, u32[]{:S(2)}, u32[]{:S(2)}) collective-permute-start(bf16[4,64,512]{2,1,0:T(8,128)(2,1)} %get-tuple-element.138), channel_id=1, source_target_pairs={{0,4},{1,5},{2,6},{3,7},{4,0},{5,1},{6,2},{7,3},{8,12},{9,13},{10,... | collective-permute-start | bytes 786440 | tf_op jit(solution)/shard_map/ppermute | solution.py:257
  162.2 8.3 %collective-permute-done.18.refs_3_ = bf16[4,128,512]{2,1,0:T(8,128)(2,1)S(1)} collective-permute-done((bf16[4,128,512]{2,1,0:T(8,128)(2,1)}, bf16[4,128,512]{2,1,0:T(8,128)(2,1)S(1)}, u32[]{:S(2)}, u32[]{:S(2)}) %collective-permute-start.18) | collective-permute-done | bytes 524320 | tf_op jit(solution)/shard_map/ppermute | solution.py:257
  170.6 9.7 %collective-permute-done.24.refs_3_ = bf16[4,64,512]{2,1,0:T(8,128)(2,1)S(1)} collective-permute-done((bf16[4,64,512]{2,1,0:T(8,128)(2,1)}, bf16[4,64,512]{2,1,0:T(8,128)(2,1)S(1)}, u32[]{:S(2)}, u32[]{:S(2)}) %collective-permute-start.24) | collective-permute-done | bytes 262176 | tf_op jit(solution)/shard_map/ppermute | solution.py:257
  181.7 9.9 %psum.7 = f32[2,512]{1,0:T(2,128)S(1)} all-reduce(f32[2,512]{1,0:T(2,128)S(1)} %reshape.21), channel_id=1, replica_groups=mesh['dp'=4,'ctx'=8] {'dp'}, use_global_device_ids=true, to_apply=%region_0.1 | all-reduce | flops 1024 | bytes 8192 | tf_op jit(solution)/shard_map/psum | solution.py:295
  199.0 3.9 %shard_map.150 = (bf16[64,4096]{1,0:T(8,128)(2,1)}, bf16[64,4096]{1,0:T(8,128)(2,1)}, bf16[64,4096]{1,0:T(8,128)(2,1)}, bf16[64,4096]{1,0:T(8,128)(2,1)}, bf16[1...) custom-call(s32[4]{0:T(128)S(1)} %copy-done.16, bf16[4,128,512]{2,1,0:T(8,128)(2,1)S(1)} %copy-done.9, ...), custom_call_target="tpu_custom_call" | custom-call | bytes 8388608 | tf_op jit(solution)/shard_map/pallas_call | solution.py:98
  207.8 11.7 %collective-permute-done.26.refs_4_ = bf16[4,64,512]{2,1,0:T(8,128)(2,1)S(1)} collective-permute-done((bf16[4,64,512]{2,1,0:T(8,128)(2,1)}, bf16[4,64,512]{2,1,0:T(8,128)(2,1)S(1)}, u32[]{:S(2)}, u32[]{:S(2)}) %collective-permute-start.26) | collective-permute-done | bytes 262176 | tf_op jit(solution)/shard_map/ppermute | solution.py:257
  219.5 8.1 %collective-permute-done.27.refs_5_ = bf16[4,64,512]{2,1,0:T(8,128)(2,1)S(1)} collective-permute-done((bf16[4,64,512]{2,1,0:T(8,128)(2,1)S(1)}, bf16[4,64,512]{2,1,0:T(8,128)(2,1)S(1)}, u32[]{:S(2)}, u32[]{:S(2)}) %collective-permute-start.27) | collective-permute-done | bytes 262176 | tf_op jit(solution)/shard_map/ppermute | solution.py:257
  227.6 3.6 %shard_map.151 = (bf16[64,4096]{1,0:T(8,128)(2,1)}, bf16[64,4096]{1,0:T(8,128)(2,1)}, bf16[64,4096]{1,0:T(8,128)(2,1)}, bf16[64,4096]{1,0:T(8,128)(2,1)}, bf16[1...) custom-call(s32[3]{0:T(128)S(1)} %pad_add_fusion.1.table_ref, ...), custom_call_target="tpu_custom_call", output_to_operand_aliasing={{0}: (7, {}), {1}: (8, {}), {2}: (9, {}), {3}: (10, {}), {4... | custom-call | bytes 8388608 | tf_op jit(solution)/shard_map/pallas_call | solution.py:98
  (137 shorter events, 45.6 us)
Async XLA Ops:
  14.7 44.5 %collective-permute-start.2 = (bf16[4,192,512]{2,1,0:T(8,128)(2,1)S(1)}, bf16[4,192,512]{2,1,0:T(8,128)(2,1)S(1)}, u32[]{:S(2)}, u32[]{:S(2)}) collective-permute-start(bf16[4,192,512]{2,1,0:T(8,128)(2,1)S(1)} %get-tuple-element.91), channel_id=1, source_target_pairs={{0,2},{1,3},{2,0},{3,1},{4,6},{5,7},{6,4},{7,5},{8,10},{9,11},{10,... | collective-permute-start | bytes 2359304 | tf_op jit(solution)/shard_map/ppermute | solution.py:257
  15.2 47.9 %collective-permute-start.3 = (bf16[4,192,512]{2,1,0:T(8,128)(2,1)S(1)}, bf16[4,192,512]{2,1,0:T(8,128)(2,1)S(1)}, u32[]{:S(2)}, u32[]{:S(2)}) collective-permute-start(bf16[4,192,512]{2,1,0:T(8,128)(2,1)S(1)} %get-tuple-element.92), channel_id=1, source_target_pairs={{0,3},{1,2},{2,1},{3,0},{4,7},{5,6},{6,5},{7,4},{8,11},{9,10},{10,... | collective-permute-start | bytes 2359304 | tf_op jit(solution)/shard_map/ppermute | solution.py:257
  18.6 48.9 %collective-permute-start.1 = (bf16[4,192,512]{2,1,0:T(8,128)(2,1)S(1)}, bf16[4,192,512]{2,1,0:T(8,128)(2,1)S(1)}, u32[]{:S(2)}, u32[]{:S(2)}) collective-permute-start(bf16[4,192,512]{2,1,0:T(8,128)(2,1)S(1)} %get-tuple-element.90), channel_id=1, source_target_pairs={{0,1},{1,0},{2,3},{3,2},{4,5},{5,4},{6,7},{7,6},{8,9},{9,8},{10,11... | collective-permute-start | bytes 2359304 | tf_op jit(solution)/shard_map/ppermute | solution.py:257
  19.4 34.5 %collective-permute-start.4 = (bf16[4,64,512]{2,1,0:T(8,128)(2,1)S(1)}, bf16[4,64,512]{2,1,0:T(8,128)(2,1)S(1)}, u32[]{:S(2)}, u32[]{:S(2)}) collective-permute-start(bf16[4,64,512]{2,1,0:T(8,128)(2,1)S(1)} %copy-done.41), channel_id=1, source_target_pairs={{0,5},{1,4},{2,7},{3,6},{4,1},{5,0},{6,3},{7,2},{8,13},{9,12},{10,... | collective-permute-start | bytes 786440 | tf_op jit(solution)/shard_map/ppermute | solution.py:257
  59.3 56.2 %collective-permute-start.12 = (bf16[4,192,512]{2,1,0:T(8,128)(2,1)}, bf16[4,192,512]{2,1,0:T(8,128)(2,1)S(1)}, u32[]{:S(2)}, u32[]{:S(2)}) collective-permute-start(bf16[4,192,512]{2,1,0:T(8,128)(2,1)} %get-tuple-element.109), channel_id=1, source_target_pairs={{0,3},{1,2},{2,1},{3,0},{4,7},{5,6},{6,5},{7,4},{8,11},{9,10},{10,... | collective-permute-start | bytes 2359304 | tf_op jit(solution)/shard_map/ppermute | solution.py:257
  63.2 26.7 %collective-permute-start.5 = (bf16[4,64,512]{2,1,0:T(8,128)(2,1)S(1)}, bf16[4,64,512]{2,1,0:T(8,128)(2,1)S(1)}, u32[]{:S(2)}, u32[]{:S(2)}) collective-permute-start(bf16[4,64,512]{2,1,0:T(8,128)(2,1)S(1)} %copy-done.34), channel_id=1, source_target_pairs={{0,6},{1,7},{2,4},{3,5},{4,2},{5,3},{6,0},{7,1},{8,14},{9,15},{10,... | collective-permute-start | bytes 786440 | tf_op jit(solution)/shard_map/ppermute | solution.py:257
  67.6 50.5 %collective-permute-start.10 = (bf16[4,192,512]{2,1,0:T(8,128)(2,1)}, bf16[4,192,512]{2,1,0:T(8,128)(2,1)S(1)}, u32[]{:S(2)}, u32[]{:S(2)}) collective-permute-start(bf16[4,192,512]{2,1,0:T(8,128)(2,1)} %get-tuple-element.105), channel_id=1, source_target_pairs={{0,1},{1,0},{2,3},{3,2},{4,5},{5,4},{6,7},{7,6},{8,9},{9,8},{10,11... | collective-permute-start | bytes 2359304 | tf_op jit(solution)/shard_map/ppermute | solution.py:257
  67.6 70.3 %collective-permute-start.11 = (bf16[4,192,512]{2,1,0:T(8,128)(2,1)}, bf16[4,192,512]{2,1,0:T(8,128)(2,1)}, u32[]{:S(2)}, u32[]{:S(2)}) collective-permute-start(bf16[4,192,512]{2,1,0:T(8,128)(2,1)} %get-tuple-element.107), channel_id=1, source_target_pairs={{0,2},{1,3},{2,0},{3,1},{4,6},{5,7},{6,4},{7,5},{8,10},{9,11},{10,... | collective-permute-start | bytes 2359304 | tf_op jit(solution)/shard_map/ppermute | solution.py:257
  75.9 39.0 %collective-permute-start.7 = (bf16[4,64,512]{2,1,0:T(8,128)(2,1)}, bf16[4,64,512]{2,1,0:T(8,128)(2,1)S(1)}, u32[]{:S(2)}, u32[]{:S(2)}) collective-permute-start(bf16[4,64,512]{2,1,0:T(8,128)(2,1)} %get-tuple-element.99), channel_id=1, source_target_pairs={{0,5},{1,4},{2,7},{3,6},{4,1},{5,0},{6,3},{7,2},{8,13},{9,12},{10,... | collective-permute-start | bytes 786440 | tf_op jit(solution)/shard_map/ppermute | solution.py:257
  89.9 30.7 %collective-permute-start.14 = (bf16[4,64,512]{2,1,0:T(8,128)(2,1)}, bf16[4,64,512]{2,1,0:T(8,128)(2,1)S(1)}, u32[]{:S(2)}, u32[]{:S(2)}) collective-permute-start(bf16[4,64,512]{2,1,0:T(8,128)(2,1)} %get-tuple-element.113), channel_id=1, source_target_pairs={{0,7},{1,6},{2,5},{3,4},{4,3},{5,2},{6,1},{7,0},{8,15},{9,14},{10,... | collective-permute-start | bytes 786440 | tf_op jit(solution)/shard_map/ppermute | solution.py:257
  114.9 23.0 %collective-permute-start.8 = (bf16[4,64,512]{2,1,0:T(8,128)(2,1)}, bf16[4,64,512]{2,1,0:T(8,128)(2,1)S(1)}, u32[]{:S(2)}, u32[]{:S(2)}) collective-permute-start(bf16[4,64,512]{2,1,0:T(8,128)(2,1)} %get-tuple-element.100), channel_id=1, source_target_pairs={{0,4},{1,5},{2,6},{3,7},{4,0},{5,1},{6,2},{7,3},{8,12},{9,13},{10,... | collective-permute-start | bytes 786440 | tf_op jit(solution)/shard_map/ppermute | solution.py:257
  115.4 28.6 %collective-permute-start.13 = (bf16[4,64,512]{2,1,0:T(8,128)(2,1)S(1)}, bf16[4,64,512]{2,1,0:T(8,128)(2,1)S(1)}, u32[]{:S(2)}, u32[]{:S(2)}) collective-permute-start(bf16[4,64,512]{2,1,0:T(8,128)(2,1)S(1)} %copy-done.20), channel_id=1, source_target_pairs={{0,6},{1,7},{2,4},{3,5},{4,2},{5,3},{6,0},{7,1},{8,14},{9,15},{10,... | collective-permute-start | bytes 786440 | tf_op jit(solution)/shard_map/ppermute | solution.py:257
  119.0 39.4 %collective-permute-start.17 = (bf16[4,128,512]{2,1,0:T(8,128)(2,1)}, bf16[4,128,512]{2,1,0:T(8,128)(2,1)S(1)}, u32[]{:S(2)}, u32[]{:S(2)}) collective-permute-start(bf16[4,128,512]{2,1,0:T(8,128)(2,1)} %get-tuple-element.121), channel_id=1, source_target_pairs={{0,2},{1,3},{2,0},{3,1},{4,6},{5,7},{6,4},{7,5},{8,10},{9,11},{10,... | collective-permute-start | bytes 1572872 | tf_op jit(solution)/shard_map/ppermute | solution.py:257
  121.3 37.1 %collective-permute-start.19 = (bf16[4,64,512]{2,1,0:T(8,128)(2,1)}, bf16[4,64,512]{2,1,0:T(8,128)(2,1)S(1)}, u32[]{:S(2)}, u32[]{:S(2)}) collective-permute-start(bf16[4,64,512]{2,1,0:T(8,128)(2,1)} %get-tuple-element.125), channel_id=1, source_target_pairs={{0,5},{1,4},{2,7},{3,6},{4,1},{5,0},{6,3},{7,2},{8,13},{9,12},{10,... | collective-permute-start | bytes 786440 | tf_op jit(solution)/shard_map/ppermute | solution.py:257
  137.9 43.1 %collective-permute-start.15 = (bf16[4,128,512]{2,1,0:T(8,128)(2,1)}, bf16[4,128,512]{2,1,0:T(8,128)(2,1)S(1)}, u32[]{:S(2)}, u32[]{:S(2)}) collective-permute-start(bf16[4,128,512]{2,1,0:T(8,128)(2,1)} %get-tuple-element.116), channel_id=1, source_target_pairs={{0,1},{1,0},{2,3},{3,2},{4,5},{5,4},{6,7},{7,6},{8,9},{9,8},{10,11... | collective-permute-start | bytes 1572872 | tf_op jit(solution)/shard_map/ppermute | solution.py:257
  137.9 32.7 %collective-permute-start.18 = (bf16[4,128,512]{2,1,0:T(8,128)(2,1)}, bf16[4,128,512]{2,1,0:T(8,128)(2,1)S(1)}, u32[]{:S(2)}, u32[]{:S(2)}) collective-permute-start(bf16[4,128,512]{2,1,0:T(8,128)(2,1)} %get-tuple-element.123), channel_id=1, source_target_pairs={{0,3},{1,2},{2,1},{3,0},{4,7},{5,6},{6,5},{7,4},{8,11},{9,10},{10,... | collective-permute-start | bytes 1572872 | tf_op jit(solution)/shard_map/ppermute | solution.py:257
  158.3 34.7 %collective-permute-start.22 = (bf16[4,128,512]{2,1,0:T(8,128)(2,1)}, bf16[4,128,512]{2,1,0:T(8,128)(2,1)S(1)}, u32[]{:S(2)}, u32[]{:S(2)}) collective-permute-start(bf16[4,128,512]{2,1,0:T(8,128)(2,1)} %get-tuple-element.133), channel_id=1, source_target_pairs={{0,3},{1,2},{2,1},{3,0},{4,7},{5,6},{6,5},{7,4},{8,11},{9,10},{10,... | collective-permute-start | bytes 1572872 | tf_op jit(solution)/shard_map/ppermute | solution.py:257
  162.2 32.7 %collective-permute-start.21 = (bf16[4,64,512]{2,1,0:T(8,128)(2,1)}, bf16[4,64,512]{2,1,0:T(8,128)(2,1)}, u32[]{:S(2)}, u32[]{:S(2)}) collective-permute-start(bf16[4,64,512]{2,1,0:T(8,128)(2,1)} %get-tuple-element.129), channel_id=1, source_target_pairs={{0,7},{1,6},{2,5},{3,4},{4,3},{5,2},{6,1},{7,0},{8,15},{9,14},{10,... | collective-permute-start | bytes 786440 | tf_op jit(solution)/shard_map/ppermute | solution.py:257
  170.6 26.8 %collective-permute-start.20 = (bf16[4,64,512]{2,1,0:T(8,128)(2,1)}, bf16[4,64,512]{2,1,0:T(8,128)(2,1)}, u32[]{:S(2)}, u32[]{:S(2)}) collective-permute-start(bf16[4,64,512]{2,1,0:T(8,128)(2,1)} %get-tuple-element.127), channel_id=1, source_target_pairs={{0,6},{1,7},{2,4},{3,5},{4,2},{5,3},{6,0},{7,1},{8,14},{9,15},{10,... | collective-permute-start | bytes 786440 | tf_op jit(solution)/shard_map/ppermute | solution.py:257
  180.9 38.6 %collective-permute-start.25 = (bf16[4,128,512]{2,1,0:T(8,128)(2,1)}, bf16[4,128,512]{2,1,0:T(8,128)(2,1)}, u32[]{:S(2)}, u32[]{:S(2)}) collective-permute-start(bf16[4,128,512]{2,1,0:T(8,128)(2,1)} %get-tuple-element.139), channel_id=1, source_target_pairs={{0,1},{1,0},{2,3},{3,2},{4,5},{5,4},{6,7},{7,6},{8,9},{9,8},{10,11... | collective-permute-start | bytes 1572872 | tf_op jit(solution)/shard_map/ppermute | solution.py:257
  180.9 50.3 %collective-permute-start.16 = (bf16[4,128,512]{2,1,0:T(8,128)(2,1)}, bf16[4,128,512]{2,1,0:T(8,128)(2,1)S(1)}, u32[]{:S(2)}, u32[]{:S(2)}) collective-permute-start(bf16[4,128,512]{2,1,0:T(8,128)(2,1)} %get-tuple-element.117), channel_id=1, source_target_pairs={{0,2},{1,3},{2,0},{3,1},{4,6},{5,7},{6,4},{7,5},{8,10},{9,11},{10,... | collective-permute-start | bytes 1572872 | tf_op jit(solution)/shard_map/ppermute | solution.py:257
  197.4 22.1 %collective-permute-start.26 = (bf16[4,64,512]{2,1,0:T(8,128)(2,1)}, bf16[4,64,512]{2,1,0:T(8,128)(2,1)S(1)}, u32[]{:S(2)}, u32[]{:S(2)}) collective-permute-start(bf16[4,64,512]{2,1,0:T(8,128)(2,1)} %get-tuple-element.141), channel_id=1, source_target_pairs={{0,5},{1,4},{2,7},{3,6},{4,1},{5,0},{6,3},{7,2},{8,13},{9,12},{10,... | collective-permute-start | bytes 786440 | tf_op jit(solution)/shard_map/ppermute | solution.py:257
  202.9 24.6 %collective-permute-start.27 = (bf16[4,64,512]{2,1,0:T(8,128)(2,1)S(1)}, bf16[4,64,512]{2,1,0:T(8,128)(2,1)S(1)}, u32[]{:S(2)}, u32[]{:S(2)}) collective-permute-start(bf16[4,64,512]{2,1,0:T(8,128)(2,1)S(1)} %copy-done.30), channel_id=1, source_target_pairs={{0,7},{1,6},{2,5},{3,4},{4,3},{5,2},{6,1},{7,0},{8,15},{9,14},{10,... | collective-permute-start | bytes 786440 | tf_op jit(solution)/shard_map/ppermute | solution.py:257
  204.5 29.6 %collective-permute-start.23 = (bf16[4,64,512]{2,1,0:T(8,128)(2,1)S(1)}, bf16[4,64,512]{2,1,0:T(8,128)(2,1)S(1)}, u32[]{:S(2)}, u32[]{:S(2)}) collective-permute-start(bf16[4,64,512]{2,1,0:T(8,128)(2,1)S(1)} %copy-done.29), channel_id=1, source_target_pairs={{0,6},{1,7},{2,4},{3,5},{4,2},{5,3},{6,0},{7,1},{8,14},{9,15},{10,... | collective-permute-start | bytes 786440 | tf_op jit(solution)/shard_map/ppermute | solution.py:257
  (48 other events, 579.0 us)

commit v8 on v7

--- a/solution.py
+++ b/solution.py
@@ -274,7 +274,7 @@
         far_pieces = pack(
             table, arrays, local_heads, first, half, VMEM if first == 0 else VMEM // 2
         )
-        near = pack(table, arrays + rows_in, local_heads, first, half, VMEM // 2)
+        near = pack(table, arrays + rows_in, local_heads, first, half, VMEM)
         return spread(near, list(far_pieces) * (groups - 1), 1)
 
     def attend(first, pieces, *before):

time: 235 us -> 232 us (0.987)
  local copies, waits for them, and re-layouts: 13.2 us -> 6.14 us
  waiting for transfers between devices: 111 us -> 114 us
    unnamed x84 -> x58, local copies, waits for them, and re-layouts: 12.5 us -> 5.51 us
    ppermute x28, waiting for transfers between devices: 111 us -> 114 us  [send(): flow.append(lax.ppermute(array, 'ctx', pairs))]
  transfers between devices with their start and end apart: 30 -> 30, of which waited for: 14 -> 14; matrix products, arithmetic and copies ran while one was open for 1% -> 1% of each run, Pallas kernels for 19% -> 20%
where the time goes in v8:
time: 232 us
  waiting for transfers between devices  114 us (49%)
  Pallas kernels  49.8 us (21%)
  starting transfers between devices  49.6 us (21%)
  blocking collectives  9.92 us (4%)
  local copies, waits for them, and re-layouts  6.14 us (3%)
    ppermute x28, waiting for transfers between devices, send(): flow.append(lax.ppermute(array, 'ctx', pairs))  114 us
    ppermute x28, starting transfers between devices, send(): flow.append(lax.ppermute(array, 'ctx', pairs))  47.4 us
    pallas_call x2, Pallas kernels, attention(): pl.pallas_call(functools.partial(attention_kernel, len(pieces), key_rows,...  27.2 us
    pallas_call x4, Pallas kernels, pack(): pl.pallas_call(functools.partial(pack_kernel, len(arrays) // 4), grid_spe...  14.2 us
    psum x1, blocking collectives, per_device(): gain_mine = lax.psum(gain_mine, 'dp')  9.92 us
    pallas_call x3, Pallas kernels, unpack(): pl.pallas_call(functools.partial(unpack_kernel, len(chosen), len(pieces))...  8.4 us
    unnamed x58, local copies, waits for them, and re-layouts  5.51 us
  transfers between devices with their start and end apart: 30, of which 14 were waited for; matrix products, arithmetic and copies ran while one was open for 1% of the time, Pallas kernels for 20%

profile of v8, /device:TPU:8, one launch (start us, length us, event | category | flops | bytes accessed | tf_op | source)
XLA Modules:
  0.0 231.9 jit_solution(16408493127324244970)
XLA Ops:
  1.3 3.1 %shard_map.146 = (bf16[4,64,512]{2,1,0:T(8,128)(2,1)}, bf16[4,64,512]{2,1,0:T(8,128)(2,1)}, bf16[4,64,512]{2,1,0:T(8,128)(2,1)}, bf16[4,64,512]{2,1,0:T(8,128)(2,1)}) custom-call(s32[4]{0:T(128)} %pad_add_fusion.table_ref, bf16[64,4096]{1,0:T(8,128)(2,1)} %bitcast.20, bf16[64,4096]{1,0:T(8,128)(2,1)} %bitcast.36, bf16[64,4096]{1,0:T(8,128)(2,1)} %bitcast.52, ...), custom_call_target="tpu_custom_call" | custom-call | bytes 2097152 | tf_op jit(solution)/shard_map/pallas_call | solution.py:52
  7.0 4.8 %shard_map.145 = (bf16[4,192,512]{2,1,0:T(8,128)(2,1)}, bf16[4,192,512]{2,1,0:T(8,128)(2,1)}, bf16[4,192,512]{2,1,0:T(8,128)(2,1)}, bf16[4,192,512]{2,1,0:T(8,128)(2,1)}) custom-call(s32[4]{0:T(128)} %pad_add_fusion.table_ref, bf16[64,4096]{1,0:T(8,128)(2,1)} %bitcast.24, bf16[64,4096]{1,0:T(8,128)(2,1)} %bitcast.40, bf16[64,4096]{1,0:T(8,128)(2,1)} %bitcast.56, ...), custom_call_target="tpu_custom_call" | custom-call | bytes 6291456 | tf_op jit(solution)/shard_map/pallas_call | solution.py:52
  12.8 5.6 %collective-permute-done.refs_4_ = bf16[4,64,512]{2,1,0:T(8,128)(2,1)S(1)} collective-permute-done((bf16[4,64,512]{2,1,0:T(8,128)(2,1)}, bf16[4,64,512]{2,1,0:T(8,128)(2,1)S(1)}, u32[]{:S(2)}, u32[]{:S(2)}) %collective-permute-start) | collective-permute-done | bytes 262176 | tf_op jit(solution)/shard_map/ppermute | solution.py:257
  19.1 2.9 %collective-permute-start.4 = (bf16[4,64,512]{2,1,0:T(8,128)(2,1)}, bf16[4,64,512]{2,1,0:T(8,128)(2,1)S(1)}, u32[]{:S(2)}, u32[]{:S(2)}) collective-permute-start(bf16[4,64,512]{2,1,0:T(8,128)(2,1)} %get-tuple-element.93), channel_id=1, source_target_pairs={{0,5},{1,4},{2,7},{3,6},{4,1},{5,0},{6,3},{7,2},{8,13},{9,12},{10,... | collective-permute-start | bytes 786440 | tf_op jit(solution)/shard_map/ppermute | solution.py:257
  23.8 28.6 %collective-permute-done.4.refs_5_ = bf16[4,64,512]{2,1,0:T(8,128)(2,1)S(1)} collective-permute-done((bf16[4,64,512]{2,1,0:T(8,128)(2,1)}, bf16[4,64,512]{2,1,0:T(8,128)(2,1)S(1)}, u32[]{:S(2)}, u32[]{:S(2)}) %collective-permute-start.4) | collective-permute-done | bytes 262176 | tf_op jit(solution)/shard_map/ppermute | solution.py:257
  53.3 4.6 %shard_map.144 = (bf16[4,192,512]{2,1,0:T(8,128)(2,1)}, bf16[4,192,512]{2,1,0:T(8,128)(2,1)}, bf16[4,192,512]{2,1,0:T(8,128)(2,1)}, bf16[4,192,512]{2,1,0:T(8,128)(2,1)}) custom-call(s32[4]{0:T(128)} %pad_add_fusion.table_ref, bf16[64,4096]{1,0:T(8,128)(2,1)} %bitcast.28, bf16[64,4096]{1,0:T(8,128)(2,1)} %bitcast.44, bf16[64,4096]{1,0:T(8,128)(2,1)} %bitcast.60, ...), custom_call_target="tpu_custom_call" | custom-call | bytes 6291456 | tf_op jit(solution)/shard_map/pallas_call | solution.py:52
  57.9 3.1 %collective-permute-start.12 = (bf16[4,192,512]{2,1,0:T(8,128)(2,1)}, bf16[4,192,512]{2,1,0:T(8,128)(2,1)S(1)}, u32[]{:S(2)}, u32[]{:S(2)}) collective-permute-start(bf16[4,192,512]{2,1,0:T(8,128)(2,1)} %get-tuple-element.109), channel_id=1, source_target_pairs={{0,3},{1,2},{2,1},{3,0},{4,7},{5,6},{6,5},{7,4},{8,11},{9,10},{10,... | collective-permute-start | bytes 2359304 | tf_op jit(solution)/shard_map/ppermute | solution.py:257
  62.2 3.4 %collective-permute-done.9.refs_4_ = bf16[4,64,512]{2,1,0:T(8,128)(2,1)S(1)} collective-permute-done((bf16[4,64,512]{2,1,0:T(8,128)(2,1)S(1)}, bf16[4,64,512]{2,1,0:T(8,128)(2,1)S(1)}, u32[]{:S(2)}, u32[]{:S(2)}) %collective-permute-start.9) | collective-permute-done | bytes 262176 | tf_op jit(solution)/shard_map/ppermute | solution.py:257
  65.7 4.1 %collective-permute-start.11 = (bf16[4,192,512]{2,1,0:T(8,128)(2,1)}, bf16[4,192,512]{2,1,0:T(8,128)(2,1)}, u32[]{:S(2)}, u32[]{:S(2)}) collective-permute-start(bf16[4,192,512]{2,1,0:T(8,128)(2,1)} %get-tuple-element.107), channel_id=1, source_target_pairs={{0,2},{1,3},{2,0},{3,1},{4,6},{5,7},{6,4},{7,5},{8,10},{9,11},{10,... | collective-permute-start | bytes 2359304 | tf_op jit(solution)/shard_map/ppermute | solution.py:257
  72.9 14.3 %collective-permute-start.7 = (bf16[4,64,512]{2,1,0:T(8,128)(2,1)S(1)}, bf16[4,64,512]{2,1,0:T(8,128)(2,1)S(1)}, u32[]{:S(2)}, u32[]{:S(2)}) collective-permute-start(bf16[4,64,512]{2,1,0:T(8,128)(2,1)S(1)} %get-tuple-element.99), channel_id=1, source_target_pairs={{0,5},{1,4},{2,7},{3,6},{4,1},{5,0},{6,3},{7,2},{8,13},{9,12},{10,... | collective-permute-start | bytes 786440 | tf_op jit(solution)/shard_map/ppermute | solution.py:257
  87.9 13.6 %shard_map.147 = (f32[4,1,128]{2,1,0:T(1,128)}, bf16[4,128,512]{2,1,0:T(8,128)(2,1)}, bf16[4,128,512]{2,1,0:T(8,128)(2,1)}, bf16[4,128,512]{2,1,0:T(8,128)(2,1)}...) custom-call(s32[4]{0:T(128)} %pad_add_fusion.table_ref, ...), custom_call_target="tpu_custom_call" | custom-call | flops 4831838208 | bytes 8388608 | tf_op jit(solution)/shard_map/pallas_call | solution.py:206
  101.5 11.5 %collective-permute-done.7.refs_5_ = bf16[4,64,512]{2,1,0:T(8,128)(2,1)S(1)} collective-permute-done((bf16[4,64,512]{2,1,0:T(8,128)(2,1)S(1)}, bf16[4,64,512]{2,1,0:T(8,128)(2,1)S(1)}, u32[]{:S(2)}, u32[]{:S(2)}) %collective-permute-start.7) | collective-permute-done | bytes 262176 | tf_op jit(solution)/shard_map/ppermute | solution.py:257
  117.4 3.7 %collective-permute-start.19 = (bf16[4,64,512]{2,1,0:T(8,128)(2,1)}, bf16[4,64,512]{2,1,0:T(8,128)(2,1)S(1)}, u32[]{:S(2)}, u32[]{:S(2)}) collective-permute-start(bf16[4,64,512]{2,1,0:T(8,128)(2,1)} %get-tuple-element.125), channel_id=1, source_target_pairs={{0,5},{1,4},{2,7},{3,6},{4,1},{5,0},{6,3},{7,2},{8,13},{9,12},{10,... | collective-permute-start | bytes 786440 | tf_op jit(solution)/shard_map/ppermute | solution.py:257
  121.1 14.2 %collective-permute-done.8.refs_4_ = bf16[4,64,512]{2,1,0:T(8,128)(2,1)S(1)} collective-permute-done((bf16[4,64,512]{2,1,0:T(8,128)(2,1)}, bf16[4,64,512]{2,1,0:T(8,128)(2,1)S(1)}, u32[]{:S(2)}, u32[]{:S(2)}) %collective-permute-start.8) | collective-permute-done | bytes 262176 | tf_op jit(solution)/shard_map/ppermute | solution.py:257
  137.7 4.5 %collective-permute-done.13.refs_6_ = bf16[4,64,512]{2,1,0:T(8,128)(2,1)} collective-permute-done((bf16[4,64,512]{2,1,0:T(8,128)(2,1)S(1)}, bf16[4,64,512]{2,1,0:T(8,128)(2,1)}, u32[]{:S(2)}, u32[]{:S(2)}) %collective-permute-start.13) | collective-permute-done | bytes 262176 | tf_op jit(solution)/shard_map/ppermute | solution.py:257
  142.2 13.6 %shard_map.149 = (f32[4,1,128]{2,1,0:T(1,128)}, bf16[4,128,512]{2,1,0:T(8,128)(2,1)}, bf16[4,128,512]{2,1,0:T(8,128)(2,1)}, bf16[4,128,512]{2,1,0:T(8,128)(2,1)}...) custom-call(s32[4]{0:T(128)} %pad_add_fusion.table_ref, ...), custom_call_target="tpu_custom_call" | custom-call | flops 4831838208 | bytes 8388608 | tf_op jit(solution)/shard_map/pallas_call | solution.py:206
  159.5 8.5 %collective-permute-done.18.refs_3_ = bf16[4,128,512]{2,1,0:T(8,128)(2,1)S(1)} collective-permute-done((bf16[4,128,512]{2,1,0:T(8,128)(2,1)}, bf16[4,128,512]{2,1,0:T(8,128)(2,1)S(1)}, u32[]{:S(2)}, u32[]{:S(2)}) %collective-permute-start.18) | collective-permute-done | bytes 524320 | tf_op jit(solution)/shard_map/ppermute | solution.py:257
  168.0 9.0 %collective-permute-done.24.refs_3_ = bf16[4,64,512]{2,1,0:T(8,128)(2,1)S(1)} collective-permute-done((bf16[4,64,512]{2,1,0:T(8,128)(2,1)}, bf16[4,64,512]{2,1,0:T(8,128)(2,1)S(1)}, u32[]{:S(2)}, u32[]{:S(2)}) %collective-permute-start.24) | collective-permute-done | bytes 262176 | tf_op jit(solution)/shard_map/ppermute | solution.py:257
  178.5 9.9 %psum.7 = f32[2,512]{1,0:T(2,128)S(1)} all-reduce(f32[2,512]{1,0:T(2,128)S(1)} %reshape.21), channel_id=1, replica_groups=mesh['dp'=4,'ctx'=8] {'dp'}, use_global_device_ids=true, to_apply=%region_0.1 | all-reduce | flops 1024 | bytes 8192 | tf_op jit(solution)/shard_map/psum | solution.py:295
  196.5 3.9 %shard_map.150 = (bf16[64,4096]{1,0:T(8,128)(2,1)}, bf16[64,4096]{1,0:T(8,128)(2,1)}, bf16[64,4096]{1,0:T(8,128)(2,1)}, bf16[64,4096]{1,0:T(8,128)(2,1)}, bf16[1...) custom-call(s32[4]{0:T(128)S(1)} %copy-done.11, bf16[4,128,512]{2,1,0:T(8,128)(2,1)S(1)} %copy-done.4, ...), custom_call_target="tpu_custom_call" | custom-call | bytes 8388608 | tf_op jit(solution)/shard_map/pallas_call | solution.py:98
  201.5 3.1 %collective-permute-start.23 = (bf16[4,64,512]{2,1,0:T(8,128)(2,1)S(1)}, bf16[4,64,512]{2,1,0:T(8,128)(2,1)S(1)}, u32[]{:S(2)}, u32[]{:S(2)}) collective-permute-start(bf16[4,64,512]{2,1,0:T(8,128)(2,1)S(1)} %copy-done.18), channel_id=1, source_target_pairs={{0,6},{1,7},{2,4},{3,5},{4,2},{5,3},{6,0},{7,1},{8,14},{9,15},{10,... | collective-permute-start | bytes 786440 | tf_op jit(solution)/shard_map/ppermute | solution.py:257
  205.2 11.7 %collective-permute-done.26.refs_4_ = bf16[4,64,512]{2,1,0:T(8,128)(2,1)S(1)} collective-permute-done((bf16[4,64,512]{2,1,0:T(8,128)(2,1)}, bf16[4,64,512]{2,1,0:T(8,128)(2,1)S(1)}, u32[]{:S(2)}, u32[]{:S(2)}) %collective-permute-start.26) | collective-permute-done | bytes 262176 | tf_op jit(solution)/shard_map/ppermute | solution.py:257
  216.9 7.8 %collective-permute-done.27.refs_5_ = bf16[4,64,512]{2,1,0:T(8,128)(2,1)S(1)} collective-permute-done((bf16[4,64,512]{2,1,0:T(8,128)(2,1)S(1)}, bf16[4,64,512]{2,1,0:T(8,128)(2,1)S(1)}, u32[]{:S(2)}, u32[]{:S(2)}) %collective-permute-start.27) | collective-permute-done | bytes 262176 | tf_op jit(solution)/shard_map/ppermute | solution.py:257
  224.7 3.6 %shard_map.151 = (bf16[64,4096]{1,0:T(8,128)(2,1)}, bf16[64,4096]{1,0:T(8,128)(2,1)}, bf16[64,4096]{1,0:T(8,128)(2,1)}, bf16[64,4096]{1,0:T(8,128)(2,1)}, bf16[1...) custom-call(s32[3]{0:T(128)S(1)} %pad_add_fusion.1.table_ref, ...), custom_call_target="tpu_custom_call", output_to_operand_aliasing={{0}: (7, {}), {1}: (8, {}), {2}: (9, {}), {3}: (10, {}), {4... | custom-call | bytes 8388608 | tf_op jit(solution)/shard_map/pallas_call | solution.py:98
  (111 shorter events, 38.0 us)
Async XLA Ops:
  11.9 46.1 %collective-permute-start.2 = (bf16[4,192,512]{2,1,0:T(8,128)(2,1)}, bf16[4,192,512]{2,1,0:T(8,128)(2,1)S(1)}, u32[]{:S(2)}, u32[]{:S(2)}) collective-permute-start(bf16[4,192,512]{2,1,0:T(8,128)(2,1)} %get-tuple-element.91), channel_id=1, source_target_pairs={{0,2},{1,3},{2,0},{3,1},{4,6},{5,7},{6,4},{7,5},{8,10},{9,11},{10,... | collective-permute-start | bytes 2359304 | tf_op jit(solution)/shard_map/ppermute | solution.py:257
  12.4 48.7 %collective-permute-start.3 = (bf16[4,192,512]{2,1,0:T(8,128)(2,1)}, bf16[4,192,512]{2,1,0:T(8,128)(2,1)}, u32[]{:S(2)}, u32[]{:S(2)}) collective-permute-start(bf16[4,192,512]{2,1,0:T(8,128)(2,1)} %get-tuple-element.92), channel_id=1, source_target_pairs={{0,3},{1,2},{2,1},{3,0},{4,7},{5,6},{6,5},{7,4},{8,11},{9,10},{10,... | collective-permute-start | bytes 2359304 | tf_op jit(solution)/shard_map/ppermute | solution.py:257
  18.5 47.2 %collective-permute-start.1 = (bf16[4,192,512]{2,1,0:T(8,128)(2,1)}, bf16[4,192,512]{2,1,0:T(8,128)(2,1)}, u32[]{:S(2)}, u32[]{:S(2)}) collective-permute-start(bf16[4,192,512]{2,1,0:T(8,128)(2,1)} %get-tuple-element.90), channel_id=1, source_target_pairs={{0,1},{1,0},{2,3},{3,2},{4,5},{5,4},{6,7},{7,6},{8,9},{9,8},{10,11... | collective-permute-start | bytes 2359304 | tf_op jit(solution)/shard_map/ppermute | solution.py:257
  19.1 33.2 %collective-permute-start.4 = (bf16[4,64,512]{2,1,0:T(8,128)(2,1)}, bf16[4,64,512]{2,1,0:T(8,128)(2,1)S(1)}, u32[]{:S(2)}, u32[]{:S(2)}) collective-permute-start(bf16[4,64,512]{2,1,0:T(8,128)(2,1)} %get-tuple-element.93), channel_id=1, source_target_pairs={{0,5},{1,4},{2,7},{3,6},{4,1},{5,0},{6,3},{7,2},{8,13},{9,12},{10,... | collective-permute-start | bytes 786440 | tf_op jit(solution)/shard_map/ppermute | solution.py:257
  57.9 55.4 %collective-permute-start.12 = (bf16[4,192,512]{2,1,0:T(8,128)(2,1)}, bf16[4,192,512]{2,1,0:T(8,128)(2,1)S(1)}, u32[]{:S(2)}, u32[]{:S(2)}) collective-permute-start(bf16[4,192,512]{2,1,0:T(8,128)(2,1)} %get-tuple-element.109), channel_id=1, source_target_pairs={{0,3},{1,2},{2,1},{3,0},{4,7},{5,6},{6,5},{7,4},{8,11},{9,10},{10,... | collective-permute-start | bytes 2359304 | tf_op jit(solution)/shard_map/ppermute | solution.py:257
  61.1 26.1 %collective-permute-start.5 = (bf16[4,64,512]{2,1,0:T(8,128)(2,1)S(1)}, bf16[4,64,512]{2,1,0:T(8,128)(2,1)S(1)}, u32[]{:S(2)}, u32[]{:S(2)}) collective-permute-start(bf16[4,64,512]{2,1,0:T(8,128)(2,1)S(1)} %copy-done.23), channel_id=1, source_target_pairs={{0,6},{1,7},{2,4},{3,5},{4,2},{5,3},{6,0},{7,1},{8,14},{9,15},{10,... | collective-permute-start | bytes 786440 | tf_op jit(solution)/shard_map/ppermute | solution.py:257
  65.7 49.8 %collective-permute-start.10 = (bf16[4,192,512]{2,1,0:T(8,128)(2,1)}, bf16[4,192,512]{2,1,0:T(8,128)(2,1)S(1)}, u32[]{:S(2)}, u32[]{:S(2)}) collective-permute-start(bf16[4,192,512]{2,1,0:T(8,128)(2,1)} %get-tuple-element.105), channel_id=1, source_target_pairs={{0,1},{1,0},{2,3},{3,2},{4,5},{5,4},{6,7},{7,6},{8,9},{9,8},{10,11... | collective-permute-start | bytes 2359304 | tf_op jit(solution)/shard_map/ppermute | solution.py:257
  65.7 69.7 %collective-permute-start.11 = (bf16[4,192,512]{2,1,0:T(8,128)(2,1)}, bf16[4,192,512]{2,1,0:T(8,128)(2,1)}, u32[]{:S(2)}, u32[]{:S(2)}) collective-permute-start(bf16[4,192,512]{2,1,0:T(8,128)(2,1)} %get-tuple-element.107), channel_id=1, source_target_pairs={{0,2},{1,3},{2,0},{3,1},{4,6},{5,7},{6,4},{7,5},{8,10},{9,11},{10,... | collective-permute-start | bytes 2359304 | tf_op jit(solution)/shard_map/ppermute | solution.py:257
  72.9 40.1 %collective-permute-start.7 = (bf16[4,64,512]{2,1,0:T(8,128)(2,1)S(1)}, bf16[4,64,512]{2,1,0:T(8,128)(2,1)S(1)}, u32[]{:S(2)}, u32[]{:S(2)}) collective-permute-start(bf16[4,64,512]{2,1,0:T(8,128)(2,1)S(1)} %get-tuple-element.99), channel_id=1, source_target_pairs={{0,5},{1,4},{2,7},{3,6},{4,1},{5,0},{6,3},{7,2},{8,13},{9,12},{10,... | collective-permute-start | bytes 786440 | tf_op jit(solution)/shard_map/ppermute | solution.py:257
  87.2 30.2 %collective-permute-start.14 = (bf16[4,64,512]{2,1,0:T(8,128)(2,1)S(1)}, bf16[4,64,512]{2,1,0:T(8,128)(2,1)S(1)}, u32[]{:S(2)}, u32[]{:S(2)}) collective-permute-start(bf16[4,64,512]{2,1,0:T(8,128)(2,1)S(1)} %get-tuple-element.113), channel_id=1, source_target_pairs={{0,7},{1,6},{2,5},{3,4},{4,3},{5,2},{6,1},{7,0},{8,15},{9,14},{10,... | collective-permute-start | bytes 786440 | tf_op jit(solution)/shard_map/ppermute | solution.py:257
  113.0 22.3 %collective-permute-start.8 = (bf16[4,64,512]{2,1,0:T(8,128)(2,1)}, bf16[4,64,512]{2,1,0:T(8,128)(2,1)S(1)}, u32[]{:S(2)}, u32[]{:S(2)}) collective-permute-start(bf16[4,64,512]{2,1,0:T(8,128)(2,1)} %get-tuple-element.100), channel_id=1, source_target_pairs={{0,4},{1,5},{2,6},{3,7},{4,0},{5,1},{6,2},{7,3},{8,12},{9,13},{10,... | collective-permute-start | bytes 786440 | tf_op jit(solution)/shard_map/ppermute | solution.py:257
  113.4 28.8 %collective-permute-start.13 = (bf16[4,64,512]{2,1,0:T(8,128)(2,1)S(1)}, bf16[4,64,512]{2,1,0:T(8,128)(2,1)}, u32[]{:S(2)}, u32[]{:S(2)}) collective-permute-start(bf16[4,64,512]{2,1,0:T(8,128)(2,1)S(1)} %get-tuple-element.111), channel_id=1, source_target_pairs={{0,6},{1,7},{2,4},{3,5},{4,2},{5,3},{6,0},{7,1},{8,14},{9,15},{10,... | collective-permute-start | bytes 786440 | tf_op jit(solution)/shard_map/ppermute | solution.py:257
  115.5 40.3 %collective-permute-start.17 = (bf16[4,128,512]{2,1,0:T(8,128)(2,1)}, bf16[4,128,512]{2,1,0:T(8,128)(2,1)S(1)}, u32[]{:S(2)}, u32[]{:S(2)}) collective-permute-start(bf16[4,128,512]{2,1,0:T(8,128)(2,1)} %get-tuple-element.121), channel_id=1, source_target_pairs={{0,2},{1,3},{2,0},{3,1},{4,6},{5,7},{6,4},{7,5},{8,10},{9,11},{10,... | collective-permute-start | bytes 1572872 | tf_op jit(solution)/shard_map/ppermute | solution.py:257
  117.4 38.5 %collective-permute-start.19 = (bf16[4,64,512]{2,1,0:T(8,128)(2,1)}, bf16[4,64,512]{2,1,0:T(8,128)(2,1)S(1)}, u32[]{:S(2)}, u32[]{:S(2)}) collective-permute-start(bf16[4,64,512]{2,1,0:T(8,128)(2,1)} %get-tuple-element.125), channel_id=1, source_target_pairs={{0,5},{1,4},{2,7},{3,6},{4,1},{5,0},{6,3},{7,2},{8,13},{9,12},{10,... | collective-permute-start | bytes 786440 | tf_op jit(solution)/shard_map/ppermute | solution.py:257
  135.3 42.5 %collective-permute-start.15 = (bf16[4,128,512]{2,1,0:T(8,128)(2,1)}, bf16[4,128,512]{2,1,0:T(8,128)(2,1)S(1)}, u32[]{:S(2)}, u32[]{:S(2)}) collective-permute-start(bf16[4,128,512]{2,1,0:T(8,128)(2,1)} %get-tuple-element.116), channel_id=1, source_target_pairs={{0,1},{1,0},{2,3},{3,2},{4,5},{5,4},{6,7},{7,6},{8,9},{9,8},{10,11... | collective-permute-start | bytes 1572872 | tf_op jit(solution)/shard_map/ppermute | solution.py:257
  135.3 32.7 %collective-permute-start.18 = (bf16[4,128,512]{2,1,0:T(8,128)(2,1)}, bf16[4,128,512]{2,1,0:T(8,128)(2,1)S(1)}, u32[]{:S(2)}, u32[]{:S(2)}) collective-permute-start(bf16[4,128,512]{2,1,0:T(8,128)(2,1)} %get-tuple-element.123), channel_id=1, source_target_pairs={{0,3},{1,2},{2,1},{3,0},{4,7},{5,6},{6,5},{7,4},{8,11},{9,10},{10,... | collective-permute-start | bytes 1572872 | tf_op jit(solution)/shard_map/ppermute | solution.py:257
  155.8 34.7 %collective-permute-start.22 = (bf16[4,128,512]{2,1,0:T(8,128)(2,1)}, bf16[4,128,512]{2,1,0:T(8,128)(2,1)S(1)}, u32[]{:S(2)}, u32[]{:S(2)}) collective-permute-start(bf16[4,128,512]{2,1,0:T(8,128)(2,1)} %get-tuple-element.133), channel_id=1, source_target_pairs={{0,3},{1,2},{2,1},{3,0},{4,7},{5,6},{6,5},{7,4},{8,11},{9,10},{10,... | collective-permute-start | bytes 1572872 | tf_op jit(solution)/shard_map/ppermute | solution.py:257
  159.1 33.3 %collective-permute-start.21 = (bf16[4,64,512]{2,1,0:T(8,128)(2,1)}, bf16[4,64,512]{2,1,0:T(8,128)(2,1)}, u32[]{:S(2)}, u32[]{:S(2)}) collective-permute-start(bf16[4,64,512]{2,1,0:T(8,128)(2,1)} %get-tuple-element.129), channel_id=1, source_target_pairs={{0,7},{1,6},{2,5},{3,4},{4,3},{5,2},{6,1},{7,0},{8,15},{9,14},{10,... | collective-permute-start | bytes 786440 | tf_op jit(solution)/shard_map/ppermute | solution.py:257
  168.0 26.8 %collective-permute-start.20 = (bf16[4,64,512]{2,1,0:T(8,128)(2,1)}, bf16[4,64,512]{2,1,0:T(8,128)(2,1)}, u32[]{:S(2)}, u32[]{:S(2)}) collective-permute-start(bf16[4,64,512]{2,1,0:T(8,128)(2,1)} %get-tuple-element.127), channel_id=1, source_target_pairs={{0,6},{1,7},{2,4},{3,5},{4,2},{5,3},{6,0},{7,1},{8,14},{9,15},{10,... | collective-permute-start | bytes 786440 | tf_op jit(solution)/shard_map/ppermute | solution.py:257
  177.8 39.2 %collective-permute-start.25 = (bf16[4,128,512]{2,1,0:T(8,128)(2,1)}, bf16[4,128,512]{2,1,0:T(8,128)(2,1)}, u32[]{:S(2)}, u32[]{:S(2)}) collective-permute-start(bf16[4,128,512]{2,1,0:T(8,128)(2,1)} %get-tuple-element.139), channel_id=1, source_target_pairs={{0,1},{1,0},{2,3},{3,2},{4,5},{5,4},{6,7},{7,6},{8,9},{9,8},{10,11... | collective-permute-start | bytes 1572872 | tf_op jit(solution)/shard_map/ppermute | solution.py:257
  177.8 50.5 %collective-permute-start.16 = (bf16[4,128,512]{2,1,0:T(8,128)(2,1)}, bf16[4,128,512]{2,1,0:T(8,128)(2,1)S(1)}, u32[]{:S(2)}, u32[]{:S(2)}) collective-permute-start(bf16[4,128,512]{2,1,0:T(8,128)(2,1)} %get-tuple-element.117), channel_id=1, source_target_pairs={{0,2},{1,3},{2,0},{3,1},{4,6},{5,7},{6,4},{7,5},{8,10},{9,11},{10,... | collective-permute-start | bytes 1572872 | tf_op jit(solution)/shard_map/ppermute | solution.py:257
  194.8 22.1 %collective-permute-start.26 = (bf16[4,64,512]{2,1,0:T(8,128)(2,1)}, bf16[4,64,512]{2,1,0:T(8,128)(2,1)S(1)}, u32[]{:S(2)}, u32[]{:S(2)}) collective-permute-start(bf16[4,64,512]{2,1,0:T(8,128)(2,1)} %get-tuple-element.141), channel_id=1, source_target_pairs={{0,5},{1,4},{2,7},{3,6},{4,1},{5,0},{6,3},{7,2},{8,13},{9,12},{10,... | collective-permute-start | bytes 786440 | tf_op jit(solution)/shard_map/ppermute | solution.py:257
  200.4 24.3 %collective-permute-start.27 = (bf16[4,64,512]{2,1,0:T(8,128)(2,1)S(1)}, bf16[4,64,512]{2,1,0:T(8,128)(2,1)S(1)}, u32[]{:S(2)}, u32[]{:S(2)}) collective-permute-start(bf16[4,64,512]{2,1,0:T(8,128)(2,1)S(1)} %copy-done.19), channel_id=1, source_target_pairs={{0,7},{1,6},{2,5},{3,4},{4,3},{5,2},{6,1},{7,0},{8,15},{9,14},{10,... | collective-permute-start | bytes 786440 | tf_op jit(solution)/shard_map/ppermute | solution.py:257
  201.5 29.5 %collective-permute-start.23 = (bf16[4,64,512]{2,1,0:T(8,128)(2,1)S(1)}, bf16[4,64,512]{2,1,0:T(8,128)(2,1)S(1)}, u32[]{:S(2)}, u32[]{:S(2)}) collective-permute-start(bf16[4,64,512]{2,1,0:T(8,128)(2,1)S(1)} %copy-done.18), channel_id=1, source_target_pairs={{0,6},{1,7},{2,4},{3,5},{4,2},{5,3},{6,0},{7,1},{8,14},{9,15},{10,... | collective-permute-start | bytes 786440 | tf_op jit(solution)/shard_map/ppermute | solution.py:257
  (35 other events, 448.1 us)

commit v9 on v8

--- a/solution.py
+++ b/solution.py
@@ -40,7 +40,7 @@
 
 def pack(table, arrays, local_heads, first, count, vmem):
     rows = sum(a.shape[0] for a in arrays) // 4
-    block = math.gcd(count, first, 2)
+    block = math.gcd(count, first, 4)
     steps = count // block
 
     def columns(array, j):

time: 232 us -> 233 us (level)
  no operation moved by 1% of the time
where the time goes in v9:
time: 233 us; the launch traced here: 232 us
  waiting for transfers between devices  114 us (49%)
  starting transfers between devices  51.1 us (22%)
  Pallas kernels  49.3 us (21%)
  blocking collectives  9.92 us (4%)
  local copies, waits for them, and re-layouts  5.89 us (3%)
    ppermute x28, waiting for transfers between devices, send(): flow.append(lax.ppermute(array, 'ctx', pairs))  114 us
    ppermute x28, starting transfers between devices, send(): flow.append(lax.ppermute(array, 'ctx', pairs))  47.9 us
    pallas_call x2, Pallas kernels, attention(): pl.pallas_call(functools.partial(attention_kernel, len(pieces), key_rows,...  27.1 us
    pallas_call x4, Pallas kernels, pack(): pl.pallas_call(functools.partial(pack_kernel, len(arrays) // 4), grid_spe...  13.8 us
    psum x1, blocking collectives, per_device(): gain_mine = lax.psum(gain_mine, 'dp')  9.92 us
    pallas_call x3, Pallas kernels, unpack(): pl.pallas_call(functools.partial(unpack_kernel, len(chosen), len(pieces))...  8.4 us
    unnamed x58, local copies, waits for them, and re-layouts  5.26 us
  transfers between devices with their start and end apart: 30, of which 14 were waited for; matrix products, arithmetic and copies ran while one was open for 1% of the time, Pallas kernels for 20%

profile of v9, /device:TPU:8, one launch (start us, length us, event | category | flops | bytes accessed | tf_op | source)
XLA Modules:
  0.0 232.2 jit_solution(3789591062874341708)
XLA Ops:
  1.3 3.1 %shard_map.146 = (bf16[4,64,512]{2,1,0:T(8,128)(2,1)}, bf16[4,64,512]{2,1,0:T(8,128)(2,1)}, bf16[4,64,512]{2,1,0:T(8,128)(2,1)}, bf16[4,64,512]{2,1,0:T(8,128)(2,1)}) custom-call(s32[4]{0:T(128)} %pad_add_fusion.table_ref, bf16[64,4096]{1,0:T(8,128)(2,1)} %bitcast.20, bf16[64,4096]{1,0:T(8,128)(2,1)} %bitcast.36, bf16[64,4096]{1,0:T(8,128)(2,1)} %bitcast.52, ...), custom_call_target="tpu_custom_call" | custom-call | bytes 2097152 | tf_op jit(solution)/shard_map/pallas_call | solution.py:52
  7.0 5.1 %shard_map.145 = (bf16[4,192,512]{2,1,0:T(8,128)(2,1)}, bf16[4,192,512]{2,1,0:T(8,128)(2,1)}, bf16[4,192,512]{2,1,0:T(8,128)(2,1)}, bf16[4,192,512]{2,1,0:T(8,128)(2,1)}) custom-call(s32[4]{0:T(128)} %pad_add_fusion.table_ref, bf16[64,4096]{1,0:T(8,128)(2,1)} %bitcast.24, bf16[64,4096]{1,0:T(8,128)(2,1)} %bitcast.40, bf16[64,4096]{1,0:T(8,128)(2,1)} %bitcast.56, ...), custom_call_target="tpu_custom_call" | custom-call | bytes 6291456 | tf_op jit(solution)/shard_map/pallas_call | solution.py:52
  13.0 5.4 %collective-permute-done.refs_4_ = bf16[4,64,512]{2,1,0:T(8,128)(2,1)S(1)} collective-permute-done((bf16[4,64,512]{2,1,0:T(8,128)(2,1)}, bf16[4,64,512]{2,1,0:T(8,128)(2,1)S(1)}, u32[]{:S(2)}, u32[]{:S(2)}) %collective-permute-start) | collective-permute-done | bytes 262176 | tf_op jit(solution)/shard_map/ppermute | solution.py:257
  19.1 2.9 %collective-permute-start.4 = (bf16[4,64,512]{2,1,0:T(8,128)(2,1)}, bf16[4,64,512]{2,1,0:T(8,128)(2,1)S(1)}, u32[]{:S(2)}, u32[]{:S(2)}) collective-permute-start(bf16[4,64,512]{2,1,0:T(8,128)(2,1)} %get-tuple-element.93), channel_id=1, source_target_pairs={{0,5},{1,4},{2,7},{3,6},{4,1},{5,0},{6,3},{7,2},{8,13},{9,12},{10,... | collective-permute-start | bytes 786440 | tf_op jit(solution)/shard_map/ppermute | solution.py:257
  22.8 29.2 %collective-permute-done.4.refs_5_ = bf16[4,64,512]{2,1,0:T(8,128)(2,1)S(1)} collective-permute-done((bf16[4,64,512]{2,1,0:T(8,128)(2,1)}, bf16[4,64,512]{2,1,0:T(8,128)(2,1)S(1)}, u32[]{:S(2)}, u32[]{:S(2)}) %collective-permute-start.4) | collective-permute-done | bytes 262176 | tf_op jit(solution)/shard_map/ppermute | solution.py:257
  53.3 4.8 %shard_map.144 = (bf16[4,192,512]{2,1,0:T(8,128)(2,1)}, bf16[4,192,512]{2,1,0:T(8,128)(2,1)}, bf16[4,192,512]{2,1,0:T(8,128)(2,1)}, bf16[4,192,512]{2,1,0:T(8,128)(2,1)}) custom-call(s32[4]{0:T(128)} %pad_add_fusion.table_ref, bf16[64,4096]{1,0:T(8,128)(2,1)} %bitcast.28, bf16[64,4096]{1,0:T(8,128)(2,1)} %bitcast.44, bf16[64,4096]{1,0:T(8,128)(2,1)} %bitcast.60, ...), custom_call_target="tpu_custom_call" | custom-call | bytes 6291456 | tf_op jit(solution)/shard_map/pallas_call | solution.py:52
  58.1 3.4 %collective-permute-start.12 = (bf16[4,192,512]{2,1,0:T(8,128)(2,1)}, bf16[4,192,512]{2,1,0:T(8,128)(2,1)S(1)}, u32[]{:S(2)}, u32[]{:S(2)}) collective-permute-start(bf16[4,192,512]{2,1,0:T(8,128)(2,1)} %get-tuple-element.109), channel_id=1, source_target_pairs={{0,3},{1,2},{2,1},{3,0},{4,7},{5,6},{6,5},{7,4},{8,11},{9,10},{10,... | collective-permute-start | bytes 2359304 | tf_op jit(solution)/shard_map/ppermute | solution.py:257
  62.7 2.9 %collective-permute-done.9.refs_4_ = bf16[4,64,512]{2,1,0:T(8,128)(2,1)S(1)} collective-permute-done((bf16[4,64,512]{2,1,0:T(8,128)(2,1)S(1)}, bf16[4,64,512]{2,1,0:T(8,128)(2,1)S(1)}, u32[]{:S(2)}, u32[]{:S(2)}) %collective-permute-start.9) | collective-permute-done | bytes 262176 | tf_op jit(solution)/shard_map/ppermute | solution.py:257
  65.6 4.2 %collective-permute-start.11 = (bf16[4,192,512]{2,1,0:T(8,128)(2,1)}, bf16[4,192,512]{2,1,0:T(8,128)(2,1)}, u32[]{:S(2)}, u32[]{:S(2)}) collective-permute-start(bf16[4,192,512]{2,1,0:T(8,128)(2,1)} %get-tuple-element.107), channel_id=1, source_target_pairs={{0,2},{1,3},{2,0},{3,1},{4,6},{5,7},{6,4},{7,5},{8,10},{9,11},{10,... | collective-permute-start | bytes 2359304 | tf_op jit(solution)/shard_map/ppermute | solution.py:257
  73.3 14.2 %collective-permute-start.7 = (bf16[4,64,512]{2,1,0:T(8,128)(2,1)S(1)}, bf16[4,64,512]{2,1,0:T(8,128)(2,1)S(1)}, u32[]{:S(2)}, u32[]{:S(2)}) collective-permute-start(bf16[4,64,512]{2,1,0:T(8,128)(2,1)S(1)} %get-tuple-element.99), channel_id=1, source_target_pairs={{0,5},{1,4},{2,7},{3,6},{4,1},{5,0},{6,3},{7,2},{8,13},{9,12},{10,... | collective-permute-start | bytes 786440 | tf_op jit(solution)/shard_map/ppermute | solution.py:257
  88.1 13.6 %shard_map.147 = (f32[4,1,128]{2,1,0:T(1,128)}, bf16[4,128,512]{2,1,0:T(8,128)(2,1)}, bf16[4,128,512]{2,1,0:T(8,128)(2,1)}, bf16[4,128,512]{2,1,0:T(8,128)(2,1)}...) custom-call(s32[4]{0:T(128)} %pad_add_fusion.table_ref, ...), custom_call_target="tpu_custom_call" | custom-call | flops 4831838208 | bytes 8388608 | tf_op jit(solution)/shard_map/pallas_call | solution.py:206
  101.7 11.7 %collective-permute-done.7.refs_5_ = bf16[4,64,512]{2,1,0:T(8,128)(2,1)S(1)} collective-permute-done((bf16[4,64,512]{2,1,0:T(8,128)(2,1)S(1)}, bf16[4,64,512]{2,1,0:T(8,128)(2,1)S(1)}, u32[]{:S(2)}, u32[]{:S(2)}) %collective-permute-start.7) | collective-permute-done | bytes 262176 | tf_op jit(solution)/shard_map/ppermute | solution.py:257
  117.8 3.4 %collective-permute-start.19 = (bf16[4,64,512]{2,1,0:T(8,128)(2,1)}, bf16[4,64,512]{2,1,0:T(8,128)(2,1)S(1)}, u32[]{:S(2)}, u32[]{:S(2)}) collective-permute-start(bf16[4,64,512]{2,1,0:T(8,128)(2,1)} %get-tuple-element.125), channel_id=1, source_target_pairs={{0,5},{1,4},{2,7},{3,6},{4,1},{5,0},{6,3},{7,2},{8,13},{9,12},{10,... | collective-permute-start | bytes 786440 | tf_op jit(solution)/shard_map/ppermute | solution.py:257
  121.3 14.2 %collective-permute-done.8.refs_4_ = bf16[4,64,512]{2,1,0:T(8,128)(2,1)S(1)} collective-permute-done((bf16[4,64,512]{2,1,0:T(8,128)(2,1)}, bf16[4,64,512]{2,1,0:T(8,128)(2,1)S(1)}, u32[]{:S(2)}, u32[]{:S(2)}) %collective-permute-start.8) | collective-permute-done | bytes 262176 | tf_op jit(solution)/shard_map/ppermute | solution.py:257
  138.2 4.5 %collective-permute-done.13.refs_6_ = bf16[4,64,512]{2,1,0:T(8,128)(2,1)} collective-permute-done((bf16[4,64,512]{2,1,0:T(8,128)(2,1)S(1)}, bf16[4,64,512]{2,1,0:T(8,128)(2,1)}, u32[]{:S(2)}, u32[]{:S(2)}) %collective-permute-start.13) | collective-permute-done | bytes 262176 | tf_op jit(solution)/shard_map/ppermute | solution.py:257
  142.6 13.6 %shard_map.149 = (f32[4,1,128]{2,1,0:T(1,128)}, bf16[4,128,512]{2,1,0:T(8,128)(2,1)}, bf16[4,128,512]{2,1,0:T(8,128)(2,1)}, bf16[4,128,512]{2,1,0:T(8,128)(2,1)}...) custom-call(s32[4]{0:T(128)} %pad_add_fusion.table_ref, ...), custom_call_target="tpu_custom_call" | custom-call | flops 4831838208 | bytes 8388608 | tf_op jit(solution)/shard_map/pallas_call | solution.py:206
  159.9 8.3 %collective-permute-done.18.refs_3_ = bf16[4,128,512]{2,1,0:T(8,128)(2,1)S(1)} collective-permute-done((bf16[4,128,512]{2,1,0:T(8,128)(2,1)}, bf16[4,128,512]{2,1,0:T(8,128)(2,1)S(1)}, u32[]{:S(2)}, u32[]{:S(2)}) %collective-permute-start.18) | collective-permute-done | bytes 524320 | tf_op jit(solution)/shard_map/ppermute | solution.py:257
  168.2 9.1 %collective-permute-done.24.refs_3_ = bf16[4,64,512]{2,1,0:T(8,128)(2,1)S(1)} collective-permute-done((bf16[4,64,512]{2,1,0:T(8,128)(2,1)}, bf16[4,64,512]{2,1,0:T(8,128)(2,1)S(1)}, u32[]{:S(2)}, u32[]{:S(2)}) %collective-permute-start.24) | collective-permute-done | bytes 262176 | tf_op jit(solution)/shard_map/ppermute | solution.py:257
  178.8 9.9 %psum.7 = f32[2,512]{1,0:T(2,128)S(1)} all-reduce(f32[2,512]{1,0:T(2,128)S(1)} %reshape.21), channel_id=1, replica_groups=mesh['dp'=4,'ctx'=8] {'dp'}, use_global_device_ids=true, to_apply=%region_0.1 | all-reduce | flops 1024 | bytes 8192 | tf_op jit(solution)/shard_map/psum | solution.py:295
  196.9 3.9 %shard_map.150 = (bf16[64,4096]{1,0:T(8,128)(2,1)}, bf16[64,4096]{1,0:T(8,128)(2,1)}, bf16[64,4096]{1,0:T(8,128)(2,1)}, bf16[64,4096]{1,0:T(8,128)(2,1)}, bf16[1...) custom-call(s32[4]{0:T(128)S(1)} %copy-done.11, bf16[4,128,512]{2,1,0:T(8,128)(2,1)S(1)} %copy-done.4, ...), custom_call_target="tpu_custom_call" | custom-call | bytes 8388608 | tf_op jit(solution)/shard_map/pallas_call | solution.py:98
  201.8 3.1 %collective-permute-start.23 = (bf16[4,64,512]{2,1,0:T(8,128)(2,1)S(1)}, bf16[4,64,512]{2,1,0:T(8,128)(2,1)S(1)}, u32[]{:S(2)}, u32[]{:S(2)}) collective-permute-start(bf16[4,64,512]{2,1,0:T(8,128)(2,1)S(1)} %copy-done.18), channel_id=1, source_target_pairs={{0,6},{1,7},{2,4},{3,5},{4,2},{5,3},{6,0},{7,1},{8,14},{9,15},{10,... | collective-permute-start | bytes 786440 | tf_op jit(solution)/shard_map/ppermute | solution.py:257
  205.5 12.0 %collective-permute-done.26.refs_4_ = bf16[4,64,512]{2,1,0:T(8,128)(2,1)S(1)} collective-permute-done((bf16[4,64,512]{2,1,0:T(8,128)(2,1)}, bf16[4,64,512]{2,1,0:T(8,128)(2,1)S(1)}, u32[]{:S(2)}, u32[]{:S(2)}) %collective-permute-start.26) | collective-permute-done | bytes 262176 | tf_op jit(solution)/shard_map/ppermute | solution.py:257
  217.5 7.5 %collective-permute-done.27.refs_5_ = bf16[4,64,512]{2,1,0:T(8,128)(2,1)S(1)} collective-permute-done((bf16[4,64,512]{2,1,0:T(8,128)(2,1)S(1)}, bf16[4,64,512]{2,1,0:T(8,128)(2,1)S(1)}, u32[]{:S(2)}, u32[]{:S(2)}) %collective-permute-start.27) | collective-permute-done | bytes 262176 | tf_op jit(solution)/shard_map/ppermute | solution.py:257
  225.0 3.6 %shard_map.151 = (bf16[64,4096]{1,0:T(8,128)(2,1)}, bf16[64,4096]{1,0:T(8,128)(2,1)}, bf16[64,4096]{1,0:T(8,128)(2,1)}, bf16[64,4096]{1,0:T(8,128)(2,1)}, bf16[1...) custom-call(s32[3]{0:T(128)S(1)} %pad_add_fusion.1.table_ref, ...), custom_call_target="tpu_custom_call", output_to_operand_aliasing={{0}: (7, {}), {1}: (8, {}), {2}: (9, {}), {3}: (10, {}), {4... | custom-call | bytes 8388608 | tf_op jit(solution)/shard_map/pallas_call | solution.py:98
  (111 shorter events, 37.8 us)
Async XLA Ops:
  12.1 46.1 %collective-permute-start.2 = (bf16[4,192,512]{2,1,0:T(8,128)(2,1)}, bf16[4,192,512]{2,1,0:T(8,128)(2,1)S(1)}, u32[]{:S(2)}, u32[]{:S(2)}) collective-permute-start(bf16[4,192,512]{2,1,0:T(8,128)(2,1)} %get-tuple-element.91), channel_id=1, source_target_pairs={{0,2},{1,3},{2,0},{3,1},{4,6},{5,7},{6,4},{7,5},{8,10},{9,11},{10,... | collective-permute-start | bytes 2359304 | tf_op jit(solution)/shard_map/ppermute | solution.py:257
  12.6 49.0 %collective-permute-start.3 = (bf16[4,192,512]{2,1,0:T(8,128)(2,1)}, bf16[4,192,512]{2,1,0:T(8,128)(2,1)}, u32[]{:S(2)}, u32[]{:S(2)}) collective-permute-start(bf16[4,192,512]{2,1,0:T(8,128)(2,1)} %get-tuple-element.92), channel_id=1, source_target_pairs={{0,3},{1,2},{2,1},{3,0},{4,7},{5,6},{6,5},{7,4},{8,11},{9,10},{10,... | collective-permute-start | bytes 2359304 | tf_op jit(solution)/shard_map/ppermute | solution.py:257
  18.4 47.2 %collective-permute-start.1 = (bf16[4,192,512]{2,1,0:T(8,128)(2,1)}, bf16[4,192,512]{2,1,0:T(8,128)(2,1)}, u32[]{:S(2)}, u32[]{:S(2)}) collective-permute-start(bf16[4,192,512]{2,1,0:T(8,128)(2,1)} %get-tuple-element.90), channel_id=1, source_target_pairs={{0,1},{1,0},{2,3},{3,2},{4,5},{5,4},{6,7},{7,6},{8,9},{9,8},{10,11... | collective-permute-start | bytes 2359304 | tf_op jit(solution)/shard_map/ppermute | solution.py:257
  19.1 33.0 %collective-permute-start.4 = (bf16[4,64,512]{2,1,0:T(8,128)(2,1)}, bf16[4,64,512]{2,1,0:T(8,128)(2,1)S(1)}, u32[]{:S(2)}, u32[]{:S(2)}) collective-permute-start(bf16[4,64,512]{2,1,0:T(8,128)(2,1)} %get-tuple-element.93), channel_id=1, source_target_pairs={{0,5},{1,4},{2,7},{3,6},{4,1},{5,0},{6,3},{7,2},{8,13},{9,12},{10,... | collective-permute-start | bytes 786440 | tf_op jit(solution)/shard_map/ppermute | solution.py:257
  58.1 55.7 %collective-permute-start.12 = (bf16[4,192,512]{2,1,0:T(8,128)(2,1)}, bf16[4,192,512]{2,1,0:T(8,128)(2,1)S(1)}, u32[]{:S(2)}, u32[]{:S(2)}) collective-permute-start(bf16[4,192,512]{2,1,0:T(8,128)(2,1)} %get-tuple-element.109), channel_id=1, source_target_pairs={{0,3},{1,2},{2,1},{3,0},{4,7},{5,6},{6,5},{7,4},{8,11},{9,10},{10,... | collective-permute-start | bytes 2359304 | tf_op jit(solution)/shard_map/ppermute | solution.py:257
  61.6 25.9 %collective-permute-start.5 = (bf16[4,64,512]{2,1,0:T(8,128)(2,1)S(1)}, bf16[4,64,512]{2,1,0:T(8,128)(2,1)S(1)}, u32[]{:S(2)}, u32[]{:S(2)}) collective-permute-start(bf16[4,64,512]{2,1,0:T(8,128)(2,1)S(1)} %copy-done.23), channel_id=1, source_target_pairs={{0,6},{1,7},{2,4},{3,5},{4,2},{5,3},{6,0},{7,1},{8,14},{9,15},{10,... | collective-permute-start | bytes 786440 | tf_op jit(solution)/shard_map/ppermute | solution.py:257
  65.6 50.1 %collective-permute-start.10 = (bf16[4,192,512]{2,1,0:T(8,128)(2,1)}, bf16[4,192,512]{2,1,0:T(8,128)(2,1)S(1)}, u32[]{:S(2)}, u32[]{:S(2)}) collective-permute-start(bf16[4,192,512]{2,1,0:T(8,128)(2,1)} %get-tuple-element.105), channel_id=1, source_target_pairs={{0,1},{1,0},{2,3},{3,2},{4,5},{5,4},{6,7},{7,6},{8,9},{9,8},{10,11... | collective-permute-start | bytes 2359304 | tf_op jit(solution)/shard_map/ppermute | solution.py:257
  65.6 69.9 %collective-permute-start.11 = (bf16[4,192,512]{2,1,0:T(8,128)(2,1)}, bf16[4,192,512]{2,1,0:T(8,128)(2,1)}, u32[]{:S(2)}, u32[]{:S(2)}) collective-permute-start(bf16[4,192,512]{2,1,0:T(8,128)(2,1)} %get-tuple-element.107), channel_id=1, source_target_pairs={{0,2},{1,3},{2,0},{3,1},{4,6},{5,7},{6,4},{7,5},{8,10},{9,11},{10,... | collective-permute-start | bytes 2359304 | tf_op jit(solution)/shard_map/ppermute | solution.py:257
  73.3 40.2 %collective-permute-start.7 = (bf16[4,64,512]{2,1,0:T(8,128)(2,1)S(1)}, bf16[4,64,512]{2,1,0:T(8,128)(2,1)S(1)}, u32[]{:S(2)}, u32[]{:S(2)}) collective-permute-start(bf16[4,64,512]{2,1,0:T(8,128)(2,1)S(1)} %get-tuple-element.99), channel_id=1, source_target_pairs={{0,5},{1,4},{2,7},{3,6},{4,1},{5,0},{6,3},{7,2},{8,13},{9,12},{10,... | collective-permute-start | bytes 786440 | tf_op jit(solution)/shard_map/ppermute | solution.py:257
  87.4 30.4 %collective-permute-start.14 = (bf16[4,64,512]{2,1,0:T(8,128)(2,1)S(1)}, bf16[4,64,512]{2,1,0:T(8,128)(2,1)S(1)}, u32[]{:S(2)}, u32[]{:S(2)}) collective-permute-start(bf16[4,64,512]{2,1,0:T(8,128)(2,1)S(1)} %get-tuple-element.113), channel_id=1, source_target_pairs={{0,7},{1,6},{2,5},{3,4},{4,3},{5,2},{6,1},{7,0},{8,15},{9,14},{10,... | collective-permute-start | bytes 786440 | tf_op jit(solution)/shard_map/ppermute | solution.py:257
  113.4 22.0 %collective-permute-start.8 = (bf16[4,64,512]{2,1,0:T(8,128)(2,1)}, bf16[4,64,512]{2,1,0:T(8,128)(2,1)S(1)}, u32[]{:S(2)}, u32[]{:S(2)}) collective-permute-start(bf16[4,64,512]{2,1,0:T(8,128)(2,1)} %get-tuple-element.100), channel_id=1, source_target_pairs={{0,4},{1,5},{2,6},{3,7},{4,0},{5,1},{6,2},{7,3},{8,12},{9,13},{10,... | collective-permute-start | bytes 786440 | tf_op jit(solution)/shard_map/ppermute | solution.py:257
  113.8 28.8 %collective-permute-start.13 = (bf16[4,64,512]{2,1,0:T(8,128)(2,1)S(1)}, bf16[4,64,512]{2,1,0:T(8,128)(2,1)}, u32[]{:S(2)}, u32[]{:S(2)}) collective-permute-start(bf16[4,64,512]{2,1,0:T(8,128)(2,1)S(1)} %get-tuple-element.111), channel_id=1, source_target_pairs={{0,6},{1,7},{2,4},{3,5},{4,2},{5,3},{6,0},{7,1},{8,14},{9,15},{10,... | collective-permute-start | bytes 786440 | tf_op jit(solution)/shard_map/ppermute | solution.py:257
  115.7 40.5 %collective-permute-start.17 = (bf16[4,128,512]{2,1,0:T(8,128)(2,1)}, bf16[4,128,512]{2,1,0:T(8,128)(2,1)S(1)}, u32[]{:S(2)}, u32[]{:S(2)}) collective-permute-start(bf16[4,128,512]{2,1,0:T(8,128)(2,1)} %get-tuple-element.121), channel_id=1, source_target_pairs={{0,2},{1,3},{2,0},{3,1},{4,6},{5,7},{6,4},{7,5},{8,10},{9,11},{10,... | collective-permute-start | bytes 1572872 | tf_op jit(solution)/shard_map/ppermute | solution.py:257
  117.8 38.5 %collective-permute-start.19 = (bf16[4,64,512]{2,1,0:T(8,128)(2,1)}, bf16[4,64,512]{2,1,0:T(8,128)(2,1)S(1)}, u32[]{:S(2)}, u32[]{:S(2)}) collective-permute-start(bf16[4,64,512]{2,1,0:T(8,128)(2,1)} %get-tuple-element.125), channel_id=1, source_target_pairs={{0,5},{1,4},{2,7},{3,6},{4,1},{5,0},{6,3},{7,2},{8,13},{9,12},{10,... | collective-permute-start | bytes 786440 | tf_op jit(solution)/shard_map/ppermute | solution.py:257
  135.5 42.5 %collective-permute-start.15 = (bf16[4,128,512]{2,1,0:T(8,128)(2,1)}, bf16[4,128,512]{2,1,0:T(8,128)(2,1)S(1)}, u32[]{:S(2)}, u32[]{:S(2)}) collective-permute-start(bf16[4,128,512]{2,1,0:T(8,128)(2,1)} %get-tuple-element.116), channel_id=1, source_target_pairs={{0,1},{1,0},{2,3},{3,2},{4,5},{5,4},{6,7},{7,6},{8,9},{9,8},{10,11... | collective-permute-start | bytes 1572872 | tf_op jit(solution)/shard_map/ppermute | solution.py:257
  135.5 32.7 %collective-permute-start.18 = (bf16[4,128,512]{2,1,0:T(8,128)(2,1)}, bf16[4,128,512]{2,1,0:T(8,128)(2,1)S(1)}, u32[]{:S(2)}, u32[]{:S(2)}) collective-permute-start(bf16[4,128,512]{2,1,0:T(8,128)(2,1)} %get-tuple-element.123), channel_id=1, source_target_pairs={{0,3},{1,2},{2,1},{3,0},{4,7},{5,6},{6,5},{7,4},{8,11},{9,10},{10,... | collective-permute-start | bytes 1572872 | tf_op jit(solution)/shard_map/ppermute | solution.py:257
  156.2 34.5 %collective-permute-start.22 = (bf16[4,128,512]{2,1,0:T(8,128)(2,1)}, bf16[4,128,512]{2,1,0:T(8,128)(2,1)S(1)}, u32[]{:S(2)}, u32[]{:S(2)}) collective-permute-start(bf16[4,128,512]{2,1,0:T(8,128)(2,1)} %get-tuple-element.133), channel_id=1, source_target_pairs={{0,3},{1,2},{2,1},{3,0},{4,7},{5,6},{6,5},{7,4},{8,11},{9,10},{10,... | collective-permute-start | bytes 1572872 | tf_op jit(solution)/shard_map/ppermute | solution.py:257
  159.3 33.3 %collective-permute-start.21 = (bf16[4,64,512]{2,1,0:T(8,128)(2,1)}, bf16[4,64,512]{2,1,0:T(8,128)(2,1)}, u32[]{:S(2)}, u32[]{:S(2)}) collective-permute-start(bf16[4,64,512]{2,1,0:T(8,128)(2,1)} %get-tuple-element.129), channel_id=1, source_target_pairs={{0,7},{1,6},{2,5},{3,4},{4,3},{5,2},{6,1},{7,0},{8,15},{9,14},{10,... | collective-permute-start | bytes 786440 | tf_op jit(solution)/shard_map/ppermute | solution.py:257
  168.2 27.0 %collective-permute-start.20 = (bf16[4,64,512]{2,1,0:T(8,128)(2,1)}, bf16[4,64,512]{2,1,0:T(8,128)(2,1)}, u32[]{:S(2)}, u32[]{:S(2)}) collective-permute-start(bf16[4,64,512]{2,1,0:T(8,128)(2,1)} %get-tuple-element.127), channel_id=1, source_target_pairs={{0,6},{1,7},{2,4},{3,5},{4,2},{5,3},{6,0},{7,1},{8,14},{9,15},{10,... | collective-permute-start | bytes 786440 | tf_op jit(solution)/shard_map/ppermute | solution.py:257
  178.0 39.5 %collective-permute-start.25 = (bf16[4,128,512]{2,1,0:T(8,128)(2,1)}, bf16[4,128,512]{2,1,0:T(8,128)(2,1)}, u32[]{:S(2)}, u32[]{:S(2)}) collective-permute-start(bf16[4,128,512]{2,1,0:T(8,128)(2,1)} %get-tuple-element.139), channel_id=1, source_target_pairs={{0,1},{1,0},{2,3},{3,2},{4,5},{5,4},{6,7},{7,6},{8,9},{9,8},{10,11... | collective-permute-start | bytes 1572872 | tf_op jit(solution)/shard_map/ppermute | solution.py:257
  178.0 50.7 %collective-permute-start.16 = (bf16[4,128,512]{2,1,0:T(8,128)(2,1)}, bf16[4,128,512]{2,1,0:T(8,128)(2,1)S(1)}, u32[]{:S(2)}, u32[]{:S(2)}) collective-permute-start(bf16[4,128,512]{2,1,0:T(8,128)(2,1)} %get-tuple-element.117), channel_id=1, source_target_pairs={{0,2},{1,3},{2,0},{3,1},{4,6},{5,7},{6,4},{7,5},{8,10},{9,11},{10,... | collective-permute-start | bytes 1572872 | tf_op jit(solution)/shard_map/ppermute | solution.py:257
  195.2 22.3 %collective-permute-start.26 = (bf16[4,64,512]{2,1,0:T(8,128)(2,1)}, bf16[4,64,512]{2,1,0:T(8,128)(2,1)S(1)}, u32[]{:S(2)}, u32[]{:S(2)}) collective-permute-start(bf16[4,64,512]{2,1,0:T(8,128)(2,1)} %get-tuple-element.141), channel_id=1, source_target_pairs={{0,5},{1,4},{2,7},{3,6},{4,1},{5,0},{6,3},{7,2},{8,13},{9,12},{10,... | collective-permute-start | bytes 786440 | tf_op jit(solution)/shard_map/ppermute | solution.py:257
  200.8 24.2 %collective-permute-start.27 = (bf16[4,64,512]{2,1,0:T(8,128)(2,1)S(1)}, bf16[4,64,512]{2,1,0:T(8,128)(2,1)S(1)}, u32[]{:S(2)}, u32[]{:S(2)}) collective-permute-start(bf16[4,64,512]{2,1,0:T(8,128)(2,1)S(1)} %copy-done.19), channel_id=1, source_target_pairs={{0,7},{1,6},{2,5},{3,4},{4,3},{5,2},{6,1},{7,0},{8,15},{9,14},{10,... | collective-permute-start | bytes 786440 | tf_op jit(solution)/shard_map/ppermute | solution.py:257
  201.8 29.5 %collective-permute-start.23 = (bf16[4,64,512]{2,1,0:T(8,128)(2,1)S(1)}, bf16[4,64,512]{2,1,0:T(8,128)(2,1)S(1)}, u32[]{:S(2)}, u32[]{:S(2)}) collective-permute-start(bf16[4,64,512]{2,1,0:T(8,128)(2,1)S(1)} %copy-done.18), channel_id=1, source_target_pairs={{0,6},{1,7},{2,4},{3,5},{4,2},{5,3},{6,0},{7,1},{8,14},{9,15},{10,... | collective-permute-start | bytes 786440 | tf_op jit(solution)/shard_map/ppermute | solution.py:257
  (35 other events, 449.2 us)
